TPU v7x, 128 devices: a whole 4x4x4 slice. The times are simulated.
128 devices in a mesh: seed: 8 (over y, z_hi), tok: 16 (over z_lo, x, core).
Axes of the slice: x: 4, y: 4, z: 4 (z_hi: 2, z_lo: 2; z = z_hi * 2 + z_lo), core: 2. Of those that a mesh axis runs over, the one named last changes fastest.
Arguments:
- atom_feats: bfloat16 [16384, 16, 128], P('tok', 'seed'), may hold values from -6 to 6
- atom_index: int32 [16384], P('tok'), may hold values from 0 to 2047, as said below
- token_cond: bfloat16 [2048, 768], P('tok'), may hold values from -6 to 6
- pair_bias: bfloat16 [16, 2048, 2048], P('seed', 'tok'), may hold values from -8 to 248
- atom_bias_enc: bfloat16 [16384, 4, 128], P('tok'), may hold values from -8 to 248
- atom_bias_dec: bfloat16 [16384, 4, 128], P('tok'), may hold values from -8 to 248
- enc_project: bfloat16 [128, 384], replicated, may hold values from -0.5 to 0.5
- enc_mix: bfloat16 [128, 128], replicated, may hold values from -0.5 to 0.5
- pool_weight: bfloat16 [128, 768], replicated, may hold values from -0.5 to 0.5
- token_project: bfloat16 [768, 3072], replicated, may hold values from -0.21875 to 0.21875
- token_mix: bfloat16 [768, 768], replicated, may hold values from -0.21875 to 0.21875
- swiglu_in: bfloat16 [768, 3072], replicated, may hold values from -0.21875 to 0.21875
- swiglu_out: bfloat16 [1536, 768], replicated, may hold values from -0.15625 to 0.15625
- spread_weight: bfloat16 [768, 128], replicated, may hold values from -0.21875 to 0.21875
- dec_project: bfloat16 [128, 384], replicated, may hold values from -0.5 to 0.5
- dec_mix: bfloat16 [128, 128], replicated, may hold values from -0.5 to 0.5
Outputs:
- token_state: bfloat16 [2048, 16, 768], P('tok', 'seed')
- atom_update: bfloat16 [16384, 16, 128], P('tok', 'seed')
Inputs may be any that keep to these rules, and one draw needn't show every extreme that they name: `atom_index`: Nondecreasing. The atoms of token t are rows 8 t + e(t) to 8 (t + 1) + e(t + 1) - 1, every e between -3 and 3, e(0) = e(2048) = 0, and e(t) between -3 and -2 for every other t that is a multiple of 128; so every token has 2 to 14 atoms.
All inputs are finite; a program needn't handle non-finite values.
Results may differ from a plain program's by a relative error of at most 0.015.
Values may be sent and summed in bfloat16 or wider, within the bound.
No kernel may reach another device: no remote copies, remote signals or barrier semaphores. Data moves between devices by JAX's collectives and lax.ppermute only.
A program may use at most 192 MiB of HBM per device.

v0:
```python
import jax
import jax.numpy as jnp
from jax import lax
from jax.sharding import PartitionSpec as P

HEADS = 16
QUERY_BLOCK = 32


EPS = 1e-05
NEGATIVE = -1000000000.0


def padded_2(block, sides, width):
    for axis, dim in sides:
        count = lax.axis_size(axis)
        forward = [(i, i + 1) for i in range(count - 1)]
        backward = [(target, source) for source, target in forward]
        low = lax.ppermute(
            lax.slice_in_dim(block, block.shape[dim] - width, None, axis=dim), axis, forward
        )
        high = lax.ppermute(lax.slice_in_dim(block, 0, width, axis=dim), axis, backward)
        block = jnp.concatenate([low, block, high], axis=dim)
    return block


def shifted(shard, axis, by):
    length = lax.axis_size(axis)
    pairs = [(i, i + by) for i in range(length) if 0 <= i + by < length]
    return lax.ppermute(shard, axis, pairs)


def layer_norm(values):
    centre = values - jnp.mean(values, axis=-1, keepdims=True)
    variance = jnp.mean(centre * centre, axis=-1, keepdims=True)
    return centre * lax.rsqrt(variance + EPS)


def atom_block(inputs, bias, project, mix):
    atom_rows, seed_count, atom_width = inputs.shape
    head_count = bias.shape[1]
    window_size = bias.shape[2]
    head_size = atom_width // head_count
    query_block = QUERY_BLOCK
    margin = (window_size - query_block) // 2
    block_count = atom_rows // query_block
    extra_tiles = window_size // query_block - 1
    normed = layer_norm(inputs.astype(jnp.float32)).astype(jnp.bfloat16)
    packed = jnp.dot(
        normed.reshape(atom_rows * seed_count, atom_width),
        project,
        preferred_element_type=jnp.float32,
    )
    packed = packed.astype(jnp.bfloat16).reshape(atom_rows, seed_count, 3 * atom_width)
    queries = packed[:, :, :atom_width].reshape(
        block_count, query_block, seed_count, head_count, head_size
    )
    padded = padded_2(packed[:, :, atom_width:], (("tok", 0),), margin)
    key_tiles = padded.reshape(block_count + extra_tiles, query_block, seed_count, 2 * atom_width)
    windows = jnp.concatenate(
        [key_tiles[offset : offset + block_count] for offset in range(extra_tiles + 1)], axis=1
    )
    key_rows = windows[..., :atom_width].reshape(
        block_count, window_size, seed_count, head_count, head_size
    )
    value_rows = windows[..., atom_width:].reshape(
        block_count, window_size, seed_count, head_count, head_size
    )
    scores = jnp.einsum(
        "bqshd,bkshd->bshqk", queries, key_rows, preferred_element_type=jnp.float32
    ) * head_size ** (-0.5)
    scores = (
        scores
        + bias.astype(jnp.float32)
        .reshape(block_count, query_block, head_count, window_size)
        .transpose(0, 2, 1, 3)[:, None]
    )
    first_atom = lax.axis_index("tok") * atom_rows
    position = (
        first_atom
        + query_block * jnp.arange(block_count, dtype=jnp.int32)[:, None]
        - margin
        + jnp.arange(window_size, dtype=jnp.int32)[None, :]
    )
    in_range = (position >= 0) & (position < atom_rows * lax.axis_size("tok"))
    scores = jnp.where(in_range[:, None, None, None, :], scores, NEGATIVE)
    row_max = jnp.max(scores, axis=-1, keepdims=True)
    weights = jnp.exp(scores - row_max)
    attended_atoms = jnp.einsum(
        "bshqk,bkshd->bqshd",
        weights.astype(jnp.bfloat16),
        value_rows,
        preferred_element_type=jnp.float32,
    )
    attended_atoms = attended_atoms / jnp.sum(weights, axis=-1).transpose(0, 3, 1, 2)[..., None]
    attended_atoms = attended_atoms.reshape(atom_rows * seed_count, atom_width).astype(jnp.bfloat16)
    update = jnp.dot(attended_atoms, mix, preferred_element_type=jnp.float32).reshape(
        atom_rows, seed_count, atom_width
    )
    return (inputs.astype(jnp.float32) + update).astype(jnp.bfloat16)


def token_attention(queries, key_rows, value_rows, bias):
    tok_rows, seed_count, head_count, head_size = queries.shape
    scale = head_size ** (-0.5)
    running_max = jnp.full((seed_count, head_count, tok_rows), NEGATIVE, jnp.float32)
    piece_keys = lax.all_gather(key_rows, "tok", axis=0, tiled=True)
    piece_values = lax.all_gather(value_rows, "tok", axis=0, tiled=True)
    bias_part = bias.astype(jnp.float32)
    scores = (
        jnp.einsum("qshd,kshd->shqk", queries, piece_keys, preferred_element_type=jnp.float32)
        * scale
        + bias_part[None]
    )
    new_max = jnp.maximum(running_max, jnp.max(scores, axis=-1))
    weights = jnp.exp(scores - new_max[..., None])
    running_sum = jnp.sum(weights, axis=-1)
    contribution = jnp.einsum(
        "shqk,kshd->shqd",
        weights.astype(jnp.bfloat16),
        piece_values,
        preferred_element_type=jnp.float32,
    )
    result = contribution / running_sum[..., None]
    return result.transpose(2, 0, 1, 3)


def per_device(
    atom_feats,
    atom_index,
    token_cond,
    pair_bias,
    atom_bias_enc,
    atom_bias_dec,
    enc_project,
    enc_mix,
    pool_weight,
    token_project,
    token_mix,
    swiglu_in,
    swiglu_out,
    spread_weight,
    dec_project,
    dec_mix,
):
    atom_rows, seed_count, atom_width = atom_feats.shape
    tok_rows, token_width = token_cond.shape
    head_count = HEADS
    head_size = token_width // head_count
    edge_rows = min(8, tok_rows)
    span_rows = tok_rows + edge_rows
    base_token = lax.axis_index("tok") * tok_rows
    encoded = atom_block(atom_feats, atom_bias_enc, enc_project, enc_mix)
    lifted = jnp.dot(
        encoded.reshape(atom_rows * seed_count, atom_width),
        pool_weight,
        preferred_element_type=jnp.float32,
    )
    lifted = (
        jnp.maximum(lifted, 0.0).astype(jnp.bfloat16).reshape(atom_rows, seed_count * token_width)
    )
    chosen = (
        atom_index[None, :] - base_token == jnp.arange(span_rows, dtype=jnp.int32)[:, None]
    ).astype(jnp.bfloat16)
    pool_terms = jnp.dot(chosen, lifted, preferred_element_type=jnp.float32)
    tallies = jnp.sum(chosen.astype(jnp.float32), axis=1)
    from_left = (
        shifted(pool_terms[tok_rows:].astype(jnp.bfloat16), "tok", 1).astype(jnp.float32),
        shifted(tallies[tok_rows:].astype(jnp.bfloat16), "tok", 1).astype(jnp.float32),
    )
    inner_rows = tok_rows - edge_rows
    pooled_sums = pool_terms[:tok_rows] + jnp.pad(from_left[0], ((0, inner_rows), (0, 0)))
    counts = tallies[:tok_rows] + jnp.pad(from_left[1], (0, inner_rows))
    residual = (
        token_cond.astype(jnp.float32)[:, None, :]
        + pooled_sums.reshape(tok_rows, seed_count, token_width) / counts[:, None, None]
    )
    normed = layer_norm(residual).astype(jnp.bfloat16).reshape(tok_rows * seed_count, token_width)
    projected = jnp.dot(normed, token_project, preferred_element_type=jnp.float32).reshape(
        tok_rows, seed_count, 4, head_count, head_size
    )
    queries = projected[:, :, 0].astype(jnp.bfloat16)
    key_rows = projected[:, :, 1].astype(jnp.bfloat16)
    value_rows = projected[:, :, 2].astype(jnp.bfloat16)
    gate_open = jax.nn.sigmoid(projected[:, :, 3])
    whole_bias = lax.all_gather(pair_bias, "seed", axis=0, tiled=True)
    attended = token_attention(queries, key_rows, value_rows, whole_bias)
    gated_out = (
        (attended * gate_open).astype(jnp.bfloat16).reshape(tok_rows * seed_count, token_width)
    )
    residual = residual + jnp.dot(gated_out, token_mix, preferred_element_type=jnp.float32).reshape(
        tok_rows, seed_count, token_width
    )
    normed = layer_norm(residual).astype(jnp.bfloat16).reshape(tok_rows * seed_count, token_width)
    widened = jnp.dot(normed, swiglu_in, preferred_element_type=jnp.float32)
    inner_width = swiglu_out.shape[0]
    hidden = (jax.nn.silu(widened[:, :inner_width]) * widened[:, inner_width:]).astype(jnp.bfloat16)
    lowered = jnp.dot(hidden, swiglu_out, preferred_element_type=jnp.float32).reshape(
        tok_rows, seed_count, token_width
    )
    token_state = (residual + lowered).astype(jnp.bfloat16)
    spread = jnp.dot(
        token_state.reshape(tok_rows * seed_count, token_width),
        spread_weight,
        preferred_element_type=jnp.float32,
    )
    spread = spread.astype(jnp.bfloat16).reshape(tok_rows, seed_count * atom_width)
    upper = shifted(spread[:edge_rows], "tok", -1)
    beside_all = jnp.concatenate([spread, upper], axis=0)
    picker = (
        atom_index[:, None] - base_token == jnp.arange(span_rows, dtype=jnp.int32)[None, :]
    ).astype(jnp.bfloat16)
    carried = jnp.dot(picker, beside_all, preferred_element_type=jnp.float32)
    decoded_in = (
        encoded.astype(jnp.float32) + carried.reshape(atom_rows, seed_count, atom_width)
    ).astype(jnp.bfloat16)
    atom_update = atom_block(decoded_in, atom_bias_dec, dec_project, dec_mix)
    return (token_state, atom_update)


def solution(mesh):
    placed = (
        P("tok", "seed", None),
        P("tok"),
        P("tok", None),
        P("seed", "tok", None),
        P("tok", None, None),
        P("tok", None, None),
        P(),
        P(),
        P(),
        P(),
        P(),
        P(),
        P(),
        P(),
        P(),
        P(),
    )
    return jax.shard_map(
        per_device,
        mesh=mesh,
        in_specs=placed,
        out_specs=(P("tok", "seed", None), P("tok", "seed", None)),
        check_vma=False,
    )
```

profile of v0, /device:TPU:7, one launch (start us, length us, event | category | flops | bytes accessed | tf_op | source)
XLA Modules:
  0.0 378.8 jit_solution(9175183054705026711)
XLA Ops:
  26.6 6.2 %collective-permute-start.3 = (bf16[8]{0:T(256)(128)(2,1)S(1)}, bf16[8]{0:T(256)(128)(2,1)S(1)}, u32[]{:S(2)}, u32[]{:S(2)}) collective-permute-start(bf16[8]{0:T(256)(128)(2,1)S(1)} %slice.154), channel_id=1, source_target_pairs={{0,1},{1,2},{2,3},{3,4},{4,5},{5,6},{6,7},{7,8},{8,9},{9,10},{10,1... | collective-permute-start | bytes 56 | tf_op jit(solution)/shard_map/ppermute | solution.py:30
  40.9 6.8 %copy.124 = bf16[768,3072]{0,1:T(8,128)(2,1)} copy(bf16[768,3072]{1,0:T(8,128)(2,1)} %param.25) | data formatting | bytes 9437184 | tf_op args[9]
  47.7 13.9 %fusion.63 = (bf16[1024,2,256]{2,1,0:T(2,128)(2,1)}, bf16[1024,2,256]{2,1,0:T(2,128)(2,1)}, bf16[1024,2,256]{2,1,0:T(2,128)(2,1)}, bf16[1024,2,256]{2,1,0:T(2,128)(2,1)}) fusion(bf16[48,2,256]{2,1,0:T(2,128)(2,1)} %collective-permute-done, bf16[1024,2,256]{2,1,0:T(2,128)(2,1)S(1)} %slice-done, bf16[48,2,256]{2,1,0:T(2,128)(2,1)} %collective-permute-done.1), kind=kLoop, calls=%fused_computation.76 | loop fusion | flops 2097152 | bytes 5341184 | tf_op jit(solution)/shard_map/concatenate | solution.py:23
  61.7 5.6 %copy.110 = bf16[32,32,2,256]{1,3,2,0:T(8,128)(2,1)} copy(bf16[32,32,2,256]{3,2,1,0:T(2,128)(2,1)} %bitcast.144) | data formatting | bytes 2097152 | tf_op jit(solution)/shard_map/slice | solution.py:61
  67.3 5.8 %copy.111 = bf16[32,32,2,256]{1,3,2,0:T(8,128)(2,1)} copy(bf16[32,32,2,256]{3,2,1,0:T(2,128)(2,1)} %bitcast.142) | data formatting | bytes 2097152 | tf_op jit(solution)/shard_map/slice | solution.py:61
  73.0 5.7 %copy.112 = bf16[32,32,2,256]{1,3,2,0:T(8,128)(2,1)} copy(bf16[32,32,2,256]{3,2,1,0:T(2,128)(2,1)} %bitcast.140) | data formatting | bytes 2097152 | tf_op jit(solution)/shard_map/slice | solution.py:61
  78.7 4.9 %copy.113 = bf16[32,32,2,256]{1,3,2,0:T(8,128)(2,1)} copy(bf16[32,32,2,256]{3,2,1,0:T(2,128)(2,1)S(1)} %bitcast.138) | data formatting | bytes 2097152 | tf_op jit(solution)/shard_map/slice | solution.py:61
  83.6 8.8 %pad_maximum_fusion = bf16[32,128,2,256]{1,3,2,0:T(8,128)(2,1)S(1)} fusion(bf16[32,32,2,256]{1,3,2,0:T(8,128)(2,1)} %copy.113, bf16[32,32,2,256]{1,3,2,0:T(8,128)(2,1)} %copy.112, bf16[32,32,2,256]{1,3,2,0:T(8,128)(2,1)} %copy.111, bf16[32,32,2,256]{1,3,2,0:T(8,128)(2,1)} %copy.110), kind=kLoop, calls=%fused_computation.10 | loop fusion | flops 16777216 | bytes 8388608 | tf_op jit(solution)/shard_map/concatenate | solution.py:60
  112.4 5.6 %reshape.241 = bf16[1024,1536]{1,0:T(8,128)(2,1)} reshape(bf16[2048,768]{1,0:T(8,128)(2,1)} %maximum_convert_fusion) | data formatting | bytes 6291456 | tf_op jit(solution)/shard_map/reshape | solution.py:160
  128.0 5.5 %fusion.105 = (bf16[128,2,4,16,48]{0,4,3,2,1:T(8,128)(2,1)S(1)}, f32[128,2,4,16,48]{0,4,3,2,1:T(8,128)}) fusion(bf16[4,16,48,768,1]{3,2,1,0,4:T(8,128)(2,1)} %bitcast.128, bf16[128,2,768,1,1]{2,1,0,4,3:T(2,128)(2,1)} %bitcast.159), kind=kOutput, calls=%fused_computation.147 | convolution fusion | flops 1208745984 | bytes 9830400 | tf_op jit(solution)/shard_map/dot_general | solution.py:179
  136.4 11.2 %convert_element_type.135 = f32[16,128,2048]{2,1,0:T(8,128)} convert(bf16[16,128,2048]{2,1,0:T(8,128)(2,1)} %all-gather.6.cloned.1.call-done) | non-fusion elementwise | flops 4194304 | bytes 25165824 | tf_op jit(solution)/shard_map/convert_element_type | solution.py:109
  147.6 42.9 %all-gather.8.cloned.1.call-done = bf16[2048,2,1,16,48]{0,4,3,2,1:T(8,128)(2,1)} async-done(((bf16[128,2,1,16,48]{0,4,3,2,1:T(8,128)(2,1)}), bf16[2048,2,1,16,48]{0,4,3,2,1:T(8,128)(2,1)}) %all-gather.8.cloned.1.call-update) | async-done | bytes 6291472 | tf_op jit(solution)/shard_map/all_gather | solution.py:107
  190.6 19.2 %fusion = (f32[2,16,128]{2,1,0:T(8,128)S(1)}, f32[2,16,128,2048]{3,2,1,0:T(8,128)}) fusion(f32[16,128,2048]{2,1,0:T(8,128)} %convert_element_type.135, bf16[2048,2,1,16,48]{0,4,3,2,1:T(8,128)(2,1)} %all-gather.8.cloned.1.call-done, bf16[128,2,4,16,48]{0,4,3,2,1:T(8,128)(2,1)} %copy-done.3), kind=kOutput, calls=%fused_computation.2 | convolution fusion | flops 830468096 | bytes 57032704 | tf_op jit(solution)/shard_map/qshd,kshd->shqk/dot_general | solution.py:111
  209.8 17.9 %fusion.1 = f32[2,16,128]{2,1,0:T(8,128)S(1)} fusion(f32[2,16,128,2048]{3,2,1,0:T(8,128)} %get-tuple-element.41, f32[2,16,128]{2,1,0:T(8,128)S(1)} %broadcast_maximum_fusion, f32[16,128,2048]{2,1,0:T(8,128)} %convert_element_type.135), kind=kLoop, calls=%fused_computation.3 | loop fusion | flops 33550336 | bytes 50364416 | tf_op jit(solution)/shard_map/reduce_sum | solution.py:117
  227.7 16.8 %all-gather.10.cloned.1.call-done = bf16[2048,2,1,16,48]{0,4,3,2,1:T(8,128)(2,1)} async-done(((bf16[128,2,1,16,48]{0,4,3,2,1:T(8,128)(2,1)}), bf16[2048,2,1,16,48]{0,4,3,2,1:T(8,128)(2,1)}) %all-gather.10.cloned.1.call-update) | async-done | bytes 6291472 | tf_op jit(solution)/shard_map/all_gather | solution.py:108
  244.5 19.9 %fusion.55 = bf16[128,2,16,48]{0,3,2,1:T(8,128)(2,1)S(1)} fusion(bf16[2048,2,1,16,48]{0,4,3,2,1:T(8,128)(2,1)} %all-gather.10.cloned.1.call-done, f32[2,16,128,2048]{3,2,1,0:T(8,128)} %get-tuple-element.41, f32[2,16,128]{2,1,0:T(8,128)S(1)} %broadcast_maximum_fusion, f32[16,128,2048]{2,1,0:T(8,128)} %convert_element_type.135, ...), kind=kOutput, calls=%fused_computation.63 | convolution fusion | flops 840040448 | bytes 57835520 | tf_op jit(solution)/shard_map/shqk,kshd->shqd/dot_general | solution.py:118
  281.2 4.8 %collective-permute-done.4 = bf16[8,256]{1,0:T(8,128)(2,1)S(1)} collective-permute-done((bf16[8,256]{1,0:T(8,128)(2,1)S(1)}, bf16[8,256]{1,0:T(8,128)(2,1)S(1)}, u32[]{:S(2)}, u32[]{:S(2)}) %collective-permute-start.4) | collective-permute-done | bytes 4128 | tf_op jit(solution)/shard_map/ppermute | solution.py:30
  295.2 4.5 %reshape.249 = bf16[1024,2,384]{2,1,0:T(2,128)(2,1)} reshape(bf16[2048,384]{1,0:T(8,128)(2,1)} %convolution_convert_fusion) | data formatting | bytes 3145728 | tf_op jit(solution)/shard_map/reshape | solution.py:54
  312.8 11.6 %fusion.61 = (bf16[1024,2,256]{2,1,0:T(2,128)(2,1)}, bf16[1024,2,256]{2,1,0:T(2,128)(2,1)}, bf16[1024,2,256]{2,1,0:T(2,128)(2,1)}, bf16[1024,2,256]{2,1,0:T(2,128)(2,1)}) fusion(bf16[48,2,256]{2,1,0:T(2,128)(2,1)} %collective-permute-done.5, bf16[1024,2,256]{2,1,0:T(2,128)(2,1)} %slice.197, bf16[48,2,256]{2,1,0:T(2,128)(2,1)} %collective-permute-done.6), kind=kLoop, calls=%fused_computation.74 | loop fusion | flops 2097152 | bytes 5341184 | tf_op jit(solution)/shard_map/concatenate | solution.py:23
  324.4 5.6 %copy.132 = bf16[32,32,2,256]{1,3,2,0:T(8,128)(2,1)} copy(bf16[32,32,2,256]{3,2,1,0:T(2,128)(2,1)} %bitcast.145) | data formatting | bytes 2097152 | tf_op jit(solution)/shard_map/slice | solution.py:61
  330.0 5.7 %copy.133 = bf16[32,32,2,256]{1,3,2,0:T(8,128)(2,1)} copy(bf16[32,32,2,256]{3,2,1,0:T(2,128)(2,1)} %bitcast.143) | data formatting | bytes 2097152 | tf_op jit(solution)/shard_map/slice | solution.py:61
  335.7 5.7 %copy.134 = bf16[32,32,2,256]{1,3,2,0:T(8,128)(2,1)} copy(bf16[32,32,2,256]{3,2,1,0:T(2,128)(2,1)} %bitcast.141) | data formatting | bytes 2097152 | tf_op jit(solution)/shard_map/slice | solution.py:61
  341.4 5.6 %copy.135 = bf16[32,32,2,256]{1,3,2,0:T(8,128)(2,1)} copy(bf16[32,32,2,256]{3,2,1,0:T(2,128)(2,1)} %bitcast.139) | data formatting | bytes 2097152 | tf_op jit(solution)/shard_map/slice | solution.py:61
  347.1 8.8 %pad_maximum_fusion.1 = bf16[32,128,2,256]{1,3,2,0:T(8,128)(2,1)S(1)} fusion(bf16[32,32,2,256]{1,3,2,0:T(8,128)(2,1)} %copy.135, bf16[32,32,2,256]{1,3,2,0:T(8,128)(2,1)} %copy.134, bf16[32,32,2,256]{1,3,2,0:T(8,128)(2,1)} %copy.133, bf16[32,32,2,256]{1,3,2,0:T(8,128)(2,1)} %copy.132), kind=kLoop, calls=%fused_computation.11 | loop fusion | flops 16777216 | bytes 8388608 | tf_op jit(solution)/shard_map/concatenate | solution.py:60
  (157 shorter events, 114.8 us)
Async XLA Ops:
  7.2 263.5 %copy-start = (bf16[1536,768]{1,0:T(8,128)(2,1)S(1)}, bf16[1536,768]{1,0:T(8,128)(2,1)}, u32[]{:S(2)}) copy-start(bf16[1536,768]{1,0:T(8,128)(2,1)} %param.28) | copy-start | bytes 7077892
  7.2 129.2 %all-gather.6.cloned.1.call-start = ((), (), s32[]{:S(2)}) async-start(), calls=%async_computation | async-start | bytes 9437184 | tf_op jit(solution)/shard_map/all_gather | solution.py:186
  7.9 182.6 %all-gather.8.cloned.1.call-start = ((), (), s32[]{:S(2)}) async-start(), calls=%async_computation.1 | async-start | bytes 6684672 | tf_op jit(solution)/shard_map/all_gather | solution.py:107
  9.4 17.0 %copy-start.23 = (s32[1024]{0:T(1024)S(1)}, s32[1024]{0:T(1024)}, u32[]{:S(2)}) copy-start(s32[1024]{0:T(1024)} %param.17) | copy-start | bytes 12292
  20.4 27.3 %collective-permute-start = (bf16[48,2,256]{2,1,0:T(2,128)(2,1)S(1)}, bf16[48,2,256]{2,1,0:T(2,128)(2,1)}, u32[]{:S(2)}, u32[]{:S(2)}) collective-permute-start(bf16[48,2,256]{2,1,0:T(2,128)(2,1)S(1)} %get-tuple-element.22), channel_id=1, source_target_pairs={{0,1},{1,2},{2,3},{3,4},{4,5},{5,6},{6,7},{7,8},{8,9},{9,10},{10,1... | collective-permute-start | bytes 147464 | tf_op jit(solution)/shard_map/ppermute | solution.py:19
  24.5 23.2 %collective-permute-start.1 = (bf16[48,2,256]{2,1,0:T(2,128)(2,1)S(1)}, bf16[48,2,256]{2,1,0:T(2,128)(2,1)}, u32[]{:S(2)}, u32[]{:S(2)}) collective-permute-start(bf16[48,2,256]{2,1,0:T(2,128)(2,1)S(1)} %get-tuple-element.23), channel_id=1, source_target_pairs={{1,0},{2,1},{3,2},{4,3},{5,4},{6,5},{7,6},{8,7},{9,8},{10,9},{11,1... | collective-permute-start | bytes 147464 | tf_op jit(solution)/shard_map/ppermute | solution.py:22
  26.6 96.0 %collective-permute-start.3 = (bf16[8]{0:T(256)(128)(2,1)S(1)}, bf16[8]{0:T(256)(128)(2,1)S(1)}, u32[]{:S(2)}, u32[]{:S(2)}) collective-permute-start(bf16[8]{0:T(256)(128)(2,1)S(1)} %slice.154), channel_id=1, source_target_pairs={{0,1},{1,2},{2,3},{3,4},{4,5},{5,6},{6,7},{7,8},{8,9},{9,10},{10,1... | collective-permute-start | bytes 56 | tf_op jit(solution)/shard_map/ppermute | solution.py:30
  40.9 6.8 %slice-start = ((bf16[1024,2,384]{2,1,0:T(2,128)(2,1)}), bf16[1024,2,256]{2,1,0:T(2,128)(2,1)S(1)}, s32[]{:S(2)}) async-start(bf16[1024,2,384]{2,1,0:T(2,128)(2,1)} %reshape.235), calls=%async_computation.3 | async-start | bytes 2097152 | tf_op jit(solution)/shard_map/slice | solution.py:58
  67.3 11.5 %copy-start.13 = (bf16[1024,2,256]{2,1,0:T(2,128)(2,1)S(1)}, bf16[1024,2,256]{2,1,0:T(2,128)(2,1)}, u32[]{:S(2)}) copy-start(bf16[1024,2,256]{2,1,0:T(2,128)(2,1)} %get-tuple-element.34) | copy-start | bytes 3145732
  100.8 6.4 %copy-start.6 = (bf16[1024,2,128]{2,1,0:T(2,128)(2,1)S(1)}, bf16[1024,2,128]{2,1,0:T(2,128)(2,1)}, u32[]{:S(2)}) copy-start(bf16[1024,2,128]{2,1,0:T(2,128)(2,1)} %param.16) | copy-start | bytes 1572868
  100.8 6.4 %copy-start.21 = (bf16[128,128]{1,0:T(8,128)(2,1)S(1)}, bf16[128,128]{1,0:T(8,128)(2,1)}, u32[]{:S(2)}) copy-start(bf16[128,128]{1,0:T(8,128)(2,1)} %param.23) | copy-start | bytes 98308
  118.1 6.6 %copy-start.16 = (f32[128,768]{1,0:T(8,128)S(1)}, f32[128,768]{1,0:T(8,128)}, u32[]{:S(2)}) copy-start(f32[128,768]{1,0:T(8,128)} %convert_element_type.120) | copy-start | bytes 1179652
  120.7 3.1 collective-permute-start.2
  135.6 108.9 %all-gather.10.cloned.1.call-start = ((), (), s32[]{:S(2)}) async-start(), calls=%async_computation.2 | async-start | bytes 6684672 | tf_op jit(solution)/shard_map/all_gather | solution.py:108
  244.5 20.0 %copy-start.8 = (f32[128,2,768]{2,0,1:T(8,128)S(1)}, f32[128,2,768]{2,0,1:T(8,128)}, u32[]{:S(2)}) copy-start(f32[128,2,768]{2,0,1:T(8,128)} %copy-done.7) | copy-start | bytes 2359300
  244.5 20.0 %copy-start.17 = (bf16[768,768]{1,0:T(8,128)(2,1)S(1)}, bf16[768,768]{1,0:T(8,128)(2,1)}, u32[]{:S(2)}) copy-start(bf16[768,768]{1,0:T(8,128)(2,1)} %param.26) | copy-start | bytes 3538948
  276.3 13.7 %copy-start.12 = (bf16[1024,2,128]{2,0,1:T(8,128)(2,1)S(1)}, bf16[1024,2,128]{2,0,1:T(8,128)(2,1)}, u32[]{:S(2)}) copy-start(bf16[1024,2,128]{2,0,1:T(8,128)(2,1)} %copy-done.11) | copy-start | bytes 1572868
  276.7 10.7 %copy-start.15 = (bf16[128,2,768]{2,1,0:T(2,128)(2,1)}, bf16[128,2,768]{2,1,0:T(2,128)(2,1)S(1)}, u32[]{:S(2)}) copy-start(bf16[128,2,768]{2,1,0:T(2,128)(2,1)S(1)} %copy.141) | copy-start | bytes 1179652
  278.9 14.5 %copy-start.20 = (bf16[128,384]{1,0:T(8,128)(2,1)S(1)}, bf16[128,384]{1,0:T(8,128)(2,1)}, u32[]{:S(2)}) copy-start(bf16[128,384]{1,0:T(8,128)(2,1)} %param.30) | copy-start | bytes 294916
  279.0 7.0 %collective-permute-start.4 = (bf16[8,256]{1,0:T(8,128)(2,1)S(1)}, bf16[8,256]{1,0:T(8,128)(2,1)S(1)}, u32[]{:S(2)}, u32[]{:S(2)}) collective-permute-start(bf16[8,256]{1,0:T(8,128)(2,1)S(1)} %slice.162), channel_id=1, source_target_pairs={{1,0},{2,1},{3,2},{4,3},{5,4},{6,5},{7,6},{8,7},{9,8},{10,9},{11,1... | collective-permute-start | bytes 12296 | tf_op jit(solution)/shard_map/ppermute | solution.py:30
  299.7 11.1 %slice-start.1 = ((bf16[1024,2,384]{2,1,0:T(2,128)(2,1)}), bf16[1024,2,128]{2,1,0:T(2,128)(2,1)S(1)}, s32[]{:S(2)}) async-start(bf16[1024,2,384]{2,1,0:T(2,128)(2,1)} %reshape.249), calls=%async_computation.4 | async-start | bytes 1048576 | tf_op jit(solution)/shard_map/slice | solution.py:55
  300.7 12.1 %collective-permute-start.5 = (bf16[48,2,256]{2,1,0:T(2,128)(2,1)S(1)}, bf16[48,2,256]{2,1,0:T(2,128)(2,1)}, u32[]{:S(2)}, u32[]{:S(2)}) collective-permute-start(bf16[48,2,256]{2,1,0:T(2,128)(2,1)S(1)} %get-tuple-element.18), channel_id=1, source_target_pairs={{0,1},{1,2},{2,3},{3,4},{4,5},{5,6},{6,7},{7,8},{8,9},{9,10},{10,1... | collective-permute-start | bytes 147464 | tf_op jit(solution)/shard_map/ppermute | solution.py:19
  302.6 10.2 %collective-permute-start.6 = (bf16[48,2,256]{2,1,0:T(2,128)(2,1)S(1)}, bf16[48,2,256]{2,1,0:T(2,128)(2,1)}, u32[]{:S(2)}, u32[]{:S(2)}) collective-permute-start(bf16[48,2,256]{2,1,0:T(2,128)(2,1)S(1)} %get-tuple-element.19), channel_id=1, source_target_pairs={{1,0},{2,1},{3,2},{4,3},{5,4},{6,5},{7,6},{8,7},{9,8},{10,9},{11,1... | collective-permute-start | bytes 147464 | tf_op jit(solution)/shard_map/ppermute | solution.py:22
  364.2 6.2 %copy-start.22 = (bf16[128,128]{1,0:T(8,128)(2,1)S(1)}, bf16[128,128]{1,0:T(8,128)(2,1)}, u32[]{:S(2)}) copy-start(bf16[128,128]{1,0:T(8,128)(2,1)} %param.31) | copy-start | bytes 98308
  (12 other events, 27.5 us)
Sparse Core Ops, SparseCore 0:
  10.4 111.1 all-gather.5
  135.7 54.7 all-gather.7
  192.2 52.2 all-gather.9
where the time goes:
time: 386 us; the launch traced here: 379 us
  local copies, waits for them, and re-layouts  117 us (30%)
  other arithmetic  88.7 us (23%)
  matrix products  70.8 us (18%)
  waiting for transfers between devices  67.1 us (17%)
  starting transfers between devices  20.7 us (5%)
  between operations  14.6 us (4%)
    slice x8, local copies, waits for them, and re-layouts, atom_block(): key_tiles[offset:offset + block_count]  44.6 us
    all_gather x1, waiting for transfers between devices, token_attention(): piece_keys = lax.all_gather(key_rows, 'tok', axis=0, tiled=True)  42.9 us
    concatenate x2, other arithmetic, padded_2(): block = jnp.concatenate([low, block, high], axis=dim)  25.5 us
    dot_general x1, matrix products, token_attention(): jnp.einsum('shqk,kshd->shqd', weights.astype(jnp.bfloat16), piece_values,...  19.9 us
    dot_general x1, matrix products, token_attention(): jnp.einsum('qshd,kshd->shqk', queries, piece_keys, preferred_element_type...  19.2 us
    reduce_sum x1, other arithmetic, token_attention(): running_sum = jnp.sum(weights, axis=-1)  17.9 us
    concatenate x2, other arithmetic, atom_block(): jnp.concatenate([key_tiles[offset:offset + block_count] for offset in ran...  17.6 us
    unnamed x55, local copies, waits for them, and re-layouts  17.1 us
  transfers between devices with their start and end apart: 10, of which 4 were waited for; matrix products, arithmetic and copies ran while one was open for 43% of the time, Pallas kernels for 0%

commit v1 on v0

v1 whole, which is shorter than its diff:
```python
import functools

import jax
import jax.numpy as jnp
from jax import lax
from jax.experimental import pallas as pl
from jax.experimental.pallas import tpu as pltpu
from jax.sharding import PartitionSpec as P

EPS = 1e-05
NEG = -1000000000.0
F32 = jnp.float32
BF16 = jnp.bfloat16

SEEDS = 2
ATOMS = 1024
TOKS = 128
CA = 128
CT = 768
HEADS = 16
HEAD = 48
PAIR = 96
GROUPS = 8
QB = 32
WIN = 128
MARGIN = 48
LOWER = 80
EXT = 1152
EDGE = 16
TRANS = 1536
ALL_TOKS = 2048
ALL_ATOMS = 16384


def params(limit_mb, **more):
    return pltpu.CompilerParams(vmem_limit_bytes=limit_mb * 1024 * 1024, **more)


def vmem(n):
    return [pl.BlockSpec(memory_space=pltpu.VMEM)] * n


def layer_norm(values):
    centre = values - jnp.mean(values, axis=-1, keepdims=True)
    variance = jnp.mean(centre * centre, axis=-1, keepdims=True)
    return centre * lax.rsqrt(variance + EPS)


def dot(a, b):
    return jnp.dot(a, b, preferred_element_type=F32)


def dot_t(a, b):
    return lax.dot_general(a, b, (((1,), (1,)), ((), ())), preferred_element_type=F32)


def window_blocks(packed, bias, mixed, blocks, first_atom, unroll):
    lane_head = lax.broadcasted_iota(jnp.int32, (QB, CA), 1) // 32
    lane = lax.broadcasted_iota(jnp.int32, (1, WIN), 1)

    def body(b, carry):
        rows = pl.multiple_of(b * QB, QB)
        query_rows = pl.multiple_of(b * QB + MARGIN, 16)
        bias_rows = pl.multiple_of(b * 4 * QB, 4 * QB)
        added = jnp.concatenate(
            [bias[pl.ds(bias_rows + h, QB, stride=4), :] for h in range(4)], axis=0
        )
        position = lane + (first_atom + b * QB)
        inside = (position >= 0) & (position < ALL_ATOMS)
        added = jnp.where(inside, added, NEG)
        for seed in range(SEEDS):
            query = packed[seed, pl.ds(query_rows, QB), 0:CA]
            key = packed[seed, pl.ds(rows, WIN), CA : 2 * CA]
            value = packed[seed, pl.ds(rows, WIN), 2 * CA : 3 * CA]
            stacked = jnp.concatenate(
                [jnp.where(lane_head == h, query, jnp.zeros_like(query)) for h in range(4)], axis=0
            )
            scores = dot_t(stacked, key) * (32**-0.5)
            scores = jnp.where(inside, scores + added, NEG)
            top = jnp.max(scores, axis=-1, keepdims=True)
            weights = jnp.exp(scores - top)
            total = jnp.sum(weights, axis=-1, keepdims=True)
            out = dot(weights.astype(BF16), value) / total
            joined = jnp.zeros((QB, CA), F32)
            for h in range(4):
                joined = joined + jnp.where(lane_head == h, out[h * QB : (h + 1) * QB], 0.0)
            mixed[seed, pl.ds(rows, QB), :] = joined.astype(BF16)
        return carry

    lax.fori_loop(0, blocks, body, 0, unroll=unroll)


def encode_kernel(
    tok, feats, low, high, bias, index, cond, project, mix, pool,
    encoded, residual, normed,
    rows, bias32, packed, mixed, ext,
):
    rows[0 : 2 * LOWER] = low[0 : 2 * LOWER].astype(F32)
    rows[2 * LOWER : 2 * (LOWER + ATOMS)] = feats[...].astype(F32)
    rows[2 * (LOWER + ATOMS) : 2 * EXT] = high[0 : 2 * MARGIN].astype(F32)
    bias32[0 : 4 * QB] = low[2 * LOWER : 2 * LOWER + 4 * QB].astype(F32)
    bias32[4 * QB :] = bias[...].astype(F32)
    for seed in range(SEEDS):
        values = rows[pl.ds(seed, EXT, stride=2), :]
        packed[seed] = dot(layer_norm(values).astype(BF16), project[...]).astype(BF16)
    window_blocks(packed, bias32, mixed, 33, tok[0] * ATOMS - QB - MARGIN, 3)
    chosen = (index[...] == lax.broadcasted_iota(jnp.int32, (TOKS, EXT), 0).astype(F32)).astype(F32)
    counts = jnp.sum(chosen, axis=1, keepdims=True)
    chosen = chosen.astype(BF16)
    for seed in range(SEEDS):
        values = rows[pl.ds(2 * MARGIN + seed, QB + ATOMS, stride=2), :]
        ext[0 : QB + ATOMS] = (values + dot(mixed[seed], mix[...])).astype(BF16)
        ext[QB + ATOMS :] = jnp.zeros((EXT - QB - ATOMS, CA), BF16)
        encoded[seed] = ext[QB : QB + ATOMS]
        lifted = jnp.maximum(dot(ext[...], pool[...]), 0.0).astype(BF16)
        state = cond[...].astype(F32) + dot(chosen, lifted) / counts
        residual[seed] = state
        normed[seed] = layer_norm(state).astype(BF16)


def encode(tok, feats, low, high, bias, index, cond, project, mix, pool):
    return pl.pallas_call(
        encode_kernel,
        out_shape=(
            jax.ShapeDtypeStruct((SEEDS, ATOMS, CA), BF16),
            jax.ShapeDtypeStruct((SEEDS, TOKS, CT), F32),
            jax.ShapeDtypeStruct((SEEDS, TOKS, CT), BF16),
        ),
        in_specs=[pl.BlockSpec(memory_space=pltpu.SMEM)] + vmem(9),
        out_specs=tuple(vmem(3)),
        scratch_shapes=[
            pltpu.VMEM((2 * EXT, CA), F32),
            pltpu.VMEM((33 * 4 * QB, WIN), F32),
            pltpu.VMEM((SEEDS, EXT, 3 * CA), BF16),
            pltpu.VMEM((SEEDS, QB + ATOMS, CA), BF16),
            pltpu.VMEM((EXT, CA), BF16),
        ],
        compiler_params=params(40),
        cost_estimate=pl.CostEstimate(flops=2 * 10**9, bytes_accessed=6 * 10**6, transcendentals=10**6),
        name="encode",
    )(tok, feats, low, high, bias, index, cond, project, mix, pool)


def decode_kernel(
    tok, enc, enc_low, enc_high, spread, spread_low, spread_high, bias, index, project, mix,
    update,
    rows, bias32, packed, mixed, decoded, tokens,
):
    bias32[...] = bias[...].astype(F32)
    chosen = (
        index[...] == lax.broadcasted_iota(jnp.int32, (TOKS + 2 * EDGE, EXT), 0).astype(F32)
    ).astype(BF16)
    for seed in range(SEEDS):
        tokens[0:EDGE] = spread_low[seed]
        tokens[EDGE : EDGE + TOKS] = spread[seed]
        tokens[EDGE + TOKS :] = spread_high[seed]
        carried = lax.dot_general(
            chosen, tokens[...], (((0,), (0,)), ((), ())), preferred_element_type=F32
        )
        decoded[0:MARGIN] = enc_low[seed]
        decoded[MARGIN : MARGIN + ATOMS] = enc[seed]
        decoded[MARGIN + ATOMS : 2 * MARGIN + ATOMS] = enc_high[seed]
        decoded[2 * MARGIN + ATOMS :] = jnp.zeros((EXT - 2 * MARGIN - ATOMS, CA), BF16)
        values = (decoded[...].astype(F32) + carried).astype(BF16).astype(F32)
        rows[pl.ds(seed, EXT, stride=2), :] = values
        packed[seed] = dot(layer_norm(values).astype(BF16), project[...]).astype(BF16)
    window_blocks(packed, bias32, mixed, 32, tok[0] * ATOMS - MARGIN, 4)
    for seed in range(SEEDS):
        place = pl.ds(2 * MARGIN + seed, ATOMS, stride=2)
        rows[place, :] = rows[place, :] + dot(mixed[seed], mix[...])
    update[...] = rows[2 * MARGIN : 2 * (MARGIN + ATOMS)].astype(BF16)


def decode(*args):
    return pl.pallas_call(
        decode_kernel,
        out_shape=jax.ShapeDtypeStruct((SEEDS * ATOMS, CA), BF16),
        in_specs=[pl.BlockSpec(memory_space=pltpu.SMEM)] + vmem(10),
        out_specs=vmem(1)[0],
        scratch_shapes=[
            pltpu.VMEM((2 * EXT, CA), F32),
            pltpu.VMEM((32 * 4 * QB, WIN), F32),
            pltpu.VMEM((SEEDS, EXT, 3 * CA), BF16),
            pltpu.VMEM((SEEDS, ATOMS, CA), BF16),
            pltpu.VMEM((EXT, CA), BF16),
            pltpu.VMEM((TOKS + 2 * EDGE, CA), BF16),
        ],
        compiler_params=params(40),
        cost_estimate=pl.CostEstimate(flops=10**9, bytes_accessed=4 * 10**6, transcendentals=10**6),
        name="decode",
    )(*args)


def spaced_kernel(weight, out):
    for group in range(4):
        start = PAIR * group // 128 * 128
        shift = PAIR * group - start
        width = min(256, 384 - start)
        row = lax.broadcasted_iota(jnp.int32, (width, 128), 0)
        lane = lax.broadcasted_iota(jnp.int32, (width, 128), 1)
        pick = ((row == lane + shift) & (lane < PAIR)).astype(F32).astype(BF16)
        out[0, group] = dot(weight[:, start : start + width], pick).astype(BF16)


def spaced(weight):
    return pl.pallas_call(
        spaced_kernel,
        grid=(8,),
        out_shape=jax.ShapeDtypeStruct((2, GROUPS, CT, 256), BF16),
        in_specs=[pl.BlockSpec((CT, 384), lambda i: (0, i))],
        out_specs=pl.BlockSpec(
            (1, 4, CT, 128),
            lambda i: (((i >= 2) & (i < 6)).astype(jnp.int32), i % 2, 0, (i >= 4).astype(jnp.int32)),
        ),
        compiler_params=params(32),
        cost_estimate=pl.CostEstimate(flops=10**9, bytes_accessed=11 * 10**6, transcendentals=0),
        name="spaced",
    )(weight)


def keys_kernel(tokens, weight, out):
    count = tokens.shape[0]
    values = jnp.concatenate([tokens[i].reshape(SEEDS * TOKS, CT) for i in range(count)], axis=0)
    ones = (lax.broadcasted_iota(jnp.int32, (1, 256), 1) == 128 + PAIR).astype(F32)
    for group in range(GROUPS):
        product = (dot(values, weight[0, group]) + ones).astype(BF16)
        for i in range(count):
            for seed in range(SEEDS):
                start = (i * SEEDS + seed) * TOKS
                out[group, seed, i * TOKS : (i + 1) * TOKS] = product[start : start + TOKS]


def keys(tokens, weight):
    step = 2
    return pl.pallas_call(
        keys_kernel,
        grid=(tokens.shape[0] // step,),
        out_shape=jax.ShapeDtypeStruct((GROUPS, SEEDS, ALL_TOKS, 256), BF16),
        in_specs=[
            pl.BlockSpec((step, SEEDS, TOKS, CT), lambda i: (i, 0, 0, 0)),
            pl.BlockSpec((1, GROUPS, CT, 256), lambda i: (1, 0, 0, 0)),
        ],
        out_specs=pl.BlockSpec((GROUPS, SEEDS, step * TOKS, 256), lambda i: (0, 0, i, 0)),
        compiler_params=params(40),
        cost_estimate=pl.CostEstimate(flops=13 * 10**9, bytes_accessed=26 * 10**6, transcendentals=0),
        name="keys",
    )(tokens, weight)


def attend_kernel(count, pieces, group_ids, normed, weight, key_value, mix, start, *rest):
    biases, (out, bias, scores, weights) = rest[:-4], rest[-4:]
    step = pl.program_id(0)
    seed = step % 2

    @pl.when(step == 0)
    def _():
        out[...] = start[...]

    at = 0
    for i, parts in enumerate(pieces):
        refs = biases[at : at + parts]
        at += parts

        @pl.when(step == 2 * i)
        def _(refs=refs):
            place = 0
            for ref in refs:
                size = ref.shape[1]
                for j in range(2):
                    bias[j * TOKS + place : j * TOKS + place + size] = ref[j]
                place += size

    query_gate = dot(normed[0], weight[0, 0])
    lane = lax.broadcasted_iota(jnp.int32, (TOKS, 128), 1)
    query = query_gate[:, :128] * (HEAD**-0.5)
    gate = jax.nn.sigmoid(query_gate[:, 128:])
    stacked = jnp.concatenate(
        [jnp.where(lane < HEAD, query, 0.0), jnp.where(lane < HEAD, 0.0, query)], axis=0
    ).astype(BF16)
    width = 512
    peak = None
    for c in range(ALL_TOKS // width):
        cols = slice(c * width, (c + 1) * width)
        part = dot_t(stacked, key_value[0, 0, cols, 0:128]) + bias[:, cols].astype(F32)
        scores[:, cols] = part
        for w in range(width // 128):
            tile = part[:, w * 128 : (w + 1) * 128]
            peak = tile if peak is None else jnp.maximum(peak, tile)
    top = jnp.max(peak, axis=-1, keepdims=True)
    for c in range(ALL_TOKS // width):
        cols = slice(c * width, (c + 1) * width)
        weights[:, cols] = jnp.exp(scores[:, cols] - top).astype(BF16)
    total = dot(weights[...], key_value[0, 0, :, 128:256])
    joined = total / total[:, PAIR : PAIR + 1]
    joined = jnp.where(lane < HEAD, joined[:TOKS], joined[TOKS:])
    gated = (joined * gate).astype(BF16)
    out[seed] = out[seed] + dot(gated[:, :PAIR], mix[0])


def attend(group_ids, normed, weight, key_value, mix, start, pieces):
    count = len(pieces)
    flat = [ref for parts in pieces for ref in parts]
    grid_spec = pltpu.PrefetchScalarGridSpec(
        num_scalar_prefetch=1,
        grid=(2 * count,),
        in_specs=[
            pl.BlockSpec((1, TOKS, CT), lambda i, ids: (i % 2, 0, 0)),
            pl.BlockSpec((1, 1, CT, 256), lambda i, ids: (0, ids[i // 2], 0, 0)),
            pl.BlockSpec((1, 1, ALL_TOKS, 256), lambda i, ids: (ids[i // 2], i % 2, 0, 0)),
            pl.BlockSpec((1, PAIR, CT), lambda i, ids: (ids[i // 2], 0, 0)),
            pl.BlockSpec((SEEDS, TOKS, CT), lambda i, ids: (0, 0, 0)),
        ]
        + vmem(len(flat)),
        out_specs=pl.BlockSpec((SEEDS, TOKS, CT), lambda i, ids: (0, 0, 0)),
        scratch_shapes=[
            pltpu.VMEM((2 * TOKS, ALL_TOKS), BF16),
            pltpu.VMEM((2 * TOKS, ALL_TOKS), F32),
            pltpu.VMEM((2 * TOKS, ALL_TOKS), BF16),
        ],
    )
    return pl.pallas_call(
        functools.partial(attend_kernel, count, tuple(len(parts) for parts in pieces)),
        grid_spec=grid_spec,
        out_shape=jax.ShapeDtypeStruct((SEEDS, TOKS, CT), F32),
        compiler_params=params(40),
        cost_estimate=pl.CostEstimate(
            flops=count * 10**9, bytes_accessed=count * 4 * 10**6, transcendentals=count * 10**6
        ),
        name="attend",
    )(group_ids, normed, weight, key_value, mix, start, *flat)


def transition_kernel(residual, wide, narrow, spread_weight, state, spread):
    values = residual[...].reshape(SEEDS * TOKS, CT)
    normed = layer_norm(values).astype(BF16)
    total = values
    step = 512
    for c in range(TRANS // step):
        gate = dot(normed, wide[:, c * step : (c + 1) * step])
        up = dot(normed, wide[:, TRANS + c * step : TRANS + (c + 1) * step])
        hidden = (jax.nn.silu(gate) * up).astype(BF16)
        total = total + dot(hidden, narrow[c * step : (c + 1) * step, :])
    rounded = total.astype(BF16)
    state[...] = rounded.reshape(SEEDS, TOKS, CT)
    spread[...] = dot(rounded, spread_weight[...]).astype(BF16).reshape(SEEDS, TOKS, CA)


def transition(residual, wide, narrow, spread_weight):
    return pl.pallas_call(
        transition_kernel,
        out_shape=(
            jax.ShapeDtypeStruct((SEEDS, TOKS, CT), BF16),
            jax.ShapeDtypeStruct((SEEDS, TOKS, CA), BF16),
        ),
        in_specs=vmem(4),
        out_specs=tuple(vmem(2)),
        compiler_params=params(40),
        cost_estimate=pl.CostEstimate(flops=2 * 10**9, bytes_accessed=9 * 10**6, transcendentals=4 * 10**5),
        name="transition",
    )(residual, wide, narrow, spread_weight)


def along_tok(values, by):
    return lax.ppermute(values, "tok", [(i, (i + by) % 16) for i in range(16)])


def along_y(values, by):
    return lax.ppermute(values, "seed", [(i, (i + 2 * by) % 8) for i in range(8)])


def along_z(values):
    return lax.ppermute(values, "seed", [(i, i ^ 1) for i in range(8)])


def y_ring(own):
    below = along_y(own, 1)
    above = along_y(own, -1)
    half = own.shape[1] // 2
    far = (along_y(below[:, :half], 1), along_y(above[:, half:], -1))
    return below, above, far


def per_device(
    atom_feats, atom_index, token_cond, pair_bias, atom_bias_enc, atom_bias_dec,
    enc_project, enc_mix, pool_weight, token_project, token_mix, swiglu_in, swiglu_out,
    spread_weight, dec_project, dec_mix,
):
    tok = lax.axis_index("tok")
    seed = lax.axis_index("seed")
    tok_ref = tok.astype(jnp.int32).reshape(1)
    feats = atom_feats.reshape(SEEDS * ATOMS, CA)
    bias_enc = atom_bias_enc.reshape(4 * ATOMS, WIN)
    bias_dec = atom_bias_dec.reshape(4 * ATOMS, WIN)

    place = (atom_index - tok * TOKS).astype(F32)
    tail = jnp.pad((place[-MARGIN:] - TOKS).astype(BF16)[None], ((0, 15), (0, WIN - MARGIN)))
    head = jnp.pad(place[:MARGIN].astype(BF16)[None], ((0, 15), (0, WIN - MARGIN)))
    low = along_tok(jnp.concatenate([feats[-2 * LOWER :], bias_enc[-4 * QB :], tail], axis=0), 1)
    high = along_tok(jnp.concatenate([feats[: 2 * MARGIN], head], axis=0), -1)

    below, above, far = y_ring(pair_bias)
    other = along_z(pair_bias)
    other_below, other_above, other_far = y_ring(other)

    place_low = low[2 * LOWER + 4 * QB, :MARGIN].astype(F32)
    place_high = high[2 * MARGIN, :MARGIN].astype(F32) + TOKS
    place_low = jnp.where(tok == 0, -1000.0, place_low)
    place_high = jnp.where(tok == 15, 1000.0, place_high)
    pool_index = jnp.concatenate(
        [place_low[-QB:], place, jnp.full((EXT - QB - ATOMS,), -1000.0, F32)]
    )[None]
    spread_index = (
        jnp.concatenate(
            [place_low, place, place_high, jnp.full((EXT - 2 * MARGIN - ATOMS,), -1000.0, F32)]
        )
        + EDGE
    )[None]

    weights = spaced(token_project)
    encoded, residual, normed = encode(
        tok_ref, feats, low, high, bias_enc, pool_index, token_cond, enc_project, enc_mix, pool_weight
    )
    enc_low = along_tok(encoded[:, -MARGIN:], 1)
    enc_high = along_tok(encoded[:, :MARGIN], -1)

    everyone = lax.all_gather(normed, "tok", axis=0)
    key_value = keys(everyone, weights)

    level, side = seed // 2, seed % 2

    def ids(*offsets):
        return jnp.stack([(level + dy) % 4 * 2 + (side ^ dz) for dy, dz in offsets]).astype(jnp.int32)

    mix = token_mix.reshape(GROUPS, PAIR, CT)
    residual = attend(
        ids((0, 0), (3, 0), (1, 0), (2, 0), (0, 1)), normed, weights, key_value, mix, residual,
        ((pair_bias,), (below,), (above,), far, (other,)),
    )
    residual = attend(
        ids((3, 1), (1, 1), (2, 1)), normed, weights, key_value, mix, residual,
        ((other_below,), (other_above,), other_far),
    )
    state, spread = transition(residual, swiglu_in, swiglu_out, spread_weight)
    spread_low = along_tok(spread[:, -EDGE:], 1)
    spread_high = along_tok(spread[:, :EDGE], -1)
    update = decode(
        tok_ref, encoded, enc_low, enc_high, spread, spread_low, spread_high, bias_dec,
        spread_index, dec_project, dec_mix,
    )
    return state.transpose(1, 0, 2), update.reshape(ATOMS, SEEDS, CA)


def solution(mesh):
    placed = (
        P("tok", "seed", None),
        P("tok"),
        P("tok", None),
        P("seed", "tok", None),
        P("tok", None, None),
        P("tok", None, None),
    ) + (P(),) * 10
    return jax.shard_map(
        per_device,
        mesh=mesh,
        in_specs=placed,
        out_specs=(P("tok", "seed", None), P("tok", "seed", None)),
        check_vma=False,
    )
```

time: 386 us -> 213 us (0.55); the launches traced: 379 us -> 211 us
  Pallas kernels: 0 us -> 98.2 us
  other arithmetic: 88.7 us -> 0.87 us
  local copies, waits for them, and re-layouts: 117 us -> 30.2 us
  matrix products: 70.8 us -> 0 us
  waiting for transfers between devices: 67.1 us -> 42.9 us
  starting transfers between devices: 20.7 us -> 24.6 us
    pallas_call x0 -> x7, Pallas kernels: none -> 98.2 us  [the longest x2 32.9 us: attend(): pl.pallas_call(functools.partial(attend_kernel, count, tuple((len(parts)...]
    dot_general x18 -> x0, matrix products: 70.8 us -> none  [the longest x1 19.9 us: token_attention(): jnp.einsum('shqk,kshd->shqd', weights.astype(jnp.bfloat16), piece_values,...]
    all_gather x3 -> x1, waiting for transfers between devices: 59.8 us -> 0.01 us  [per_device(): everyone = lax.all_gather(normed, 'tok', axis=0)]
    slice x23 -> x10, local copies, waits for them, and re-layouts: 52.4 us -> 9.1 us  [the longest x4 6.68 us: y_ring(): far = (along_y(below[:, :half], 1), along_y(above[:, half:], -1))]
    concatenate x4 -> x2, other arithmetic: 43.1 us -> 0.02 us  [the longest x1 0.01 us: per_device(): jnp.concatenate([feats[-2 * LOWER:], bias_enc[-4 * QB:], tail], axis=0)]
    ppermute x7 -> x15, waiting for transfers between devices: 5.95 us -> 42.9 us  [the longest x1 33.7 us: along_z(): return lax.ppermute(values, 'seed', [(i, i ^ 1) for i in range(8)])]
    reduce_sum x11 -> x0, other arithmetic: 29.4 us -> none  [the longest x1 17.9 us: token_attention(): running_sum = jnp.sum(weights, axis=-1)]
    reshape x10 -> x0, local copies, waits for them, and re-layouts: 25.3 us -> none  [the longest x2 9.02 us: atom_block(): packed.astype(jnp.bfloat16).reshape(atom_rows, seed_count, 3 * atom_width)]
  transfers between devices with their start and end apart: 10 -> 16, of which waited for: 4 -> 4; matrix products, arithmetic and copies ran while one was open for 43% -> 4% of each run, Pallas kernels for 0% -> 27%
where the time goes in v1:
time: 213 us; the launch traced here: 211 us
  Pallas kernels  98.2 us (46%)
  waiting for transfers between devices  42.9 us (20%)
  local copies, waits for them, and re-layouts  30.2 us (14%)
  starting transfers between devices  24.6 us (12%)
  between operations  14.3 us (7%)
    ppermute x1, waiting for transfers between devices, along_z(): return lax.ppermute(values, 'seed', [(i, i ^ 1) for i in range(8)])  33.7 us
    pallas_call x2, Pallas kernels, attend(): pl.pallas_call(functools.partial(attend_kernel, count, tuple((len(parts)...  32.9 us
    pallas_call x1, Pallas kernels, encode(): pl.pallas_call(encode_kernel, out_shape=(jax.ShapeDtypeStruct((SEEDS, ATO...  21.5 us
    unnamed x47, local copies, waits for them, and re-layouts  20.8 us
    pallas_call x1, Pallas kernels, decode(): pl.pallas_call(decode_kernel, out_shape=jax.ShapeDtypeStruct((SEEDS * ATO...  19.5 us
    pallas_call x1, Pallas kernels, keys(): pl.pallas_call(keys_kernel, grid=(tokens.shape[0] // step,), out_shape=ja...  15.8 us
    ppermute x6, starting transfers between devices, along_tok(): return lax.ppermute(values, 'tok', [(i, (i + by) % 16) for i in range(16)])  11 us
    ppermute x8, starting transfers between devices, along_y(): lax.ppermute(values, 'seed', [(i, (i + 2 * by) % 8) for i in range(8)])  10.1 us
  transfers between devices with their start and end apart: 16, of which 4 were waited for; matrix products, arithmetic and copies ran while one was open for 4% of the time, Pallas kernels for 27%

profile of v1, /device:TPU:7, one launch (start us, length us, event | category | flops | bytes accessed | tf_op | source)
XLA Modules:
  0.0 211.1 jit_solution(9616355939899796231)
XLA Ops:
  9.6 2.2 %collective-permute-start = (bf16[304,128]{1,0:T(8,128)(2,1)S(1)}, bf16[304,128]{1,0:T(8,128)(2,1)S(1)}, u32[]{:S(2)}, u32[]{:S(2)}) collective-permute-start(bf16[304,128]{1,0:T(8,128)(2,1)S(1)} %fusion.1), channel_id=1, source_target_pairs={{0,1},{1,2},{2,3},{3,4},{4,5},{5,6},{6,7},{7,8},{8,9},{9,10},{10,1... | collective-permute-start | bytes 233480 | tf_op jit(solution)/shard_map/ppermute | solution.py:364
  13.4 4.6 %collective-permute-done.1.high = bf16[112,128]{1,0:T(8,128)(2,1)S(1)} collective-permute-done((bf16[112,128]{1,0:T(8,128)(2,1)S(1)}, bf16[112,128]{1,0:T(8,128)(2,1)S(1)}, u32[]{:S(2)}, u32[]{:S(2)}) %collective-permute-start.1) | collective-permute-done | bytes 28704 | tf_op jit(solution)/shard_map/ppermute | solution.py:364
  23.8 21.5 %encode.1 = (bf16[2,1024,128]{2,1,0:T(8,128)(2,1)S(1)}, f32[2,128,768]{2,1,0:T(8,128)S(1)}, bf16[2,128,768]{2,1,0:T(8,128)(2,1)}) custom-call(s32[1]{0:T(128)} %bitcast.3.tok, bf16[2048,128]{1,0:T(8,128)(2,1)S(1)} %bitcast.31, bf16[304,128]{1,0:T(8,128)(2,1)S(1)} %collective-permute-done.low, bf16[112,128]{1,0:T(8,128)(2,1)S(1)} %collective-permute-done.1.high, ...), custom_call_target="tpu_custom_call" | custom-call | flops 2000000000 | bytes 6000000 | tf_op jit(solution)/shard_map/encode/pallas_call | solution.py:122
  46.2 3.4 %collective-permute-start.6 = (bf16[2,128,2048]{2,1,0:T(8,128)(2,1)}, bf16[2,128,2048]{2,1,0:T(8,128)(2,1)}, u32[]{:S(2)}, u32[]{:S(2)}) collective-permute-start(bf16[2,128,2048]{2,1,0:T(8,128)(2,1)} %rest_0_.1), channel_id=1, source_target_pairs={{0,16},{16,0},{32,48},{48,32},{64,80},{80,64},{96,112},{112,96},{1... | collective-permute-start | bytes 3145736 | tf_op jit(solution)/shard_map/ppermute | solution.py:372
  52.3 33.7 %collective-permute-done.6.rest_5_ = bf16[2,128,2048]{2,1,0:T(8,128)(2,1)} collective-permute-done((bf16[2,128,2048]{2,1,0:T(8,128)(2,1)}, bf16[2,128,2048]{2,1,0:T(8,128)(2,1)}, u32[]{:S(2)}, u32[]{:S(2)}) %collective-permute-start.6) | collective-permute-done | bytes 1048608 | tf_op jit(solution)/shard_map/ppermute | solution.py:372
  86.0 3.0 %collective-permute-start.8 = (bf16[2,128,2048]{2,1,0:T(8,128)(2,1)}, bf16[2,128,2048]{2,1,0:T(8,128)(2,1)S(1)}, u32[]{:S(2)}, u32[]{:S(2)}) collective-permute-start(bf16[2,128,2048]{2,1,0:T(8,128)(2,1)} %collective-permute-done.6.rest_5_), channel_id=1, source_target_pairs={{0,96},{16,112},{32,0},{48,16},{64,32},{80,48},{96,64},{112,80},{1... | collective-permute-start | bytes 3145736 | tf_op jit(solution)/shard_map/ppermute | solution.py:368
  89.1 2.4 %copy-done.4 = bf16[768,3072]{1,0:T(8,128)(2,1)S(1)} copy-done((bf16[768,3072]{1,0:T(8,128)(2,1)S(1)}, bf16[768,3072]{1,0:T(8,128)(2,1)}, u32[]{:S(2)}) %copy-start.4) | copy-done | bytes 4718616
  91.5 5.8 %spaced.1.weight = bf16[2,8,768,256]{3,2,1,0:T(8,128)(2,1)S(1)} custom-call(bf16[768,3072]{1,0:T(8,128)(2,1)S(1)} %copy-done.4), custom_call_target="tpu_custom_call" | custom-call | flops 1000000000 | bytes 11000000 | tf_op jit(solution)/shard_map/spaced/pallas_call | solution.py:206
  97.4 2.7 %copy-done = bf16[2,8,768,256]{3,2,1,0:T(8,128)(2,1)} copy-done((bf16[2,8,768,256]{3,2,1,0:T(8,128)(2,1)}, bf16[2,8,768,256]{3,2,1,0:T(8,128)(2,1)S(1)}, u32[]{:S(2)}) %copy-start) | copy-done | bytes 6291480
  101.1 2.1 slice.82
  103.3 1.9 slice.83
  105.2 2.8 %collective-permute-start.5 = (bf16[2,64,2048]{2,1,0:T(8,128)(2,1)}, bf16[2,64,2048]{2,1,0:T(8,128)(2,1)}, u32[]{:S(2)}, u32[]{:S(2)}) collective-permute-start(bf16[2,64,2048]{2,1,0:T(8,128)(2,1)} %slice.83), channel_id=1, source_target_pairs={{0,96},{16,112},{32,0},{48,16},{64,32},{80,48},{96,64},{112,80},{1... | collective-permute-start | bytes 1572872 | tf_op jit(solution)/shard_map/ppermute | solution.py:368
  108.8 1.5 collective-permute-start.10
  110.3 1.9 slice.84
  112.2 2.8 %copy-done.1 = bf16[2,8,768,256]{3,2,1,0:T(8,128)(2,1)S(1)} copy-done((bf16[2,8,768,256]{3,2,1,0:T(8,128)(2,1)S(1)}, bf16[2,8,768,256]{3,2,1,0:T(8,128)(2,1)}, u32[]{:S(2)}) %copy-start.1) | copy-done | bytes 6291480
  115.0 2.8 %copy-done.13 = bf16[32,128,768]{2,1,0:T(8,128)(2,1)S(1)} copy-done((bf16[32,128,768]{2,1,0:T(8,128)(2,1)S(1)}, bf16[32,128,768]{2,1,0:T(8,128)(2,1)}, u32[]{:S(2)}) %copy-start.13) | copy-done | bytes 6291480
  117.8 15.8 %keys.1.key_value = bf16[8,2,2048,256]{3,2,1,0:T(8,128)(2,1)} custom-call(bf16[16,2,128,768]{3,2,1,0:T(8,128)(2,1)S(1)} %bitcast.33, bf16[2,8,768,256]{3,2,1,0:T(8,128)(2,1)S(1)} %copy-done.1), custom_call_target="tpu_custom_call" | custom-call | flops 12999999488 | bytes 26000000 | tf_op jit(solution)/shard_map/keys/pallas_call | solution.py:235
  134.2 20.4 %attend.2.start = f32[2,128,768]{2,1,0:T(8,128)S(1)} custom-call(s32[5]{0:T(128)S(1)} %stack.39.group_ids, bf16[2,128,768]{2,1,0:T(8,128)(2,1)} %get-tuple-element.7.normed, bf16[2,8,768,256]{3,2,1,0:T(8,128)(2,1)} %copy-done, bf16[8,2,2048,256]{3,2,1,0:T(8,128)(2,1)} %keys.1.key_value, bf16[8,96,768]{2,1,0:T(8,128)(2,1)S(1)} %bitcast.28, ...), custom_call_target="tpu_custom_call" | custom-call | flops 5000000000 | bytes 20000000 | tf_op jit(solution)/shard_map/attend/pallas_call | solution.py:321
  154.7 12.6 %attend.3.residual = f32[2,128,768]{2,1,0:T(8,128)S(1)} custom-call(s32[3]{0:T(128)S(1)} %pad_add_fusion.group_ids, bf16[2,128,768]{2,1,0:T(8,128)(2,1)} %get-tuple-element.7.normed, bf16[2,8,768,256]{3,2,1,0:T(8,128)(2,1)S(1)} %bitcast.27, bf16[8,2,2048,256]{3,2,1,0:T(8,128)(2,1)} %keys.1.key_value, bf16[8,96,768]{2,1,0:T(8,128)(2,1)S(1)} %bitcast.29, ...), custom_call_target="tpu_custom_call" | custom-call | flops 3000000000 | bytes 12000000 | tf_op jit(solution)/shard_map/attend/pallas_call | solution.py:321
  167.3 2.3 %copy-done.3 = bf16[768,3072]{1,0:T(8,128)(2,1)S(1)} copy-done((bf16[768,3072]{1,0:T(8,128)(2,1)S(1)}, bf16[768,3072]{1,0:T(8,128)(2,1)}, u32[]{:S(2)}) %copy-start.3) | copy-done | bytes 4718616
  169.6 2.6 %transition.1 = (bf16[2,128,768]{2,1,0:T(8,128)(2,1)S(1)}, bf16[2,128,128]{2,1,0:T(8,128)(2,1)S(1)}) custom-call(f32[2,128,768]{2,1,0:T(8,128)S(1)} %attend.3.residual, bf16[768,3072]{1,0:T(8,128)(2,1)S(1)} %copy-done.3, bf16[1536,768]{1,0:T(8,128)(2,1)S(1)} %copy-done.5, bf16[768,128]{1,0:T(8,128)(2,1)S(1)} %copy-done.8), custom_call_target="tpu_custom_call" | custom-call | flops 2000000000 | bytes 9000000 | tf_op jit(solution)/shard_map/transition/pallas_call | solution.py:349
  172.2 7.3 %collective-permute-start.13 = (bf16[2,16,128]{2,1,0:T(8,128)(2,1)S(1)}, bf16[2,16,128]{2,1,0:T(8,128)(2,1)S(1)}, u32[]{:S(2)}, u32[]{:S(2)}) collective-permute-start(bf16[2,16,128]{2,1,0:T(8,128)(2,1)S(1)} %get-tuple-element.21), channel_id=1, source_target_pairs={{0,1},{1,2},{2,3},{3,4},{4,5},{5,6},{6,7},{7,8},{8,9},{9,10},{10,1... | collective-permute-start | bytes 24584 | tf_op jit(solution)/shard_map/ppermute | solution.py:364
  180.8 4.0 %collective-permute-done.14.spread_high = bf16[2,16,128]{2,1,0:T(8,128)(2,1)S(1)} collective-permute-done((bf16[2,16,128]{2,1,0:T(8,128)(2,1)S(1)}, bf16[2,16,128]{2,1,0:T(8,128)(2,1)S(1)}, u32[]{:S(2)}, u32[]{:S(2)}) %collective-permute-start.14) | collective-permute-done | bytes 8224 | tf_op jit(solution)/shard_map/ppermute | solution.py:364
  184.8 19.5 %decode.1 = bf16[2048,128]{1,0:T(8,128)(2,1)} custom-call(s32[1]{0:T(128)} %bitcast.3.tok, bf16[2,1024,128]{2,1,0:T(8,128)(2,1)S(1)} %copy-done.11, bf16[2,48,128]{2,1,0:T(8,128)(2,1)S(1)} %collective-permute-done.11.enc_low, bf16[2,48,128]{2,1,0:T(8,128)(2,1)S(1)} %collective-permute-done.12.enc_high, bf16[2,128,128]{2,1,0:T(8,128)(2,1)S(1)} %get-tuple-element.11.spread, ...), custom_call_target="tpu_custom_call" | custom-call | flops 1000000000 | bytes 4000000 | tf_op jit(solution)/shard_map/decode/pallas_call | solution.py:175
  (89 shorter events, 17.3 us)
Async XLA Ops:
  7.2 105.0 %all-gather.3.cloned.1.call-start = ((), (), s32[]{:S(2)}) async-start(), calls=%async_computation | async-start | bytes 6684672 | tf_op jit(solution)/shard_map/all_gather | solution.py:426
  9.6 3.6 %collective-permute-start = (bf16[304,128]{1,0:T(8,128)(2,1)S(1)}, bf16[304,128]{1,0:T(8,128)(2,1)S(1)}, u32[]{:S(2)}, u32[]{:S(2)}) collective-permute-start(bf16[304,128]{1,0:T(8,128)(2,1)S(1)} %fusion.1), channel_id=1, source_target_pairs={{0,1},{1,2},{2,3},{3,4},{4,5},{5,6},{6,7},{7,8},{8,9},{9,10},{10,1... | collective-permute-start | bytes 233480 | tf_op jit(solution)/shard_map/ppermute | solution.py:364
  12.6 5.5 %collective-permute-start.1 = (bf16[112,128]{1,0:T(8,128)(2,1)S(1)}, bf16[112,128]{1,0:T(8,128)(2,1)S(1)}, u32[]{:S(2)}, u32[]{:S(2)}) collective-permute-start(bf16[112,128]{1,0:T(8,128)(2,1)S(1)} %fusion.3), channel_id=1, source_target_pairs={{0,15},{1,0},{2,1},{3,2},{4,3},{5,4},{6,5},{7,6},{8,7},{9,8},{10,9... | collective-permute-start | bytes 86024 | tf_op jit(solution)/shard_map/ppermute | solution.py:364
  46.2 53.9 %copy-start.10 = (bf16[2,1024,128]{2,1,0:T(8,128)(2,1)}, bf16[2,1024,128]{2,1,0:T(8,128)(2,1)S(1)}, u32[]{:S(2)}) copy-start(bf16[2,1024,128]{2,1,0:T(8,128)(2,1)S(1)} %get-tuple-element.10.enc) | copy-start | bytes 1572868
  46.2 39.8 %collective-permute-start.6 = (bf16[2,128,2048]{2,1,0:T(8,128)(2,1)}, bf16[2,128,2048]{2,1,0:T(8,128)(2,1)}, u32[]{:S(2)}, u32[]{:S(2)}) collective-permute-start(bf16[2,128,2048]{2,1,0:T(8,128)(2,1)} %rest_0_.1), channel_id=1, source_target_pairs={{0,16},{16,0},{32,48},{48,32},{64,80},{80,64},{96,112},{112,96},{1... | collective-permute-start | bytes 3145736 | tf_op jit(solution)/shard_map/ppermute | solution.py:372
  49.6 51.5 %collective-permute-start.2 = (bf16[2,128,2048]{2,1,0:T(8,128)(2,1)}, bf16[2,128,2048]{2,1,0:T(8,128)(2,1)}, u32[]{:S(2)}, u32[]{:S(2)}) collective-permute-start(bf16[2,128,2048]{2,1,0:T(8,128)(2,1)} %rest_0_.1), channel_id=1, source_target_pairs={{0,32},{16,48},{32,64},{48,80},{64,96},{80,112},{96,0},{112,16},{1... | collective-permute-start | bytes 3145736 | tf_op jit(solution)/shard_map/ppermute | solution.py:368
  50.9 52.4 %collective-permute-start.3 = (bf16[2,128,2048]{2,1,0:T(8,128)(2,1)}, bf16[2,128,2048]{2,1,0:T(8,128)(2,1)}, u32[]{:S(2)}, u32[]{:S(2)}) collective-permute-start(bf16[2,128,2048]{2,1,0:T(8,128)(2,1)} %rest_0_.1), channel_id=1, source_target_pairs={{0,96},{16,112},{32,0},{48,16},{64,32},{80,48},{96,64},{112,80},{1... | collective-permute-start | bytes 3145736 | tf_op jit(solution)/shard_map/ppermute | solution.py:368
  86.0 22.0 %collective-permute-start.8 = (bf16[2,128,2048]{2,1,0:T(8,128)(2,1)}, bf16[2,128,2048]{2,1,0:T(8,128)(2,1)S(1)}, u32[]{:S(2)}, u32[]{:S(2)}) collective-permute-start(bf16[2,128,2048]{2,1,0:T(8,128)(2,1)} %collective-permute-done.6.rest_5_), channel_id=1, source_target_pairs={{0,96},{16,112},{32,0},{48,16},{64,32},{80,48},{96,64},{112,80},{1... | collective-permute-start | bytes 3145736 | tf_op jit(solution)/shard_map/ppermute | solution.py:368
  89.0 21.3 %collective-permute-start.7 = (bf16[2,128,2048]{2,1,0:T(8,128)(2,1)}, bf16[2,128,2048]{2,1,0:T(8,128)(2,1)}, u32[]{:S(2)}, u32[]{:S(2)}) collective-permute-start(bf16[2,128,2048]{2,1,0:T(8,128)(2,1)} %collective-permute-done.6.rest_5_), channel_id=1, source_target_pairs={{0,32},{16,48},{32,64},{48,80},{64,96},{80,112},{96,0},{112,16},{1... | collective-permute-start | bytes 3145736 | tf_op jit(solution)/shard_map/ppermute | solution.py:368
  100.1 80.6 %collective-permute-start.11 = (bf16[2,48,128]{2,1,0:T(8,128)(2,1)S(1)}, bf16[2,48,128]{2,1,0:T(8,128)(2,1)S(1)}, u32[]{:S(2)}, u32[]{:S(2)}) collective-permute-start(bf16[2,48,128]{2,1,0:T(8,128)(2,1)S(1)} %get-tuple-element.19), channel_id=1, source_target_pairs={{0,1},{1,2},{2,3},{3,4},{4,5},{5,6},{6,7},{7,8},{8,9},{9,10},{10,1... | collective-permute-start | bytes 73736 | tf_op jit(solution)/shard_map/ppermute | solution.py:364
  101.1 53.5 %slice-start = ((s8[6291456]{0:T(1024)(128)(4,1)}), s8[2097152]{0:T(1024)(128)(4,1)S(1)}, s32[]{:S(2)}) async-start(s8[6291456]{0:T(1024)(128)(4,1)} %bitcast.26), calls=%async_computation.1 | async-start | bytes 4194304
  103.2 30.5 %collective-permute-start.4 = (bf16[2,64,2048]{2,1,0:T(8,128)(2,1)}, bf16[2,64,2048]{2,1,0:T(8,128)(2,1)}, u32[]{:S(2)}, u32[]{:S(2)}) collective-permute-start(bf16[2,64,2048]{2,1,0:T(8,128)(2,1)} %slice.82), channel_id=1, source_target_pairs={{0,32},{16,48},{32,64},{48,80},{64,96},{80,112},{96,0},{112,16},{1... | collective-permute-start | bytes 1572872 | tf_op jit(solution)/shard_map/ppermute | solution.py:368
  105.2 29.0 %collective-permute-start.5 = (bf16[2,64,2048]{2,1,0:T(8,128)(2,1)}, bf16[2,64,2048]{2,1,0:T(8,128)(2,1)}, u32[]{:S(2)}, u32[]{:S(2)}) collective-permute-start(bf16[2,64,2048]{2,1,0:T(8,128)(2,1)} %slice.83), channel_id=1, source_target_pairs={{0,96},{16,112},{32,0},{48,16},{64,32},{80,48},{96,64},{112,80},{1... | collective-permute-start | bytes 1572872 | tf_op jit(solution)/shard_map/ppermute | solution.py:368
  108.8 45.8 %collective-permute-start.10 = (bf16[2,64,2048]{2,1,0:T(8,128)(2,1)}, bf16[2,64,2048]{2,1,0:T(8,128)(2,1)}, u32[]{:S(2)}, u32[]{:S(2)}) collective-permute-start(bf16[2,64,2048]{2,1,0:T(8,128)(2,1)} %slice.85), channel_id=1, source_target_pairs={{0,96},{16,112},{32,0},{48,16},{64,32},{80,48},{96,64},{112,80},{1... | collective-permute-start | bytes 1572872 | tf_op jit(solution)/shard_map/ppermute | solution.py:368
  112.2 42.4 %collective-permute-start.9 = (bf16[2,64,2048]{2,1,0:T(8,128)(2,1)}, bf16[2,64,2048]{2,1,0:T(8,128)(2,1)}, u32[]{:S(2)}, u32[]{:S(2)}) collective-permute-start(bf16[2,64,2048]{2,1,0:T(8,128)(2,1)} %slice.84), channel_id=1, source_target_pairs={{0,32},{16,48},{32,64},{48,80},{64,96},{80,112},{96,0},{112,16},{1... | collective-permute-start | bytes 1572872 | tf_op jit(solution)/shard_map/ppermute | solution.py:368
  117.8 16.4 %copy-start.2 = (bf16[768,768]{1,0:T(8,128)(2,1)S(1)}, bf16[768,768]{1,0:T(8,128)(2,1)}, u32[]{:S(2)}) copy-start(bf16[768,768]{1,0:T(8,128)(2,1)} %param.26) | copy-start | bytes 3538948
  117.8 16.4 %copy-start.7 = (f32[2,128,768]{2,1,0:T(8,128)S(1)}, f32[2,128,768]{2,1,0:T(8,128)}, u32[]{:S(2)}) copy-start(f32[2,128,768]{2,1,0:T(8,128)} %copy-done.6) | copy-start | bytes 2359300
  117.8 36.9 %slice-start.1 = ((s8[6291456]{0:T(1024)(128)(4,1)}), s8[4194304]{0:T(1024)(128)(4,1)S(1)}, s32[]{:S(2)}) async-start(s8[6291456]{0:T(1024)(128)(4,1)} %bitcast.26), calls=%async_computation.2 | async-start | bytes 8388608
  133.6 47.1 %collective-permute-start.12 = (bf16[2,48,128]{2,1,0:T(8,128)(2,1)S(1)}, bf16[2,48,128]{2,1,0:T(8,128)(2,1)S(1)}, u32[]{:S(2)}, u32[]{:S(2)}) collective-permute-start(bf16[2,48,128]{2,1,0:T(8,128)(2,1)S(1)} %get-tuple-element.18), channel_id=1, source_target_pairs={{0,15},{1,0},{2,1},{3,2},{4,3},{5,4},{6,5},{7,6},{8,7},{9,8},{10,9... | collective-permute-start | bytes 73736 | tf_op jit(solution)/shard_map/ppermute | solution.py:364
  169.6 15.2 %copy-start.14 = (bf16[1024,4,128]{2,1,0:T(4,128)(2,1)S(1)}, bf16[1024,4,128]{2,1,0:T(4,128)(2,1)}, u32[]{:S(2)}) copy-start(bf16[1024,4,128]{2,1,0:T(4,128)(2,1)} %param.21) | copy-start | bytes 3145732
  169.6 15.2 %copy-start.18 = (bf16[128,384]{1,0:T(8,128)(2,1)S(1)}, bf16[128,384]{1,0:T(8,128)(2,1)}, u32[]{:S(2)}) copy-start(bf16[128,384]{1,0:T(8,128)(2,1)} %project.3) | copy-start | bytes 294916
  169.6 15.2 %copy-start.20 = (bf16[128,128]{1,0:T(8,128)(2,1)S(1)}, bf16[128,128]{1,0:T(8,128)(2,1)}, u32[]{:S(2)}) copy-start(bf16[128,128]{1,0:T(8,128)(2,1)} %mix.3) | copy-start | bytes 98308
  172.2 8.5 %collective-permute-start.13 = (bf16[2,16,128]{2,1,0:T(8,128)(2,1)S(1)}, bf16[2,16,128]{2,1,0:T(8,128)(2,1)S(1)}, u32[]{:S(2)}, u32[]{:S(2)}) collective-permute-start(bf16[2,16,128]{2,1,0:T(8,128)(2,1)S(1)} %get-tuple-element.21), channel_id=1, source_target_pairs={{0,1},{1,2},{2,3},{3,4},{4,5},{5,6},{6,7},{7,8},{8,9},{9,10},{10,1... | collective-permute-start | bytes 24584 | tf_op jit(solution)/shard_map/ppermute | solution.py:364
  179.6 5.2 %collective-permute-start.14 = (bf16[2,16,128]{2,1,0:T(8,128)(2,1)S(1)}, bf16[2,16,128]{2,1,0:T(8,128)(2,1)S(1)}, u32[]{:S(2)}, u32[]{:S(2)}) collective-permute-start(bf16[2,16,128]{2,1,0:T(8,128)(2,1)S(1)} %get-tuple-element.20), channel_id=1, source_target_pairs={{0,15},{1,0},{2,1},{3,2},{4,3},{5,4},{6,5},{7,6},{8,7},{9,8},{10,9... | collective-permute-start | bytes 24584 | tf_op jit(solution)/shard_map/ppermute | solution.py:364
  (15 other events, 60.1 us)
Sparse Core Ops, SparseCore 0:
  46.3 56.3 all-gather.2

commit v2 on v1

--- a/solution.py
+++ b/solution.py
@@ -32,12 +32,19 @@
 ALL_ATOMS = 16384
 
 
+SMALL = pl.CostEstimate(flops=10**6, bytes_accessed=10**4, transcendentals=0)
+
+
 def params(limit_mb, **more):
     return pltpu.CompilerParams(vmem_limit_bytes=limit_mb * 1024 * 1024, **more)
 
 
 def vmem(n):
     return [pl.BlockSpec(memory_space=pltpu.VMEM)] * n
+
+
+def anywhere(n):
+    return [pl.BlockSpec(memory_space=pl.ANY)] * n
 
 
 def layer_norm(values):
@@ -56,38 +63,44 @@
 
 def window_blocks(packed, bias, mixed, blocks, first_atom, unroll):
     lane_head = lax.broadcasted_iota(jnp.int32, (QB, CA), 1) // 32
+    head_mask = [(lane_head == h).astype(BF16) for h in range(4)]
     lane = lax.broadcasted_iota(jnp.int32, (1, WIN), 1)
-
-    def body(b, carry):
-        rows = pl.multiple_of(b * QB, QB)
-        query_rows = pl.multiple_of(b * QB + MARGIN, 16)
-        bias_rows = pl.multiple_of(b * 4 * QB, 4 * QB)
-        added = jnp.concatenate(
-            [bias[pl.ds(bias_rows + h, QB, stride=4), :] for h in range(4)], axis=0
-        )
+    ones = jnp.ones((WIN, CA), BF16)
+    for b in (0, 1, 2, blocks - 2, blocks - 1):
         position = lane + (first_atom + b * QB)
         inside = (position >= 0) & (position < ALL_ATOMS)
-        added = jnp.where(inside, added, NEG)
-        for seed in range(SEEDS):
+        place = slice(b * 4 * QB, (b + 1) * 4 * QB)
+        bias[place] = jnp.where(inside, bias[place], NEG)
+
+    def body(i, carry):
+        work = []
+        for u in range(unroll):
+            b = i * unroll + u
+            rows = pl.multiple_of(b * QB, QB)
+            query_rows = pl.multiple_of(b * QB + MARGIN, 16)
+            bias_rows = pl.multiple_of(b * 4 * QB, 4 * QB)
+            added = jnp.concatenate(
+                [bias[pl.ds(bias_rows + h, QB, stride=4), :] for h in range(4)], axis=0
+            )
+            for seed in range(SEEDS):
+                work.append((rows, query_rows, added, seed))
+        scores = []
+        for rows, query_rows, added, seed in work:
             query = packed[seed, pl.ds(query_rows, QB), 0:CA]
             key = packed[seed, pl.ds(rows, WIN), CA : 2 * CA]
-            value = packed[seed, pl.ds(rows, WIN), 2 * CA : 3 * CA]
-            stacked = jnp.concatenate(
-                [jnp.where(lane_head == h, query, jnp.zeros_like(query)) for h in range(4)], axis=0
-            )
-            scores = dot_t(stacked, key) * (32**-0.5)
-            scores = jnp.where(inside, scores + added, NEG)
-            top = jnp.max(scores, axis=-1, keepdims=True)
-            weights = jnp.exp(scores - top)
-            total = jnp.sum(weights, axis=-1, keepdims=True)
-            out = dot(weights.astype(BF16), value) / total
-            joined = jnp.zeros((QB, CA), F32)
-            for h in range(4):
-                joined = joined + jnp.where(lane_head == h, out[h * QB : (h + 1) * QB], 0.0)
-            mixed[seed, pl.ds(rows, QB), :] = joined.astype(BF16)
+            stacked = jnp.concatenate([query * head_mask[h] for h in range(4)], axis=0)
+            scores.append(dot_t(stacked, key) * (32**-0.5) + added)
+        weights = [jnp.exp(s - jnp.max(s, axis=-1, keepdims=True)).astype(BF16) for s in scores]
+        for (rows, _, _, seed), w in zip(work, weights):
+            value = jnp.concatenate([packed[seed, pl.ds(rows, WIN), 2 * CA : 3 * CA], ones], axis=1)
+            out = dot(w, value)
+            joined = out[3 * QB :]
+            for h in range(3):
+                joined = jnp.where(jnp.concatenate([lane_head, lane_head], axis=1) == h, out[h * QB : (h + 1) * QB], joined)
+            mixed[seed, pl.ds(rows, QB), :] = (joined[:, :CA] / joined[:, CA:]).astype(BF16)
         return carry
 
-    lax.fori_loop(0, blocks, body, 0, unroll=unroll)
+    lax.fori_loop(0, blocks // unroll, body, 0)
 
 
 def encode_kernel(
@@ -103,7 +116,7 @@
     for seed in range(SEEDS):
         values = rows[pl.ds(seed, EXT, stride=2), :]
         packed[seed] = dot(layer_norm(values).astype(BF16), project[...]).astype(BF16)
-    window_blocks(packed, bias32, mixed, 33, tok[0] * ATOMS - QB - MARGIN, 3)
+    window_blocks(packed, bias32, mixed, 33, tok[0] * ATOMS - QB - MARGIN, 11)
     chosen = (index[...] == lax.broadcasted_iota(jnp.int32, (TOKS, EXT), 0).astype(F32)).astype(F32)
     counts = jnp.sum(chosen, axis=1, keepdims=True)
     chosen = chosen.astype(BF16)
@@ -135,8 +148,8 @@
             pltpu.VMEM((SEEDS, QB + ATOMS, CA), BF16),
             pltpu.VMEM((EXT, CA), BF16),
         ],
-        compiler_params=params(40),
-        cost_estimate=pl.CostEstimate(flops=2 * 10**9, bytes_accessed=6 * 10**6, transcendentals=10**6),
+        compiler_params=params(58),
+        cost_estimate=SMALL,
         name="encode",
     )(tok, feats, low, high, bias, index, cond, project, mix, pool)
 
@@ -164,7 +177,7 @@
         values = (decoded[...].astype(F32) + carried).astype(BF16).astype(F32)
         rows[pl.ds(seed, EXT, stride=2), :] = values
         packed[seed] = dot(layer_norm(values).astype(BF16), project[...]).astype(BF16)
-    window_blocks(packed, bias32, mixed, 32, tok[0] * ATOMS - MARGIN, 4)
+    window_blocks(packed, bias32, mixed, 32, tok[0] * ATOMS - MARGIN, 8)
     for seed in range(SEEDS):
         place = pl.ds(2 * MARGIN + seed, ATOMS, stride=2)
         rows[place, :] = rows[place, :] + dot(mixed[seed], mix[...])
@@ -185,8 +198,8 @@
             pltpu.VMEM((EXT, CA), BF16),
             pltpu.VMEM((TOKS + 2 * EDGE, CA), BF16),
         ],
-        compiler_params=params(40),
-        cost_estimate=pl.CostEstimate(flops=10**9, bytes_accessed=4 * 10**6, transcendentals=10**6),
+        compiler_params=params(58),
+        cost_estimate=SMALL,
         name="decode",
     )(*args)
 
@@ -212,45 +225,79 @@
             (1, 4, CT, 128),
             lambda i: (((i >= 2) & (i < 6)).astype(jnp.int32), i % 2, 0, (i >= 4).astype(jnp.int32)),
         ),
-        compiler_params=params(32),
-        cost_estimate=pl.CostEstimate(flops=10**9, bytes_accessed=11 * 10**6, transcendentals=0),
+        compiler_params=params(58),
+        cost_estimate=SMALL,
         name="spaced",
     )(weight)
 
 
-def keys_kernel(tokens, weight, out):
-    count = tokens.shape[0]
-    values = jnp.concatenate([tokens[i].reshape(SEEDS * TOKS, CT) for i in range(count)], axis=0)
+def keys_kernel(pieces, passed, at, *refs):
+    count = sum(a + b for a, b in pieces)
+    chunks, weight = refs[:count], refs[count]
+    out, both = refs[-2 - passed], refs[-1]
+    step = pl.program_id(0)
+    core = at[0]
+    first = 0
+    for i, sizes in enumerate(pieces):
+        sides = (chunks[first : first + sizes[0]], chunks[first + sizes[0] : first + sum(sizes)])
+        first += sum(sizes)
+
+        @pl.when(step == i)
+        def _(sides=sides):
+            for side, parts in zip((core, 1 - core), sides):
+                seed = 0
+                for part in parts:
+                    for j in range(part.shape[0]):
+                        both[side, seed] = part[j]
+                        seed += 1
+
+    values = both[...].reshape(2 * SEEDS * TOKS, CT)
     ones = (lax.broadcasted_iota(jnp.int32, (1, 256), 1) == 128 + PAIR).astype(F32)
     for group in range(GROUPS):
         product = (dot(values, weight[0, group]) + ones).astype(BF16)
-        for i in range(count):
+        for side in range(2):
             for seed in range(SEEDS):
-                start = (i * SEEDS + seed) * TOKS
-                out[group, seed, i * TOKS : (i + 1) * TOKS] = product[start : start + TOKS]
-
-
-def keys(tokens, weight):
-    step = 2
+                start = (side * SEEDS + seed) * TOKS
+                out[group, seed, side * TOKS : (side + 1) * TOKS] = product[start : start + TOKS]
+
+
+def keys(core, chips, pieces, weight, before, passed=()):
+    flat = [part for sides in pieces for parts in sides for part in parts]
+    at = jnp.concatenate([core, chips])
+    more = ([] if before is None else [before]) + list(passed)
+    aliases = {} if before is None else {len(flat) + 2: 0}
+    for i in range(len(passed)):
+        aliases[len(flat) + 2 + len(more) - len(passed) + i] = 1 + i
+    grid_spec = pltpu.PrefetchScalarGridSpec(
+        num_scalar_prefetch=1,
+        grid=(len(pieces),),
+        in_specs=vmem(len(flat))
+        + [pl.BlockSpec((1, GROUPS, CT, 256), lambda i, at: (1, 0, 0, 0))]
+        + anywhere(len(more)),
+        out_specs=tuple(
+            [pl.BlockSpec((GROUPS, SEEDS, 2 * TOKS, 256), lambda i, at: (0, 0, at[1 + i], 0))]
+            + anywhere(len(passed))
+        ),
+        scratch_shapes=[pltpu.VMEM((2, SEEDS, TOKS, CT), BF16)],
+    )
+    sizes = tuple((len(same), len(other)) for same, other in pieces)
     return pl.pallas_call(
-        keys_kernel,
-        grid=(tokens.shape[0] // step,),
-        out_shape=jax.ShapeDtypeStruct((GROUPS, SEEDS, ALL_TOKS, 256), BF16),
-        in_specs=[
-            pl.BlockSpec((step, SEEDS, TOKS, CT), lambda i: (i, 0, 0, 0)),
-            pl.BlockSpec((1, GROUPS, CT, 256), lambda i: (1, 0, 0, 0)),
-        ],
-        out_specs=pl.BlockSpec((GROUPS, SEEDS, step * TOKS, 256), lambda i: (0, 0, i, 0)),
-        compiler_params=params(40),
-        cost_estimate=pl.CostEstimate(flops=13 * 10**9, bytes_accessed=26 * 10**6, transcendentals=0),
+        functools.partial(keys_kernel, sizes, len(passed)),
+        grid_spec=grid_spec,
+        out_shape=tuple(
+            [jax.ShapeDtypeStruct((GROUPS, SEEDS, ALL_TOKS, 256), BF16)]
+            + [jax.ShapeDtypeStruct(array.shape, array.dtype) for array in passed]
+        ),
+        input_output_aliases=aliases,
+        compiler_params=params(50),
+        cost_estimate=SMALL,
         name="keys",
-    )(tokens, weight)
-
-
-def attend_kernel(count, pieces, group_ids, normed, weight, key_value, mix, start, *rest):
-    biases, (out, bias, scores, weights) = rest[:-4], rest[-4:]
+    )(at, *flat, weight, *more)
+
+
+def attend_kernel(pieces, group_ids, normed, weight, key_value, mix, start, *rest):
+    biases, (out, bias, scores) = rest[: sum(pieces)], rest[-3:]
     step = pl.program_id(0)
-    seed = step % 2
 
     @pl.when(step == 0)
     def _():
@@ -261,7 +308,7 @@
         refs = biases[at : at + parts]
         at += parts
 
-        @pl.when(step == 2 * i)
+        @pl.when(step == i)
         def _(refs=refs):
             place = 0
             for ref in refs:
@@ -270,31 +317,38 @@
                     bias[j * TOKS + place : j * TOKS + place + size] = ref[j]
                 place += size
 
-    query_gate = dot(normed[0], weight[0, 0])
     lane = lax.broadcasted_iota(jnp.int32, (TOKS, 128), 1)
-    query = query_gate[:, :128] * (HEAD**-0.5)
+    query_gate = dot(normed[...].reshape(SEEDS * TOKS, CT), weight[0, 0])
     gate = jax.nn.sigmoid(query_gate[:, 128:])
-    stacked = jnp.concatenate(
-        [jnp.where(lane < HEAD, query, 0.0), jnp.where(lane < HEAD, 0.0, query)], axis=0
-    ).astype(BF16)
     width = 512
-    peak = None
-    for c in range(ALL_TOKS // width):
-        cols = slice(c * width, (c + 1) * width)
-        part = dot_t(stacked, key_value[0, 0, cols, 0:128]) + bias[:, cols].astype(F32)
-        scores[:, cols] = part
-        for w in range(width // 128):
-            tile = part[:, w * 128 : (w + 1) * 128]
-            peak = tile if peak is None else jnp.maximum(peak, tile)
-    top = jnp.max(peak, axis=-1, keepdims=True)
-    for c in range(ALL_TOKS // width):
-        cols = slice(c * width, (c + 1) * width)
-        weights[:, cols] = jnp.exp(scores[:, cols] - top).astype(BF16)
-    total = dot(weights[...], key_value[0, 0, :, 128:256])
-    joined = total / total[:, PAIR : PAIR + 1]
-    joined = jnp.where(lane < HEAD, joined[:TOKS], joined[TOKS:])
-    gated = (joined * gate).astype(BF16)
-    out[seed] = out[seed] + dot(gated[:, :PAIR], mix[0])
+    tops = []
+    for seed in range(SEEDS):
+        query = query_gate[seed * TOKS : (seed + 1) * TOKS, :128] * (HEAD**-0.5)
+        stacked = jnp.concatenate(
+            [jnp.where(lane < HEAD, query, 0.0), jnp.where(lane < HEAD, 0.0, query)], axis=0
+        ).astype(BF16)
+        peak = None
+        for c in range(ALL_TOKS // width):
+            cols = slice(c * width, (c + 1) * width)
+            part = dot_t(stacked, key_value[0, seed, cols, 0:128]) + bias[:, cols].astype(F32)
+            scores[seed, :, cols] = part
+            for w in range(width // 128):
+                tile = part[:, w * 128 : (w + 1) * 128]
+                peak = tile if peak is None else jnp.maximum(peak, tile)
+        tops.append(jnp.max(peak, axis=-1, keepdims=True))
+    for seed in range(SEEDS):
+        total = None
+        for c in range(ALL_TOKS // width):
+            cols = slice(c * width, (c + 1) * width)
+            part = dot(
+                jnp.exp(scores[seed, :, cols] - tops[seed]).astype(BF16),
+                key_value[0, seed, cols, 128:256],
+            )
+            total = part if total is None else total + part
+        joined = total / total[:, PAIR : PAIR + 1]
+        joined = jnp.where(lane < HEAD, joined[:TOKS], joined[TOKS:])
+        gated = (joined * gate[seed * TOKS : (seed + 1) * TOKS]).astype(BF16)
+        out[seed] = out[seed] + dot(gated[:, :PAIR], mix[0])
 
 
 def attend(group_ids, normed, weight, key_value, mix, start, pieces):
@@ -302,40 +356,54 @@
     flat = [ref for parts in pieces for ref in parts]
     grid_spec = pltpu.PrefetchScalarGridSpec(
         num_scalar_prefetch=1,
-        grid=(2 * count,),
+        grid=(count,),
         in_specs=[
-            pl.BlockSpec((1, TOKS, CT), lambda i, ids: (i % 2, 0, 0)),
-            pl.BlockSpec((1, 1, CT, 256), lambda i, ids: (0, ids[i // 2], 0, 0)),
-            pl.BlockSpec((1, 1, ALL_TOKS, 256), lambda i, ids: (ids[i // 2], i % 2, 0, 0)),
-            pl.BlockSpec((1, PAIR, CT), lambda i, ids: (ids[i // 2], 0, 0)),
+            pl.BlockSpec((SEEDS, TOKS, CT), lambda i, ids: (0, 0, 0)),
+            pl.BlockSpec((1, 1, CT, 256), lambda i, ids: (0, ids[i], 0, 0)),
+            pl.BlockSpec((1, SEEDS, ALL_TOKS, 256), lambda i, ids: (ids[i], 0, 0, 0)),
+            pl.BlockSpec((1, PAIR, CT), lambda i, ids: (ids[i], 0, 0)),
             pl.BlockSpec((SEEDS, TOKS, CT), lambda i, ids: (0, 0, 0)),
         ]
         + vmem(len(flat)),
         out_specs=pl.BlockSpec((SEEDS, TOKS, CT), lambda i, ids: (0, 0, 0)),
         scratch_shapes=[
             pltpu.VMEM((2 * TOKS, ALL_TOKS), BF16),
-            pltpu.VMEM((2 * TOKS, ALL_TOKS), F32),
-            pltpu.VMEM((2 * TOKS, ALL_TOKS), BF16),
+            pltpu.VMEM((SEEDS, 2 * TOKS, ALL_TOKS), F32),
         ],
     )
     return pl.pallas_call(
-        functools.partial(attend_kernel, count, tuple(len(parts) for parts in pieces)),
+        functools.partial(attend_kernel, tuple(len(parts) for parts in pieces)),
         grid_spec=grid_spec,
         out_shape=jax.ShapeDtypeStruct((SEEDS, TOKS, CT), F32),
-        compiler_params=params(40),
-        cost_estimate=pl.CostEstimate(
-            flops=count * 10**9, bytes_accessed=count * 4 * 10**6, transcendentals=count * 10**6
-        ),
+        compiler_params=params(50),
+        cost_estimate=SMALL,
         name="attend",
     )(group_ids, normed, weight, key_value, mix, start, *flat)
 
 
-def transition_kernel(residual, wide, narrow, spread_weight, state, spread):
+def transition_kernel(residual, wide_hbm, narrow_hbm, spread_weight, state, spread, wide, narrow, sems):
+    step = 512
+    count = TRANS // step
+    copies = []
+    for c in range(count):
+        gate_cols = pl.ds(c * step, step)
+        up_cols = pl.ds(TRANS + c * step, step)
+        copies.append(
+            [
+                pltpu.make_async_copy(wide_hbm.at[:, gate_cols], wide.at[:, gate_cols], sems.at[c, 0]),
+                pltpu.make_async_copy(wide_hbm.at[:, up_cols], wide.at[:, up_cols], sems.at[c, 1]),
+                pltpu.make_async_copy(narrow_hbm.at[gate_cols], narrow.at[gate_cols], sems.at[c, 2]),
+            ]
+        )
+    for group in copies:
+        for copy in group:
+            copy.start()
     values = residual[...].reshape(SEEDS * TOKS, CT)
     normed = layer_norm(values).astype(BF16)
     total = values
-    step = 512
-    for c in range(TRANS // step):
+    for c in range(count):
+        for copy in copies[c]:
+            copy.wait()
         gate = dot(normed, wide[:, c * step : (c + 1) * step])
         up = dot(normed, wide[:, TRANS + c * step : TRANS + (c + 1) * step])
         hidden = (jax.nn.silu(gate) * up).astype(BF16)
@@ -352,10 +420,15 @@
             jax.ShapeDtypeStruct((SEEDS, TOKS, CT), BF16),
             jax.ShapeDtypeStruct((SEEDS, TOKS, CA), BF16),
         ),
-        in_specs=vmem(4),
+        in_specs=vmem(1) + anywhere(2) + vmem(1),
         out_specs=tuple(vmem(2)),
-        compiler_params=params(40),
-        cost_estimate=pl.CostEstimate(flops=2 * 10**9, bytes_accessed=9 * 10**6, transcendentals=4 * 10**5),
+        scratch_shapes=[
+            pltpu.VMEM((CT, 2 * TRANS), BF16),
+            pltpu.VMEM((TRANS, CT), BF16),
+            pltpu.SemaphoreType.DMA((3, 3)),
+        ],
+        compiler_params=params(58),
+        cost_estimate=SMALL,
         name="transition",
     )(residual, wide, narrow, spread_weight)
 
@@ -364,20 +437,24 @@
     return lax.ppermute(values, "tok", [(i, (i + by) % 16) for i in range(16)])
 
 
+def along_x(values, by):
+    return lax.ppermute(values, "tok", [(i, i // 8 * 8 + (i + 2 * by) % 8) for i in range(16)])
+
+
+def across_z(values):
+    return lax.ppermute(values, "tok", [(i, i ^ 8) for i in range(16)])
+
+
+def across_core(values):
+    return lax.ppermute(values, "tok", [(i, i ^ 1) for i in range(16)])
+
+
 def along_y(values, by):
     return lax.ppermute(values, "seed", [(i, (i + 2 * by) % 8) for i in range(8)])
 
 
 def along_z(values):
     return lax.ppermute(values, "seed", [(i, i ^ 1) for i in range(8)])
-
-
-def y_ring(own):
-    below = along_y(own, 1)
-    above = along_y(own, -1)
-    half = own.shape[1] // 2
-    far = (along_y(below[:, :half], 1), along_y(above[:, half:], -1))
-    return below, above, far
 
 
 def per_device(
@@ -398,9 +475,9 @@
     low = along_tok(jnp.concatenate([feats[-2 * LOWER :], bias_enc[-4 * QB :], tail], axis=0), 1)
     high = along_tok(jnp.concatenate([feats[: 2 * MARGIN], head], axis=0), -1)
 
-    below, above, far = y_ring(pair_bias)
+    below = along_y(pair_bias, 1)
+    above = along_y(pair_bias, -1)
     other = along_z(pair_bias)
-    other_below, other_above, other_far = y_ring(other)
 
     place_low = low[2 * LOWER + 4 * QB, :MARGIN].astype(F32)
     place_high = high[2 * MARGIN, :MARGIN].astype(F32) + TOKS
@@ -423,8 +500,40 @@
     enc_low = along_tok(encoded[:, -MARGIN:], 1)
     enc_high = along_tok(encoded[:, :MARGIN], -1)
 
-    everyone = lax.all_gather(normed, "tok", axis=0)
-    key_value = keys(everyone, weights)
+    core = (tok % 2).astype(jnp.int32).reshape(1)
+    column, floor = tok // 2 % 4, tok // 8
+
+    def chips(*offsets):
+        return jnp.stack([(floor ^ dz) * 4 + (column + dx) % 4 for dx, dz in offsets]).astype(jnp.int32)
+
+    def chip(*parts):
+        return parts, tuple(across_core(part) for part in parts)
+
+    x_below = along_x(normed, 1)
+    x_above = along_x(normed, -1)
+    z_own = across_z(normed)
+    key_value, below, above, other, x_below, x_above, z_own = keys(
+        core, chips((0, 0)), (chip(normed),), weights, None,
+        (below, above, other, x_below, x_above, z_own),
+    )
+    x_far = (along_x(x_below[:1], 1), along_x(x_above[1:], -1))
+    z_below = along_x(z_own, 1)
+    z_above = along_x(z_own, -1)
+    half = TOKS // 2
+    far = (along_y(below[:, :half], 1), along_y(above[:, half:], -1))
+    other_below = along_y(other, 1)
+    other_above = along_y(other, -1)
+    key_value, z_below, z_above = keys(
+        core, chips((3, 0), (1, 0), (0, 1)), (chip(x_below), chip(x_above), chip(z_own)),
+        weights, key_value, (z_below, z_above),
+    )
+    z_far = (along_x(z_below[:1], 1), along_x(z_above[1:], -1))
+    key_value, other_below, other_above = keys(
+        core, chips((2, 0), (3, 1), (1, 1), (2, 1)),
+        (chip(*x_far), chip(z_below), chip(z_above), chip(*z_far)),
+        weights, key_value, (other_below, other_above),
+    )
+    other_far = (along_y(other_below[:, :half], 1), along_y(other_above[:, half:], -1))
 
     level, side = seed // 2, seed % 2
 
@@ -437,9 +546,10 @@
         ((pair_bias,), (below,), (above,), far, (other,)),
     )
     residual = attend(
-        ids((3, 1), (1, 1), (2, 1)), normed, weights, key_value, mix, residual,
-        ((other_below,), (other_above,), other_far),
-    )
+        ids((3, 1), (1, 1)), normed, weights, key_value, mix, residual,
+        ((other_below,), (other_above,)),
+    )
+    residual = attend(ids((2, 1)), normed, weights, key_value, mix, residual, (other_far,))
     state, spread = transition(residual, swiglu_in, swiglu_out, spread_weight)
     spread_low = along_tok(spread[:, -EDGE:], 1)
     spread_high = along_tok(spread[:, :EDGE], -1)

time: 213 us -> 195 us (0.915)
  starting transfers between devices: 24.6 us -> 42.4 us
  waiting for transfers between devices: 42.9 us -> 28.2 us
  between operations: 14.3 us -> 0.91 us
  Pallas kernels: 98.2 us -> 89.4 us
    ppermute x1, waiting for transfers between devices: 33.7 us -> 0.01 us  [along_z(): return lax.ppermute(values, 'seed', [(i, i ^ 1) for i in range(8)])]
    ppermute x0 -> x19, starting transfers between devices: none -> 20.8 us  [the longest x10 15.9 us: across_core(): return lax.ppermute(values, 'tok', [(i, i ^ 1) for i in range(16)])]
    ppermute x0 -> x19, waiting for transfers between devices: none -> 20.7 us  [the longest x8 18.6 us: along_x(): lax.ppermute(values, 'tok', [(i, i // 8 * 8 + (i + 2 * by) % 8) for i in...]
    pallas_call x1, Pallas kernels: 21.5 us -> 9.14 us  [encode(): pl.pallas_call(encode_kernel, out_shape=(jax.ShapeDtypeStruct((SEEDS, ATO...]
    pallas_call x1, Pallas kernels: 19.5 us -> 7.88 us  [decode(): pl.pallas_call(decode_kernel, out_shape=jax.ShapeDtypeStruct((SEEDS * ATO...]
    pallas_call x3 -> x6, Pallas kernels: 48.8 us -> 57.2 us  [the longest x3 29.6 us: attend(): pl.pallas_call(functools.partial(attend_kernel, tuple((len(parts) for par...]
    unnamed x47 -> x53, local copies, waits for them, and re-layouts: 20.8 us -> 15.3 us
    ppermute x6, starting transfers between devices: 11 us -> 7.1 us  [along_tok(): return lax.ppermute(values, 'tok', [(i, (i + by) % 16) for i in range(16)])]
  transfers between devices with their start and end apart: 16 -> 34, of which waited for: 4 -> 10; matrix products, arithmetic and copies ran while one was open for 4% -> 10% of each run, Pallas kernels for 27% -> 39%
where the time goes in v2:
time: 195 us; the launch traced here: 193 us
  Pallas kernels  89.4 us (46%)
  starting transfers between devices  42.4 us (22%)
  local copies, waits for them, and re-layouts  30 us (15%)
  waiting for transfers between devices  28.2 us (14%)
  other arithmetic  2.24 us (1%)
    pallas_call x3, Pallas kernels, attend(): pl.pallas_call(functools.partial(attend_kernel, tuple((len(parts) for par...  29.6 us
    pallas_call x3, Pallas kernels, keys(): pl.pallas_call(functools.partial(keys_kernel, sizes, len(passed)), grid_s...  27.6 us
    ppermute x8, waiting for transfers between devices, along_x(): lax.ppermute(values, 'tok', [(i, i // 8 * 8 + (i + 2 * by) % 8) for i in...  18.6 us
    ppermute x10, starting transfers between devices, across_core(): return lax.ppermute(values, 'tok', [(i, i ^ 1) for i in range(16)])  15.9 us
    unnamed x53, local copies, waits for them, and re-layouts  15.3 us
    ppermute x8, starting transfers between devices, along_y(): lax.ppermute(values, 'seed', [(i, (i + 2 * by) % 8) for i in range(8)])  10.9 us
    pallas_call x1, Pallas kernels, encode(): pl.pallas_call(encode_kernel, out_shape=(jax.ShapeDtypeStruct((SEEDS, ATO...  9.14 us
    pallas_call x1, Pallas kernels, spaced(): pl.pallas_call(spaced_kernel, grid=(8,), out_shape=jax.ShapeDtypeStruct((...  8.86 us
  transfers between devices with their start and end apart: 34, of which 10 were waited for; matrix products, arithmetic and copies ran while one was open for 10% of the time, Pallas kernels for 39%

profile of v2, /device:TPU:7, one launch (start us, length us, event | category | flops | bytes accessed | tf_op | source)
XLA Modules:
  0.0 193.2 jit_solution(13536791307409419021)
XLA Ops:
  3.5 3.6 %collective-permute-start.5 = (bf16[2,128,2048]{2,1,0:T(8,128)(2,1)}, bf16[2,128,2048]{2,1,0:T(8,128)(2,1)}, u32[]{:S(2)}, u32[]{:S(2)}) collective-permute-start(bf16[2,128,2048]{2,1,0:T(8,128)(2,1)} %rest_0_.1), channel_id=1, source_target_pairs={{0,16},{16,0},{32,48},{48,32},{64,80},{80,64},{96,112},{112,96},{1... | collective-permute-start | bytes 3145736 | tf_op jit(solution)/shard_map/ppermute | solution.py:457
  13.7 4.5 %collective-permute-done.1.high = bf16[112,128]{1,0:T(8,128)(2,1)S(1)} collective-permute-done((bf16[112,128]{1,0:T(8,128)(2,1)S(1)}, bf16[112,128]{1,0:T(8,128)(2,1)S(1)}, u32[]{:S(2)}, u32[]{:S(2)}) %collective-permute-start.1) | collective-permute-done | bytes 28704 | tf_op jit(solution)/shard_map/ppermute | solution.py:437
  18.7 9.1 %encode.1 = (bf16[2,1024,128]{2,1,0:T(8,128)(2,1)}, f32[2,128,768]{2,1,0:T(8,128)}, bf16[2,128,768]{2,1,0:T(8,128)(2,1)}) custom-call(s32[1]{0:T(128)} %bitcast.1.tok, bf16[2048,128]{1,0:T(8,128)(2,1)} %bitcast.39, bf16[304,128]{1,0:T(8,128)(2,1)} %copy-done.20, bf16[112,128]{1,0:T(8,128)(2,1)} %copy-done.21, bf16[4096,128]{1,0:T(8,128)(2,1)} %bitcast.37, ...), custom_call_target="tpu_custom_call" | custom-call | flops 1000000 | bytes 10000 | tf_op jit(solution)/shard_map/encode/pallas_call | solution.py:135
  29.8 8.7 %collective-permute-done.6.refs_6_ = bf16[2,128,768]{2,1,0:T(8,128)(2,1)} collective-permute-done((bf16[2,128,768]{2,1,0:T(8,128)(2,1)}, bf16[2,128,768]{2,1,0:T(8,128)(2,1)}, u32[]{:S(2)}, u32[]{:S(2)}) %collective-permute-start.6) | collective-permute-done | bytes 393248 | tf_op jit(solution)/shard_map/ppermute | solution.py:441
  38.9 8.9 %spaced.1.refs_2_.refs_6_.refs_12_.weight = bf16[2,8,768,256]{3,2,1,0:T(8,128)(2,1)} custom-call(bf16[768,3072]{1,0:T(8,128)(2,1)} %weight.1), custom_call_target="tpu_custom_call" | custom-call | flops 1000000 | bytes 10000 | tf_op jit(solution)/shard_map/spaced/pallas_call | solution.py:219
  48.2 5.6 %keys.3 = (bf16[8,2,2048,256]{3,2,1,0:T(8,128)(2,1)}, bf16[2,128,2048]{2,1,0:T(8,128)(2,1)S(1)}, bf16[2,128,2048]{2,1,0:T(8,128)(2,1)S(1)}, bf16[2,128,2048]{2,1...) custom-call(s32[2]{0:T(128)S(1)} %pad_add_fusion.at, ...), custom_call_target="tpu_custom_call", output_to_operand_aliasing={{1}: (4, {}), {2}: (5, {}), {3}: (6, {}), {4}: (7, {}), {5}... | custom-call | flops 1000000 | bytes 10000 | tf_op jit(solution)/shard_map/keys/pallas_call | solution.py:284
  59.5 3.4 %collective-permute-done.9.refs_0_ = bf16[1,128,768]{2,1,0:T(8,128)(2,1)} collective-permute-done((bf16[1,128,768]{2,1,0:T(8,128)(2,1)S(1)}, bf16[1,128,768]{2,1,0:T(8,128)(2,1)}, u32[]{:S(2)}, u32[]{:S(2)}) %collective-permute-start.9) | collective-permute-done | bytes 196640 | tf_op jit(solution)/shard_map/ppermute | solution.py:441
  63.8 2.6 %collective-permute-start.25 = (bf16[2,128,2048]{2,1,0:T(8,128)(2,1)}, bf16[2,128,2048]{2,1,0:T(8,128)(2,1)}, u32[]{:S(2)}, u32[]{:S(2)}) collective-permute-start(bf16[2,128,2048]{2,1,0:T(8,128)(2,1)} %get-tuple-element.28.rest_5_), channel_id=1, source_target_pairs={{0,96},{16,112},{32,0},{48,16},{64,32},{80,48},{96,64},{112,80},{1... | collective-permute-start | bytes 3145736 | tf_op jit(solution)/shard_map/ppermute | solution.py:453
  71.4 2.5 %collective-permute-start.11 = (bf16[1,128,768]{2,1,0:T(8,128)(2,1)}, bf16[1,128,768]{2,1,0:T(8,128)(2,1)}, u32[]{:S(2)}, u32[]{:S(2)}) collective-permute-start(bf16[1,128,768]{2,1,0:T(8,128)(2,1)} %collective-permute-done.9.refs_0_), channel_id=1, source_target_pairs={{0,1},{1,0},{2,3},{3,2},{4,5},{5,4},{6,7},{7,6},{8,9},{9,8},{10,11... | collective-permute-start | bytes 589832 | tf_op jit(solution)/shard_map/ppermute | solution.py:449
  74.0 2.3 %collective-permute-done.17.refs_9_ = bf16[2,128,768]{2,1,0:T(8,128)(2,1)} collective-permute-done((bf16[2,128,768]{2,1,0:T(8,128)(2,1)}, bf16[2,128,768]{2,1,0:T(8,128)(2,1)}, u32[]{:S(2)}, u32[]{:S(2)}) %collective-permute-start.17) | collective-permute-done | bytes 393248 | tf_op jit(solution)/shard_map/ppermute | solution.py:441
  79.2 9.8 %keys.4 = (bf16[8,2,2048,256]{3,2,1,0:T(8,128)(2,1)}, bf16[2,128,768]{2,1,0:T(8,128)(2,1)}, bf16[2,128,768]{2,1,0:T(8,128)(2,1)}) custom-call(s32[4]{0:T(128)S(1)} %pad_add_fusion.1.at, bf16[2,128,768]{2,1,0:T(8,128)(2,1)} %get-tuple-element.21.refs_0_, ...), custom_call_target="tpu_custom_call", output_to_operand_aliasing={{0}: (8, {}), {1}: (9, {}), {2}: (10, {})} | custom-call | flops 1000000 | bytes 10000 | tf_op jit(solution)/shard_map/keys/pallas_call | solution.py:284
  91.4 6.5 %collective-permute-start.12 = (bf16[1,128,768]{2,1,0:T(8,128)(2,1)}, bf16[1,128,768]{2,1,0:T(8,128)(2,1)S(1)}, u32[]{:S(2)}, u32[]{:S(2)}) collective-permute-start(bf16[1,128,768]{2,1,0:T(8,128)(2,1)} %collective-permute-done.10.refs_1_), channel_id=1, source_target_pairs={{0,1},{1,0},{2,3},{3,2},{4,5},{5,4},{6,7},{7,6},{8,9},{9,8},{10,11... | collective-permute-start | bytes 589832 | tf_op jit(solution)/shard_map/ppermute | solution.py:449
  98.9 2.9 %collective-permute-start.22 = (bf16[1,128,768]{2,1,0:T(8,128)(2,1)S(1)}, bf16[1,128,768]{2,1,0:T(8,128)(2,1)S(1)}, u32[]{:S(2)}, u32[]{:S(2)}) collective-permute-start(bf16[1,128,768]{2,1,0:T(8,128)(2,1)S(1)} %collective-permute-done.20.refs_8_), channel_id=1, source_target_pairs={{0,1},{1,0},{2,3},{3,2},{4,5},{5,4},{6,7},{7,6},{8,9},{9,8},{10,11... | collective-permute-start | bytes 589832 | tf_op jit(solution)/shard_map/ppermute | solution.py:449
  103.2 3.6 %collective-permute-done.21.refs_9_ = bf16[1,128,768]{2,1,0:T(8,128)(2,1)} collective-permute-done((bf16[1,128,768]{2,1,0:T(8,128)(2,1)S(1)}, bf16[1,128,768]{2,1,0:T(8,128)(2,1)}, u32[]{:S(2)}, u32[]{:S(2)}) %collective-permute-start.21) | collective-permute-done | bytes 196640 | tf_op jit(solution)/shard_map/ppermute | solution.py:441
  110.1 2.7 %collective-permute-start.27 = (bf16[2,64,2048]{2,1,0:T(8,128)(2,1)}, bf16[2,64,2048]{2,1,0:T(8,128)(2,1)}, u32[]{:S(2)}, u32[]{:S(2)}) collective-permute-start(bf16[2,64,2048]{2,1,0:T(8,128)(2,1)} %slice.89), channel_id=1, source_target_pairs={{0,96},{16,112},{32,0},{48,16},{64,32},{80,48},{96,64},{112,80},{1... | collective-permute-start | bytes 1572872 | tf_op jit(solution)/shard_map/ppermute | solution.py:453
  116.5 12.3 %keys.5 = (bf16[8,2,2048,256]{3,2,1,0:T(8,128)(2,1)}, bf16[2,128,2048]{2,1,0:T(8,128)(2,1)}, bf16[2,128,2048]{2,1,0:T(8,128)(2,1)}) custom-call(s32[5]{0:T(128)S(1)} %concatenate.33.at, bf16[1,128,768]{2,1,0:T(8,128)(2,1)} %collective-permute-done.9.refs_0_, ...), custom_call_target="tpu_custom_call", output_to_operand_aliasing={{0}: (14, {}), {1}: (15, {}), {2}: (16, {})} | custom-call | flops 1000000 | bytes 10000 | tf_op jit(solution)/shard_map/keys/pallas_call | solution.py:284
  132.6 2.7 %collective-permute-start.29 = (bf16[2,64,2048]{2,1,0:T(8,128)(2,1)}, bf16[2,64,2048]{2,1,0:T(8,128)(2,1)S(1)}, u32[]{:S(2)}, u32[]{:S(2)}) collective-permute-start(bf16[2,64,2048]{2,1,0:T(8,128)(2,1)} %slice.91), channel_id=1, source_target_pairs={{0,96},{16,112},{32,0},{48,16},{64,32},{80,48},{96,64},{112,80},{1... | collective-permute-start | bytes 1572872 | tf_op jit(solution)/shard_map/ppermute | solution.py:453
  138.8 17.1 %attend.3.start = f32[2,128,768]{2,1,0:T(8,128)S(1)} custom-call(s32[5]{0:T(128)S(1)} %stack.71.group_ids, bf16[2,128,768]{2,1,0:T(8,128)(2,1)S(1)} %copy-done.4, bf16[2,8,768,256]{3,2,1,0:T(8,128)(2,1)} %spaced.1.refs_2_.refs_6_.refs_12_.weight, bf16[8,2,2048,256]{3,2,1,0:T(8,128)(2,1)} %get-tuple-element.29.key_value, bf16[8,96,768]{2,1,0:T(8,128)(2,1)} %bitcast.34, ...), custom_call_target="tpu_custom_call" | custom-call | flops 1000000 | bytes 10000 | tf_op jit(solution)/shard_map/attend/pallas_call | solution.py:374
  155.9 8.4 %attend.4.start = f32[2,128,768]{2,1,0:T(8,128)S(1)} custom-call(s32[2]{0:T(128)S(1)} %pad_add_fusion.2.group_ids, bf16[2,128,768]{2,1,0:T(8,128)(2,1)S(1)} %copy-done.4, bf16[2,8,768,256]{3,2,1,0:T(8,128)(2,1)} %spaced.1.refs_2_.refs_6_.refs_12_.weight, bf16[8,2,2048,256]{3,2,1,0:T(8,128)(2,1)} %get-tuple-element.29.key_value, ...), custom_call_target="tpu_custom_call" | custom-call | flops 1000000 | bytes 10000 | tf_op jit(solution)/shard_map/attend/pallas_call | solution.py:374
  164.4 4.1 %attend.5.residual = f32[2,128,768]{2,1,0:T(8,128)S(1)} custom-call(s32[1]{0:T(128)} %bitcast.group_ids, bf16[2,128,768]{2,1,0:T(8,128)(2,1)S(1)} %copy-done.4, bf16[2,8,768,256]{3,2,1,0:T(8,128)(2,1)} %spaced.1.refs_2_.refs_6_.refs_12_.weight, bf16[8,2,2048,256]{3,2,1,0:T(8,128)(2,1)} %get-tuple-element.29.key_value, bf16[8,96,768]{2,1,0:T(8,128)(2,1)} %bitcast.36, ...), custom_call_target="tpu_custom_call" | custom-call | flops 1000000 | bytes 10000 | tf_op jit(solution)/shard_map/attend/pallas_call | solution.py:374
  169.4 6.3 %transition.1 = (bf16[2,128,768]{2,1,0:T(8,128)(2,1)}, bf16[2,128,128]{2,1,0:T(8,128)(2,1)}) custom-call(f32[2,128,768]{2,1,0:T(8,128)} %copy-done.5, bf16[768,3072]{1,0:T(8,128)(2,1)} %wide_hbm.1, bf16[1536,768]{1,0:T(8,128)(2,1)} %narrow_hbm.1, bf16[768,128]{1,0:T(8,128)(2,1)} %spread_weight.1), custom_call_target="tpu_custom_call" | custom-call | flops 1000000 | bytes 10000 | tf_op jit(solution)/shard_map/transition/pallas_call | solution.py:417
  176.4 3.1 %collective-permute-start.32 = (bf16[2,16,128]{2,1,0:T(8,128)(2,1)S(1)}, bf16[2,16,128]{2,1,0:T(8,128)(2,1)S(1)}, u32[]{:S(2)}, u32[]{:S(2)}) collective-permute-start(bf16[2,16,128]{2,1,0:T(8,128)(2,1)S(1)} %get-tuple-element.45), channel_id=1, source_target_pairs={{0,1},{1,2},{2,3},{3,4},{4,5},{5,6},{6,7},{7,8},{8,9},{9,10},{10,1... | collective-permute-start | bytes 24584 | tf_op jit(solution)/shard_map/ppermute | solution.py:437
  182.3 2.4 %collective-permute-done.33.spread_high = bf16[2,16,128]{2,1,0:T(8,128)(2,1)S(1)} collective-permute-done((bf16[2,16,128]{2,1,0:T(8,128)(2,1)S(1)}, bf16[2,16,128]{2,1,0:T(8,128)(2,1)S(1)}, u32[]{:S(2)}, u32[]{:S(2)}) %collective-permute-start.33) | collective-permute-done | bytes 8224 | tf_op jit(solution)/shard_map/ppermute | solution.py:437
  185.3 7.9 %decode.1 = bf16[2048,128]{1,0:T(8,128)(2,1)} custom-call(s32[1]{0:T(128)} %bitcast.1.tok, bf16[2,1024,128]{2,1,0:T(8,128)(2,1)} %get-tuple-element.36.enc, bf16[2,48,128]{2,1,0:T(8,128)(2,1)} %copy-done.22, bf16[2,48,128]{2,1,0:T(8,128)(2,1)} %copy-done.23, bf16[2,128,128]{2,1,0:T(8,128)(2,1)} %get-tuple-element.37.spread, bf16[2,16,128]{2,1,0:T(8,128)(2,1)} %copy-done.24, ...), custom_call_target="tpu_custom_call" | custom-call | flops 1000000 | bytes 10000 | tf_op jit(solution)/shard_map/decode/pallas_call | solution.py:188
  (139 shorter events, 51.5 us)
Async XLA Ops:
  0.6 47.5 %collective-permute-start.3 = (bf16[2,128,2048]{2,1,0:T(8,128)(2,1)}, bf16[2,128,2048]{2,1,0:T(8,128)(2,1)S(1)}, u32[]{:S(2)}, u32[]{:S(2)}) collective-permute-start(bf16[2,128,2048]{2,1,0:T(8,128)(2,1)} %rest_0_.1), channel_id=1, source_target_pairs={{0,32},{16,48},{32,64},{48,80},{64,96},{80,112},{96,0},{112,16},{1... | collective-permute-start | bytes 3145736 | tf_op jit(solution)/shard_map/ppermute | solution.py:453
  2.0 46.2 %collective-permute-start.4 = (bf16[2,128,2048]{2,1,0:T(8,128)(2,1)}, bf16[2,128,2048]{2,1,0:T(8,128)(2,1)S(1)}, u32[]{:S(2)}, u32[]{:S(2)}) collective-permute-start(bf16[2,128,2048]{2,1,0:T(8,128)(2,1)} %rest_0_.1), channel_id=1, source_target_pairs={{0,96},{16,112},{32,0},{48,16},{64,32},{80,48},{96,64},{112,80},{1... | collective-permute-start | bytes 3145736 | tf_op jit(solution)/shard_map/ppermute | solution.py:453
  3.5 44.7 %collective-permute-start.5 = (bf16[2,128,2048]{2,1,0:T(8,128)(2,1)}, bf16[2,128,2048]{2,1,0:T(8,128)(2,1)}, u32[]{:S(2)}, u32[]{:S(2)}) collective-permute-start(bf16[2,128,2048]{2,1,0:T(8,128)(2,1)} %rest_0_.1), channel_id=1, source_target_pairs={{0,16},{16,0},{32,48},{48,32},{64,80},{80,64},{96,112},{112,96},{1... | collective-permute-start | bytes 3145736 | tf_op jit(solution)/shard_map/ppermute | solution.py:457
  27.9 10.6 %collective-permute-start.6 = (bf16[2,128,768]{2,1,0:T(8,128)(2,1)}, bf16[2,128,768]{2,1,0:T(8,128)(2,1)}, u32[]{:S(2)}, u32[]{:S(2)}) collective-permute-start(bf16[2,128,768]{2,1,0:T(8,128)(2,1)} %get-tuple-element.20.refs_0_.normed), channel_id=1, source_target_pairs={{0,2},{1,3},{2,4},{3,5},{4,6},{5,7},{6,0},{7,1},{8,10},{9,11},{10,... | collective-permute-start | bytes 1179656 | tf_op jit(solution)/shard_map/ppermute | solution.py:441
  29.8 18.1 %collective-permute-start.7 = (bf16[2,128,768]{2,1,0:T(8,128)(2,1)}, bf16[2,128,768]{2,1,0:T(8,128)(2,1)}, u32[]{:S(2)}, u32[]{:S(2)}) collective-permute-start(bf16[2,128,768]{2,1,0:T(8,128)(2,1)} %get-tuple-element.20.refs_0_.normed), channel_id=1, source_target_pairs={{0,6},{1,7},{2,0},{3,1},{4,2},{5,3},{6,4},{7,5},{8,14},{9,15},{10,... | collective-permute-start | bytes 1179656 | tf_op jit(solution)/shard_map/ppermute | solution.py:441
  38.5 9.6 %collective-permute-start.8 = (bf16[2,128,768]{2,1,0:T(8,128)(2,1)}, bf16[2,128,768]{2,1,0:T(8,128)(2,1)}, u32[]{:S(2)}, u32[]{:S(2)}) collective-permute-start(bf16[2,128,768]{2,1,0:T(8,128)(2,1)} %get-tuple-element.20.refs_0_.normed), channel_id=1, source_target_pairs={{0,8},{1,9},{2,10},{3,11},{4,12},{5,13},{6,14},{7,15},{8,0},{9,1},... | collective-permute-start | bytes 1179656 | tf_op jit(solution)/shard_map/ppermute | solution.py:445
  53.7 9.3 %collective-permute-start.13 = (bf16[2,128,768]{2,1,0:T(8,128)(2,1)}, bf16[2,128,768]{2,1,0:T(8,128)(2,1)S(1)}, u32[]{:S(2)}, u32[]{:S(2)}) collective-permute-start(bf16[2,128,768]{2,1,0:T(8,128)(2,1)} %get-tuple-element.21.refs_0_), channel_id=1, source_target_pairs={{0,1},{1,0},{2,3},{3,2},{4,5},{5,4},{6,7},{7,6},{8,9},{9,8},{10,11... | collective-permute-start | bytes 1179656 | tf_op jit(solution)/shard_map/ppermute | solution.py:449
  55.9 10.4 %collective-permute-start.14 = (bf16[2,128,768]{2,1,0:T(8,128)(2,1)}, bf16[2,128,768]{2,1,0:T(8,128)(2,1)S(1)}, u32[]{:S(2)}, u32[]{:S(2)}) collective-permute-start(bf16[2,128,768]{2,1,0:T(8,128)(2,1)} %get-tuple-element.22.refs_2_), channel_id=1, source_target_pairs={{0,1},{1,0},{2,3},{3,2},{4,5},{5,4},{6,7},{7,6},{8,9},{9,8},{10,11... | collective-permute-start | bytes 1179656 | tf_op jit(solution)/shard_map/ppermute | solution.py:449
  58.6 10.2 %collective-permute-start.15 = (bf16[2,128,768]{2,1,0:T(8,128)(2,1)}, bf16[2,128,768]{2,1,0:T(8,128)(2,1)S(1)}, u32[]{:S(2)}, u32[]{:S(2)}) collective-permute-start(bf16[2,128,768]{2,1,0:T(8,128)(2,1)} %get-tuple-element.23.refs_4_), channel_id=1, source_target_pairs={{0,1},{1,0},{2,3},{3,2},{4,5},{5,4},{6,7},{7,6},{8,9},{9,8},{10,11... | collective-permute-start | bytes 1179656 | tf_op jit(solution)/shard_map/ppermute | solution.py:449
  59.5 11.9 %collective-permute-start.16 = (bf16[2,128,768]{2,1,0:T(8,128)(2,1)}, bf16[2,128,768]{2,1,0:T(8,128)(2,1)}, u32[]{:S(2)}, u32[]{:S(2)}) collective-permute-start(bf16[2,128,768]{2,1,0:T(8,128)(2,1)} %get-tuple-element.23.refs_4_), channel_id=1, source_target_pairs={{0,2},{1,3},{2,4},{3,5},{4,6},{5,7},{6,0},{7,1},{8,10},{9,11},{10,... | collective-permute-start | bytes 1179656 | tf_op jit(solution)/shard_map/ppermute | solution.py:441
  62.9 49.8 %collective-permute-start.24 = (bf16[2,128,2048]{2,1,0:T(8,128)(2,1)}, bf16[2,128,2048]{2,1,0:T(8,128)(2,1)S(1)}, u32[]{:S(2)}, u32[]{:S(2)}) collective-permute-start(bf16[2,128,2048]{2,1,0:T(8,128)(2,1)} %get-tuple-element.28.rest_5_), channel_id=1, source_target_pairs={{0,32},{16,48},{32,64},{48,80},{64,96},{80,112},{96,0},{112,16},{1... | collective-permute-start | bytes 3145736 | tf_op jit(solution)/shard_map/ppermute | solution.py:453
  63.8 49.0 %collective-permute-start.25 = (bf16[2,128,2048]{2,1,0:T(8,128)(2,1)}, bf16[2,128,2048]{2,1,0:T(8,128)(2,1)}, u32[]{:S(2)}, u32[]{:S(2)}) collective-permute-start(bf16[2,128,2048]{2,1,0:T(8,128)(2,1)} %get-tuple-element.28.rest_5_), channel_id=1, source_target_pairs={{0,96},{16,112},{32,0},{48,16},{64,32},{80,48},{96,64},{112,80},{1... | collective-permute-start | bytes 3145736 | tf_op jit(solution)/shard_map/ppermute | solution.py:453
  67.1 9.1 %collective-permute-start.17 = (bf16[2,128,768]{2,1,0:T(8,128)(2,1)}, bf16[2,128,768]{2,1,0:T(8,128)(2,1)}, u32[]{:S(2)}, u32[]{:S(2)}) collective-permute-start(bf16[2,128,768]{2,1,0:T(8,128)(2,1)} %get-tuple-element.23.refs_4_), channel_id=1, source_target_pairs={{0,6},{1,7},{2,0},{3,1},{4,2},{5,3},{6,4},{7,5},{8,14},{9,15},{10,... | collective-permute-start | bytes 1179656 | tf_op jit(solution)/shard_map/ppermute | solution.py:441
  69.5 21.9 %collective-permute-start.10 = (bf16[1,128,768]{2,1,0:T(8,128)(2,1)}, bf16[1,128,768]{2,1,0:T(8,128)(2,1)}, u32[]{:S(2)}, u32[]{:S(2)}) collective-permute-start(bf16[1,128,768]{2,1,0:T(8,128)(2,1)} %slice.85), channel_id=1, source_target_pairs={{0,6},{1,7},{2,0},{3,1},{4,2},{5,3},{6,4},{7,5},{8,14},{9,15},{10,... | collective-permute-start | bytes 589832 | tf_op jit(solution)/shard_map/ppermute | solution.py:441
  71.4 27.5 %collective-permute-start.11 = (bf16[1,128,768]{2,1,0:T(8,128)(2,1)}, bf16[1,128,768]{2,1,0:T(8,128)(2,1)}, u32[]{:S(2)}, u32[]{:S(2)}) collective-permute-start(bf16[1,128,768]{2,1,0:T(8,128)(2,1)} %collective-permute-done.9.refs_0_), channel_id=1, source_target_pairs={{0,1},{1,0},{2,3},{3,2},{4,5},{5,4},{6,7},{7,6},{8,9},{9,8},{10,11... | collective-permute-start | bytes 589832 | tf_op jit(solution)/shard_map/ppermute | solution.py:449
  89.9 9.0 %collective-permute-start.20 = (bf16[1,128,768]{2,1,0:T(8,128)(2,1)S(1)}, bf16[1,128,768]{2,1,0:T(8,128)(2,1)S(1)}, u32[]{:S(2)}, u32[]{:S(2)}) collective-permute-start(bf16[1,128,768]{2,1,0:T(8,128)(2,1)S(1)} %slice.86), channel_id=1, source_target_pairs={{0,2},{1,3},{2,4},{3,5},{4,6},{5,7},{6,0},{7,1},{8,10},{9,11},{10,... | collective-permute-start | bytes 589832 | tf_op jit(solution)/shard_map/ppermute | solution.py:441
  91.4 11.1 %collective-permute-start.12 = (bf16[1,128,768]{2,1,0:T(8,128)(2,1)}, bf16[1,128,768]{2,1,0:T(8,128)(2,1)S(1)}, u32[]{:S(2)}, u32[]{:S(2)}) collective-permute-start(bf16[1,128,768]{2,1,0:T(8,128)(2,1)} %collective-permute-done.10.refs_1_), channel_id=1, source_target_pairs={{0,1},{1,0},{2,3},{3,2},{4,5},{5,4},{6,7},{7,6},{8,9},{9,8},{10,11... | collective-permute-start | bytes 589832 | tf_op jit(solution)/shard_map/ppermute | solution.py:449
  98.9 8.6 %collective-permute-start.22 = (bf16[1,128,768]{2,1,0:T(8,128)(2,1)S(1)}, bf16[1,128,768]{2,1,0:T(8,128)(2,1)S(1)}, u32[]{:S(2)}, u32[]{:S(2)}) collective-permute-start(bf16[1,128,768]{2,1,0:T(8,128)(2,1)S(1)} %collective-permute-done.20.refs_8_), channel_id=1, source_target_pairs={{0,1},{1,0},{2,3},{3,2},{4,5},{5,4},{6,7},{7,6},{8,9},{9,8},{10,11... | collective-permute-start | bytes 589832 | tf_op jit(solution)/shard_map/ppermute | solution.py:449
  110.1 27.7 %collective-permute-start.26 = (bf16[2,64,2048]{2,1,0:T(8,128)(2,1)}, bf16[2,64,2048]{2,1,0:T(8,128)(2,1)}, u32[]{:S(2)}, u32[]{:S(2)}) collective-permute-start(bf16[2,64,2048]{2,1,0:T(8,128)(2,1)} %slice.88), channel_id=1, source_target_pairs={{0,32},{16,48},{32,64},{48,80},{64,96},{80,112},{96,0},{112,16},{1... | collective-permute-start | bytes 1572872 | tf_op jit(solution)/shard_map/ppermute | solution.py:453
  110.1 28.7 %collective-permute-start.27 = (bf16[2,64,2048]{2,1,0:T(8,128)(2,1)}, bf16[2,64,2048]{2,1,0:T(8,128)(2,1)}, u32[]{:S(2)}, u32[]{:S(2)}) collective-permute-start(bf16[2,64,2048]{2,1,0:T(8,128)(2,1)} %slice.89), channel_id=1, source_target_pairs={{0,96},{16,112},{32,0},{48,16},{64,32},{80,48},{96,64},{112,80},{1... | collective-permute-start | bytes 1572872 | tf_op jit(solution)/shard_map/ppermute | solution.py:453
  130.7 33.7 %collective-permute-start.28 = (bf16[2,64,2048]{2,1,0:T(8,128)(2,1)}, bf16[2,64,2048]{2,1,0:T(8,128)(2,1)S(1)}, u32[]{:S(2)}, u32[]{:S(2)}) collective-permute-start(bf16[2,64,2048]{2,1,0:T(8,128)(2,1)} %slice.90), channel_id=1, source_target_pairs={{0,32},{16,48},{32,64},{48,80},{64,96},{80,112},{96,0},{112,16},{1... | collective-permute-start | bytes 1572872 | tf_op jit(solution)/shard_map/ppermute | solution.py:453
  132.6 31.8 %collective-permute-start.29 = (bf16[2,64,2048]{2,1,0:T(8,128)(2,1)}, bf16[2,64,2048]{2,1,0:T(8,128)(2,1)S(1)}, u32[]{:S(2)}, u32[]{:S(2)}) collective-permute-start(bf16[2,64,2048]{2,1,0:T(8,128)(2,1)} %slice.91), channel_id=1, source_target_pairs={{0,96},{16,112},{32,0},{48,16},{64,32},{80,48},{96,64},{112,80},{1... | collective-permute-start | bytes 1572872 | tf_op jit(solution)/shard_map/ppermute | solution.py:453
  136.7 45.5 %collective-permute-start.30 = (bf16[2,48,128]{2,1,0:T(8,128)(2,1)S(1)}, bf16[2,48,128]{2,1,0:T(8,128)(2,1)S(1)}, u32[]{:S(2)}, u32[]{:S(2)}) collective-permute-start(bf16[2,48,128]{2,1,0:T(8,128)(2,1)S(1)} %get-tuple-element.43), channel_id=1, source_target_pairs={{0,1},{1,2},{2,3},{3,4},{4,5},{5,6},{6,7},{7,8},{8,9},{9,10},{10,1... | collective-permute-start | bytes 73736 | tf_op jit(solution)/shard_map/ppermute | solution.py:437
  137.7 44.5 %collective-permute-start.31 = (bf16[2,48,128]{2,1,0:T(8,128)(2,1)S(1)}, bf16[2,48,128]{2,1,0:T(8,128)(2,1)S(1)}, u32[]{:S(2)}, u32[]{:S(2)}) collective-permute-start(bf16[2,48,128]{2,1,0:T(8,128)(2,1)S(1)} %get-tuple-element.42), channel_id=1, source_target_pairs={{0,15},{1,0},{2,1},{3,2},{4,3},{5,4},{6,5},{7,6},{8,7},{9,8},{10,9... | collective-permute-start | bytes 73736 | tf_op jit(solution)/shard_map/ppermute | solution.py:437
  (36 other events, 268.6 us)

commit v3 on v2

v3 whole, which is shorter than its diff:
```python
import functools

import jax
import jax.numpy as jnp
from jax import lax
from jax.experimental import pallas as pl
from jax.experimental.pallas import tpu as pltpu
from jax.sharding import PartitionSpec as P

EPS = 1e-05
NEG = -1000000000.0
F32 = jnp.float32
BF16 = jnp.bfloat16

SEEDS = 2
ATOMS = 1024
TOKS = 128
CA = 128
CT = 768
HEADS = 16
HEAD = 48
PAIR = 96
GROUPS = 8
QB = 32
WIN = 128
MARGIN = 48
LOWER = 80
EXT = 1152
EDGE = 16
TRANS = 1536
ALL_TOKS = 2048
ALL_ATOMS = 16384
UP_ROWS = 2 * LOWER + 4 * QB + 16
DOWN_ROWS = 2 * MARGIN + 16


SMALL = pl.CostEstimate(flops=10**6, bytes_accessed=10**4, transcendentals=0)
LARGE = pl.CostEstimate(flops=10**11, bytes_accessed=10**4, transcendentals=0)


def params(limit_mb, **more):
    return pltpu.CompilerParams(vmem_limit_bytes=limit_mb * 1024 * 1024, **more)


def vmem(n):
    return [pl.BlockSpec(memory_space=pltpu.VMEM)] * n


def anywhere(n):
    return [pl.BlockSpec(memory_space=pltpu.HBM)] * n


def layer_norm(values):
    centre = values - jnp.mean(values, axis=-1, keepdims=True)
    variance = jnp.mean(centre * centre, axis=-1, keepdims=True)
    return centre * lax.rsqrt(variance + EPS)


def dot(a, b):
    return jnp.dot(a, b, preferred_element_type=F32)


def dot_t(a, b):
    return lax.dot_general(a, b, (((1,), (1,)), ((), ())), preferred_element_type=F32)


def window_blocks(packed, bias, mixed, blocks, first_atom, unroll):
    lane_head = lax.broadcasted_iota(jnp.int32, (QB, CA), 1) // 32
    head_mask = [(lane_head == h).astype(BF16) for h in range(4)]
    lane = lax.broadcasted_iota(jnp.int32, (1, WIN), 1)
    ones = jnp.ones((WIN, CA), BF16)
    for b in (0, 1, 2, blocks - 2, blocks - 1):
        position = lane + (first_atom + b * QB)
        inside = (position >= 0) & (position < ALL_ATOMS)
        place = slice(b * 4 * QB, (b + 1) * 4 * QB)
        bias[place] = jnp.where(inside, bias[place], NEG)

    def body(i, carry):
        work = []
        for u in range(unroll):
            b = i * unroll + u
            rows = pl.multiple_of(b * QB, QB)
            query_rows = pl.multiple_of(b * QB + MARGIN, 16)
            bias_rows = pl.multiple_of(b * 4 * QB, 4 * QB)
            added = jnp.concatenate(
                [bias[pl.ds(bias_rows + h, QB, stride=4), :] for h in range(4)], axis=0
            )
            for seed in range(SEEDS):
                work.append((rows, query_rows, added, seed))
        scores = []
        for rows, query_rows, added, seed in work:
            query = packed[seed, pl.ds(query_rows, QB), 0:CA]
            key = packed[seed, pl.ds(rows, WIN), CA : 2 * CA]
            stacked = jnp.concatenate([query * head_mask[h] for h in range(4)], axis=0)
            scores.append(dot_t(stacked, key) * (32**-0.5) + added)
        weights = [jnp.exp(s - jnp.max(s, axis=-1, keepdims=True)).astype(BF16) for s in scores]
        for (rows, _, _, seed), w in zip(work, weights):
            value = jnp.concatenate([packed[seed, pl.ds(rows, WIN), 2 * CA : 3 * CA], ones], axis=1)
            out = dot(w, value)
            joined = out[3 * QB :]
            for h in range(3):
                joined = jnp.where(jnp.concatenate([lane_head, lane_head], axis=1) == h, out[h * QB : (h + 1) * QB], joined)
            mixed[seed, pl.ds(rows, QB), :] = (joined[:, :CA] / joined[:, CA:]).astype(BF16)
        return carry

    lax.fori_loop(0, blocks // unroll, body, 0)


def pack_kernel(place, feats, bias, index, pair_bias, up, down, send, joined, rows, sems):
    base, core = place[0] * TOKS, place[1]
    rows[0:16] = jnp.broadcast_to((index[7:8] - (base + TOKS)).astype(F32).astype(BF16), (16, CA))
    rows[16:32] = jnp.broadcast_to((index[0:1] - base).astype(F32).astype(BF16), (16, CA))
    moves = (
        (pair_bias.at[1 - core], send),
        (pair_bias.at[core], joined.at[pl.ds(0, TOKS)]),
        (feats.at[pl.ds(2 * (ATOMS - LOWER), 2 * LOWER)], up.at[pl.ds(0, 2 * LOWER)]),
        (bias.at[pl.ds(4 * (ATOMS - QB), 4 * QB)], up.at[pl.ds(2 * LOWER, 4 * QB)]),
        (rows.at[pl.ds(0, 16)], up.at[pl.ds(2 * LOWER + 4 * QB, 16)]),
        (feats.at[pl.ds(0, 2 * MARGIN)], down.at[pl.ds(0, 2 * MARGIN)]),
        (rows.at[pl.ds(16, 16)], down.at[pl.ds(2 * MARGIN, 16)]),
    )
    copies = [pltpu.make_async_copy(a, b, sems.at[i]) for i, (a, b) in enumerate(moves)]
    for copy in copies:
        copy.start()
    for copy in copies:
        copy.wait()


def pack(place, feats, bias, index, pair_bias):
    return pl.pallas_call(
        pack_kernel,
        out_shape=(
            jax.ShapeDtypeStruct((UP_ROWS, CA), BF16),
            jax.ShapeDtypeStruct((DOWN_ROWS, CA), BF16),
            jax.ShapeDtypeStruct((TOKS, ALL_TOKS), BF16),
            jax.ShapeDtypeStruct((2 * TOKS, ALL_TOKS), BF16),
        ),
        in_specs=[pl.BlockSpec(memory_space=pltpu.SMEM)] + anywhere(2) + vmem(1) + anywhere(1),
        out_specs=tuple(anywhere(4)),
        scratch_shapes=[pltpu.VMEM((32, CA), BF16), pltpu.SemaphoreType.DMA((7,))],
        compiler_params=params(58),
        cost_estimate=SMALL,
        name="pack",
    )(place, feats, bias, index, pair_bias)


def join_kernel(joined, received, out, sem):
    copy = pltpu.make_async_copy(received, out.at[pl.ds(TOKS, TOKS)], sem)
    copy.start()
    copy.wait()


def join(joined, received):
    return pl.pallas_call(
        join_kernel,
        out_shape=jax.ShapeDtypeStruct(joined.shape, BF16),
        in_specs=anywhere(2),
        out_specs=anywhere(1)[0],
        input_output_aliases={0: 0},
        scratch_shapes=[pltpu.SemaphoreType.DMA],
        compiler_params=params(58),
        cost_estimate=SMALL,
        name="join",
    )(joined, received)


def hold_kernel(*refs):
    del refs


def hold(*arrays):
    return pl.pallas_call(
        hold_kernel,
        out_shape=tuple(jax.ShapeDtypeStruct(array.shape, array.dtype) for array in arrays),
        in_specs=anywhere(len(arrays)),
        out_specs=tuple(anywhere(len(arrays))),
        input_output_aliases={i: i for i in range(len(arrays))},
        compiler_params=params(58),
        cost_estimate=SMALL,
        name="hold",
    )(*arrays)


def encode_kernel(
    place, feats, low, high, bias, index, cond, project, mix, pool, fence,
    encoded, first, last, residual, normed,
    rows, bias32, packed, mixed, ext,
):
    rows[0 : 2 * LOWER] = low[0 : 2 * LOWER].astype(F32)
    rows[2 * LOWER : 2 * (LOWER + ATOMS)] = feats[...].astype(F32)
    rows[2 * (LOWER + ATOMS) : 2 * EXT] = high[0 : 2 * MARGIN].astype(F32)
    bias32[0 : 4 * QB] = low[2 * LOWER : 2 * LOWER + 4 * QB].astype(F32)
    bias32[4 * QB :] = bias[...].astype(F32)
    for seed in range(SEEDS):
        values = rows[pl.ds(seed, EXT, stride=2), :]
        packed[seed] = dot(layer_norm(values).astype(BF16), project[...]).astype(BF16)
    window_blocks(packed, bias32, mixed, 33, place[0] * ATOMS - QB - MARGIN, 11)
    token = lax.broadcasted_iota(jnp.int32, (TOKS, CA), 0)
    below = low[2 * LOWER + 4 * QB :].astype(F32)[0:1].astype(jnp.int32)
    below = jnp.where(place[0] == 0, -1000, below)
    base = place[0] * TOKS
    chosen = jnp.concatenate(
        [(index[i : i + 1] - base == token).astype(F32) for i in range(8)]
        + [(below == token).astype(F32)],
        axis=1,
    )
    counts = jnp.sum(chosen, axis=1, keepdims=True)
    chosen = chosen.astype(BF16)
    for seed in range(SEEDS):
        values = rows[pl.ds(2 * MARGIN + seed, QB + ATOMS, stride=2), :]
        result = (values + dot(mixed[seed], mix[...])).astype(BF16)
        ext[0:ATOMS] = result[QB:]
        ext[ATOMS : EXT - QB] = jnp.zeros((EXT - QB - ATOMS, CA), BF16)
        ext[EXT - QB :] = result[0:QB]
        encoded[seed] = ext[0:ATOMS]
        first[seed] = ext[0:MARGIN]
        last[seed] = ext[ATOMS - MARGIN : ATOMS]
        lifted = jnp.maximum(dot(ext[...], pool[...]), 0.0).astype(BF16)
        state = cond[...].astype(F32) + dot(chosen, lifted) / counts
        residual[seed] = state
        normed[seed] = layer_norm(state).astype(BF16)


def encode(*args):
    return pl.pallas_call(
        encode_kernel,
        out_shape=(
            jax.ShapeDtypeStruct((SEEDS, ATOMS, CA), BF16),
            jax.ShapeDtypeStruct((SEEDS, MARGIN, CA), BF16),
            jax.ShapeDtypeStruct((SEEDS, MARGIN, CA), BF16),
            jax.ShapeDtypeStruct((SEEDS, TOKS, CT), F32),
            jax.ShapeDtypeStruct((SEEDS, TOKS, CT), BF16),
        ),
        in_specs=[pl.BlockSpec(memory_space=pltpu.SMEM)] + vmem(9) + anywhere(1),
        out_specs=tuple(vmem(5)),
        scratch_shapes=[
            pltpu.VMEM((2 * EXT, CA), F32),
            pltpu.VMEM((33 * 4 * QB, WIN), F32),
            pltpu.VMEM((SEEDS, EXT, 3 * CA), BF16),
            pltpu.VMEM((SEEDS, QB + ATOMS, CA), BF16),
            pltpu.VMEM((EXT, CA), BF16),
        ],
        compiler_params=params(58),
        cost_estimate=SMALL,
        name="encode",
    )(*args)


def decode_kernel(
    place, enc, enc_low, enc_high, spread, spread_low, spread_high, bias, index, low, high,
    project, mix,
    update,
    rows, bias32, packed, mixed, decoded, tokens, moved,
):
    bias32[...] = bias[...].astype(F32)
    token = lax.broadcasted_iota(jnp.int32, (TOKS + 2 * EDGE, CA), 0) - EDGE
    below = low[2 * LOWER + 4 * QB :].astype(F32)[0:1].astype(jnp.int32)
    above = high[2 * MARGIN :].astype(F32)[0:1].astype(jnp.int32) + TOKS
    base = place[0] * TOKS
    chosen = jnp.concatenate(
        [(index[i : i + 1] - base == token).astype(F32) for i in range(8)]
        + [(below == token).astype(F32), (above == token).astype(F32)],
        axis=1,
    ).astype(BF16)
    end = MARGIN + ATOMS
    for seed in range(SEEDS):
        tokens[0:EDGE] = spread_low[seed]
        tokens[EDGE : EDGE + TOKS] = spread[seed]
        tokens[EDGE + TOKS :] = spread_high[seed]
        moved[...] = lax.dot_general(
            chosen, tokens[...], (((0,), (0,)), ((), ())), preferred_element_type=F32
        )
        decoded[0:MARGIN] = enc_low[seed].astype(F32) + moved[ATOMS + CA - MARGIN : ATOMS + CA]
        decoded[MARGIN:end] = enc[seed].astype(F32) + moved[0:ATOMS]
        decoded[end : end + MARGIN] = (
            enc_high[seed].astype(F32) + moved[ATOMS + CA : ATOMS + CA + MARGIN]
        )
        decoded[end + MARGIN :] = jnp.zeros((EXT - end - MARGIN, CA), F32)
        values = decoded[...].astype(BF16).astype(F32)
        rows[pl.ds(seed, EXT, stride=2), :] = values
        packed[seed] = dot(layer_norm(values).astype(BF16), project[...]).astype(BF16)
    window_blocks(packed, bias32, mixed, 32, place[0] * ATOMS - MARGIN, 8)
    for seed in range(SEEDS):
        at = pl.ds(2 * MARGIN + seed, ATOMS, stride=2)
        rows[at, :] = rows[at, :] + dot(mixed[seed], mix[...])
    update[...] = rows[2 * MARGIN : 2 * (MARGIN + ATOMS)].astype(BF16)


def decode(*args):
    return pl.pallas_call(
        decode_kernel,
        out_shape=jax.ShapeDtypeStruct((SEEDS * ATOMS, CA), BF16),
        in_specs=[pl.BlockSpec(memory_space=pltpu.SMEM)] + vmem(12),
        out_specs=vmem(1)[0],
        scratch_shapes=[
            pltpu.VMEM((2 * EXT, CA), F32),
            pltpu.VMEM((32 * 4 * QB, WIN), F32),
            pltpu.VMEM((SEEDS, EXT, 3 * CA), BF16),
            pltpu.VMEM((SEEDS, ATOMS, CA), BF16),
            pltpu.VMEM((EXT, CA), F32),
            pltpu.VMEM((TOKS + 2 * EDGE, CA), BF16),
            pltpu.VMEM((ATOMS + 2 * CA, CA), F32),
        ],
        compiler_params=params(58),
        cost_estimate=SMALL,
        name="decode",
    )(*args)


def spaced_kernel(place, first, second, fence, out):
    core = place[1]
    for group in range(4):
        start = PAIR * group // 128 * 128
        shift = PAIR * group - start + HEAD * core
        width = min(256, 384 - start)
        row = lax.broadcasted_iota(jnp.int32, (width, 128), 0) - shift
        lane = lax.broadcasted_iota(jnp.int32, (width, 128), 1)

        def pick(side):
            at = lane - HEAD * side
            return ((row == at) & (at >= 0) & (at < HEAD)).astype(F32).astype(BF16)

        block = dot(first[:, start : start + width], pick(1 - core)) + dot(
            second[:, start : start + width], pick(core)
        )
        out[0, group // 2, :, group % 2 * 128 : group % 2 * 128 + 128] = block.astype(BF16)


def spaced(place, weight, fence):
    return pl.pallas_call(
        spaced_kernel,
        grid=(4,),
        out_shape=jax.ShapeDtypeStruct((2, GROUPS // 2, CT, 256), BF16),
        in_specs=[
            pl.BlockSpec(memory_space=pltpu.SMEM),
            pl.BlockSpec((CT, 384), lambda i: (0, i)),
            pl.BlockSpec((CT, 384), lambda i: (0, jnp.where(i < 2, 6 + i, 2 + i))),
        ]
        + anywhere(1),
        out_specs=pl.BlockSpec((1, 2, CT, 256), lambda i: (i // 2, i % 2, 0, 0)),
        compiler_params=params(58),
        cost_estimate=SMALL,
        name="spaced",
    )(place, weight, weight, fence)


def queries_kernel(place, normed, other, weight, fence, query, gate):
    core = place[1]
    lane = lax.broadcasted_iota(jnp.int32, (1, 128), 1)
    in_query = (lane // HEAD == 1 - core) & (lane < PAIR)
    in_gate = (lane // HEAD == core) & (lane < PAIR)
    values = jnp.concatenate([normed[0], other[0], normed[1], other[1]], axis=0)
    for pair in range(GROUPS // 2):
        product = dot(values, weight[0, pair])
        for side in range(2):
            part = product[:, side * 128 : side * 128 + 128]
            group = 2 * pair + side
            queried = jnp.where(in_query, part * (HEAD**-0.5), 0.0).astype(BF16)
            opened = jnp.where(in_gate, jax.nn.sigmoid(part), 0.0)
            for seed in range(SEEDS):
                at = slice(seed * 2 * TOKS, (seed + 1) * 2 * TOKS)
                query[group, seed] = queried[at]
                gate[group, seed] = opened[at]


def queries(place, normed, other, weight, fence):
    return pl.pallas_call(
        queries_kernel,
        grid=(1,),
        out_shape=(
            jax.ShapeDtypeStruct((GROUPS, SEEDS, 2 * TOKS, 128), BF16),
            jax.ShapeDtypeStruct((GROUPS, SEEDS, 2 * TOKS, 128), F32),
        ),
        in_specs=[pl.BlockSpec(memory_space=pltpu.SMEM)]
        + vmem(2)
        + [pl.BlockSpec((1, GROUPS // 2, CT, 256), lambda i: (0, 0, 0, 0))]
        + anywhere(1),
        out_specs=tuple(vmem(2)),
        compiler_params=params(50),
        cost_estimate=LARGE,
        name="queries",
    )(place, normed, other, weight, fence)


def keys_kernel(tokens, weight, out):
    count = tokens.shape[0]
    values = jnp.concatenate([tokens[i].reshape(SEEDS * TOKS, CT) for i in range(count)], axis=0)
    ones = (lax.broadcasted_iota(jnp.int32, (1, 256), 1) % 128 == PAIR).astype(F32)
    for pair in range(GROUPS // 2):
        product = (dot(values, weight[0, pair]) + ones).astype(BF16)
        for side in range(2):
            for i in range(count):
                for seed in range(SEEDS):
                    start = (i * SEEDS + seed) * TOKS
                    out[2 * pair + side, seed, i * TOKS : (i + 1) * TOKS] = product[
                        start : start + TOKS, side * 128 : side * 128 + 128
                    ]


def keys(tokens, weight):
    step = 4
    return pl.pallas_call(
        keys_kernel,
        grid=(tokens.shape[0] // step,),
        out_shape=jax.ShapeDtypeStruct((GROUPS, SEEDS, ALL_TOKS, 128), BF16),
        in_specs=[
            pl.BlockSpec((step, SEEDS, TOKS, CT), lambda i: (i, 0, 0, 0)),
            pl.BlockSpec((1, GROUPS // 2, CT, 256), lambda i: (1, 0, 0, 0)),
        ],
        out_specs=pl.BlockSpec((GROUPS, SEEDS, step * TOKS, 128), lambda i: (0, 0, i, 0)),
        compiler_params=params(50),
        cost_estimate=SMALL,
        name="keys",
    )(tokens, weight)


def attend_kernel(pieces, extra, group_ids, query, gate, key_value, *rest):
    biases = rest[: sum(pieces)]
    own, sent, bias, scores = rest[sum(pieces) + extra :]
    step = pl.program_id(0)
    at = 0
    for i, parts in enumerate(pieces):
        refs = biases[at : at + parts]
        at += parts

        @pl.when(step == i)
        def _(refs=refs):
            place = 0
            for ref in refs:
                size = ref.shape[0]
                bias[place : place + size] = ref[...]
                place += size

    width = 512
    tops = []
    for seed in range(SEEDS):
        peak = None
        for c in range(ALL_TOKS // width):
            cols = slice(c * width, (c + 1) * width)
            part = dot_t(query[0, seed], key_value[0, seed, cols, :]) + bias[:, cols].astype(F32)
            scores[seed, :, cols] = part
            for w in range(width // 128):
                tile = part[:, w * 128 : (w + 1) * 128]
                peak = tile if peak is None else jnp.maximum(peak, tile)
        tops.append(jnp.max(peak, axis=-1, keepdims=True))
    for seed in range(SEEDS):
        total = None
        for c in range(ALL_TOKS // width):
            cols = slice(c * width, (c + 1) * width)
            part = dot(
                jnp.exp(scores[seed, :, cols] - tops[seed]).astype(BF16), key_value[0, seed, cols, :]
            )
            total = part if total is None else total + part
        gated = (total / total[:, PAIR : PAIR + 1] * gate[0, seed]).astype(BF16)
        own[0, seed] = gated[:TOKS]
        sent[0, seed] = gated[TOKS:]


def attend(group_ids, query, gate, key_value, before, pieces):
    flat = [ref for parts in pieces for ref in parts]
    shape = jax.ShapeDtypeStruct((GROUPS, SEEDS, TOKS, 128), BF16)

    def by_group(*block):
        return pl.BlockSpec((1,) + block, lambda i, ids: (ids[i],) + (0,) * len(block))

    grid_spec = pltpu.PrefetchScalarGridSpec(
        num_scalar_prefetch=1,
        grid=(len(pieces),),
        in_specs=[
            by_group(SEEDS, 2 * TOKS, 128),
            by_group(SEEDS, 2 * TOKS, 128),
            by_group(SEEDS, ALL_TOKS, 128),
        ]
        + vmem(len(flat))
        + anywhere(len(before)),
        out_specs=(by_group(SEEDS, TOKS, 128),) * 2,
        scratch_shapes=[
            pltpu.VMEM((2 * TOKS, ALL_TOKS), BF16),
            pltpu.VMEM((SEEDS, 2 * TOKS, ALL_TOKS), F32),
        ],
    )
    return pl.pallas_call(
        functools.partial(attend_kernel, tuple(len(parts) for parts in pieces), len(before)),
        grid_spec=grid_spec,
        out_shape=(shape, shape),
        input_output_aliases={4 + len(flat) + i: i for i in range(len(before))},
        compiler_params=params(50),
        cost_estimate=SMALL,
        name="attend",
    )(group_ids, query, gate, key_value, *flat, *before)


def finish_kernel(
    residual, own, received, mix, wide_hbm, narrow_hbm, spread_weight,
    state, spread, first, last,
    wide, narrow, mix_tile, total, hidden, sems,
):
    step = 512
    count = TRANS // step
    copies = []
    for c in range(count):
        gate_cols = pl.ds(c * step, step)
        up_cols = pl.ds(TRANS + c * step, step)
        copies.append(
            [
                pltpu.make_async_copy(wide_hbm.at[:, gate_cols], wide.at[:, gate_cols], sems.at[c, 0]),
                pltpu.make_async_copy(wide_hbm.at[:, up_cols], wide.at[:, up_cols], sems.at[c, 1]),
                pltpu.make_async_copy(narrow_hbm.at[gate_cols], narrow.at[gate_cols], sems.at[c, 2]),
            ]
        )
    for group in copies:
        for copy in group:
            copy.start()
    values = residual[...].reshape(SEEDS * TOKS, CT)
    for group in range(GROUPS):
        gated = (own[group] + received[group]).reshape(SEEDS * TOKS, 128)
        mix_tile[group, 0:PAIR] = mix[group]
        mix_tile[group, PAIR:128] = jnp.zeros((128 - PAIR, CT), BF16)
        values = values + dot(gated, mix_tile[group])
    total[...] = values
    normed = layer_norm(values).astype(BF16)
    for c in range(count):
        for copy in copies[c]:
            copy.wait()
        gate = dot(normed, wide[:, c * step : (c + 1) * step])
        up = dot(normed, wide[:, TRANS + c * step : TRANS + (c + 1) * step])
        hidden[:, c * step : (c + 1) * step] = (jax.nn.silu(gate) * up).astype(BF16)
    rounded = (total[...] + dot(hidden[...], narrow[...])).astype(BF16)
    state[...] = rounded.reshape(SEEDS, TOKS, CT)
    carried = dot(rounded, spread_weight[...]).astype(BF16).reshape(SEEDS, TOKS, CA)
    spread[...] = carried
    first[...] = carried[:, :EDGE]
    last[...] = carried[:, TOKS - EDGE :]


def finish(residual, own, received, mix, wide, narrow, spread_weight):
    return pl.pallas_call(
        finish_kernel,
        out_shape=(
            jax.ShapeDtypeStruct((SEEDS, TOKS, CT), BF16),
            jax.ShapeDtypeStruct((SEEDS, TOKS, CA), BF16),
            jax.ShapeDtypeStruct((SEEDS, EDGE, CA), BF16),
            jax.ShapeDtypeStruct((SEEDS, EDGE, CA), BF16),
        ),
        in_specs=vmem(4) + anywhere(2) + vmem(1),
        out_specs=tuple(vmem(4)),
        scratch_shapes=[
            pltpu.VMEM((CT, 2 * TRANS), BF16),
            pltpu.VMEM((TRANS, CT), BF16),
            pltpu.VMEM((GROUPS, 128, CT), BF16),
            pltpu.VMEM((SEEDS * TOKS, CT), F32),
            pltpu.VMEM((SEEDS * TOKS, TRANS), BF16),
            pltpu.SemaphoreType.DMA((3, 3)),
        ],
        compiler_params=params(58),
        cost_estimate=SMALL,
        name="finish",
    )(residual, own, received, mix, wide, narrow, spread_weight)


def along_tok(values, by):
    return lax.ppermute(values, "tok", [(i, (i + by) % 16) for i in range(16)])


def across_core(values):
    return lax.ppermute(values, "tok", [(i, i ^ 1) for i in range(16)])


def along_y(values, by):
    return lax.ppermute(values, "seed", [(i, (i + 2 * by) % 8) for i in range(8)])


def along_z(values):
    return lax.ppermute(values, "seed", [(i, i ^ 1) for i in range(8)])


def per_device(
    atom_feats, atom_index, token_cond, pair_bias, atom_bias_enc, atom_bias_dec,
    enc_project, enc_mix, pool_weight, token_project, token_mix, swiglu_in, swiglu_out,
    spread_weight, dec_project, dec_mix,
):
    tok = lax.axis_index("tok")
    seed = lax.axis_index("seed")
    place = jnp.stack([tok, tok % 2]).astype(jnp.int32)
    feats = atom_feats.reshape(SEEDS * ATOMS, CA)
    bias_enc = atom_bias_enc.reshape(4 * ATOMS, WIN)
    bias_dec = atom_bias_dec.reshape(4 * ATOMS, WIN)
    index = atom_index.reshape(8, CA)

    up, down, send, joined = pack(place, feats, bias_enc, index, pair_bias)
    mine = join(joined, across_core(send))
    low = along_tok(up, 1)
    high = along_tok(down, -1)
    below = along_y(mine, 1)
    above = along_y(mine, -1)
    other = along_z(mine)

    encoded, first, last, residual, normed = encode(
        place, feats, low, high, bias_enc, index, token_cond, enc_project, enc_mix, pool_weight,
        mine,
    )
    everyone = lax.all_gather(normed, "tok", axis=0)
    below, above, other, first, last = hold(below, above, other, first, last)
    far = (along_y(below[:TOKS], 1), along_y(above[TOKS:], -1))
    other_below = along_y(other, 1)
    other_above = along_y(other, -1)
    enc_low = along_tok(last, 1)
    enc_high = along_tok(first, -1)
    weights = spaced(place, token_project, below)
    query, gate = queries(place, normed, across_core(normed), weights, below)

    everyone, other_below, other_above, query, enc_low, enc_high = hold(
        everyone, other_below, other_above, query, enc_low, enc_high
    )
    other_far = (along_y(other_below[:TOKS], 1), along_y(other_above[TOKS:], -1))
    key_value = keys(everyone, weights)

    level, side = seed // 2, seed % 2

    def ids(*offsets):
        return jnp.stack([(level + dy) % 4 * 2 + (side ^ dz) for dy, dz in offsets]).astype(jnp.int32)

    done = attend(
        ids((0, 0), (3, 0), (1, 0), (2, 0), (0, 1)), query, gate, key_value, (),
        ((mine,), (below,), (above,), far, (other,)),
    )
    done = attend(
        ids((3, 1), (1, 1)), query, gate, key_value, done, ((other_below,), (other_above,))
    )
    own, sent = attend(ids((2, 1)), query, gate, key_value, done, (other_far,))

    state, spread, spread_first, spread_last = finish(
        residual, own, across_core(sent), token_mix.reshape(GROUPS, PAIR, CT), swiglu_in,
        swiglu_out, spread_weight,
    )
    update = decode(
        place, encoded, enc_low, enc_high, spread, along_tok(spread_last, 1),
        along_tok(spread_first, -1), bias_dec, index, low, high, dec_project, dec_mix,
    )
    return state.transpose(1, 0, 2), update.reshape(ATOMS, SEEDS, CA)


def solution(mesh):
    placed = (
        P("tok", "seed", None),
        P("tok"),
        P("tok", None),
        P("seed", "tok", None),
        P("tok", None, None),
        P("tok", None, None),
    ) + (P(),) * 10
    return jax.shard_map(
        per_device,
        mesh=mesh,
        in_specs=placed,
        out_specs=(P("tok", "seed", None), P("tok", "seed", None)),
        check_vma=False,
    )
```

time: 195 us -> 226 us (1.16)
  Pallas kernels: 89.4 us -> 121 us
  waiting for transfers between devices: 28.2 us -> 42.3 us
  local copies, waits for them, and re-layouts: 30 us -> 16.1 us
  between operations: 0.91 us -> 14.2 us
  starting transfers between devices: 42.4 us -> 31.1 us
    pallas_call x5 -> x8, Pallas kernels: 42.7 us -> 81.8 us  [the longest x1 36.6 us: pack(): pl.pallas_call(pack_kernel, out_shape=(jax.ShapeDtypeStruct((UP_ROWS, CA)...]
    ppermute x1, waiting for transfers between devices: 0.01 us -> 19.2 us  [along_z(): return lax.ppermute(values, 'seed', [(i, i ^ 1) for i in range(8)])]
    ppermute x9 -> x0, waiting for transfers between devices: 18.8 us -> none  [the longest x8 18.6 us: along_x(): lax.ppermute(values, 'tok', [(i, i // 8 * 8 + (i + 2 * by) % 8) for i in...]
    ppermute x8, waiting for transfers between devices: 0.02 us -> 18.5 us  [along_y(): lax.ppermute(values, 'seed', [(i, (i + 2 * by) % 8) for i in range(8)])]
    ppermute x10 -> x3, starting transfers between devices: 15.9 us -> 7.74 us  [across_core(): return lax.ppermute(values, 'tok', [(i, i ^ 1) for i in range(16)])]
    pallas_call x3, Pallas kernels: 29.6 us -> 21.8 us  [attend(): pl.pallas_call(functools.partial(attend_kernel, tuple((len(parts) for par...]
    slice x14 -> x4, local copies, waits for them, and re-layouts: 13.8 us -> 6.72 us  [the longest x2 2.76 us: per_device(): far = (along_y(below[:TOKS], 1), along_y(above[TOKS:], -1))]
    unnamed x53 -> x41, local copies, waits for them, and re-layouts: 15.3 us -> 9.28 us
  transfers between devices with their start and end apart: 34 -> 19, of which waited for: 10 -> 5; matrix products, arithmetic and copies ran while one was open for 10% -> 4% of each run, Pallas kernels for 39% -> 25%
where the time goes in v3:
time: 226 us; the launch traced here: 225 us
  Pallas kernels  121 us (54%)
  waiting for transfers between devices  42.3 us (19%)
  starting transfers between devices  31.1 us (14%)
  local copies, waits for them, and re-layouts  16.1 us (7%)
  between operations  14.2 us (6%)
    pallas_call x1, Pallas kernels, pack(): pl.pallas_call(pack_kernel, out_shape=(jax.ShapeDtypeStruct((UP_ROWS, CA)...  36.6 us
    pallas_call x3, Pallas kernels, attend(): pl.pallas_call(functools.partial(attend_kernel, tuple((len(parts) for par...  21.8 us
    ppermute x1, waiting for transfers between devices, along_z(): return lax.ppermute(values, 'seed', [(i, i ^ 1) for i in range(8)])  19.2 us
    ppermute x8, waiting for transfers between devices, along_y(): lax.ppermute(values, 'seed', [(i, (i + 2 * by) % 8) for i in range(8)])  18.5 us
    pallas_call x1, Pallas kernels, join(): pl.pallas_call(join_kernel, out_shape=jax.ShapeDtypeStruct(joined.shape,...  17 us
    ppermute x8, starting transfers between devices, along_y(): lax.ppermute(values, 'seed', [(i, (i + 2 * by) % 8) for i in range(8)])  10.9 us
    pallas_call x1, Pallas kernels, keys(): pl.pallas_call(keys_kernel, grid=(tokens.shape[0] // step,), out_shape=ja...  10.5 us
    unnamed x41, local copies, waits for them, and re-layouts  9.28 us
  transfers between devices with their start and end apart: 19, of which 5 were waited for; matrix products, arithmetic and copies ran while one was open for 4% of the time, Pallas kernels for 25%

profile of v3, /device:TPU:7, one launch (start us, length us, event | category | flops | bytes accessed | tf_op | source)
XLA Modules:
  0.0 225.2 jit_solution(4508244736491473917)
XLA Ops:
  7.8 36.6 %pack.1 = (bf16[304,128]{1,0:T(8,128)(2,1)}, bf16[112,128]{1,0:T(8,128)(2,1)}, bf16[128,2048]{1,0:T(8,128)(2,1)}, bf16[256,2048]{1,0:T(8,128)(2,1)}) custom-call(s32[2]{0:T(128)} %pad_add_fusion.place, bf16[2048,128]{1,0:T(8,128)(2,1)} %bitcast.21, bf16[4096,128]{1,0:T(8,128)(2,1)} %bitcast.19, s32[8,128]{1,0:T(8,128)} %bitcast.27, ...), custom_call_target="tpu_custom_call" | custom-call | flops 1000000 | bytes 10000 | tf_op jit(solution)/shard_map/pack/pallas_call | solution.py:130
  47.7 17.0 %join.1.fence.rest_0_ = bf16[256,2048]{1,0:T(8,128)(2,1)} custom-call(bf16[256,2048]{1,0:T(8,128)(2,1)} %get-tuple-element.36.joined, bf16[128,2048]{1,0:T(8,128)(2,1)} %copy-done.12), custom_call_target="tpu_custom_call", output_to_operand_aliasing={{}: (0, {})} | custom-call | flops 1000000 | bytes 10000 | tf_op jit(solution)/shard_map/join/pallas_call | solution.py:154
  66.0 9.1 %encode.1 = (bf16[2,1024,128]{2,1,0:T(8,128)(2,1)}, bf16[2,48,128]{2,1,0:T(8,128)(2,1)}, bf16[2,48,128]{2,1,0:T(8,128)(2,1)}, f32[2,128,768]{2,1,0:T(8,128)}, bf16[2,128,768]{2,1,0:T(8,128)(2,1)}) custom-call(s32[2]{0:T(128)} %pad_add_fusion.place, bf16[2048,128]{1,0:T(8,128)(2,1)} %bitcast.22, bf16[304,128]{1,0:T(8,128)(2,1)} %copy-done.14, ...), custom_call_target="tpu_custom_call" | custom-call | flops 1000000 | bytes 10000 | tf_op jit(solution)/shard_map/encode/pallas_call | solution.py:225
  78.0 3.6 %collective-permute-start.5 = (bf16[256,2048]{1,0:T(8,128)(2,1)}, bf16[256,2048]{1,0:T(8,128)(2,1)S(1)}, u32[]{:S(2)}, u32[]{:S(2)}) collective-permute-start(bf16[256,2048]{1,0:T(8,128)(2,1)} %join.1.fence.rest_0_), channel_id=1, source_target_pairs={{0,16},{16,0},{32,48},{48,32},{64,80},{80,64},{96,112},{112,96},{1... | collective-permute-start | bytes 3145736 | tf_op jit(solution)/shard_map/ppermute | solution.py:574
  82.6 18.4 %collective-permute-done.3.refs_0_ = bf16[256,2048]{1,0:T(8,128)(2,1)S(1)} collective-permute-done((bf16[256,2048]{1,0:T(8,128)(2,1)}, bf16[256,2048]{1,0:T(8,128)(2,1)S(1)}, u32[]{:S(2)}, u32[]{:S(2)}) %collective-permute-start.3) | collective-permute-done | bytes 1048608 | tf_op jit(solution)/shard_map/ppermute | solution.py:570
  101.1 19.2 %collective-permute-done.5.refs_2_ = bf16[256,2048]{1,0:T(8,128)(2,1)S(1)} collective-permute-done((bf16[256,2048]{1,0:T(8,128)(2,1)}, bf16[256,2048]{1,0:T(8,128)(2,1)S(1)}, u32[]{:S(2)}, u32[]{:S(2)}) %collective-permute-start.5) | collective-permute-done | bytes 1048608 | tf_op jit(solution)/shard_map/ppermute | solution.py:574
  121.3 2.7 %collective-permute-start.7 = (bf16[256,2048]{1,0:T(8,128)(2,1)}, bf16[256,2048]{1,0:T(8,128)(2,1)S(1)}, u32[]{:S(2)}, u32[]{:S(2)}) collective-permute-start(bf16[256,2048]{1,0:T(8,128)(2,1)} %get-tuple-element.42.rest_5_), channel_id=1, source_target_pairs={{0,96},{16,112},{32,0},{48,16},{64,32},{80,48},{96,64},{112,80},{1... | collective-permute-start | bytes 3145736 | tf_op jit(solution)/shard_map/ppermute | solution.py:570
  123.9 4.8 %collective-permute-start.10 = (bf16[2,48,128]{2,1,0:T(8,128)(2,1)}, bf16[2,48,128]{2,1,0:T(8,128)(2,1)S(1)}, u32[]{:S(2)}, u32[]{:S(2)}) collective-permute-start(bf16[2,48,128]{2,1,0:T(8,128)(2,1)} %get-tuple-element.46), channel_id=1, source_target_pairs={{0,15},{1,0},{2,1},{3,2},{4,3},{5,4},{6,5},{7,6},{8,7},{9,8},{10,9... | collective-permute-start | bytes 73736 | tf_op jit(solution)/shard_map/ppermute | solution.py:562
  130.5 1.9 slice.14
  132.5 6.6 %spaced.1.weight = bf16[2,4,768,256]{3,2,1,0:T(8,128)(2,1)} custom-call(s32[2]{0:T(128)} %pad_add_fusion.place, bf16[768,3072]{1,0:T(8,128)(2,1)} %second.1, bf16[768,3072]{1,0:T(8,128)(2,1)} %second.1, bf16[256,2048]{1,0:T(8,128)(2,1)} %get-tuple-element.43.fence.rest_1_), custom_call_target="tpu_custom_call" | custom-call | flops 1000000 | bytes 10000 | tf_op jit(solution)/shard_map/spaced/pallas_call | solution.py:330
  139.2 3.8 %queries.1 = (bf16[8,2,256,128]{3,2,1,0:T(8,128)(2,1)S(1)}, f32[8,2,256,128]{3,2,1,0:T(8,128)}) custom-call(s32[2]{0:T(128)S(1)} %copy-done.7, bf16[2,128,768]{2,1,0:T(8,128)(2,1)S(1)} %copy-done.6, bf16[2,128,768]{2,1,0:T(8,128)(2,1)S(1)} %collective-permute-done.8.other, bf16[2,4,768,256]{3,2,1,0:T(8,128)(2,1)} %spaced.1.weight, ...), custom_call_target="tpu_custom_call" | custom-call | flops 99999997952 | bytes 10000 | tf_op jit(solution)/shard_map/queries/pallas_call | solution.py:367
  144.9 2.6 %collective-permute-start.14 = (bf16[128,2048]{1,0:T(8,128)(2,1)}, bf16[128,2048]{1,0:T(8,128)(2,1)}, u32[]{:S(2)}, u32[]{:S(2)}) collective-permute-start(bf16[128,2048]{1,0:T(8,128)(2,1)} %slice.15), channel_id=1, source_target_pairs={{0,96},{16,112},{32,0},{48,16},{64,32},{80,48},{96,64},{112,80},{1... | collective-permute-start | bytes 1572872 | tf_op jit(solution)/shard_map/ppermute | solution.py:570
  148.5 2.0 slice.12
  150.5 1.9 slice.13
  152.4 2.7 %collective-permute-start.12 = (bf16[128,2048]{1,0:T(8,128)(2,1)}, bf16[128,2048]{1,0:T(8,128)(2,1)}, u32[]{:S(2)}, u32[]{:S(2)}) collective-permute-start(bf16[128,2048]{1,0:T(8,128)(2,1)} %slice.13), channel_id=1, source_target_pairs={{0,96},{16,112},{32,0},{48,16},{64,32},{80,48},{96,64},{112,80},{1... | collective-permute-start | bytes 1572872 | tf_op jit(solution)/shard_map/ppermute | solution.py:570
  155.3 10.5 %keys.1.key_value = bf16[8,2,2048,128]{3,2,1,0:T(8,128)(2,1)} custom-call(bf16[16,2,128,768]{3,2,1,0:T(8,128)(2,1)} %get-tuple-element.49.tokens, bf16[2,4,768,256]{3,2,1,0:T(8,128)(2,1)S(1)} %copy-done.4), custom_call_target="tpu_custom_call" | custom-call | flops 1000000 | bytes 10000 | tf_op jit(solution)/shard_map/keys/pallas_call | solution.py:402
  165.8 12.5 %attend.3 = (bf16[8,2,128,128]{3,2,1,0:T(8,128)(2,1)S(1)}, bf16[8,2,128,128]{3,2,1,0:T(8,128)(2,1)S(1)}) custom-call(s32[5]{0:T(128)S(1)} %stack.51.group_ids, bf16[8,2,256,128]{3,2,1,0:T(8,128)(2,1)S(1)} %copy-done.1, f32[8,2,256,128]{3,2,1,0:T(8,128)} %get-tuple-element.48.gate, bf16[8,2,2048,128]{3,2,1,0:T(8,128)(2,1)} %keys.1.key_value, ...), custom_call_target="tpu_custom_call" | custom-call | flops 1000000 | bytes 10000 | tf_op jit(solution)/shard_map/attend/pallas_call | solution.py:482
  178.3 6.1 %attend.4 = (bf16[8,2,128,128]{3,2,1,0:T(8,128)(2,1)S(1)}, bf16[8,2,128,128]{3,2,1,0:T(8,128)(2,1)S(1)}) custom-call(s32[2]{0:T(128)S(1)} %pad_add_fusion.1.group_ids, bf16[8,2,256,128]{3,2,1,0:T(8,128)(2,1)S(1)} %copy-done.1, f32[8,2,256,128]{3,2,1,0:T(8,128)} %get-tuple-element.48.gate, ...), custom_call_target="tpu_custom_call", output_to_operand_aliasing={{0}: (6, {}), {1}: (7, {})} | custom-call | flops 1000000 | bytes 10000 | tf_op jit(solution)/shard_map/attend/pallas_call | solution.py:482
  184.5 3.2 %attend.5 = (bf16[8,2,128,128]{3,2,1,0:T(8,128)(2,1)S(1)}, bf16[8,2,128,128]{3,2,1,0:T(8,128)(2,1)S(1)}) custom-call(s32[1]{0:T(128)} %bitcast.5.group_ids, bf16[8,2,256,128]{3,2,1,0:T(8,128)(2,1)S(1)} %copy-done.1, f32[8,2,256,128]{3,2,1,0:T(8,128)} %get-tuple-element.48.gate, ...), custom_call_target="tpu_custom_call", output_to_operand_aliasing={{0}: (6, {}), {1}: (7, {})} | custom-call | flops 1000000 | bytes 10000 | tf_op jit(solution)/shard_map/attend/pallas_call | solution.py:482
  188.4 5.9 %collective-permute-start.15 = (bf16[8,2,128,128]{3,2,1,0:T(8,128)(2,1)S(1)}, bf16[8,2,128,128]{3,2,1,0:T(8,128)(2,1)S(1)}, u32[]{:S(2)}, u32[]{:S(2)}) collective-permute-start(bf16[8,2,128,128]{3,2,1,0:T(8,128)(2,1)S(1)} %get-tuple-element.58), channel_id=1, source_target_pairs={{0,1},{1,0},{2,3},{3,2},{4,5},{5,4},{6,7},{7,6},{8,9},{9,8},{10,11... | collective-permute-start | bytes 1572872 | tf_op jit(solution)/shard_map/ppermute | solution.py:566
  196.7 7.2 %finish.1 = (bf16[2,128,768]{2,1,0:T(8,128)(2,1)}, bf16[2,128,128]{2,1,0:T(8,128)(2,1)}, bf16[2,16,128]{2,1,0:T(8,128)(2,1)}, bf16[2,16,128]{2,1,0:T(8,128)(2,1)}) custom-call(f32[2,128,768]{2,1,0:T(8,128)} %get-tuple-element.38.residual, bf16[8,2,128,128]{3,2,1,0:T(8,128)(2,1)} %copy-done.5, bf16[8,2,128,128]{3,2,1,0:T(8,128)(2,1)} %copy-done.13, ...), custom_call_target="tpu_custom_call" | custom-call | flops 1000000 | bytes 10000 | tf_op jit(solution)/shard_map/finish/pallas_call | solution.py:537
  204.6 2.1 copy.35
  206.8 2.9 %collective-permute-done.17.spread_high = bf16[2,16,128]{2,1,0:T(8,128)(2,1)S(1)} collective-permute-done((bf16[2,16,128]{2,1,0:T(8,128)(2,1)}, bf16[2,16,128]{2,1,0:T(8,128)(2,1)S(1)}, u32[]{:S(2)}, u32[]{:S(2)}) %collective-permute-start.17) | collective-permute-done | bytes 8224 | tf_op jit(solution)/shard_map/ppermute | solution.py:562
  210.2 8.1 %decode.1 = bf16[2048,128]{1,0:T(8,128)(2,1)} custom-call(s32[2]{0:T(128)} %pad_add_fusion.place, bf16[2,1024,128]{2,1,0:T(8,128)(2,1)} %get-tuple-element.60.enc, bf16[2,48,128]{2,1,0:T(8,128)(2,1)} %get-tuple-element.61.enc_low, bf16[2,48,128]{2,1,0:T(8,128)(2,1)} %get-tuple-element.62.enc_high, bf16[2,128,128]{2,1,0:T(8,128)(2,1)} %get-tuple-element.63.spread, ...), custom_call_target="tpu_custom_call" | custom-call | flops 1000000 | bytes 10000 | tf_op jit(solution)/shard_map/decode/pallas_call | solution.py:290
  (76 shorter events, 19.5 us)
Async XLA Ops:
  7.2 140.4 %all-gather.3.cloned.1.call-start = ((), (), s32[]{:S(2)}) async-start(), calls=%async_computation | async-start | bytes 6684672 | tf_op jit(solution)/shard_map/all_gather | solution.py:602
  44.4 2.5 %collective-permute-start.2 = (bf16[128,2048]{1,0:T(8,128)(2,1)}, bf16[128,2048]{1,0:T(8,128)(2,1)S(1)}, u32[]{:S(2)}, u32[]{:S(2)}) collective-permute-start(bf16[128,2048]{1,0:T(8,128)(2,1)} %get-tuple-element.37), channel_id=1, source_target_pairs={{0,1},{1,0},{2,3},{3,2},{4,5},{5,4},{6,7},{7,6},{8,9},{9,8},{10,11... | collective-permute-start | bytes 1572872 | tf_op jit(solution)/shard_map/ppermute | solution.py:566
  45.2 19.6 %collective-permute-start = (bf16[304,128]{1,0:T(8,128)(2,1)}, bf16[304,128]{1,0:T(8,128)(2,1)S(1)}, u32[]{:S(2)}, u32[]{:S(2)}) collective-permute-start(bf16[304,128]{1,0:T(8,128)(2,1)} %get-tuple-element.34), channel_id=1, source_target_pairs={{0,1},{1,2},{2,3},{3,4},{4,5},{5,6},{6,7},{7,8},{8,9},{9,10},{10,1... | collective-permute-start | bytes 233480 | tf_op jit(solution)/shard_map/ppermute | solution.py:562
  46.7 18.0 %collective-permute-start.1 = (bf16[112,128]{1,0:T(8,128)(2,1)}, bf16[112,128]{1,0:T(8,128)(2,1)S(1)}, u32[]{:S(2)}, u32[]{:S(2)}) collective-permute-start(bf16[112,128]{1,0:T(8,128)(2,1)} %get-tuple-element.35), channel_id=1, source_target_pairs={{0,15},{1,0},{2,1},{3,2},{4,3},{5,4},{6,5},{7,6},{8,7},{9,8},{10,9... | collective-permute-start | bytes 86024 | tf_op jit(solution)/shard_map/ppermute | solution.py:562
  75.1 26.0 %collective-permute-start.3 = (bf16[256,2048]{1,0:T(8,128)(2,1)}, bf16[256,2048]{1,0:T(8,128)(2,1)S(1)}, u32[]{:S(2)}, u32[]{:S(2)}) collective-permute-start(bf16[256,2048]{1,0:T(8,128)(2,1)} %join.1.fence.rest_0_), channel_id=1, source_target_pairs={{0,32},{16,48},{32,64},{48,80},{64,96},{80,112},{96,0},{112,16},{1... | collective-permute-start | bytes 3145736 | tf_op jit(solution)/shard_map/ppermute | solution.py:570
  76.5 24.6 %collective-permute-start.4 = (bf16[256,2048]{1,0:T(8,128)(2,1)}, bf16[256,2048]{1,0:T(8,128)(2,1)S(1)}, u32[]{:S(2)}, u32[]{:S(2)}) collective-permute-start(bf16[256,2048]{1,0:T(8,128)(2,1)} %join.1.fence.rest_0_), channel_id=1, source_target_pairs={{0,96},{16,112},{32,0},{48,16},{64,32},{80,48},{96,64},{112,80},{1... | collective-permute-start | bytes 3145736 | tf_op jit(solution)/shard_map/ppermute | solution.py:570
  78.0 42.3 %collective-permute-start.5 = (bf16[256,2048]{1,0:T(8,128)(2,1)}, bf16[256,2048]{1,0:T(8,128)(2,1)S(1)}, u32[]{:S(2)}, u32[]{:S(2)}) collective-permute-start(bf16[256,2048]{1,0:T(8,128)(2,1)} %join.1.fence.rest_0_), channel_id=1, source_target_pairs={{0,16},{16,0},{32,48},{48,32},{64,80},{80,64},{96,112},{112,96},{1... | collective-permute-start | bytes 3145736 | tf_op jit(solution)/shard_map/ppermute | solution.py:574
  81.6 57.5 %collective-permute-start.8 = (bf16[2,128,768]{2,1,0:T(8,128)(2,1)}, bf16[2,128,768]{2,1,0:T(8,128)(2,1)S(1)}, u32[]{:S(2)}, u32[]{:S(2)}) collective-permute-start(bf16[2,128,768]{2,1,0:T(8,128)(2,1)} %get-tuple-element.39.normed), channel_id=1, source_target_pairs={{0,1},{1,0},{2,3},{3,2},{4,5},{5,4},{6,7},{7,6},{8,9},{9,8},{10,11... | collective-permute-start | bytes 1179656 | tf_op jit(solution)/shard_map/ppermute | solution.py:566
  101.1 19.2 %copy-start.2 = (bf16[256,2048]{1,0:T(8,128)(2,1)}, bf16[256,2048]{1,0:T(8,128)(2,1)S(1)}, u32[]{:S(2)}) copy-start(bf16[256,2048]{1,0:T(8,128)(2,1)S(1)} %collective-permute-done.3.refs_0_) | copy-start | bytes 3145732
  101.1 19.2 %copy-start.9 = (bf16[256,2048]{1,0:T(8,128)(2,1)}, bf16[256,2048]{1,0:T(8,128)(2,1)S(1)}, u32[]{:S(2)}) copy-start(bf16[256,2048]{1,0:T(8,128)(2,1)S(1)} %collective-permute-done.4.refs_1_) | copy-start | bytes 3145732
  121.3 26.2 %collective-permute-start.6 = (bf16[256,2048]{1,0:T(8,128)(2,1)}, bf16[256,2048]{1,0:T(8,128)(2,1)}, u32[]{:S(2)}, u32[]{:S(2)}) collective-permute-start(bf16[256,2048]{1,0:T(8,128)(2,1)} %get-tuple-element.42.rest_5_), channel_id=1, source_target_pairs={{0,32},{16,48},{32,64},{48,80},{64,96},{80,112},{96,0},{112,16},{1... | collective-permute-start | bytes 3145736 | tf_op jit(solution)/shard_map/ppermute | solution.py:570
  121.3 26.2 %collective-permute-start.7 = (bf16[256,2048]{1,0:T(8,128)(2,1)}, bf16[256,2048]{1,0:T(8,128)(2,1)S(1)}, u32[]{:S(2)}, u32[]{:S(2)}) collective-permute-start(bf16[256,2048]{1,0:T(8,128)(2,1)} %get-tuple-element.42.rest_5_), channel_id=1, source_target_pairs={{0,96},{16,112},{32,0},{48,16},{64,32},{80,48},{96,64},{112,80},{1... | collective-permute-start | bytes 3145736 | tf_op jit(solution)/shard_map/ppermute | solution.py:570
  123.9 21.0 %collective-permute-start.10 = (bf16[2,48,128]{2,1,0:T(8,128)(2,1)}, bf16[2,48,128]{2,1,0:T(8,128)(2,1)S(1)}, u32[]{:S(2)}, u32[]{:S(2)}) collective-permute-start(bf16[2,48,128]{2,1,0:T(8,128)(2,1)} %get-tuple-element.46), channel_id=1, source_target_pairs={{0,15},{1,0},{2,1},{3,2},{4,3},{5,4},{6,5},{7,6},{8,7},{9,8},{10,9... | collective-permute-start | bytes 73736 | tf_op jit(solution)/shard_map/ppermute | solution.py:562
  128.7 18.8 %collective-permute-start.9 = (bf16[2,48,128]{2,1,0:T(8,128)(2,1)}, bf16[2,48,128]{2,1,0:T(8,128)(2,1)S(1)}, u32[]{:S(2)}, u32[]{:S(2)}) collective-permute-start(bf16[2,48,128]{2,1,0:T(8,128)(2,1)} %get-tuple-element.45), channel_id=1, source_target_pairs={{0,1},{1,2},{2,3},{3,4},{4,5},{5,6},{6,7},{7,8},{8,9},{9,10},{10,1... | collective-permute-start | bytes 73736 | tf_op jit(solution)/shard_map/ppermute | solution.py:562
  132.5 6.7 %copy-start.7 = (s32[2]{0:T(128)S(1)}, s32[2]{0:T(128)}, u32[]{:S(2)}) copy-start(s32[2]{0:T(128)} %pad_add_fusion.place) | copy-start | bytes 28
  139.1 26.7 %collective-permute-start.13 = (bf16[128,2048]{1,0:T(8,128)(2,1)}, bf16[128,2048]{1,0:T(8,128)(2,1)}, u32[]{:S(2)}, u32[]{:S(2)}) collective-permute-start(bf16[128,2048]{1,0:T(8,128)(2,1)} %slice.14), channel_id=1, source_target_pairs={{0,32},{16,48},{32,64},{48,80},{64,96},{80,112},{96,0},{112,16},{1... | collective-permute-start | bytes 1572872 | tf_op jit(solution)/shard_map/ppermute | solution.py:570
  144.9 20.9 %collective-permute-start.14 = (bf16[128,2048]{1,0:T(8,128)(2,1)}, bf16[128,2048]{1,0:T(8,128)(2,1)}, u32[]{:S(2)}, u32[]{:S(2)}) collective-permute-start(bf16[128,2048]{1,0:T(8,128)(2,1)} %slice.15), channel_id=1, source_target_pairs={{0,96},{16,112},{32,0},{48,16},{64,32},{80,48},{96,64},{112,80},{1... | collective-permute-start | bytes 1572872 | tf_op jit(solution)/shard_map/ppermute | solution.py:570
  148.5 6.8 %copy-start.4 = (bf16[2,4,768,256]{3,2,1,0:T(8,128)(2,1)S(1)}, bf16[2,4,768,256]{3,2,1,0:T(8,128)(2,1)}, u32[]{:S(2)}) copy-start(bf16[2,4,768,256]{3,2,1,0:T(8,128)(2,1)} %spaced.1.weight) | copy-start | bytes 9437188
  150.5 33.9 %collective-permute-start.11 = (bf16[128,2048]{1,0:T(8,128)(2,1)}, bf16[128,2048]{1,0:T(8,128)(2,1)}, u32[]{:S(2)}, u32[]{:S(2)}) collective-permute-start(bf16[128,2048]{1,0:T(8,128)(2,1)} %slice.12), channel_id=1, source_target_pairs={{0,32},{16,48},{32,64},{48,80},{64,96},{80,112},{96,0},{112,16},{1... | collective-permute-start | bytes 1572872 | tf_op jit(solution)/shard_map/ppermute | solution.py:570
  152.4 32.0 %collective-permute-start.12 = (bf16[128,2048]{1,0:T(8,128)(2,1)}, bf16[128,2048]{1,0:T(8,128)(2,1)}, u32[]{:S(2)}, u32[]{:S(2)}) collective-permute-start(bf16[128,2048]{1,0:T(8,128)(2,1)} %slice.13), channel_id=1, source_target_pairs={{0,96},{16,112},{32,0},{48,16},{64,32},{80,48},{96,64},{112,80},{1... | collective-permute-start | bytes 1572872 | tf_op jit(solution)/shard_map/ppermute | solution.py:570
  155.3 10.5 %copy-start.1 = (bf16[8,2,256,128]{3,2,1,0:T(8,128)(2,1)S(1)}, bf16[8,2,256,128]{3,2,1,0:T(8,128)(2,1)}, u32[]{:S(2)}) copy-start(bf16[8,2,256,128]{3,2,1,0:T(8,128)(2,1)} %get-tuple-element.47.query) | copy-start | bytes 3145732
  188.4 7.4 %collective-permute-start.15 = (bf16[8,2,128,128]{3,2,1,0:T(8,128)(2,1)S(1)}, bf16[8,2,128,128]{3,2,1,0:T(8,128)(2,1)S(1)}, u32[]{:S(2)}, u32[]{:S(2)}) collective-permute-start(bf16[8,2,128,128]{3,2,1,0:T(8,128)(2,1)S(1)} %get-tuple-element.58), channel_id=1, source_target_pairs={{0,1},{1,0},{2,3},{3,2},{4,5},{5,4},{6,7},{7,6},{8,9},{9,8},{10,11... | collective-permute-start | bytes 1572872 | tf_op jit(solution)/shard_map/ppermute | solution.py:566
  203.9 2.9 %collective-permute-start.16 = (bf16[2,16,128]{2,1,0:T(8,128)(2,1)}, bf16[2,16,128]{2,1,0:T(8,128)(2,1)S(1)}, u32[]{:S(2)}, u32[]{:S(2)}) collective-permute-start(bf16[2,16,128]{2,1,0:T(8,128)(2,1)} %get-tuple-element.64), channel_id=1, source_target_pairs={{0,1},{1,2},{2,3},{3,4},{4,5},{5,6},{6,7},{7,8},{8,9},{9,10},{10,1... | collective-permute-start | bytes 24584 | tf_op jit(solution)/shard_map/ppermute | solution.py:562
  204.0 5.7 %collective-permute-start.17 = (bf16[2,16,128]{2,1,0:T(8,128)(2,1)}, bf16[2,16,128]{2,1,0:T(8,128)(2,1)S(1)}, u32[]{:S(2)}, u32[]{:S(2)}) collective-permute-start(bf16[2,16,128]{2,1,0:T(8,128)(2,1)} %get-tuple-element.65), channel_id=1, source_target_pairs={{0,15},{1,0},{2,1},{3,2},{4,3},{5,4},{6,5},{7,6},{8,7},{9,8},{10,9... | collective-permute-start | bytes 24584 | tf_op jit(solution)/shard_map/ppermute | solution.py:562
  (15 other events, 33.0 us)
Sparse Core Ops, SparseCore 0:
  75.2 62.4 all-gather.2

commit v4 on v3

--- a/solution.py
+++ b/solution.py
@@ -35,7 +35,7 @@
 
 
 SMALL = pl.CostEstimate(flops=10**6, bytes_accessed=10**4, transcendentals=0)
-LARGE = pl.CostEstimate(flops=10**11, bytes_accessed=10**4, transcendentals=0)
+LARGE = pl.CostEstimate(flops=7 * 10**10, bytes_accessed=10**4, transcendentals=0)
 
 
 def params(limit_mb, **more):
@@ -106,23 +106,34 @@
     lax.fori_loop(0, blocks // unroll, body, 0)
 
 
-def pack_kernel(place, feats, bias, index, pair_bias, up, down, send, joined, rows, sems):
+def pack_kernel(place, feats, bias, index, pair_bias, up, down, send, joined, heads, rows, sems):
     base, core = place[0] * TOKS, place[1]
-    rows[0:16] = jnp.broadcast_to((index[7:8] - (base + TOKS)).astype(F32).astype(BF16), (16, CA))
-    rows[16:32] = jnp.broadcast_to((index[0:1] - base).astype(F32).astype(BF16), (16, CA))
-    moves = (
-        (pair_bias.at[1 - core], send),
-        (pair_bias.at[core], joined.at[pl.ds(0, TOKS)]),
-        (feats.at[pl.ds(2 * (ATOMS - LOWER), 2 * LOWER)], up.at[pl.ds(0, 2 * LOWER)]),
-        (bias.at[pl.ds(4 * (ATOMS - QB), 4 * QB)], up.at[pl.ds(2 * LOWER, 4 * QB)]),
-        (rows.at[pl.ds(0, 16)], up.at[pl.ds(2 * LOWER + 4 * QB, 16)]),
-        (feats.at[pl.ds(0, 2 * MARGIN)], down.at[pl.ds(0, 2 * MARGIN)]),
-        (rows.at[pl.ds(16, 16)], down.at[pl.ds(2 * MARGIN, 16)]),
-    )
-    copies = [pltpu.make_async_copy(a, b, sems.at[i]) for i, (a, b) in enumerate(moves)]
-    for copy in copies:
+    low_rows, high_rows = UP_ROWS - 16, DOWN_ROWS - 16
+    loads = (
+        (pair_bias, heads),
+        (feats.at[pl.ds(2 * (ATOMS - LOWER), 2 * LOWER)], rows.at[pl.ds(0, 2 * LOWER)]),
+        (bias.at[pl.ds(4 * (ATOMS - QB), 4 * QB)], rows.at[pl.ds(2 * LOWER, 4 * QB)]),
+        (feats.at[pl.ds(0, 2 * MARGIN)], rows.at[pl.ds(UP_ROWS, 2 * MARGIN)]),
+    )
+    loads = [pltpu.make_async_copy(a, b, sems.at[i]) for i, (a, b) in enumerate(loads)]
+    for copy in loads:
         copy.start()
-    for copy in copies:
+    tail = (index[7:8] - (base + TOKS)).astype(F32)
+    head = (index[0:1] - base).astype(F32)
+    rows[low_rows:UP_ROWS] = jnp.broadcast_to(tail, (16, CA)).astype(BF16)
+    rows[UP_ROWS + high_rows :] = jnp.broadcast_to(head, (16, CA)).astype(BF16)
+    for copy in loads:
+        copy.wait()
+    stores = (
+        (rows.at[pl.ds(0, UP_ROWS)], up),
+        (rows.at[pl.ds(UP_ROWS, DOWN_ROWS)], down),
+        (heads.at[1 - core], send),
+        (heads.at[core], joined.at[pl.ds(0, TOKS)]),
+    )
+    stores = [pltpu.make_async_copy(a, b, sems.at[4 + i]) for i, (a, b) in enumerate(stores)]
+    for copy in stores:
+        copy.start()
+    for copy in stores:
         copy.wait()
 
 
@@ -137,17 +148,24 @@
         ),
         in_specs=[pl.BlockSpec(memory_space=pltpu.SMEM)] + anywhere(2) + vmem(1) + anywhere(1),
         out_specs=tuple(anywhere(4)),
-        scratch_shapes=[pltpu.VMEM((32, CA), BF16), pltpu.SemaphoreType.DMA((7,))],
+        scratch_shapes=[
+            pltpu.VMEM((2, TOKS, ALL_TOKS), BF16),
+            pltpu.VMEM((UP_ROWS + DOWN_ROWS, CA), BF16),
+            pltpu.SemaphoreType.DMA((8,)),
+        ],
         compiler_params=params(58),
         cost_estimate=SMALL,
         name="pack",
     )(place, feats, bias, index, pair_bias)
 
 
-def join_kernel(joined, received, out, sem):
-    copy = pltpu.make_async_copy(received, out.at[pl.ds(TOKS, TOKS)], sem)
-    copy.start()
-    copy.wait()
+def join_kernel(joined, received, out, rows, sems):
+    load = pltpu.make_async_copy(received, rows, sems.at[0])
+    load.start()
+    load.wait()
+    store = pltpu.make_async_copy(rows, out.at[pl.ds(TOKS, TOKS)], sems.at[1])
+    store.start()
+    store.wait()
 
 
 def join(joined, received):
@@ -157,7 +175,7 @@
         in_specs=anywhere(2),
         out_specs=anywhere(1)[0],
         input_output_aliases={0: 0},
-        scratch_shapes=[pltpu.SemaphoreType.DMA],
+        scratch_shapes=[pltpu.VMEM((TOKS, ALL_TOKS), BF16), pltpu.SemaphoreType.DMA((2,))],
         compiler_params=params(58),
         cost_estimate=SMALL,
         name="join",
@@ -168,7 +186,7 @@
     del refs
 
 
-def hold(*arrays):
+def hold(*arrays, cost=SMALL):
     return pl.pallas_call(
         hold_kernel,
         out_shape=tuple(jax.ShapeDtypeStruct(array.shape, array.dtype) for array in arrays),
@@ -176,14 +194,14 @@
         out_specs=tuple(anywhere(len(arrays))),
         input_output_aliases={i: i for i in range(len(arrays))},
         compiler_params=params(58),
-        cost_estimate=SMALL,
+        cost_estimate=cost,
         name="hold",
     )(*arrays)
 
 
 def encode_kernel(
     place, feats, low, high, bias, index, cond, project, mix, pool, fence,
-    encoded, first, last, residual, normed,
+    encoded, first, last, residual, normed, again,
     rows, bias32, packed, mixed, ext,
 ):
     rows[0 : 2 * LOWER] = low[0 : 2 * LOWER].astype(F32)
@@ -219,6 +237,7 @@
         state = cond[...].astype(F32) + dot(chosen, lifted) / counts
         residual[seed] = state
         normed[seed] = layer_norm(state).astype(BF16)
+        again[seed] = normed[seed]
 
 
 def encode(*args):
@@ -230,9 +249,10 @@
             jax.ShapeDtypeStruct((SEEDS, MARGIN, CA), BF16),
             jax.ShapeDtypeStruct((SEEDS, TOKS, CT), F32),
             jax.ShapeDtypeStruct((SEEDS, TOKS, CT), BF16),
+            jax.ShapeDtypeStruct((SEEDS, TOKS, CT), BF16),
         ),
         in_specs=[pl.BlockSpec(memory_space=pltpu.SMEM)] + vmem(9) + anywhere(1),
-        out_specs=tuple(vmem(5)),
+        out_specs=tuple(vmem(6)),
         scratch_shapes=[
             pltpu.VMEM((2 * EXT, CA), F32),
             pltpu.VMEM((33 * 4 * QB, WIN), F32),
@@ -595,24 +615,23 @@
     above = along_y(mine, -1)
     other = along_z(mine)
 
-    encoded, first, last, residual, normed = encode(
+    encoded, first, last, residual, normed, again = encode(
         place, feats, low, high, bias_enc, index, token_cond, enc_project, enc_mix, pool_weight,
         mine,
     )
     everyone = lax.all_gather(normed, "tok", axis=0)
-    below, above, other, first, last = hold(below, above, other, first, last)
-    far = (along_y(below[:TOKS], 1), along_y(above[TOKS:], -1))
+    below, above, other, first, last, again = hold(
+        below, above, other, first, last, again, cost=LARGE
+    )
+    far = along_y(mine, 2)
     other_below = along_y(other, 1)
     other_above = along_y(other, -1)
+    other_far = along_y(other, 2)
     enc_low = along_tok(last, 1)
     enc_high = along_tok(first, -1)
     weights = spaced(place, token_project, below)
-    query, gate = queries(place, normed, across_core(normed), weights, below)
-
-    everyone, other_below, other_above, query, enc_low, enc_high = hold(
-        everyone, other_below, other_above, query, enc_low, enc_high
-    )
-    other_far = (along_y(other_below[:TOKS], 1), along_y(other_above[TOKS:], -1))
+    query, gate = queries(place, again, across_core(again), weights, below)
+    everyone, query, enc_low, enc_high = hold(everyone, query, enc_low, enc_high)
     key_value = keys(everyone, weights)
 
     level, side = seed // 2, seed % 2
@@ -622,12 +641,12 @@
 
     done = attend(
         ids((0, 0), (3, 0), (1, 0), (2, 0), (0, 1)), query, gate, key_value, (),
-        ((mine,), (below,), (above,), far, (other,)),
+        ((mine,), (below,), (above,), (far,), (other,)),
     )
     done = attend(
         ids((3, 1), (1, 1)), query, gate, key_value, done, ((other_below,), (other_above,))
     )
-    own, sent = attend(ids((2, 1)), query, gate, key_value, done, (other_far,))
+    own, sent = attend(ids((2, 1)), query, gate, key_value, done, ((other_far,),))
 
     state, spread, spread_first, spread_last = finish(
         residual, own, across_core(sent), token_mix.reshape(GROUPS, PAIR, CT), swiglu_in,

time: 226 us -> 157 us (0.69)
  Pallas kernels: 121 us -> 72.3 us
  starting transfers between devices: 31.1 us -> 18.2 us
  local copies, waits for them, and re-layouts: 16.1 us -> 7.51 us
    pallas_call x1, Pallas kernels: 36.6 us -> 3.03 us  [pack(): pl.pallas_call(pack_kernel, out_shape=(jax.ShapeDtypeStruct((UP_ROWS, CA)...]
    ppermute x1, waiting for transfers between devices: 19.2 us -> 3.78 us  [along_z(): return lax.ppermute(values, 'seed', [(i, i ^ 1) for i in range(8)])]
    pallas_call x1, Pallas kernels: 17 us -> 1.86 us  [join(): pl.pallas_call(join_kernel, out_shape=jax.ShapeDtypeStruct(joined.shape,...]
    all_gather x1, waiting for transfers between devices: 0.02 us -> 14.8 us  [per_device(): everyone = lax.all_gather(normed, 'tok', axis=0)]
    ppermute x6, waiting for transfers between devices: 2.89 us -> 10.1 us  [along_tok(): return lax.ppermute(values, 'tok', [(i, (i + by) % 16) for i in range(16)])]
    ppermute x8 -> x6, waiting for transfers between devices: 18.5 us -> 11.6 us  [along_y(): lax.ppermute(values, 'seed', [(i, (i + 2 * by) % 8) for i in range(8)])]
    slice x4 -> x0, local copies, waits for them, and re-layouts: 6.72 us -> none  [the longest x2 2.76 us: per_device(): far = (along_y(below[:TOKS], 1), along_y(above[TOKS:], -1))]
    ppermute x3, starting transfers between devices: 7.74 us -> 2.42 us  [across_core(): return lax.ppermute(values, 'tok', [(i, i ^ 1) for i in range(16)])]
  transfers between devices with their start and end apart: 19 -> 17, of which waited for: 5 -> 9; matrix products, arithmetic and copies ran while one was open for 4% -> 1% of each run, Pallas kernels for 25% -> 31%
where the time goes in v4:
time: 157 us
  Pallas kernels  72.3 us (46%)
  waiting for transfers between devices  43.6 us (28%)
  starting transfers between devices  18.2 us (12%)
  between operations  14.1 us (9%)
  local copies, waits for them, and re-layouts  7.51 us (5%)
    pallas_call x3, Pallas kernels, attend(): pl.pallas_call(functools.partial(attend_kernel, tuple((len(parts) for par...  21.9 us
    all_gather x1, waiting for transfers between devices, per_device(): everyone = lax.all_gather(normed, 'tok', axis=0)  14.8 us
    ppermute x6, waiting for transfers between devices, along_y(): lax.ppermute(values, 'seed', [(i, (i + 2 * by) % 8) for i in range(8)])  11.6 us
    pallas_call x1, Pallas kernels, keys(): pl.pallas_call(keys_kernel, grid=(tokens.shape[0] // step,), out_shape=ja...  10.5 us
    ppermute x6, waiting for transfers between devices, along_tok(): return lax.ppermute(values, 'tok', [(i, (i + by) % 16) for i in range(16)])  10.1 us
    pallas_call x1, Pallas kernels, encode(): pl.pallas_call(encode_kernel, out_shape=(jax.ShapeDtypeStruct((SEEDS, ATO...  9.21 us
    pallas_call x1, Pallas kernels, decode(): pl.pallas_call(decode_kernel, out_shape=jax.ShapeDtypeStruct((SEEDS * ATO...  8.11 us
    unnamed x37, local copies, waits for them, and re-layouts  7.43 us
  transfers between devices with their start and end apart: 17, of which 9 were waited for; matrix products, arithmetic and copies ran while one was open for 1% of the time, Pallas kernels for 31%

profile of v4, /device:TPU:7, one launch (start us, length us, event | category | flops | bytes accessed | tf_op | source)
XLA Modules:
  0.0 156.5 jit_solution(8669097124634305070)
XLA Ops:
  7.9 3.0 %pack.1 = (bf16[304,128]{1,0:T(8,128)(2,1)}, bf16[112,128]{1,0:T(8,128)(2,1)}, bf16[128,2048]{1,0:T(8,128)(2,1)}, bf16[256,2048]{1,0:T(8,128)(2,1)}) custom-call(s32[2]{0:T(128)} %pad_add_fusion.place, bf16[2048,128]{1,0:T(8,128)(2,1)} %bitcast.21, bf16[4096,128]{1,0:T(8,128)(2,1)} %bitcast.19, s32[8,128]{1,0:T(8,128)} %bitcast.27, ...), custom_call_target="tpu_custom_call" | custom-call | flops 1000000 | bytes 10000 | tf_op jit(solution)/shard_map/pack/pallas_call | solution.py:141
  11.7 1.7 %collective-permute-done.2.received = bf16[128,2048]{1,0:T(8,128)(2,1)S(1)} collective-permute-done((bf16[128,2048]{1,0:T(8,128)(2,1)}, bf16[128,2048]{1,0:T(8,128)(2,1)S(1)}, u32[]{:S(2)}, u32[]{:S(2)}) %collective-permute-start.2) | collective-permute-done | bytes 524320 | tf_op jit(solution)/shard_map/ppermute | solution.py:586
  14.2 1.9 %join.1.fence.rest_0_ = bf16[256,2048]{1,0:T(8,128)(2,1)} custom-call(bf16[256,2048]{1,0:T(8,128)(2,1)} %get-tuple-element.36.joined, bf16[128,2048]{1,0:T(8,128)(2,1)} %copy-done.10), custom_call_target="tpu_custom_call", output_to_operand_aliasing={{}: (0, {})} | custom-call | flops 1000000 | bytes 10000 | tf_op jit(solution)/shard_map/join/pallas_call | solution.py:172
  17.4 1.5 collective-permute-start.4
  19.0 3.6 %collective-permute-start.5 = (bf16[256,2048]{1,0:T(8,128)(2,1)}, bf16[256,2048]{1,0:T(8,128)(2,1)}, u32[]{:S(2)}, u32[]{:S(2)}) collective-permute-start(bf16[256,2048]{1,0:T(8,128)(2,1)} %join.1.fence.rest_0_), channel_id=1, source_target_pairs={{0,16},{16,0},{32,48},{48,32},{64,80},{80,64},{96,112},{112,96},{1... | collective-permute-start | bytes 3145736 | tf_op jit(solution)/shard_map/ppermute | solution.py:594
  22.6 1.6 %collective-permute-start = (bf16[304,128]{1,0:T(8,128)(2,1)}, bf16[304,128]{1,0:T(8,128)(2,1)S(1)}, u32[]{:S(2)}, u32[]{:S(2)}) collective-permute-start(bf16[304,128]{1,0:T(8,128)(2,1)} %get-tuple-element.34), channel_id=1, source_target_pairs={{0,1},{1,2},{2,3},{3,4},{4,5},{5,6},{6,7},{7,8},{8,9},{9,10},{10,1... | collective-permute-start | bytes 233480 | tf_op jit(solution)/shard_map/ppermute | solution.py:582
  24.2 6.0 %collective-permute-done.1.high = bf16[112,128]{1,0:T(8,128)(2,1)S(1)} collective-permute-done((bf16[112,128]{1,0:T(8,128)(2,1)}, bf16[112,128]{1,0:T(8,128)(2,1)S(1)}, u32[]{:S(2)}, u32[]{:S(2)}) %collective-permute-start.1) | collective-permute-done | bytes 28704 | tf_op jit(solution)/shard_map/ppermute | solution.py:582
  31.4 9.2 %encode.1 = (bf16[2,1024,128]{2,1,0:T(8,128)(2,1)}, bf16[2,48,128]{2,1,0:T(8,128)(2,1)}, bf16[2,48,128]{2,1,0:T(8,128)(2,1)}, f32[2,128,768]{2,1,0:T(8,128)}, bf...) custom-call(s32[2]{0:T(128)} %pad_add_fusion.place, bf16[2048,128]{1,0:T(8,128)(2,1)} %bitcast.22, ...), custom_call_target="tpu_custom_call" | custom-call | flops 1000000 | bytes 10000 | tf_op jit(solution)/shard_map/encode/pallas_call | solution.py:244
  42.2 3.8 %collective-permute-done.5.refs_2_ = bf16[256,2048]{1,0:T(8,128)(2,1)} collective-permute-done((bf16[256,2048]{1,0:T(8,128)(2,1)}, bf16[256,2048]{1,0:T(8,128)(2,1)}, u32[]{:S(2)}, u32[]{:S(2)}) %collective-permute-start.5) | collective-permute-done | bytes 1048608 | tf_op jit(solution)/shard_map/ppermute | solution.py:594
  48.9 1.6 %collective-permute-start.12 = (bf16[256,2048]{1,0:T(8,128)(2,1)}, bf16[256,2048]{1,0:T(8,128)(2,1)}, u32[]{:S(2)}, u32[]{:S(2)}) collective-permute-start(bf16[256,2048]{1,0:T(8,128)(2,1)} %join.1.fence.rest_0_), channel_id=1, source_target_pairs={{0,64},{16,80},{32,96},{48,112},{64,0},{80,16},{96,32},{112,48},{1... | collective-permute-start | bytes 3145736 | tf_op jit(solution)/shard_map/ppermute | solution.py:590
  50.9 2.3 %collective-permute-start.11 = (bf16[256,2048]{1,0:T(8,128)(2,1)}, bf16[256,2048]{1,0:T(8,128)(2,1)}, u32[]{:S(2)}, u32[]{:S(2)}) collective-permute-start(bf16[256,2048]{1,0:T(8,128)(2,1)} %get-tuple-element.51.rest_4_), channel_id=1, source_target_pairs={{0,96},{16,112},{32,0},{48,16},{64,32},{80,48},{96,64},{112,80},{1... | collective-permute-start | bytes 3145736 | tf_op jit(solution)/shard_map/ppermute | solution.py:590
  53.2 6.7 %spaced.1.weight = bf16[2,4,768,256]{3,2,1,0:T(8,128)(2,1)} custom-call(s32[2]{0:T(128)} %pad_add_fusion.place, bf16[768,3072]{1,0:T(8,128)(2,1)} %second.1, bf16[768,3072]{1,0:T(8,128)(2,1)} %second.1, bf16[256,2048]{1,0:T(8,128)(2,1)} %get-tuple-element.44.fence.rest_1_), custom_call_target="tpu_custom_call" | custom-call | flops 1000000 | bytes 10000 | tf_op jit(solution)/shard_map/spaced/pallas_call | solution.py:350
  60.4 3.8 %queries.1 = (bf16[8,2,256,128]{3,2,1,0:T(8,128)(2,1)S(1)}, f32[8,2,256,128]{3,2,1,0:T(8,128)}) custom-call(s32[2]{0:T(128)S(1)} %copy-done.6, bf16[2,128,768]{2,1,0:T(8,128)(2,1)S(1)} %copy-done.7, bf16[2,128,768]{2,1,0:T(8,128)(2,1)S(1)} %collective-permute-done.6.other, bf16[2,4,768,256]{3,2,1,0:T(8,128)(2,1)} %spaced.1.weight, ...), custom_call_target="tpu_custom_call" | custom-call | flops 70000001024 | bytes 10000 | tf_op jit(solution)/shard_map/queries/pallas_call | solution.py:387
  66.0 14.8 %all-gather.3.cloned.1.call-done = bf16[32,128,768]{2,1,0:T(8,128)(2,1)} async-done(((bf16[2,128,768]{2,1,0:T(8,128)(2,1)}), bf16[32,128,768]{2,1,0:T(8,128)(2,1)}) %all-gather.3.cloned.1.call-update) | async-done | bytes 6291472 | tf_op jit(solution)/shard_map/all_gather | solution.py:622
  80.9 10.5 %keys.1.key_value = bf16[8,2,2048,128]{3,2,1,0:T(8,128)(2,1)} custom-call(bf16[16,2,128,768]{3,2,1,0:T(8,128)(2,1)} %get-tuple-element.50.tokens, bf16[2,4,768,256]{3,2,1,0:T(8,128)(2,1)S(1)} %copy-done.2), custom_call_target="tpu_custom_call" | custom-call | flops 1000000 | bytes 10000 | tf_op jit(solution)/shard_map/keys/pallas_call | solution.py:422
  91.4 12.6 %attend.3 = (bf16[8,2,128,128]{3,2,1,0:T(8,128)(2,1)S(1)}, bf16[8,2,128,128]{3,2,1,0:T(8,128)(2,1)S(1)}) custom-call(s32[5]{0:T(128)S(1)} %stack.51.group_ids, bf16[8,2,256,128]{3,2,1,0:T(8,128)(2,1)S(1)} %copy-done.1, f32[8,2,256,128]{3,2,1,0:T(8,128)} %get-tuple-element.49.gate, bf16[8,2,2048,128]{3,2,1,0:T(8,128)(2,1)} %keys.1.key_value, ...), custom_call_target="tpu_custom_call" | custom-call | flops 1000000 | bytes 10000 | tf_op jit(solution)/shard_map/attend/pallas_call | solution.py:502
  104.0 6.1 %attend.4 = (bf16[8,2,128,128]{3,2,1,0:T(8,128)(2,1)S(1)}, bf16[8,2,128,128]{3,2,1,0:T(8,128)(2,1)S(1)}) custom-call(s32[2]{0:T(128)S(1)} %pad_add_fusion.1.group_ids, bf16[8,2,256,128]{3,2,1,0:T(8,128)(2,1)S(1)} %copy-done.1, f32[8,2,256,128]{3,2,1,0:T(8,128)} %get-tuple-element.49.gate, ...), custom_call_target="tpu_custom_call", output_to_operand_aliasing={{0}: (6, {}), {1}: (7, {})} | custom-call | flops 1000000 | bytes 10000 | tf_op jit(solution)/shard_map/attend/pallas_call | solution.py:502
  110.1 10.1 %collective-permute-done.9.rest_0_ = bf16[256,2048]{1,0:T(8,128)(2,1)} collective-permute-done((bf16[256,2048]{1,0:T(8,128)(2,1)}, bf16[256,2048]{1,0:T(8,128)(2,1)}, u32[]{:S(2)}, u32[]{:S(2)}) %collective-permute-start.9) | collective-permute-done | bytes 1048608 | tf_op jit(solution)/shard_map/ppermute | solution.py:590
  120.2 3.2 %attend.5 = (bf16[8,2,128,128]{3,2,1,0:T(8,128)(2,1)S(1)}, bf16[8,2,128,128]{3,2,1,0:T(8,128)(2,1)S(1)}) custom-call(s32[1]{0:T(128)} %bitcast.5.group_ids, bf16[8,2,256,128]{3,2,1,0:T(8,128)(2,1)S(1)} %copy-done.1, f32[8,2,256,128]{3,2,1,0:T(8,128)} %get-tuple-element.49.gate, ...), custom_call_target="tpu_custom_call", output_to_operand_aliasing={{0}: (5, {}), {1}: (6, {})} | custom-call | flops 1000000 | bytes 10000 | tf_op jit(solution)/shard_map/attend/pallas_call | solution.py:502
  124.5 1.6 %collective-permute-done.13.received = bf16[8,2,128,128]{3,2,1,0:T(8,128)(2,1)S(1)} collective-permute-done((bf16[8,2,128,128]{3,2,1,0:T(8,128)(2,1)S(1)}, bf16[8,2,128,128]{3,2,1,0:T(8,128)(2,1)S(1)}, u32[]{:S(2)}, u32[]{:S(2)}) %collective-permute-start.13) | collective-permute-done | bytes 524320 | tf_op jit(solution)/shard_map/ppermute | solution.py:586
  126.9 7.2 %finish.1 = (bf16[2,128,768]{2,1,0:T(8,128)(2,1)}, bf16[2,128,128]{2,1,0:T(8,128)(2,1)}, bf16[2,16,128]{2,1,0:T(8,128)(2,1)}, bf16[2,16,128]{2,1,0:T(8,128)(2,1)}) custom-call(f32[2,128,768]{2,1,0:T(8,128)} %get-tuple-element.38.residual, bf16[8,2,128,128]{3,2,1,0:T(8,128)(2,1)} %copy-done.3, bf16[8,2,128,128]{3,2,1,0:T(8,128)(2,1)} %copy-done.9, ...), custom_call_target="tpu_custom_call" | custom-call | flops 1000000 | bytes 10000 | tf_op jit(solution)/shard_map/finish/pallas_call | solution.py:557
  135.6 2.1 %copy.34 = bf16[128,2,768]{2,1,0:T(2,128)(2,1)} copy(bf16[128,2,768]{2,0,1:T(8,128)(2,1)} %bitcast.26) | data formatting | bytes 786432
  137.7 3.2 %collective-permute-done.15.spread_high = bf16[2,16,128]{2,1,0:T(8,128)(2,1)S(1)} collective-permute-done((bf16[2,16,128]{2,1,0:T(8,128)(2,1)}, bf16[2,16,128]{2,1,0:T(8,128)(2,1)S(1)}, u32[]{:S(2)}, u32[]{:S(2)}) %collective-permute-start.15) | collective-permute-done | bytes 8224 | tf_op jit(solution)/shard_map/ppermute | solution.py:582
  141.6 8.1 %decode.1 = bf16[2048,128]{1,0:T(8,128)(2,1)} custom-call(s32[2]{0:T(128)} %pad_add_fusion.place, bf16[2,1024,128]{2,1,0:T(8,128)(2,1)} %get-tuple-element.60.enc, bf16[2,48,128]{2,1,0:T(8,128)(2,1)} %get-tuple-element.61.enc_low, bf16[2,48,128]{2,1,0:T(8,128)(2,1)} %get-tuple-element.62.enc_high, bf16[2,128,128]{2,1,0:T(8,128)(2,1)} %get-tuple-element.63.spread, ...), custom_call_target="tpu_custom_call" | custom-call | flops 1000000 | bytes 10000 | tf_op jit(solution)/shard_map/decode/pallas_call | solution.py:310
  (64 shorter events, 16.1 us)
Async XLA Ops:
  7.2 73.7 %all-gather.3.cloned.1.call-start = ((), (), s32[]{:S(2)}) async-start(), calls=%async_computation | async-start | bytes 6684672 | tf_op jit(solution)/shard_map/all_gather | solution.py:622
  10.9 2.5 %collective-permute-start.2 = (bf16[128,2048]{1,0:T(8,128)(2,1)}, bf16[128,2048]{1,0:T(8,128)(2,1)S(1)}, u32[]{:S(2)}, u32[]{:S(2)}) collective-permute-start(bf16[128,2048]{1,0:T(8,128)(2,1)} %get-tuple-element.37), channel_id=1, source_target_pairs={{0,1},{1,0},{2,3},{3,2},{4,5},{5,4},{6,7},{7,6},{8,9},{9,8},{10,11... | collective-permute-start | bytes 1572872 | tf_op jit(solution)/shard_map/ppermute | solution.py:586
  16.1 26.1 %collective-permute-start.3 = (bf16[256,2048]{1,0:T(8,128)(2,1)}, bf16[256,2048]{1,0:T(8,128)(2,1)S(1)}, u32[]{:S(2)}, u32[]{:S(2)}) collective-permute-start(bf16[256,2048]{1,0:T(8,128)(2,1)} %join.1.fence.rest_0_), channel_id=1, source_target_pairs={{0,32},{16,48},{32,64},{48,80},{64,96},{80,112},{96,0},{112,16},{1... | collective-permute-start | bytes 3145736 | tf_op jit(solution)/shard_map/ppermute | solution.py:590
  17.4 24.7 %collective-permute-start.4 = (bf16[256,2048]{1,0:T(8,128)(2,1)}, bf16[256,2048]{1,0:T(8,128)(2,1)S(1)}, u32[]{:S(2)}, u32[]{:S(2)}) collective-permute-start(bf16[256,2048]{1,0:T(8,128)(2,1)} %join.1.fence.rest_0_), channel_id=1, source_target_pairs={{0,96},{16,112},{32,0},{48,16},{64,32},{80,48},{96,64},{112,80},{1... | collective-permute-start | bytes 3145736 | tf_op jit(solution)/shard_map/ppermute | solution.py:590
  19.0 27.0 %collective-permute-start.5 = (bf16[256,2048]{1,0:T(8,128)(2,1)}, bf16[256,2048]{1,0:T(8,128)(2,1)}, u32[]{:S(2)}, u32[]{:S(2)}) collective-permute-start(bf16[256,2048]{1,0:T(8,128)(2,1)} %join.1.fence.rest_0_), channel_id=1, source_target_pairs={{0,16},{16,0},{32,48},{48,32},{64,80},{80,64},{96,112},{112,96},{1... | collective-permute-start | bytes 3145736 | tf_op jit(solution)/shard_map/ppermute | solution.py:594
  22.6 7.6 %collective-permute-start = (bf16[304,128]{1,0:T(8,128)(2,1)}, bf16[304,128]{1,0:T(8,128)(2,1)S(1)}, u32[]{:S(2)}, u32[]{:S(2)}) collective-permute-start(bf16[304,128]{1,0:T(8,128)(2,1)} %get-tuple-element.34), channel_id=1, source_target_pairs={{0,1},{1,2},{2,3},{3,4},{4,5},{5,6},{6,7},{7,8},{8,9},{9,10},{10,1... | collective-permute-start | bytes 233480 | tf_op jit(solution)/shard_map/ppermute | solution.py:582
  24.2 6.0 %collective-permute-start.1 = (bf16[112,128]{1,0:T(8,128)(2,1)}, bf16[112,128]{1,0:T(8,128)(2,1)S(1)}, u32[]{:S(2)}, u32[]{:S(2)}) collective-permute-start(bf16[112,128]{1,0:T(8,128)(2,1)} %get-tuple-element.35), channel_id=1, source_target_pairs={{0,15},{1,0},{2,1},{3,2},{4,3},{5,4},{6,5},{7,6},{8,7},{9,8},{10,9... | collective-permute-start | bytes 86024 | tf_op jit(solution)/shard_map/ppermute | solution.py:582
  46.0 14.2 %collective-permute-start.6 = (bf16[2,128,768]{2,1,0:T(8,128)(2,1)}, bf16[2,128,768]{2,1,0:T(8,128)(2,1)S(1)}, u32[]{:S(2)}, u32[]{:S(2)}) collective-permute-start(bf16[2,128,768]{2,1,0:T(8,128)(2,1)} %get-tuple-element.43.normed), channel_id=1, source_target_pairs={{0,1},{1,0},{2,3},{3,2},{4,5},{5,4},{6,7},{7,6},{8,9},{9,8},{10,11... | collective-permute-start | bytes 1179656 | tf_op jit(solution)/shard_map/ppermute | solution.py:586
  47.3 12.6 %collective-permute-start.7 = (bf16[2,48,128]{2,1,0:T(8,128)(2,1)}, bf16[2,48,128]{2,1,0:T(8,128)(2,1)S(1)}, u32[]{:S(2)}, u32[]{:S(2)}) collective-permute-start(bf16[2,48,128]{2,1,0:T(8,128)(2,1)} %get-tuple-element.46), channel_id=1, source_target_pairs={{0,1},{1,2},{2,3},{3,4},{4,5},{5,6},{6,7},{7,8},{8,9},{9,10},{10,1... | collective-permute-start | bytes 73736 | tf_op jit(solution)/shard_map/ppermute | solution.py:582
  48.9 42.4 %collective-permute-start.12 = (bf16[256,2048]{1,0:T(8,128)(2,1)}, bf16[256,2048]{1,0:T(8,128)(2,1)}, u32[]{:S(2)}, u32[]{:S(2)}) collective-permute-start(bf16[256,2048]{1,0:T(8,128)(2,1)} %join.1.fence.rest_0_), channel_id=1, source_target_pairs={{0,64},{16,80},{32,96},{48,112},{64,0},{80,16},{96,32},{112,48},{1... | collective-permute-start | bytes 3145736 | tf_op jit(solution)/shard_map/ppermute | solution.py:590
  50.5 53.5 %collective-permute-start.10 = (bf16[256,2048]{1,0:T(8,128)(2,1)}, bf16[256,2048]{1,0:T(8,128)(2,1)}, u32[]{:S(2)}, u32[]{:S(2)}) collective-permute-start(bf16[256,2048]{1,0:T(8,128)(2,1)} %get-tuple-element.51.rest_4_), channel_id=1, source_target_pairs={{0,32},{16,48},{32,64},{48,80},{64,96},{80,112},{96,0},{112,16},{1... | collective-permute-start | bytes 3145736 | tf_op jit(solution)/shard_map/ppermute | solution.py:590
  50.9 53.1 %collective-permute-start.11 = (bf16[256,2048]{1,0:T(8,128)(2,1)}, bf16[256,2048]{1,0:T(8,128)(2,1)}, u32[]{:S(2)}, u32[]{:S(2)}) collective-permute-start(bf16[256,2048]{1,0:T(8,128)(2,1)} %get-tuple-element.51.rest_4_), channel_id=1, source_target_pairs={{0,96},{16,112},{32,0},{48,16},{64,32},{80,48},{96,64},{112,80},{1... | collective-permute-start | bytes 3145736 | tf_op jit(solution)/shard_map/ppermute | solution.py:590
  53.2 7.0 %copy-start.17 = (bf16[2,48,128]{2,1,0:T(8,128)(2,1)S(1)}, bf16[2,48,128]{2,1,0:T(8,128)(2,1)}, u32[]{:S(2)}) copy-start(bf16[2,48,128]{2,1,0:T(8,128)(2,1)} %get-tuple-element.47) | copy-start | bytes 73732
  53.2 7.2 %copy-start.5 = (bf16[256,2048]{1,0:T(8,128)(2,1)S(1)}, bf16[256,2048]{1,0:T(8,128)(2,1)}, u32[]{:S(2)}) copy-start(bf16[256,2048]{1,0:T(8,128)(2,1)} %get-tuple-element.44.fence.rest_1_) | copy-start | bytes 3145732
  53.2 7.2 %copy-start.6 = (s32[2]{0:T(128)S(1)}, s32[2]{0:T(128)}, u32[]{:S(2)}) copy-start(s32[2]{0:T(128)} %pad_add_fusion.place) | copy-start | bytes 28
  53.2 7.2 %copy-start.7 = (bf16[2,128,768]{2,1,0:T(8,128)(2,1)S(1)}, bf16[2,128,768]{2,1,0:T(8,128)(2,1)}, u32[]{:S(2)}) copy-start(bf16[2,128,768]{2,1,0:T(8,128)(2,1)} %get-tuple-element.43.normed) | copy-start | bytes 1179652
  59.9 60.2 %collective-permute-start.9 = (bf16[256,2048]{1,0:T(8,128)(2,1)}, bf16[256,2048]{1,0:T(8,128)(2,1)}, u32[]{:S(2)}, u32[]{:S(2)}) collective-permute-start(bf16[256,2048]{1,0:T(8,128)(2,1)} %get-tuple-element.51.rest_4_), channel_id=1, source_target_pairs={{0,64},{16,80},{32,96},{48,112},{64,0},{80,16},{96,32},{112,48},{1... | collective-permute-start | bytes 3145736 | tf_op jit(solution)/shard_map/ppermute | solution.py:590
  60.2 5.9 %collective-permute-start.8 = (bf16[2,48,128]{2,1,0:T(8,128)(2,1)S(1)}, bf16[2,48,128]{2,1,0:T(8,128)(2,1)S(1)}, u32[]{:S(2)}, u32[]{:S(2)}) collective-permute-start(bf16[2,48,128]{2,1,0:T(8,128)(2,1)S(1)} %copy-done.17), channel_id=1, source_target_pairs={{0,15},{1,0},{2,1},{3,2},{4,3},{5,4},{6,5},{7,6},{8,7},{9,8},{10,9... | collective-permute-start | bytes 73736 | tf_op jit(solution)/shard_map/ppermute | solution.py:582
  65.2 15.6 %copy-start.2 = (bf16[2,4,768,256]{3,2,1,0:T(8,128)(2,1)S(1)}, bf16[2,4,768,256]{3,2,1,0:T(8,128)(2,1)}, u32[]{:S(2)}) copy-start(bf16[2,4,768,256]{3,2,1,0:T(8,128)(2,1)} %spaced.1.weight) | copy-start | bytes 9437188
  66.0 14.8 %copy-start.14 = (bf16[2,48,128]{2,1,0:T(8,128)(2,1)}, bf16[2,48,128]{2,1,0:T(8,128)(2,1)S(1)}, u32[]{:S(2)}) copy-start(bf16[2,48,128]{2,1,0:T(8,128)(2,1)S(1)} %collective-permute-done.8.refs_3_) | copy-start | bytes 73732
  80.9 10.5 %copy-start.1 = (bf16[8,2,256,128]{3,2,1,0:T(8,128)(2,1)S(1)}, bf16[8,2,256,128]{3,2,1,0:T(8,128)(2,1)}, u32[]{:S(2)}) copy-start(bf16[8,2,256,128]{3,2,1,0:T(8,128)(2,1)} %get-tuple-element.48.query) | copy-start | bytes 3145732
  124.2 1.9 %collective-permute-start.13 = (bf16[8,2,128,128]{3,2,1,0:T(8,128)(2,1)S(1)}, bf16[8,2,128,128]{3,2,1,0:T(8,128)(2,1)S(1)}, u32[]{:S(2)}, u32[]{:S(2)}) collective-permute-start(bf16[8,2,128,128]{3,2,1,0:T(8,128)(2,1)S(1)} %get-tuple-element.58), channel_id=1, source_target_pairs={{0,1},{1,0},{2,3},{3,2},{4,5},{5,4},{6,7},{7,6},{8,9},{9,8},{10,11... | collective-permute-start | bytes 1572872 | tf_op jit(solution)/shard_map/ppermute | solution.py:586
  134.0 3.7 %collective-permute-start.14 = (bf16[2,16,128]{2,1,0:T(8,128)(2,1)}, bf16[2,16,128]{2,1,0:T(8,128)(2,1)S(1)}, u32[]{:S(2)}, u32[]{:S(2)}) collective-permute-start(bf16[2,16,128]{2,1,0:T(8,128)(2,1)} %get-tuple-element.64), channel_id=1, source_target_pairs={{0,1},{1,2},{2,3},{3,4},{4,5},{5,6},{6,7},{7,8},{8,9},{9,10},{10,1... | collective-permute-start | bytes 24584 | tf_op jit(solution)/shard_map/ppermute | solution.py:582
  135.6 5.4 %collective-permute-start.15 = (bf16[2,16,128]{2,1,0:T(8,128)(2,1)}, bf16[2,16,128]{2,1,0:T(8,128)(2,1)S(1)}, u32[]{:S(2)}, u32[]{:S(2)}) collective-permute-start(bf16[2,16,128]{2,1,0:T(8,128)(2,1)} %get-tuple-element.65), channel_id=1, source_target_pairs={{0,15},{1,0},{2,1},{3,2},{4,3},{5,4},{6,5},{7,6},{8,7},{9,8},{10,9... | collective-permute-start | bytes 24584 | tf_op jit(solution)/shard_map/ppermute | solution.py:582
  (11 other events, 20.4 us)
Sparse Core Ops, SparseCore 0:
  40.8 40.0 all-gather.2

commit v5 on v4

--- a/solution.py
+++ b/solution.py
@@ -159,7 +159,7 @@
     )(place, feats, bias, index, pair_bias)
 
 
-def join_kernel(joined, received, out, rows, sems):
+def join_kernel(joined, received, low, high, out, rows, sems):
     load = pltpu.make_async_copy(received, rows, sems.at[0])
     load.start()
     load.wait()
@@ -168,18 +168,18 @@
     store.wait()
 
 
-def join(joined, received):
+def join(joined, received, low, high):
     return pl.pallas_call(
         join_kernel,
         out_shape=jax.ShapeDtypeStruct(joined.shape, BF16),
-        in_specs=anywhere(2),
+        in_specs=anywhere(4),
         out_specs=anywhere(1)[0],
         input_output_aliases={0: 0},
         scratch_shapes=[pltpu.VMEM((TOKS, ALL_TOKS), BF16), pltpu.SemaphoreType.DMA((2,))],
         compiler_params=params(58),
         cost_estimate=SMALL,
         name="join",
-    )(joined, received)
+    )(joined, received, low, high)
 
 
 def hold_kernel(*refs):
@@ -359,7 +359,7 @@
         + anywhere(1),
         out_specs=pl.BlockSpec((1, 2, CT, 256), lambda i: (i // 2, i % 2, 0, 0)),
         compiler_params=params(58),
-        cost_estimate=SMALL,
+        cost_estimate=LARGE,
         name="spaced",
     )(place, weight, weight, fence)
 
@@ -397,60 +397,98 @@
         + anywhere(1),
         out_specs=tuple(vmem(2)),
         compiler_params=params(50),
-        cost_estimate=LARGE,
+        cost_estimate=SMALL,
         name="queries",
     )(place, normed, other, weight, fence)
 
 
-def keys_kernel(tokens, weight, out):
-    count = tokens.shape[0]
-    values = jnp.concatenate([tokens[i].reshape(SEEDS * TOKS, CT) for i in range(count)], axis=0)
+def stack_kernel(*refs):
+    for i, ref in enumerate(refs[:-1]):
+        refs[-1][i] = ref[...]
+
+
+def stack(*chunks):
+    return pl.pallas_call(
+        stack_kernel,
+        out_shape=jax.ShapeDtypeStruct((len(chunks),) + chunks[0].shape, BF16),
+        in_specs=vmem(len(chunks)),
+        out_specs=vmem(1)[0],
+        compiler_params=params(50),
+        cost_estimate=SMALL,
+        name="stack",
+    )(*chunks)
+
+
+def keys_kernel(place, own, received, weight, *rest):
+    out, tiles, sems = rest[-3:]
+    chunks = [ref.at[i] for ref in (own, received) for i in range(ref.shape[0])]
+    values = jnp.concatenate([chunk[...].reshape(SEEDS * TOKS, CT) for chunk in chunks], axis=0)
     ones = (lax.broadcasted_iota(jnp.int32, (1, 256), 1) % 128 == PAIR).astype(F32)
+    copies = []
     for pair in range(GROUPS // 2):
         product = (dot(values, weight[0, pair]) + ones).astype(BF16)
-        for side in range(2):
-            for i in range(count):
+        for i in range(len(chunks)):
+            for side in range(2):
                 for seed in range(SEEDS):
                     start = (i * SEEDS + seed) * TOKS
-                    out[2 * pair + side, seed, i * TOKS : (i + 1) * TOKS] = product[
+                    tiles[i, 2 * pair + side, seed] = product[
                         start : start + TOKS, side * 128 : side * 128 + 128
                     ]
-
-
-def keys(tokens, weight):
-    step = 4
+            rows = pl.ds(pl.multiple_of(place[2 + i] * TOKS, TOKS), TOKS)
+            copies.append(
+                pltpu.make_async_copy(
+                    tiles.at[i, pl.ds(2 * pair, 2)],
+                    out.at[pl.ds(2 * pair, 2), :, rows],
+                    sems.at[pair, i],
+                )
+            )
+            copies[-1].start()
+    for copy in copies:
+        copy.wait()
+
+
+def keys(place, ids, own, received, weight, before=None, fences=()):
+    more = ([] if before is None else [before]) + list(fences)
+    count = own.shape[0] + received.shape[0]
     return pl.pallas_call(
         keys_kernel,
-        grid=(tokens.shape[0] // step,),
+        grid=(1,),
         out_shape=jax.ShapeDtypeStruct((GROUPS, SEEDS, ALL_TOKS, 128), BF16),
-        in_specs=[
-            pl.BlockSpec((step, SEEDS, TOKS, CT), lambda i: (i, 0, 0, 0)),
-            pl.BlockSpec((1, GROUPS // 2, CT, 256), lambda i: (1, 0, 0, 0)),
+        in_specs=[pl.BlockSpec(memory_space=pltpu.SMEM)]
+        + vmem(2)
+        + [pl.BlockSpec((1, GROUPS // 2, CT, 256), lambda i: (1, 0, 0, 0))]
+        + anywhere(len(more)),
+        out_specs=anywhere(1)[0],
+        scratch_shapes=[
+            pltpu.VMEM((count, GROUPS, SEEDS, TOKS, 128), BF16),
+            pltpu.SemaphoreType.DMA((GROUPS // 2, count)),
         ],
-        out_specs=pl.BlockSpec((GROUPS, SEEDS, step * TOKS, 128), lambda i: (0, 0, i, 0)),
+        input_output_aliases={} if before is None else {4: 0},
         compiler_params=params(50),
         cost_estimate=SMALL,
         name="keys",
-    )(tokens, weight)
-
-
-def attend_kernel(pieces, extra, group_ids, query, gate, key_value, *rest):
-    biases = rest[: sum(pieces)]
-    own, sent, bias, scores = rest[sum(pieces) + extra :]
+    )(jnp.concatenate([place, ids]), own, received, weight, *more)
+
+
+def attend_kernel(count, extra, group_ids, query, gate, key_value, *rest):
+    biases = rest[:count]
+    own, sent, slots, scores, sems = rest[count + extra :]
     step = pl.program_id(0)
-    at = 0
-    for i, parts in enumerate(pieces):
-        refs = biases[at : at + parts]
-        at += parts
+
+    def load(i):
+        return pltpu.make_async_copy(biases[i], slots.at[i % 2], sems.at[i % 2])
+
+    for i in range(count):
 
         @pl.when(step == i)
-        def _(refs=refs):
-            place = 0
-            for ref in refs:
-                size = ref.shape[0]
-                bias[place : place + size] = ref[...]
-                place += size
-
+        def _(i=i):
+            if i == 0:
+                load(0).start()
+            if i + 1 < count:
+                load(i + 1).start()
+            load(i).wait()
+
+    bias = slots.at[step % 2]
     width = 512
     tops = []
     for seed in range(SEEDS):
@@ -476,8 +514,8 @@
         sent[0, seed] = gated[TOKS:]
 
 
-def attend(group_ids, query, gate, key_value, before, pieces):
-    flat = [ref for parts in pieces for ref in parts]
+def attend(group_ids, query, gate, key_value, before, biases):
+    count = len(biases)
     shape = jax.ShapeDtypeStruct((GROUPS, SEEDS, TOKS, 128), BF16)
 
     def by_group(*block):
@@ -485,29 +523,29 @@
 
     grid_spec = pltpu.PrefetchScalarGridSpec(
         num_scalar_prefetch=1,
-        grid=(len(pieces),),
+        grid=(count,),
         in_specs=[
             by_group(SEEDS, 2 * TOKS, 128),
             by_group(SEEDS, 2 * TOKS, 128),
             by_group(SEEDS, ALL_TOKS, 128),
         ]
-        + vmem(len(flat))
-        + anywhere(len(before)),
+        + anywhere(count + len(before)),
         out_specs=(by_group(SEEDS, TOKS, 128),) * 2,
         scratch_shapes=[
-            pltpu.VMEM((2 * TOKS, ALL_TOKS), BF16),
+            pltpu.VMEM((2, 2 * TOKS, ALL_TOKS), BF16),
             pltpu.VMEM((SEEDS, 2 * TOKS, ALL_TOKS), F32),
+            pltpu.SemaphoreType.DMA((2,)),
         ],
     )
     return pl.pallas_call(
-        functools.partial(attend_kernel, tuple(len(parts) for parts in pieces), len(before)),
+        functools.partial(attend_kernel, count, len(before)),
         grid_spec=grid_spec,
         out_shape=(shape, shape),
-        input_output_aliases={4 + len(flat) + i: i for i in range(len(before))},
+        input_output_aliases={4 + count + i: i for i in range(len(before))},
         compiler_params=params(50),
         cost_estimate=SMALL,
         name="attend",
-    )(group_ids, query, gate, key_value, *flat, *before)
+    )(group_ids, query, gate, key_value, *biases, *before)
 
 
 def finish_kernel(
@@ -586,6 +624,14 @@
     return lax.ppermute(values, "tok", [(i, i ^ 1) for i in range(16)])
 
 
+def along_x(values, by):
+    return lax.ppermute(values, "tok", [(i, i // 8 * 8 + (i + 2 * by) % 8) for i in range(16)])
+
+
+def across_floor(values):
+    return lax.ppermute(values, "tok", [(i, i ^ 8) for i in range(16)])
+
+
 def along_y(values, by):
     return lax.ppermute(values, "seed", [(i, (i + 2 * by) % 8) for i in range(8)])
 
@@ -608,9 +654,9 @@
     index = atom_index.reshape(8, CA)
 
     up, down, send, joined = pack(place, feats, bias_enc, index, pair_bias)
-    mine = join(joined, across_core(send))
     low = along_tok(up, 1)
     high = along_tok(down, -1)
+    mine = join(joined, across_core(send), low, high)
     below = along_y(mine, 1)
     above = along_y(mine, -1)
     other = along_z(mine)
@@ -619,20 +665,50 @@
         place, feats, low, high, bias_enc, index, token_cond, enc_project, enc_mix, pool_weight,
         mine,
     )
-    everyone = lax.all_gather(normed, "tok", axis=0)
-    below, above, other, first, last, again = hold(
-        below, above, other, first, last, again, cost=LARGE
+    x_below = along_x(normed, 1)
+    x_above = along_x(normed, -1)
+    below, above, other, first, last, again, mine = hold(
+        below, above, other, first, last, again, mine
     )
     far = along_y(mine, 2)
+    z_own = across_floor(again)
+    mate = across_core(again)
+    x_far = along_x(again, 2)
+    weights = spaced(place, token_project, below)
+    z_own, x_below, x_above, x_far, weights = hold(z_own, x_below, x_above, x_far, weights)
+    z_below = along_x(z_own, 1)
+    z_above = along_x(z_own, -1)
+    z_far = across_floor(x_far)
+    near = stack(again, x_below, x_above, z_own)
+    near_mate = across_core(near)
+    query, gate = queries(place, again, mate, weights, z_own)
+    enc_low = along_tok(last, 1)
+    enc_high = along_tok(first, -1)
+    far, other, z_below, z_above, query = hold(far, other, z_below, z_above, query)
     other_below = along_y(other, 1)
     other_above = along_y(other, -1)
-    other_far = along_y(other, 2)
-    enc_low = along_tok(last, 1)
-    enc_high = along_tok(first, -1)
-    weights = spaced(place, token_project, below)
-    query, gate = queries(place, again, across_core(again), weights, below)
-    everyone, query, enc_low, enc_high = hold(everyone, query, enc_low, enc_high)
-    key_value = keys(everyone, weights)
+    other_far = along_z(far)
+    rest = stack(x_far, z_below, z_above, z_far)
+    rest_mate = across_core(rest)
+
+    column, floor, core = tok // 2 % 4, tok // 8, tok % 2
+
+    def shards(*offsets):
+        return jnp.stack(
+            [
+                (floor ^ dz) * 8 + (column + dx) % 4 * 2 + (core ^ side)
+                for side in (0, 1)
+                for dx, dz in offsets
+            ]
+        ).astype(jnp.int32)
+
+    key_value = keys(
+        place, shards((0, 0), (3, 0), (1, 0), (0, 1)), near, near_mate, weights
+    )
+    key_value = keys(
+        place, shards((2, 0), (3, 1), (1, 1), (2, 1)), rest, rest_mate, weights, key_value,
+        (enc_low, enc_high),
+    )
 
     level, side = seed // 2, seed % 2
 
@@ -641,12 +717,12 @@
 
     done = attend(
         ids((0, 0), (3, 0), (1, 0), (2, 0), (0, 1)), query, gate, key_value, (),
-        ((mine,), (below,), (above,), (far,), (other,)),
-    )
-    done = attend(
-        ids((3, 1), (1, 1)), query, gate, key_value, done, ((other_below,), (other_above,))
-    )
-    own, sent = attend(ids((2, 1)), query, gate, key_value, done, ((other_far,),))
+        (mine, below, above, far, other),
+    )
+    own, sent = attend(
+        ids((3, 1), (1, 1), (2, 1)), query, gate, key_value, done,
+        (other_below, other_above, other_far),
+    )
 
     state, spread, spread_first, spread_last = finish(
         residual, own, across_core(sent), token_mix.reshape(GROUPS, PAIR, CT), swiglu_in,

time: 157 us -> 146 us (0.930)
  waiting for transfers between devices: 43.6 us -> 25.3 us
  starting transfers between devices: 18.2 us -> 32.6 us
  between operations: 14.1 us -> 1.03 us
  local copies, waits for them, and re-layouts: 7.51 us -> 13 us
    all_gather x1 -> x0, waiting for transfers between devices: 14.8 us -> none  [per_device(): everyone = lax.all_gather(normed, 'tok', axis=0)]
    ppermute x0 -> x7, starting transfers between devices: none -> 6.79 us  [the longest x5 4.3 us: along_x(): lax.ppermute(values, 'tok', [(i, i // 8 * 8 + (i + 2 * by) % 8) for i in...]
    unnamed x37 -> x63, local copies, waits for them, and re-layouts: 7.43 us -> 12.7 us
    ppermute x3 -> x5, starting transfers between devices: 2.42 us -> 5.15 us  [across_core(): return lax.ppermute(values, 'tok', [(i, i ^ 1) for i in range(16)])]
    ppermute x1 -> x2, starting transfers between devices: 3.6 us -> 6.24 us  [along_z(): return lax.ppermute(values, 'seed', [(i, i ^ 1) for i in range(8)])]
    ppermute x6, starting transfers between devices: 4.76 us -> 7.32 us  [along_tok(): return lax.ppermute(values, 'tok', [(i, (i + by) % 16) for i in range(16)])]
    ppermute x3 -> x5, waiting for transfers between devices: 3.36 us -> 1.55 us  [across_core(): return lax.ppermute(values, 'tok', [(i, i ^ 1) for i in range(16)])]
    ppermute x1 -> x2, waiting for transfers between devices: 3.78 us -> 3.25 us  [along_z(): return lax.ppermute(values, 'seed', [(i, i ^ 1) for i in range(8)])]
  transfers between devices with their start and end apart: 17 -> 25, of which waited for: 9 -> 8; matrix products, arithmetic and copies ran while one was open for 1% -> 2% of each run, Pallas kernels for 31% -> 30%
where the time goes in v5:
time: 146 us; the launch traced here: 145 us
  Pallas kernels  72.5 us (50%)
  starting transfers between devices  32.6 us (22%)
  waiting for transfers between devices  25.3 us (17%)
  local copies, waits for them, and re-layouts  13 us (9%)
    pallas_call x2, Pallas kernels, attend(): pl.pallas_call(functools.partial(attend_kernel, count, len(before)), grid...  19 us
    pallas_call x2, Pallas kernels, keys(): pl.pallas_call(keys_kernel, grid=(1,), out_shape=jax.ShapeDtypeStruct((GR...  13.7 us
    unnamed x63, local copies, waits for them, and re-layouts  12.7 us
    ppermute x5, waiting for transfers between devices, along_y(): lax.ppermute(values, 'seed', [(i, (i + 2 * by) % 8) for i in range(8)])  11.1 us
    pallas_call x1, Pallas kernels, encode(): pl.pallas_call(encode_kernel, out_shape=(jax.ShapeDtypeStruct((SEEDS, ATO...  9.22 us
    ppermute x6, waiting for transfers between devices, along_tok(): return lax.ppermute(values, 'tok', [(i, (i + by) % 16) for i in range(16)])  8.86 us
    pallas_call x1, Pallas kernels, decode(): pl.pallas_call(decode_kernel, out_shape=jax.ShapeDtypeStruct((SEEDS * ATO...  8.09 us
    ppermute x6, starting transfers between devices, along_tok(): return lax.ppermute(values, 'tok', [(i, (i + by) % 16) for i in range(16)])  7.32 us
  transfers between devices with their start and end apart: 25, of which 8 were waited for; matrix products, arithmetic and copies ran while one was open for 2% of the time, Pallas kernels for 30%

profile of v5, /device:TPU:7, one launch (start us, length us, event | category | flops | bytes accessed | tf_op | source)
XLA Modules:
  0.0 145.3 jit_solution(8724434478416261025)
XLA Ops:
  1.3 3.0 %pack.1 = (bf16[304,128]{1,0:T(8,128)(2,1)}, bf16[112,128]{1,0:T(8,128)(2,1)}, bf16[128,2048]{1,0:T(8,128)(2,1)}, bf16[256,2048]{1,0:T(8,128)(2,1)}) custom-call(s32[2]{0:T(128)} %pad_add_fusion.place, bf16[2048,128]{1,0:T(8,128)(2,1)} %bitcast.35, bf16[4096,128]{1,0:T(8,128)(2,1)} %bitcast.33, s32[8,128]{1,0:T(8,128)} %bitcast.41, ...), custom_call_target="tpu_custom_call" | custom-call | flops 1000000 | bytes 10000 | tf_op jit(solution)/shard_map/pack/pallas_call | solution.py:141
  6.6 5.6 %collective-permute-done.1.high = bf16[112,128]{1,0:T(8,128)(2,1)S(1)} collective-permute-done((bf16[112,128]{1,0:T(8,128)(2,1)}, bf16[112,128]{1,0:T(8,128)(2,1)S(1)}, u32[]{:S(2)}, u32[]{:S(2)}) %collective-permute-start.1) | collective-permute-done | bytes 28704 | tf_op jit(solution)/shard_map/ppermute | solution.py:620
  13.0 1.8 %join.1.fence.refs_6_ = bf16[256,2048]{1,0:T(8,128)(2,1)} custom-call(bf16[256,2048]{1,0:T(8,128)(2,1)} %get-tuple-element.41.joined, bf16[128,2048]{1,0:T(8,128)(2,1)} %copy-done.25, bf16[304,128]{1,0:T(8,128)(2,1)} %copy-done.23, bf16[112,128]{1,0:T(8,128)(2,1)} %copy-done.26), custom_call_target="tpu_custom_call", output_to_operand_aliasing={{}: (0, {})} | custom-call | flops 1000000 | bytes 10000 | tf_op jit(solution)/shard_map/join/pallas_call | solution.py:172
  17.8 3.3 %collective-permute-start.5 = (bf16[256,2048]{1,0:T(8,128)(2,1)}, bf16[256,2048]{1,0:T(8,128)(2,1)}, u32[]{:S(2)}, u32[]{:S(2)}) collective-permute-start(bf16[256,2048]{1,0:T(8,128)(2,1)} %join.1.fence.refs_6_), channel_id=1, source_target_pairs={{0,16},{16,0},{32,48},{48,32},{64,80},{80,64},{96,112},{112,96},{1... | collective-permute-start | bytes 3145736 | tf_op jit(solution)/shard_map/ppermute | solution.py:640
  21.1 9.2 %encode.1 = (bf16[2,1024,128]{2,1,0:T(8,128)(2,1)}, bf16[2,48,128]{2,1,0:T(8,128)(2,1)}, bf16[2,48,128]{2,1,0:T(8,128)(2,1)}, f32[2,128,768]{2,1,0:T(8,128)}, bf...) custom-call(s32[2]{0:T(128)} %pad_add_fusion.place, bf16[2048,128]{1,0:T(8,128)(2,1)} %bitcast.36, ...), custom_call_target="tpu_custom_call" | custom-call | flops 1000000 | bytes 10000 | tf_op jit(solution)/shard_map/encode/pallas_call | solution.py:244
  31.7 7.3 %collective-permute-done.3.refs_0_ = bf16[256,2048]{1,0:T(8,128)(2,1)S(1)} collective-permute-done((bf16[256,2048]{1,0:T(8,128)(2,1)}, bf16[256,2048]{1,0:T(8,128)(2,1)S(1)}, u32[]{:S(2)}, u32[]{:S(2)}) %collective-permute-start.3) | collective-permute-done | bytes 1048608 | tf_op jit(solution)/shard_map/ppermute | solution.py:636
  39.4 3.3 %collective-permute-done.5.refs_2_ = bf16[256,2048]{1,0:T(8,128)(2,1)} collective-permute-done((bf16[256,2048]{1,0:T(8,128)(2,1)}, bf16[256,2048]{1,0:T(8,128)(2,1)}, u32[]{:S(2)}, u32[]{:S(2)}) %collective-permute-start.5) | collective-permute-done | bytes 1048608 | tf_op jit(solution)/shard_map/ppermute | solution.py:640
  47.6 6.5 %spaced.1.refs_4_ = bf16[2,4,768,256]{3,2,1,0:T(8,128)(2,1)} custom-call(s32[2]{0:T(128)} %pad_add_fusion.place, bf16[768,3072]{1,0:T(8,128)(2,1)} %second.1, bf16[768,3072]{1,0:T(8,128)(2,1)} %second.1, bf16[256,2048]{1,0:T(8,128)(2,1)} %get-tuple-element.51.fence.rest_1_), custom_call_target="tpu_custom_call" | custom-call | flops 70000001024 | bytes 10000 | tf_op jit(solution)/shard_map/spaced/pallas_call | solution.py:350
  57.6 1.8 %collective-permute-start.14 = (bf16[2,128,768]{2,1,0:T(8,128)(2,1)}, bf16[2,128,768]{2,1,0:T(8,128)(2,1)S(1)}, u32[]{:S(2)}, u32[]{:S(2)}) collective-permute-start(bf16[2,128,768]{2,1,0:T(8,128)(2,1)} %get-tuple-element.57.refs_0_), channel_id=1, source_target_pairs={{0,8},{1,9},{2,10},{3,11},{4,12},{5,13},{6,14},{7,15},{8,0},{9,1},... | collective-permute-start | bytes 1179656 | tf_op jit(solution)/shard_map/ppermute | solution.py:632
  62.5 1.7 %collective-permute-start.16 = (bf16[4,2,128,768]{3,2,1,0:T(8,128)(2,1)S(1)}, bf16[4,2,128,768]{3,2,1,0:T(8,128)(2,1)}, u32[]{:S(2)}, u32[]{:S(2)}) collective-permute-start(bf16[4,2,128,768]{3,2,1,0:T(8,128)(2,1)S(1)} %stack.119.own), channel_id=1, source_target_pairs={{0,1},{1,0},{2,3},{3,2},{4,5},{5,4},{6,7},{7,6},{8,9},{9,8},{10,11... | collective-permute-start | bytes 4718600 | tf_op jit(solution)/shard_map/ppermute | solution.py:624
  64.2 3.8 %queries.1 = (bf16[8,2,256,128]{3,2,1,0:T(8,128)(2,1)S(1)}, f32[8,2,256,128]{3,2,1,0:T(8,128)}) custom-call(s32[2]{0:T(128)S(1)} %copy-done.20, bf16[2,128,768]{2,1,0:T(8,128)(2,1)S(1)} %copy-done.3, bf16[2,128,768]{2,1,0:T(8,128)(2,1)S(1)} %collective-permute-done.13.other, bf16[2,4,768,256]{3,2,1,0:T(8,128)(2,1)} %get-tuple-element.53.weight, ...), custom_call_target="tpu_custom_call" | custom-call | flops 1000000 | bytes 10000 | tf_op jit(solution)/shard_map/queries/pallas_call | solution.py:387
  69.1 3.4 %collective-permute-done.6.refs_0_ = bf16[256,2048]{1,0:T(8,128)(2,1)} collective-permute-done((bf16[256,2048]{1,0:T(8,128)(2,1)}, bf16[256,2048]{1,0:T(8,128)(2,1)}, u32[]{:S(2)}, u32[]{:S(2)}) %collective-permute-start.6) | collective-permute-done | bytes 1048608 | tf_op jit(solution)/shard_map/ppermute | solution.py:636
  75.7 1.9 %collective-permute-start.17 = (bf16[2,48,128]{2,1,0:T(8,128)(2,1)S(1)}, bf16[2,48,128]{2,1,0:T(8,128)(2,1)S(1)}, u32[]{:S(2)}, u32[]{:S(2)}) collective-permute-start(bf16[2,48,128]{2,1,0:T(8,128)(2,1)S(1)} %copy-done.28), channel_id=1, source_target_pairs={{0,1},{1,2},{2,3},{3,4},{4,5},{5,6},{6,7},{7,8},{8,9},{9,10},{10,1... | collective-permute-start | bytes 73736 | tf_op jit(solution)/shard_map/ppermute | solution.py:620
  77.6 2.7 %collective-permute-start.20 = (bf16[256,2048]{1,0:T(8,128)(2,1)}, bf16[256,2048]{1,0:T(8,128)(2,1)}, u32[]{:S(2)}, u32[]{:S(2)}) collective-permute-start(bf16[256,2048]{1,0:T(8,128)(2,1)} %get-tuple-element.64.rest_4_), channel_id=1, source_target_pairs={{0,96},{16,112},{32,0},{48,16},{64,32},{80,48},{96,64},{112,80},{1... | collective-permute-start | bytes 3145736 | tf_op jit(solution)/shard_map/ppermute | solution.py:636
  80.2 2.9 %collective-permute-start.21 = (bf16[256,2048]{1,0:T(8,128)(2,1)}, bf16[256,2048]{1,0:T(8,128)(2,1)}, u32[]{:S(2)}, u32[]{:S(2)}) collective-permute-start(bf16[256,2048]{1,0:T(8,128)(2,1)} %get-tuple-element.65.rest_3_), channel_id=1, source_target_pairs={{0,16},{16,0},{32,48},{48,32},{64,80},{80,64},{96,112},{112,96},{1... | collective-permute-start | bytes 3145736 | tf_op jit(solution)/shard_map/ppermute | solution.py:640
  83.6 6.8 %keys.2.rest_0_ = bf16[8,2,2048,128]{3,2,1,0:T(8,128)(2,1)} custom-call(s32[10]{0:T(128)S(1)} %concatenate.9.place, bf16[4,2,128,768]{3,2,1,0:T(8,128)(2,1)S(1)} %stack.119.own, bf16[4,2,128,768]{3,2,1,0:T(8,128)(2,1)} %collective-permute-done.16.received, bf16[2,4,768,256]{3,2,1,0:T(8,128)(2,1)} %get-tuple-element.53.weight), custom_call_target="tpu_custom_call" | custom-call | flops 1000000 | bytes 10000 | tf_op jit(solution)/shard_map/keys/pallas_call | solution.py:453
  90.5 6.9 %keys.3.key_value = bf16[8,2,2048,128]{3,2,1,0:T(8,128)(2,1)} custom-call(s32[10]{0:T(128)S(1)} %concatenate.8.place, bf16[4,2,128,768]{3,2,1,0:T(8,128)(2,1)S(1)} %stack.118.own, bf16[4,2,128,768]{3,2,1,0:T(8,128)(2,1)} %collective-permute-done.15.received, bf16[2,4,768,256]{3,2,1,0:T(8,128)(2,1)} %get-tuple-element.53.weight, ...), custom_call_target="tpu_custom_call", output_to_operand_aliasing={{}: (4, {})} | custom-call | flops 1000000 | bytes 10000 | tf_op jit(solution)/shard_map/keys/pallas_call | solution.py:453
  97.4 10.6 %attend.2 = (bf16[8,2,128,128]{3,2,1,0:T(8,128)(2,1)S(1)}, bf16[8,2,128,128]{3,2,1,0:T(8,128)(2,1)S(1)}) custom-call(s32[5]{0:T(128)S(1)} %stack.117.group_ids, bf16[8,2,256,128]{3,2,1,0:T(8,128)(2,1)S(1)} %copy-done.2, f32[8,2,256,128]{3,2,1,0:T(8,128)} %get-tuple-element.56.gate, bf16[8,2,2048,128]{3,2,1,0:T(8,128)(2,1)} %keys.3.key_value, ...), custom_call_target="tpu_custom_call" | custom-call | flops 1000000 | bytes 10000 | tf_op jit(solution)/shard_map/attend/pallas_call | solution.py:540
  108.1 8.4 %attend.3 = (bf16[8,2,128,128]{3,2,1,0:T(8,128)(2,1)S(1)}, bf16[8,2,128,128]{3,2,1,0:T(8,128)(2,1)S(1)}) custom-call(s32[3]{0:T(128)S(1)} %pad_add_fusion.1.group_ids, bf16[8,2,256,128]{3,2,1,0:T(8,128)(2,1)S(1)} %copy-done.2, f32[8,2,256,128]{3,2,1,0:T(8,128)} %get-tuple-element.56.gate, ...), custom_call_target="tpu_custom_call", output_to_operand_aliasing={{0}: (7, {}), {1}: (8, {})} | custom-call | flops 1000000 | bytes 10000 | tf_op jit(solution)/shard_map/attend/pallas_call | solution.py:540
  120.1 7.2 %finish.1 = (bf16[2,128,768]{2,1,0:T(8,128)(2,1)}, bf16[2,128,128]{2,1,0:T(8,128)(2,1)}, bf16[2,16,128]{2,1,0:T(8,128)(2,1)}, bf16[2,16,128]{2,1,0:T(8,128)(2,1)}) custom-call(f32[2,128,768]{2,1,0:T(8,128)} %get-tuple-element.43.residual, bf16[8,2,128,128]{3,2,1,0:T(8,128)(2,1)} %copy-done.7, bf16[8,2,128,128]{3,2,1,0:T(8,128)(2,1)} %copy-done.24, ...), custom_call_target="tpu_custom_call" | custom-call | flops 1000000 | bytes 10000 | tf_op jit(solution)/shard_map/finish/pallas_call | solution.py:595
  127.3 3.9 %collective-permute-start.23 = (bf16[2,16,128]{2,1,0:T(8,128)(2,1)}, bf16[2,16,128]{2,1,0:T(8,128)(2,1)S(1)}, u32[]{:S(2)}, u32[]{:S(2)}) collective-permute-start(bf16[2,16,128]{2,1,0:T(8,128)(2,1)} %get-tuple-element.74), channel_id=1, source_target_pairs={{0,1},{1,2},{2,3},{3,4},{4,5},{5,6},{6,7},{7,8},{8,9},{9,10},{10,1... | collective-permute-start | bytes 24584 | tf_op jit(solution)/shard_map/ppermute | solution.py:620
  131.2 2.1 %copy.39 = bf16[128,2,768]{2,1,0:T(2,128)(2,1)} copy(bf16[128,2,768]{2,0,1:T(8,128)(2,1)} %bitcast.40) | data formatting | bytes 786432
  133.3 3.2 %collective-permute-done.24.spread_high = bf16[2,16,128]{2,1,0:T(8,128)(2,1)S(1)} collective-permute-done((bf16[2,16,128]{2,1,0:T(8,128)(2,1)}, bf16[2,16,128]{2,1,0:T(8,128)(2,1)S(1)}, u32[]{:S(2)}, u32[]{:S(2)}) %collective-permute-start.24) | collective-permute-done | bytes 8224 | tf_op jit(solution)/shard_map/ppermute | solution.py:620
  137.2 8.1 %decode.1 = bf16[2048,128]{1,0:T(8,128)(2,1)} custom-call(s32[2]{0:T(128)} %pad_add_fusion.place, bf16[2,1024,128]{2,1,0:T(8,128)(2,1)} %get-tuple-element.72.enc, bf16[2,48,128]{2,1,0:T(8,128)(2,1)} %copy-done.18, bf16[2,48,128]{2,1,0:T(8,128)(2,1)} %copy-done.19, bf16[2,128,128]{2,1,0:T(8,128)(2,1)} %get-tuple-element.73.spread, ...), custom_call_target="tpu_custom_call" | custom-call | flops 1000000 | bytes 10000 | tf_op jit(solution)/shard_map/decode/pallas_call | solution.py:310
  (110 shorter events, 28.7 us)
Async XLA Ops:
  4.3 7.9 %collective-permute-start.2 = (bf16[128,2048]{1,0:T(8,128)(2,1)}, bf16[128,2048]{1,0:T(8,128)(2,1)S(1)}, u32[]{:S(2)}, u32[]{:S(2)}) collective-permute-start(bf16[128,2048]{1,0:T(8,128)(2,1)} %get-tuple-element.42), channel_id=1, source_target_pairs={{0,1},{1,0},{2,3},{3,2},{4,5},{5,4},{6,7},{7,6},{8,9},{9,8},{10,11... | collective-permute-start | bytes 1572872 | tf_op jit(solution)/shard_map/ppermute | solution.py:624
  5.1 7.1 %collective-permute-start = (bf16[304,128]{1,0:T(8,128)(2,1)}, bf16[304,128]{1,0:T(8,128)(2,1)S(1)}, u32[]{:S(2)}, u32[]{:S(2)}) collective-permute-start(bf16[304,128]{1,0:T(8,128)(2,1)} %get-tuple-element.39), channel_id=1, source_target_pairs={{0,1},{1,2},{2,3},{3,4},{4,5},{5,6},{6,7},{7,8},{8,9},{9,10},{10,1... | collective-permute-start | bytes 233480 | tf_op jit(solution)/shard_map/ppermute | solution.py:620
  6.6 5.6 %collective-permute-start.1 = (bf16[112,128]{1,0:T(8,128)(2,1)}, bf16[112,128]{1,0:T(8,128)(2,1)S(1)}, u32[]{:S(2)}, u32[]{:S(2)}) collective-permute-start(bf16[112,128]{1,0:T(8,128)(2,1)} %get-tuple-element.40), channel_id=1, source_target_pairs={{0,15},{1,0},{2,1},{3,2},{4,3},{5,4},{6,5},{7,6},{8,7},{9,8},{10,9... | collective-permute-start | bytes 86024 | tf_op jit(solution)/shard_map/ppermute | solution.py:620
  14.9 24.2 %collective-permute-start.3 = (bf16[256,2048]{1,0:T(8,128)(2,1)}, bf16[256,2048]{1,0:T(8,128)(2,1)S(1)}, u32[]{:S(2)}, u32[]{:S(2)}) collective-permute-start(bf16[256,2048]{1,0:T(8,128)(2,1)} %join.1.fence.refs_6_), channel_id=1, source_target_pairs={{0,32},{16,48},{32,64},{48,80},{64,96},{80,112},{96,0},{112,16},{1... | collective-permute-start | bytes 3145736 | tf_op jit(solution)/shard_map/ppermute | solution.py:636
  16.2 23.2 %collective-permute-start.4 = (bf16[256,2048]{1,0:T(8,128)(2,1)}, bf16[256,2048]{1,0:T(8,128)(2,1)S(1)}, u32[]{:S(2)}, u32[]{:S(2)}) collective-permute-start(bf16[256,2048]{1,0:T(8,128)(2,1)} %join.1.fence.refs_6_), channel_id=1, source_target_pairs={{0,96},{16,112},{32,0},{48,16},{64,32},{80,48},{96,64},{112,80},{1... | collective-permute-start | bytes 3145736 | tf_op jit(solution)/shard_map/ppermute | solution.py:636
  17.8 24.9 %collective-permute-start.5 = (bf16[256,2048]{1,0:T(8,128)(2,1)}, bf16[256,2048]{1,0:T(8,128)(2,1)}, u32[]{:S(2)}, u32[]{:S(2)}) collective-permute-start(bf16[256,2048]{1,0:T(8,128)(2,1)} %join.1.fence.refs_6_), channel_id=1, source_target_pairs={{0,16},{16,0},{32,48},{48,32},{64,80},{80,64},{96,112},{112,96},{1... | collective-permute-start | bytes 3145736 | tf_op jit(solution)/shard_map/ppermute | solution.py:640
  30.3 15.8 %collective-permute-start.8 = (bf16[2,128,768]{2,1,0:T(8,128)(2,1)}, bf16[2,128,768]{2,1,0:T(8,128)(2,1)S(1)}, u32[]{:S(2)}, u32[]{:S(2)}) collective-permute-start(bf16[2,128,768]{2,1,0:T(8,128)(2,1)} %get-tuple-element.50), channel_id=1, source_target_pairs={{0,2},{1,3},{2,4},{3,5},{4,6},{5,7},{6,0},{7,1},{8,10},{9,11},{10,... | collective-permute-start | bytes 1179656 | tf_op jit(solution)/shard_map/ppermute | solution.py:628
  30.3 23.9 %collective-permute-start.9 = (bf16[2,128,768]{2,1,0:T(8,128)(2,1)}, bf16[2,128,768]{2,1,0:T(8,128)(2,1)S(1)}, u32[]{:S(2)}, u32[]{:S(2)}) collective-permute-start(bf16[2,128,768]{2,1,0:T(8,128)(2,1)} %get-tuple-element.50), channel_id=1, source_target_pairs={{0,6},{1,7},{2,0},{3,1},{4,2},{5,3},{6,4},{7,5},{8,14},{9,15},{10,... | collective-permute-start | bytes 1179656 | tf_op jit(solution)/shard_map/ppermute | solution.py:628
  42.7 12.0 %collective-permute-start.10 = (bf16[2,128,768]{2,1,0:T(8,128)(2,1)}, bf16[2,128,768]{2,1,0:T(8,128)(2,1)S(1)}, u32[]{:S(2)}, u32[]{:S(2)}) collective-permute-start(bf16[2,128,768]{2,1,0:T(8,128)(2,1)} %get-tuple-element.49.normed.refs_0_), channel_id=1, source_target_pairs={{0,4},{1,5},{2,6},{3,7},{4,0},{5,1},{6,2},{7,3},{8,12},{9,13},{10,... | collective-permute-start | bytes 1179656 | tf_op jit(solution)/shard_map/ppermute | solution.py:628
  44.1 10.6 %collective-permute-start.7 = (bf16[2,128,768]{2,1,0:T(8,128)(2,1)}, bf16[2,128,768]{2,1,0:T(8,128)(2,1)S(1)}, u32[]{:S(2)}, u32[]{:S(2)}) collective-permute-start(bf16[2,128,768]{2,1,0:T(8,128)(2,1)} %get-tuple-element.49.normed.refs_0_), channel_id=1, source_target_pairs={{0,8},{1,9},{2,10},{3,11},{4,12},{5,13},{6,14},{7,15},{8,0},{9,1},... | collective-permute-start | bytes 1179656 | tf_op jit(solution)/shard_map/ppermute | solution.py:632
  44.8 17.8 %collective-permute-start.13 = (bf16[2,128,768]{2,1,0:T(8,128)(2,1)}, bf16[2,128,768]{2,1,0:T(8,128)(2,1)S(1)}, u32[]{:S(2)}, u32[]{:S(2)}) collective-permute-start(bf16[2,128,768]{2,1,0:T(8,128)(2,1)} %get-tuple-element.49.normed.refs_0_), channel_id=1, source_target_pairs={{0,1},{1,0},{2,3},{3,2},{4,5},{5,4},{6,7},{7,6},{8,9},{9,8},{10,11... | collective-permute-start | bytes 1179656 | tf_op jit(solution)/shard_map/ppermute | solution.py:624
  46.0 26.5 %collective-permute-start.6 = (bf16[256,2048]{1,0:T(8,128)(2,1)}, bf16[256,2048]{1,0:T(8,128)(2,1)}, u32[]{:S(2)}, u32[]{:S(2)}) collective-permute-start(bf16[256,2048]{1,0:T(8,128)(2,1)} %get-tuple-element.47.rest_0_), channel_id=1, source_target_pairs={{0,64},{16,80},{32,96},{48,112},{64,0},{80,16},{96,32},{112,48},{1... | collective-permute-start | bytes 3145736 | tf_op jit(solution)/shard_map/ppermute | solution.py:636
  56.2 13.0 %collective-permute-start.11 = (bf16[2,128,768]{2,1,0:T(8,128)(2,1)}, bf16[2,128,768]{2,1,0:T(8,128)(2,1)S(1)}, u32[]{:S(2)}, u32[]{:S(2)}) collective-permute-start(bf16[2,128,768]{2,1,0:T(8,128)(2,1)} %get-tuple-element.52.fence.refs_3_), channel_id=1, source_target_pairs={{0,2},{1,3},{2,4},{3,5},{4,6},{5,7},{6,0},{7,1},{8,10},{9,11},{10,... | collective-permute-start | bytes 1179656 | tf_op jit(solution)/shard_map/ppermute | solution.py:628
  57.4 11.7 %collective-permute-start.12 = (bf16[2,128,768]{2,1,0:T(8,128)(2,1)}, bf16[2,128,768]{2,1,0:T(8,128)(2,1)S(1)}, u32[]{:S(2)}, u32[]{:S(2)}) collective-permute-start(bf16[2,128,768]{2,1,0:T(8,128)(2,1)} %get-tuple-element.52.fence.refs_3_), channel_id=1, source_target_pairs={{0,6},{1,7},{2,0},{3,1},{4,2},{5,3},{6,4},{7,5},{8,14},{9,15},{10,... | collective-permute-start | bytes 1179656 | tf_op jit(solution)/shard_map/ppermute | solution.py:628
  57.6 15.0 %collective-permute-start.14 = (bf16[2,128,768]{2,1,0:T(8,128)(2,1)}, bf16[2,128,768]{2,1,0:T(8,128)(2,1)S(1)}, u32[]{:S(2)}, u32[]{:S(2)}) collective-permute-start(bf16[2,128,768]{2,1,0:T(8,128)(2,1)} %get-tuple-element.57.refs_0_), channel_id=1, source_target_pairs={{0,8},{1,9},{2,10},{3,11},{4,12},{5,13},{6,14},{7,15},{8,0},{9,1},... | collective-permute-start | bytes 1179656 | tf_op jit(solution)/shard_map/ppermute | solution.py:632
  62.5 20.7 %collective-permute-start.16 = (bf16[4,2,128,768]{3,2,1,0:T(8,128)(2,1)S(1)}, bf16[4,2,128,768]{3,2,1,0:T(8,128)(2,1)}, u32[]{:S(2)}, u32[]{:S(2)}) collective-permute-start(bf16[4,2,128,768]{3,2,1,0:T(8,128)(2,1)S(1)} %stack.119.own), channel_id=1, source_target_pairs={{0,1},{1,0},{2,3},{3,2},{4,5},{5,4},{6,7},{7,6},{8,9},{9,8},{10,11... | collective-permute-start | bytes 4718600 | tf_op jit(solution)/shard_map/ppermute | solution.py:624
  74.7 15.7 %collective-permute-start.15 = (bf16[4,2,128,768]{3,2,1,0:T(8,128)(2,1)S(1)}, bf16[4,2,128,768]{3,2,1,0:T(8,128)(2,1)}, u32[]{:S(2)}, u32[]{:S(2)}) collective-permute-start(bf16[4,2,128,768]{3,2,1,0:T(8,128)(2,1)S(1)} %stack.118.own), channel_id=1, source_target_pairs={{0,1},{1,0},{2,3},{3,2},{4,5},{5,4},{6,7},{7,6},{8,9},{9,8},{10,11... | collective-permute-start | bytes 4718600 | tf_op jit(solution)/shard_map/ppermute | solution.py:624
  75.7 4.6 %collective-permute-start.17 = (bf16[2,48,128]{2,1,0:T(8,128)(2,1)S(1)}, bf16[2,48,128]{2,1,0:T(8,128)(2,1)S(1)}, u32[]{:S(2)}, u32[]{:S(2)}) collective-permute-start(bf16[2,48,128]{2,1,0:T(8,128)(2,1)S(1)} %copy-done.28), channel_id=1, source_target_pairs={{0,1},{1,2},{2,3},{3,4},{4,5},{5,6},{6,7},{7,8},{8,9},{9,10},{10,1... | collective-permute-start | bytes 73736 | tf_op jit(solution)/shard_map/ppermute | solution.py:620
  77.6 30.5 %collective-permute-start.19 = (bf16[256,2048]{1,0:T(8,128)(2,1)}, bf16[256,2048]{1,0:T(8,128)(2,1)}, u32[]{:S(2)}, u32[]{:S(2)}) collective-permute-start(bf16[256,2048]{1,0:T(8,128)(2,1)} %get-tuple-element.64.rest_4_), channel_id=1, source_target_pairs={{0,32},{16,48},{32,64},{48,80},{64,96},{80,112},{96,0},{112,16},{1... | collective-permute-start | bytes 3145736 | tf_op jit(solution)/shard_map/ppermute | solution.py:636
  77.6 30.5 %collective-permute-start.20 = (bf16[256,2048]{1,0:T(8,128)(2,1)}, bf16[256,2048]{1,0:T(8,128)(2,1)}, u32[]{:S(2)}, u32[]{:S(2)}) collective-permute-start(bf16[256,2048]{1,0:T(8,128)(2,1)} %get-tuple-element.64.rest_4_), channel_id=1, source_target_pairs={{0,96},{16,112},{32,0},{48,16},{64,32},{80,48},{96,64},{112,80},{1... | collective-permute-start | bytes 3145736 | tf_op jit(solution)/shard_map/ppermute | solution.py:636
  80.2 27.8 %collective-permute-start.21 = (bf16[256,2048]{1,0:T(8,128)(2,1)}, bf16[256,2048]{1,0:T(8,128)(2,1)}, u32[]{:S(2)}, u32[]{:S(2)}) collective-permute-start(bf16[256,2048]{1,0:T(8,128)(2,1)} %get-tuple-element.65.rest_3_), channel_id=1, source_target_pairs={{0,16},{16,0},{32,48},{48,32},{64,80},{80,64},{96,112},{112,96},{1... | collective-permute-start | bytes 3145736 | tf_op jit(solution)/shard_map/ppermute | solution.py:640
  83.2 7.3 %collective-permute-start.18 = (bf16[2,48,128]{2,1,0:T(8,128)(2,1)S(1)}, bf16[2,48,128]{2,1,0:T(8,128)(2,1)S(1)}, u32[]{:S(2)}, u32[]{:S(2)}) collective-permute-start(bf16[2,48,128]{2,1,0:T(8,128)(2,1)S(1)} %copy-done.27), channel_id=1, source_target_pairs={{0,15},{1,0},{2,1},{3,2},{4,3},{5,4},{6,5},{7,6},{8,7},{9,8},{10,9... | collective-permute-start | bytes 73736 | tf_op jit(solution)/shard_map/ppermute | solution.py:620
  127.3 6.1 %collective-permute-start.23 = (bf16[2,16,128]{2,1,0:T(8,128)(2,1)}, bf16[2,16,128]{2,1,0:T(8,128)(2,1)S(1)}, u32[]{:S(2)}, u32[]{:S(2)}) collective-permute-start(bf16[2,16,128]{2,1,0:T(8,128)(2,1)} %get-tuple-element.74), channel_id=1, source_target_pairs={{0,1},{1,2},{2,3},{3,4},{4,5},{5,6},{6,7},{7,8},{8,9},{9,10},{10,1... | collective-permute-start | bytes 24584 | tf_op jit(solution)/shard_map/ppermute | solution.py:620
  131.2 5.4 %collective-permute-start.24 = (bf16[2,16,128]{2,1,0:T(8,128)(2,1)}, bf16[2,16,128]{2,1,0:T(8,128)(2,1)S(1)}, u32[]{:S(2)}, u32[]{:S(2)}) collective-permute-start(bf16[2,16,128]{2,1,0:T(8,128)(2,1)} %get-tuple-element.75), channel_id=1, source_target_pairs={{0,15},{1,0},{2,1},{3,2},{4,3},{5,4},{6,5},{7,6},{8,7},{9,8},{10,9... | collective-permute-start | bytes 24584 | tf_op jit(solution)/shard_map/ppermute | solution.py:620
  (32 other events, 103.2 us)

commit v6 on v5

--- a/solution.py
+++ b/solution.py
@@ -321,7 +321,7 @@
             pltpu.VMEM((TOKS + 2 * EDGE, CA), BF16),
             pltpu.VMEM((ATOMS + 2 * CA, CA), F32),
         ],
-        compiler_params=params(58),
+        compiler_params=params(30),
         cost_estimate=SMALL,
         name="decode",
     )(*args)
@@ -610,7 +610,7 @@
             pltpu.VMEM((SEEDS * TOKS, TRANS), BF16),
             pltpu.SemaphoreType.DMA((3, 3)),
         ],
-        compiler_params=params(58),
+        compiler_params=params(40),
         cost_estimate=SMALL,
         name="finish",
     )(residual, own, received, mix, wide, narrow, spread_weight)
@@ -667,15 +667,17 @@
     )
     x_below = along_x(normed, 1)
     x_above = along_x(normed, -1)
-    below, above, other, first, last, again, mine = hold(
-        below, above, other, first, last, again, mine
+    below, above, first, last, again, mine = hold(
+        below, above, first, last, again, mine
     )
     far = along_y(mine, 2)
     z_own = across_floor(again)
     mate = across_core(again)
     x_far = along_x(again, 2)
     weights = spaced(place, token_project, below)
-    z_own, x_below, x_above, x_far, weights = hold(z_own, x_below, x_above, x_far, weights)
+    z_own, x_below, x_above, x_far, weights, other = hold(
+        z_own, x_below, x_above, x_far, weights, other
+    )
     z_below = along_x(z_own, 1)
     z_above = along_x(z_own, -1)
     z_far = across_floor(x_far)

time: 146 us -> 141 us (0.966)
  starting transfers between devices: 32.6 us -> 28.3 us
  waiting for transfers between devices: 25.3 us -> 28.6 us
  local copies, waits for them, and re-layouts: 13 us -> 10.4 us
  Pallas kernels: 72.5 us -> 70.7 us
    ppermute x2, waiting for transfers between devices: 3.25 us -> 8.88 us  [along_z(): return lax.ppermute(values, 'seed', [(i, i ^ 1) for i in range(8)])]
    ppermute x5, waiting for transfers between devices: 11.1 us -> 6.48 us  [along_y(): lax.ppermute(values, 'seed', [(i, (i + 2 * by) % 8) for i in range(8)])]
    unnamed x63 -> x77, local copies, waits for them, and re-layouts: 12.7 us -> 10.2 us
    ppermute x2, starting transfers between devices: 6.24 us -> 3.75 us  [along_z(): return lax.ppermute(values, 'seed', [(i, i ^ 1) for i in range(8)])]
    pallas_call x1, Pallas kernels: 7.15 us -> 5.22 us  [finish(): pl.pallas_call(finish_kernel, out_shape=(jax.ShapeDtypeStruct((SEEDS, TOK...]
  transfers between devices with their start and end apart: 25 -> 25, of which waited for: 8 -> 10; matrix products, arithmetic and copies ran while one was open for 2% -> 1% of each run, Pallas kernels for 30% -> 32%
where the time goes in v6:
time: 141 us; the launch traced here: 140 us
  Pallas kernels  70.7 us (50%)
  waiting for transfers between devices  28.6 us (20%)
  starting transfers between devices  28.3 us (20%)
  local copies, waits for them, and re-layouts  10.4 us (7%)
    pallas_call x2, Pallas kernels, attend(): pl.pallas_call(functools.partial(attend_kernel, count, len(before)), grid...  20.1 us
    pallas_call x2, Pallas kernels, keys(): pl.pallas_call(keys_kernel, grid=(1,), out_shape=jax.ShapeDtypeStruct((GR...  13.7 us
    unnamed x77, local copies, waits for them, and re-layouts  10.2 us
    ppermute x6, waiting for transfers between devices, along_tok(): return lax.ppermute(values, 'tok', [(i, (i + by) % 16) for i in range(16)])  9.65 us
    pallas_call x1, Pallas kernels, encode(): pl.pallas_call(encode_kernel, out_shape=(jax.ShapeDtypeStruct((SEEDS, ATO...  9.25 us
    ppermute x2, waiting for transfers between devices, along_z(): return lax.ppermute(values, 'seed', [(i, i ^ 1) for i in range(8)])  8.88 us
    ppermute x5, starting transfers between devices, along_y(): lax.ppermute(values, 'seed', [(i, (i + 2 * by) % 8) for i in range(8)])  7.7 us
    pallas_call x1, Pallas kernels, decode(): pl.pallas_call(decode_kernel, out_shape=jax.ShapeDtypeStruct((SEEDS * ATO...  7.12 us
  transfers between devices with their start and end apart: 25, of which 10 were waited for; matrix products, arithmetic and copies ran while one was open for 1% of the time, Pallas kernels for 32%

profile of v6, /device:TPU:7, one launch (start us, length us, event | category | flops | bytes accessed | tf_op | source)
XLA Modules:
  0.0 140.0 jit_solution(6894897003669204117)
XLA Ops:
  1.3 3.0 %pack.1 = (bf16[304,128]{1,0:T(8,128)(2,1)}, bf16[112,128]{1,0:T(8,128)(2,1)}, bf16[128,2048]{1,0:T(8,128)(2,1)}, bf16[256,2048]{1,0:T(8,128)(2,1)}) custom-call(s32[2]{0:T(128)} %pad_add_fusion.place, bf16[2048,128]{1,0:T(8,128)(2,1)} %bitcast.43, bf16[4096,128]{1,0:T(8,128)(2,1)} %bitcast.41, s32[8,128]{1,0:T(8,128)} %bitcast.38, ...), custom_call_target="tpu_custom_call" | custom-call | flops 1000000 | bytes 10000 | tf_op jit(solution)/shard_map/pack/pallas_call | solution.py:141
  6.6 5.6 %collective-permute-done.1.high = bf16[112,128]{1,0:T(8,128)(2,1)S(1)} collective-permute-done((bf16[112,128]{1,0:T(8,128)(2,1)}, bf16[112,128]{1,0:T(8,128)(2,1)S(1)}, u32[]{:S(2)}, u32[]{:S(2)}) %collective-permute-start.1) | collective-permute-done | bytes 28704 | tf_op jit(solution)/shard_map/ppermute | solution.py:620
  13.0 1.8 %join.1.fence.refs_5_ = bf16[256,2048]{1,0:T(8,128)(2,1)} custom-call(bf16[256,2048]{1,0:T(8,128)(2,1)} %get-tuple-element.41.joined, bf16[128,2048]{1,0:T(8,128)(2,1)} %copy-done.33, bf16[304,128]{1,0:T(8,128)(2,1)} %copy-done.21, bf16[112,128]{1,0:T(8,128)(2,1)} %copy-done.24), custom_call_target="tpu_custom_call", output_to_operand_aliasing={{}: (0, {})} | custom-call | flops 1000000 | bytes 10000 | tf_op jit(solution)/shard_map/join/pallas_call | solution.py:172
  14.9 3.4 %collective-permute-start.10 = (bf16[256,2048]{1,0:T(8,128)(2,1)}, bf16[256,2048]{1,0:T(8,128)(2,1)}, u32[]{:S(2)}, u32[]{:S(2)}) collective-permute-start(bf16[256,2048]{1,0:T(8,128)(2,1)} %join.1.fence.refs_5_), channel_id=1, source_target_pairs={{0,16},{16,0},{32,48},{48,32},{64,80},{80,64},{96,112},{112,96},{1... | collective-permute-start | bytes 3145736 | tf_op jit(solution)/shard_map/ppermute | solution.py:640
  21.0 9.3 %encode.1 = (bf16[2,1024,128]{2,1,0:T(8,128)(2,1)}, bf16[2,48,128]{2,1,0:T(8,128)(2,1)}, bf16[2,48,128]{2,1,0:T(8,128)(2,1)}, f32[2,128,768]{2,1,0:T(8,128)}, bf...) custom-call(s32[2]{0:T(128)} %pad_add_fusion.place, bf16[2048,128]{1,0:T(8,128)(2,1)} %bitcast.44, ...), custom_call_target="tpu_custom_call" | custom-call | flops 1000000 | bytes 10000 | tf_op jit(solution)/shard_map/encode/pallas_call | solution.py:244
  31.7 7.7 %collective-permute-done.10.refs_5_ = bf16[256,2048]{1,0:T(8,128)(2,1)} collective-permute-done((bf16[256,2048]{1,0:T(8,128)(2,1)}, bf16[256,2048]{1,0:T(8,128)(2,1)}, u32[]{:S(2)}, u32[]{:S(2)}) %collective-permute-start.10) | collective-permute-done | bytes 1048608 | tf_op jit(solution)/shard_map/ppermute | solution.py:640
  39.5 3.4 %collective-permute-done.3.refs_0_ = bf16[256,2048]{1,0:T(8,128)(2,1)S(1)} collective-permute-done((bf16[256,2048]{1,0:T(8,128)(2,1)}, bf16[256,2048]{1,0:T(8,128)(2,1)S(1)}, u32[]{:S(2)}, u32[]{:S(2)}) %collective-permute-start.3) | collective-permute-done | bytes 1048608 | tf_op jit(solution)/shard_map/ppermute | solution.py:636
  47.0 2.3 %collective-permute-start.5 = (bf16[256,2048]{1,0:T(8,128)(2,1)}, bf16[256,2048]{1,0:T(8,128)(2,1)}, u32[]{:S(2)}, u32[]{:S(2)}) collective-permute-start(bf16[256,2048]{1,0:T(8,128)(2,1)} %get-tuple-element.47.rest_0_), channel_id=1, source_target_pairs={{0,64},{16,80},{32,96},{48,112},{64,0},{80,16},{96,32},{112,48},{1... | collective-permute-start | bytes 3145736 | tf_op jit(solution)/shard_map/ppermute | solution.py:636
  49.3 6.5 %spaced.1.refs_4_ = bf16[2,4,768,256]{3,2,1,0:T(8,128)(2,1)} custom-call(s32[2]{0:T(128)} %pad_add_fusion.place, bf16[768,3072]{1,0:T(8,128)(2,1)} %second.1, bf16[768,3072]{1,0:T(8,128)(2,1)} %second.1, bf16[256,2048]{1,0:T(8,128)(2,1)} %get-tuple-element.50.fence.rest_1_), custom_call_target="tpu_custom_call" | custom-call | flops 70000001024 | bytes 10000 | tf_op jit(solution)/shard_map/spaced/pallas_call | solution.py:350
  57.5 1.5 %collective-permute-start.11 = (bf16[2,128,768]{2,1,0:T(8,128)(2,1)}, bf16[2,128,768]{2,1,0:T(8,128)(2,1)S(1)}, u32[]{:S(2)}, u32[]{:S(2)}) collective-permute-start(bf16[2,128,768]{2,1,0:T(8,128)(2,1)} %get-tuple-element.52.fence.refs_3_), channel_id=1, source_target_pairs={{0,2},{1,3},{2,4},{3,5},{4,6},{5,7},{6,0},{7,1},{8,10},{9,11},{10,... | collective-permute-start | bytes 1179656 | tf_op jit(solution)/shard_map/ppermute | solution.py:628
  59.0 1.6 %collective-permute-start.14 = (bf16[2,128,768]{2,1,0:T(8,128)(2,1)}, bf16[2,128,768]{2,1,0:T(8,128)(2,1)S(1)}, u32[]{:S(2)}, u32[]{:S(2)}) collective-permute-start(bf16[2,128,768]{2,1,0:T(8,128)(2,1)} %get-tuple-element.57.refs_0_), channel_id=1, source_target_pairs={{0,8},{1,9},{2,10},{3,11},{4,12},{5,13},{6,14},{7,15},{8,0},{9,1},... | collective-permute-start | bytes 1179656 | tf_op jit(solution)/shard_map/ppermute | solution.py:632
  64.7 3.8 %queries.1 = (bf16[8,2,256,128]{3,2,1,0:T(8,128)(2,1)S(1)}, f32[8,2,256,128]{3,2,1,0:T(8,128)}) custom-call(s32[2]{0:T(128)S(1)} %copy-done.30, bf16[2,128,768]{2,1,0:T(8,128)(2,1)S(1)} %copy-done.6, bf16[2,128,768]{2,1,0:T(8,128)(2,1)S(1)} %collective-permute-done.13.other, bf16[2,4,768,256]{3,2,1,0:T(8,128)(2,1)} %get-tuple-element.53.weight, ...), custom_call_target="tpu_custom_call" | custom-call | flops 1000000 | bytes 10000 | tf_op jit(solution)/shard_map/queries/pallas_call | solution.py:387
  70.5 3.0 %collective-permute-done.5.refs_0_ = bf16[256,2048]{1,0:T(8,128)(2,1)} collective-permute-done((bf16[256,2048]{1,0:T(8,128)(2,1)}, bf16[256,2048]{1,0:T(8,128)(2,1)}, u32[]{:S(2)}, u32[]{:S(2)}) %collective-permute-start.5) | collective-permute-done | bytes 1048608 | tf_op jit(solution)/shard_map/ppermute | solution.py:636
  76.6 2.1 %collective-permute-start.17 = (bf16[2,48,128]{2,1,0:T(8,128)(2,1)S(1)}, bf16[2,48,128]{2,1,0:T(8,128)(2,1)S(1)}, u32[]{:S(2)}, u32[]{:S(2)}) collective-permute-start(bf16[2,48,128]{2,1,0:T(8,128)(2,1)S(1)} %copy-done.35), channel_id=1, source_target_pairs={{0,1},{1,2},{2,3},{3,4},{4,5},{5,6},{6,7},{7,8},{8,9},{9,10},{10,1... | collective-permute-start | bytes 73736 | tf_op jit(solution)/shard_map/ppermute | solution.py:620
  79.7 1.7 %collective-permute-start.20 = (bf16[256,2048]{1,0:T(8,128)(2,1)}, bf16[256,2048]{1,0:T(8,128)(2,1)}, u32[]{:S(2)}, u32[]{:S(2)}) collective-permute-start(bf16[256,2048]{1,0:T(8,128)(2,1)} %get-tuple-element.64.rest_4_), channel_id=1, source_target_pairs={{0,96},{16,112},{32,0},{48,16},{64,32},{80,48},{96,64},{112,80},{1... | collective-permute-start | bytes 3145736 | tf_op jit(solution)/shard_map/ppermute | solution.py:636
  82.2 6.7 %keys.2.rest_0_ = bf16[8,2,2048,128]{3,2,1,0:T(8,128)(2,1)} custom-call(s32[10]{0:T(128)S(1)} %concatenate.9.place, bf16[4,2,128,768]{3,2,1,0:T(8,128)(2,1)S(1)} %stack.119.own, bf16[4,2,128,768]{3,2,1,0:T(8,128)(2,1)} %collective-permute-done.16.received, bf16[2,4,768,256]{3,2,1,0:T(8,128)(2,1)} %get-tuple-element.53.weight), custom_call_target="tpu_custom_call" | custom-call | flops 1000000 | bytes 10000 | tf_op jit(solution)/shard_map/keys/pallas_call | solution.py:453
  89.0 7.0 %keys.3.key_value = bf16[8,2,2048,128]{3,2,1,0:T(8,128)(2,1)} custom-call(s32[10]{0:T(128)S(1)} %concatenate.8.place, bf16[4,2,128,768]{3,2,1,0:T(8,128)(2,1)S(1)} %stack.118.own, bf16[4,2,128,768]{3,2,1,0:T(8,128)(2,1)} %collective-permute-done.15.received, bf16[2,4,768,256]{3,2,1,0:T(8,128)(2,1)} %get-tuple-element.53.weight, ...), custom_call_target="tpu_custom_call", output_to_operand_aliasing={{}: (4, {})} | custom-call | flops 1000000 | bytes 10000 | tf_op jit(solution)/shard_map/keys/pallas_call | solution.py:453
  96.0 10.6 %attend.2 = (bf16[8,2,128,128]{3,2,1,0:T(8,128)(2,1)S(1)}, bf16[8,2,128,128]{3,2,1,0:T(8,128)(2,1)S(1)}) custom-call(s32[5]{0:T(128)S(1)} %stack.117.group_ids, bf16[8,2,256,128]{3,2,1,0:T(8,128)(2,1)S(1)} %copy-done.2, f32[8,2,256,128]{3,2,1,0:T(8,128)} %get-tuple-element.56.gate, bf16[8,2,2048,128]{3,2,1,0:T(8,128)(2,1)} %keys.3.key_value, ...), custom_call_target="tpu_custom_call" | custom-call | flops 1000000 | bytes 10000 | tf_op jit(solution)/shard_map/attend/pallas_call | solution.py:540
  107.8 9.4 %attend.3 = (bf16[8,2,128,128]{3,2,1,0:T(8,128)(2,1)S(1)}, bf16[8,2,128,128]{3,2,1,0:T(8,128)(2,1)S(1)}) custom-call(s32[3]{0:T(128)S(1)} %pad_add_fusion.1.group_ids, bf16[8,2,256,128]{3,2,1,0:T(8,128)(2,1)S(1)} %copy-done.2, f32[8,2,256,128]{3,2,1,0:T(8,128)} %get-tuple-element.56.gate, ...), custom_call_target="tpu_custom_call", output_to_operand_aliasing={{0}: (7, {}), {1}: (8, {})} | custom-call | flops 1000000 | bytes 10000 | tf_op jit(solution)/shard_map/attend/pallas_call | solution.py:540
  117.7 1.8 %collective-permute-done.22.received = bf16[8,2,128,128]{3,2,1,0:T(8,128)(2,1)S(1)} collective-permute-done((bf16[8,2,128,128]{3,2,1,0:T(8,128)(2,1)S(1)}, bf16[8,2,128,128]{3,2,1,0:T(8,128)(2,1)S(1)}, u32[]{:S(2)}, u32[]{:S(2)}) %collective-permute-start.22) | collective-permute-done | bytes 524320 | tf_op jit(solution)/shard_map/ppermute | solution.py:624
  119.6 5.2 %finish.1 = (bf16[2,128,768]{2,1,0:T(8,128)(2,1)S(1)}, bf16[2,128,128]{2,1,0:T(8,128)(2,1)S(1)}, bf16[2,16,128]{2,1,0:T(8,128)(2,1)S(1)}, bf16[2,16,128]{2,1,0:T(8,128)(2,1)S(1)}) custom-call(f32[2,128,768]{2,1,0:T(8,128)S(1)} %copy-done.20, bf16[8,2,128,128]{3,2,1,0:T(8,128)(2,1)S(1)} %get-tuple-element.69.own, ...), custom_call_target="tpu_custom_call" | custom-call | flops 1000000 | bytes 10000 | tf_op jit(solution)/shard_map/finish/pallas_call | solution.py:595
  124.8 2.8 %collective-permute-start.23 = (bf16[2,16,128]{2,1,0:T(8,128)(2,1)S(1)}, bf16[2,16,128]{2,1,0:T(8,128)(2,1)S(1)}, u32[]{:S(2)}, u32[]{:S(2)}) collective-permute-start(bf16[2,16,128]{2,1,0:T(8,128)(2,1)S(1)} %get-tuple-element.74), channel_id=1, source_target_pairs={{0,1},{1,2},{2,3},{3,4},{4,5},{5,6},{6,7},{7,8},{8,9},{9,10},{10,1... | collective-permute-start | bytes 24584 | tf_op jit(solution)/shard_map/ppermute | solution.py:620
  128.8 4.0 %collective-permute-done.24.spread_high = bf16[2,16,128]{2,1,0:T(8,128)(2,1)S(1)} collective-permute-done((bf16[2,16,128]{2,1,0:T(8,128)(2,1)S(1)}, bf16[2,16,128]{2,1,0:T(8,128)(2,1)S(1)}, u32[]{:S(2)}, u32[]{:S(2)}) %collective-permute-start.24) | collective-permute-done | bytes 8224 | tf_op jit(solution)/shard_map/ppermute | solution.py:620
  132.9 7.1 %decode.1 = bf16[2048,128]{1,0:T(8,128)(2,1)} custom-call(s32[2]{0:T(128)S(1)} %copy-done.30, bf16[2,1024,128]{2,1,0:T(8,128)(2,1)S(1)} %copy-done.23, bf16[2,48,128]{2,1,0:T(8,128)(2,1)S(1)} %collective-permute-done.17.rest_1_.enc_low, bf16[2,48,128]{2,1,0:T(8,128)(2,1)S(1)} %collective-permute-done.18.rest_2_.enc_high, ...), custom_call_target="tpu_custom_call" | custom-call | flops 1000000 | bytes 10000 | tf_op jit(solution)/shard_map/decode/pallas_call | solution.py:310
  (125 shorter events, 27.3 us)
Async XLA Ops:
  4.3 7.9 %collective-permute-start.2 = (bf16[128,2048]{1,0:T(8,128)(2,1)}, bf16[128,2048]{1,0:T(8,128)(2,1)S(1)}, u32[]{:S(2)}, u32[]{:S(2)}) collective-permute-start(bf16[128,2048]{1,0:T(8,128)(2,1)} %get-tuple-element.42), channel_id=1, source_target_pairs={{0,1},{1,0},{2,3},{3,2},{4,5},{5,4},{6,7},{7,6},{8,9},{9,8},{10,11... | collective-permute-start | bytes 1572872 | tf_op jit(solution)/shard_map/ppermute | solution.py:624
  5.1 7.1 %collective-permute-start = (bf16[304,128]{1,0:T(8,128)(2,1)}, bf16[304,128]{1,0:T(8,128)(2,1)S(1)}, u32[]{:S(2)}, u32[]{:S(2)}) collective-permute-start(bf16[304,128]{1,0:T(8,128)(2,1)} %get-tuple-element.39), channel_id=1, source_target_pairs={{0,1},{1,2},{2,3},{3,4},{4,5},{5,6},{6,7},{7,8},{8,9},{9,10},{10,1... | collective-permute-start | bytes 233480 | tf_op jit(solution)/shard_map/ppermute | solution.py:620
  6.6 5.6 %collective-permute-start.1 = (bf16[112,128]{1,0:T(8,128)(2,1)}, bf16[112,128]{1,0:T(8,128)(2,1)S(1)}, u32[]{:S(2)}, u32[]{:S(2)}) collective-permute-start(bf16[112,128]{1,0:T(8,128)(2,1)} %get-tuple-element.40), channel_id=1, source_target_pairs={{0,15},{1,0},{2,1},{3,2},{4,3},{5,4},{6,5},{7,6},{8,7},{9,8},{10,9... | collective-permute-start | bytes 86024 | tf_op jit(solution)/shard_map/ppermute | solution.py:620
  14.9 24.6 %collective-permute-start.10 = (bf16[256,2048]{1,0:T(8,128)(2,1)}, bf16[256,2048]{1,0:T(8,128)(2,1)}, u32[]{:S(2)}, u32[]{:S(2)}) collective-permute-start(bf16[256,2048]{1,0:T(8,128)(2,1)} %join.1.fence.refs_5_), channel_id=1, source_target_pairs={{0,16},{16,0},{32,48},{48,32},{64,80},{80,64},{96,112},{112,96},{1... | collective-permute-start | bytes 3145736 | tf_op jit(solution)/shard_map/ppermute | solution.py:640
  18.3 24.6 %collective-permute-start.3 = (bf16[256,2048]{1,0:T(8,128)(2,1)}, bf16[256,2048]{1,0:T(8,128)(2,1)S(1)}, u32[]{:S(2)}, u32[]{:S(2)}) collective-permute-start(bf16[256,2048]{1,0:T(8,128)(2,1)} %join.1.fence.refs_5_), channel_id=1, source_target_pairs={{0,32},{16,48},{32,64},{48,80},{64,96},{80,112},{96,0},{112,16},{1... | collective-permute-start | bytes 3145736 | tf_op jit(solution)/shard_map/ppermute | solution.py:636
  19.6 23.4 %collective-permute-start.4 = (bf16[256,2048]{1,0:T(8,128)(2,1)}, bf16[256,2048]{1,0:T(8,128)(2,1)S(1)}, u32[]{:S(2)}, u32[]{:S(2)}) collective-permute-start(bf16[256,2048]{1,0:T(8,128)(2,1)} %join.1.fence.refs_5_), channel_id=1, source_target_pairs={{0,96},{16,112},{32,0},{48,16},{64,32},{80,48},{96,64},{112,80},{1... | collective-permute-start | bytes 3145736 | tf_op jit(solution)/shard_map/ppermute | solution.py:636
  30.3 16.7 %collective-permute-start.7 = (bf16[2,128,768]{2,1,0:T(8,128)(2,1)}, bf16[2,128,768]{2,1,0:T(8,128)(2,1)S(1)}, u32[]{:S(2)}, u32[]{:S(2)}) collective-permute-start(bf16[2,128,768]{2,1,0:T(8,128)(2,1)} %get-tuple-element.49), channel_id=1, source_target_pairs={{0,2},{1,3},{2,4},{3,5},{4,6},{5,7},{6,0},{7,1},{8,10},{9,11},{10,... | collective-permute-start | bytes 1179656 | tf_op jit(solution)/shard_map/ppermute | solution.py:628
  30.3 25.6 %collective-permute-start.8 = (bf16[2,128,768]{2,1,0:T(8,128)(2,1)}, bf16[2,128,768]{2,1,0:T(8,128)(2,1)S(1)}, u32[]{:S(2)}, u32[]{:S(2)}) collective-permute-start(bf16[2,128,768]{2,1,0:T(8,128)(2,1)} %get-tuple-element.49), channel_id=1, source_target_pairs={{0,6},{1,7},{2,0},{3,1},{4,2},{5,3},{6,4},{7,5},{8,14},{9,15},{10,... | collective-permute-start | bytes 1179656 | tf_op jit(solution)/shard_map/ppermute | solution.py:628
  44.2 11.6 %collective-permute-start.6 = (bf16[2,128,768]{2,1,0:T(8,128)(2,1)}, bf16[2,128,768]{2,1,0:T(8,128)(2,1)S(1)}, u32[]{:S(2)}, u32[]{:S(2)}) collective-permute-start(bf16[2,128,768]{2,1,0:T(8,128)(2,1)} %get-tuple-element.48.normed.refs_0_), channel_id=1, source_target_pairs={{0,8},{1,9},{2,10},{3,11},{4,12},{5,13},{6,14},{7,15},{8,0},{9,1},... | collective-permute-start | bytes 1179656 | tf_op jit(solution)/shard_map/ppermute | solution.py:632
  44.7 12.0 %collective-permute-start.9 = (bf16[2,128,768]{2,1,0:T(8,128)(2,1)}, bf16[2,128,768]{2,1,0:T(8,128)(2,1)S(1)}, u32[]{:S(2)}, u32[]{:S(2)}) collective-permute-start(bf16[2,128,768]{2,1,0:T(8,128)(2,1)} %get-tuple-element.48.normed.refs_0_), channel_id=1, source_target_pairs={{0,4},{1,5},{2,6},{3,7},{4,0},{5,1},{6,2},{7,3},{8,12},{9,13},{10,... | collective-permute-start | bytes 1179656 | tf_op jit(solution)/shard_map/ppermute | solution.py:628
  45.9 17.8 %collective-permute-start.13 = (bf16[2,128,768]{2,1,0:T(8,128)(2,1)}, bf16[2,128,768]{2,1,0:T(8,128)(2,1)S(1)}, u32[]{:S(2)}, u32[]{:S(2)}) collective-permute-start(bf16[2,128,768]{2,1,0:T(8,128)(2,1)} %get-tuple-element.48.normed.refs_0_), channel_id=1, source_target_pairs={{0,1},{1,0},{2,3},{3,2},{4,5},{5,4},{6,7},{7,6},{8,9},{9,8},{10,11... | collective-permute-start | bytes 1179656 | tf_op jit(solution)/shard_map/ppermute | solution.py:624
  47.0 26.5 %collective-permute-start.5 = (bf16[256,2048]{1,0:T(8,128)(2,1)}, bf16[256,2048]{1,0:T(8,128)(2,1)}, u32[]{:S(2)}, u32[]{:S(2)}) collective-permute-start(bf16[256,2048]{1,0:T(8,128)(2,1)} %get-tuple-element.47.rest_0_), channel_id=1, source_target_pairs={{0,64},{16,80},{32,96},{48,112},{64,0},{80,16},{96,32},{112,48},{1... | collective-permute-start | bytes 3145736 | tf_op jit(solution)/shard_map/ppermute | solution.py:636
  57.5 12.1 %collective-permute-start.11 = (bf16[2,128,768]{2,1,0:T(8,128)(2,1)}, bf16[2,128,768]{2,1,0:T(8,128)(2,1)S(1)}, u32[]{:S(2)}, u32[]{:S(2)}) collective-permute-start(bf16[2,128,768]{2,1,0:T(8,128)(2,1)} %get-tuple-element.52.fence.refs_3_), channel_id=1, source_target_pairs={{0,2},{1,3},{2,4},{3,5},{4,6},{5,7},{6,0},{7,1},{8,10},{9,11},{10,... | collective-permute-start | bytes 1179656 | tf_op jit(solution)/shard_map/ppermute | solution.py:628
  59.0 11.6 %collective-permute-start.12 = (bf16[2,128,768]{2,1,0:T(8,128)(2,1)}, bf16[2,128,768]{2,1,0:T(8,128)(2,1)S(1)}, u32[]{:S(2)}, u32[]{:S(2)}) collective-permute-start(bf16[2,128,768]{2,1,0:T(8,128)(2,1)} %get-tuple-element.52.fence.refs_3_), channel_id=1, source_target_pairs={{0,6},{1,7},{2,0},{3,1},{4,2},{5,3},{6,4},{7,5},{8,14},{9,15},{10,... | collective-permute-start | bytes 1179656 | tf_op jit(solution)/shard_map/ppermute | solution.py:628
  59.0 14.6 %collective-permute-start.14 = (bf16[2,128,768]{2,1,0:T(8,128)(2,1)}, bf16[2,128,768]{2,1,0:T(8,128)(2,1)S(1)}, u32[]{:S(2)}, u32[]{:S(2)}) collective-permute-start(bf16[2,128,768]{2,1,0:T(8,128)(2,1)} %get-tuple-element.57.refs_0_), channel_id=1, source_target_pairs={{0,8},{1,9},{2,10},{3,11},{4,12},{5,13},{6,14},{7,15},{8,0},{9,1},... | collective-permute-start | bytes 1179656 | tf_op jit(solution)/shard_map/ppermute | solution.py:632
  63.7 18.1 %collective-permute-start.16 = (bf16[4,2,128,768]{3,2,1,0:T(8,128)(2,1)S(1)}, bf16[4,2,128,768]{3,2,1,0:T(8,128)(2,1)}, u32[]{:S(2)}, u32[]{:S(2)}) collective-permute-start(bf16[4,2,128,768]{3,2,1,0:T(8,128)(2,1)S(1)} %stack.119.own), channel_id=1, source_target_pairs={{0,1},{1,0},{2,3},{3,2},{4,5},{5,4},{6,7},{7,6},{8,9},{9,8},{10,11... | collective-permute-start | bytes 4718600 | tf_op jit(solution)/shard_map/ppermute | solution.py:624
  75.7 13.3 %collective-permute-start.15 = (bf16[4,2,128,768]{3,2,1,0:T(8,128)(2,1)S(1)}, bf16[4,2,128,768]{3,2,1,0:T(8,128)(2,1)}, u32[]{:S(2)}, u32[]{:S(2)}) collective-permute-start(bf16[4,2,128,768]{3,2,1,0:T(8,128)(2,1)S(1)} %stack.118.own), channel_id=1, source_target_pairs={{0,1},{1,0},{2,3},{3,2},{4,5},{5,4},{6,7},{7,6},{8,9},{9,8},{10,11... | collective-permute-start | bytes 4718600 | tf_op jit(solution)/shard_map/ppermute | solution.py:624
  76.6 4.8 %collective-permute-start.17 = (bf16[2,48,128]{2,1,0:T(8,128)(2,1)S(1)}, bf16[2,48,128]{2,1,0:T(8,128)(2,1)S(1)}, u32[]{:S(2)}, u32[]{:S(2)}) collective-permute-start(bf16[2,48,128]{2,1,0:T(8,128)(2,1)S(1)} %copy-done.35), channel_id=1, source_target_pairs={{0,1},{1,2},{2,3},{3,4},{4,5},{5,6},{6,7},{7,8},{8,9},{9,10},{10,1... | collective-permute-start | bytes 73736 | tf_op jit(solution)/shard_map/ppermute | solution.py:620
  78.7 27.9 %collective-permute-start.19 = (bf16[256,2048]{1,0:T(8,128)(2,1)}, bf16[256,2048]{1,0:T(8,128)(2,1)}, u32[]{:S(2)}, u32[]{:S(2)}) collective-permute-start(bf16[256,2048]{1,0:T(8,128)(2,1)} %get-tuple-element.64.rest_4_), channel_id=1, source_target_pairs={{0,32},{16,48},{32,64},{48,80},{64,96},{80,112},{96,0},{112,16},{1... | collective-permute-start | bytes 3145736 | tf_op jit(solution)/shard_map/ppermute | solution.py:636
  79.7 27.0 %collective-permute-start.20 = (bf16[256,2048]{1,0:T(8,128)(2,1)}, bf16[256,2048]{1,0:T(8,128)(2,1)}, u32[]{:S(2)}, u32[]{:S(2)}) collective-permute-start(bf16[256,2048]{1,0:T(8,128)(2,1)} %get-tuple-element.64.rest_4_), channel_id=1, source_target_pairs={{0,96},{16,112},{32,0},{48,16},{64,32},{80,48},{96,64},{112,80},{1... | collective-permute-start | bytes 3145736 | tf_op jit(solution)/shard_map/ppermute | solution.py:636
  81.4 26.4 %collective-permute-start.21 = (bf16[256,2048]{1,0:T(8,128)(2,1)}, bf16[256,2048]{1,0:T(8,128)(2,1)}, u32[]{:S(2)}, u32[]{:S(2)}) collective-permute-start(bf16[256,2048]{1,0:T(8,128)(2,1)} %get-tuple-element.65.rest_3_), channel_id=1, source_target_pairs={{0,16},{16,0},{32,48},{48,32},{64,80},{80,64},{96,112},{112,96},{1... | collective-permute-start | bytes 3145736 | tf_op jit(solution)/shard_map/ppermute | solution.py:640
  81.8 7.2 %collective-permute-start.18 = (bf16[2,48,128]{2,1,0:T(8,128)(2,1)S(1)}, bf16[2,48,128]{2,1,0:T(8,128)(2,1)S(1)}, u32[]{:S(2)}, u32[]{:S(2)}) collective-permute-start(bf16[2,48,128]{2,1,0:T(8,128)(2,1)S(1)} %copy-done.34), channel_id=1, source_target_pairs={{0,15},{1,0},{2,1},{3,2},{4,3},{5,4},{6,5},{7,6},{8,7},{9,8},{10,9... | collective-permute-start | bytes 73736 | tf_op jit(solution)/shard_map/ppermute | solution.py:620
  124.8 3.9 %collective-permute-start.23 = (bf16[2,16,128]{2,1,0:T(8,128)(2,1)S(1)}, bf16[2,16,128]{2,1,0:T(8,128)(2,1)S(1)}, u32[]{:S(2)}, u32[]{:S(2)}) collective-permute-start(bf16[2,16,128]{2,1,0:T(8,128)(2,1)S(1)} %get-tuple-element.74), channel_id=1, source_target_pairs={{0,1},{1,2},{2,3},{3,4},{4,5},{5,6},{6,7},{7,8},{8,9},{9,10},{10,1... | collective-permute-start | bytes 24584 | tf_op jit(solution)/shard_map/ppermute | solution.py:620
  127.6 5.2 %collective-permute-start.24 = (bf16[2,16,128]{2,1,0:T(8,128)(2,1)S(1)}, bf16[2,16,128]{2,1,0:T(8,128)(2,1)S(1)}, u32[]{:S(2)}, u32[]{:S(2)}) collective-permute-start(bf16[2,16,128]{2,1,0:T(8,128)(2,1)S(1)} %get-tuple-element.75), channel_id=1, source_target_pairs={{0,15},{1,0},{2,1},{3,2},{4,3},{5,4},{6,5},{7,6},{8,7},{9,8},{10,9... | collective-permute-start | bytes 24584 | tf_op jit(solution)/shard_map/ppermute | solution.py:620
  (39 other events, 236.2 us)

commit v7 on v6

--- a/solution.py
+++ b/solution.py
@@ -267,7 +267,7 @@
 
 
 def decode_kernel(
-    place, enc, enc_low, enc_high, spread, spread_low, spread_high, bias, index, low, high,
+    place, enc, spread, edge_low, edge_high, bias, index, low, high,
     project, mix,
     update,
     rows, bias32, packed, mixed, decoded, tokens, moved,
@@ -284,16 +284,16 @@
     ).astype(BF16)
     end = MARGIN + ATOMS
     for seed in range(SEEDS):
-        tokens[0:EDGE] = spread_low[seed]
+        tokens[0:EDGE] = edge_low[seed, 0:EDGE]
         tokens[EDGE : EDGE + TOKS] = spread[seed]
-        tokens[EDGE + TOKS :] = spread_high[seed]
+        tokens[EDGE + TOKS :] = edge_high[seed, 0:EDGE]
         moved[...] = lax.dot_general(
             chosen, tokens[...], (((0,), (0,)), ((), ())), preferred_element_type=F32
         )
-        decoded[0:MARGIN] = enc_low[seed].astype(F32) + moved[ATOMS + CA - MARGIN : ATOMS + CA]
+        decoded[0:MARGIN] = edge_low[seed, EDGE:].astype(F32) + moved[ATOMS + CA - MARGIN : ATOMS + CA]
         decoded[MARGIN:end] = enc[seed].astype(F32) + moved[0:ATOMS]
         decoded[end : end + MARGIN] = (
-            enc_high[seed].astype(F32) + moved[ATOMS + CA : ATOMS + CA + MARGIN]
+            edge_high[seed, EDGE:].astype(F32) + moved[ATOMS + CA : ATOMS + CA + MARGIN]
         )
         decoded[end + MARGIN :] = jnp.zeros((EXT - end - MARGIN, CA), F32)
         values = decoded[...].astype(BF16).astype(F32)
@@ -310,7 +310,7 @@
     return pl.pallas_call(
         decode_kernel,
         out_shape=jax.ShapeDtypeStruct((SEEDS * ATOMS, CA), BF16),
-        in_specs=[pl.BlockSpec(memory_space=pltpu.SMEM)] + vmem(12),
+        in_specs=[pl.BlockSpec(memory_space=pltpu.SMEM)] + vmem(10),
         out_specs=vmem(1)[0],
         scratch_shapes=[
             pltpu.VMEM((2 * EXT, CA), F32),
@@ -549,7 +549,7 @@
 
 
 def finish_kernel(
-    residual, own, received, mix, wide_hbm, narrow_hbm, spread_weight,
+    residual, own, received, mix, wide_hbm, narrow_hbm, spread_weight, enc_first, enc_last,
     state, spread, first, last,
     wide, narrow, mix_tile, total, hidden, sems,
 ):
@@ -587,20 +587,22 @@
     state[...] = rounded.reshape(SEEDS, TOKS, CT)
     carried = dot(rounded, spread_weight[...]).astype(BF16).reshape(SEEDS, TOKS, CA)
     spread[...] = carried
-    first[...] = carried[:, :EDGE]
-    last[...] = carried[:, TOKS - EDGE :]
-
-
-def finish(residual, own, received, mix, wide, narrow, spread_weight):
+    first[:, :EDGE] = carried[:, :EDGE]
+    first[:, EDGE:] = enc_first[...]
+    last[:, :EDGE] = carried[:, TOKS - EDGE :]
+    last[:, EDGE:] = enc_last[...]
+
+
+def finish(residual, own, received, mix, wide, narrow, spread_weight, enc_first, enc_last):
     return pl.pallas_call(
         finish_kernel,
         out_shape=(
             jax.ShapeDtypeStruct((SEEDS, TOKS, CT), BF16),
             jax.ShapeDtypeStruct((SEEDS, TOKS, CA), BF16),
-            jax.ShapeDtypeStruct((SEEDS, EDGE, CA), BF16),
-            jax.ShapeDtypeStruct((SEEDS, EDGE, CA), BF16),
+            jax.ShapeDtypeStruct((SEEDS, EDGE + MARGIN, CA), BF16),
+            jax.ShapeDtypeStruct((SEEDS, EDGE + MARGIN, CA), BF16),
         ),
-        in_specs=vmem(4) + anywhere(2) + vmem(1),
+        in_specs=vmem(4) + anywhere(2) + vmem(3),
         out_specs=tuple(vmem(4)),
         scratch_shapes=[
             pltpu.VMEM((CT, 2 * TRANS), BF16),
@@ -613,7 +615,7 @@
         compiler_params=params(40),
         cost_estimate=SMALL,
         name="finish",
-    )(residual, own, received, mix, wide, narrow, spread_weight)
+    )(residual, own, received, mix, wide, narrow, spread_weight, enc_first, enc_last)
 
 
 def along_tok(values, by):
@@ -667,9 +669,7 @@
     )
     x_below = along_x(normed, 1)
     x_above = along_x(normed, -1)
-    below, above, first, last, again, mine = hold(
-        below, above, first, last, again, mine
-    )
+    below, above, again, mine = hold(below, above, again, mine)
     far = along_y(mine, 2)
     z_own = across_floor(again)
     mate = across_core(again)
@@ -684,8 +684,6 @@
     near = stack(again, x_below, x_above, z_own)
     near_mate = across_core(near)
     query, gate = queries(place, again, mate, weights, z_own)
-    enc_low = along_tok(last, 1)
-    enc_high = along_tok(first, -1)
     far, other, z_below, z_above, query = hold(far, other, z_below, z_above, query)
     other_below = along_y(other, 1)
     other_above = along_y(other, -1)
@@ -708,8 +706,7 @@
         place, shards((0, 0), (3, 0), (1, 0), (0, 1)), near, near_mate, weights
     )
     key_value = keys(
-        place, shards((2, 0), (3, 1), (1, 1), (2, 1)), rest, rest_mate, weights, key_value,
-        (enc_low, enc_high),
+        place, shards((2, 0), (3, 1), (1, 1), (2, 1)), rest, rest_mate, weights, key_value
     )
 
     level, side = seed // 2, seed % 2
@@ -726,13 +723,12 @@
         (other_below, other_above, other_far),
     )
 
-    state, spread, spread_first, spread_last = finish(
+    state, spread, edge_first, edge_last = finish(
         residual, own, across_core(sent), token_mix.reshape(GROUPS, PAIR, CT), swiglu_in,
-        swiglu_out, spread_weight,
+        swiglu_out, spread_weight, first, last,
     )
     update = decode(
-        place, encoded, enc_low, enc_high, spread, along_tok(spread_last, 1),
-        along_tok(spread_first, -1), bias_dec, index, low, high, dec_project, dec_mix,
+        place, encoded, spread, along_tok(edge_last, 1), along_tok(edge_first, -1), bias_dec, index, low, high, dec_project, dec_mix,
     )
     return state.transpose(1, 0, 2), update.reshape(ATOMS, SEEDS, CA)
 

time: 141 us -> 138 us (0.979)
  waiting for transfers between devices: 28.6 us -> 25 us
    ppermute x5, waiting for transfers between devices: 6.48 us -> 3.62 us  [along_y(): lax.ppermute(values, 'seed', [(i, (i + 2 * by) % 8) for i in range(8)])]
    ppermute x6 -> x4, starting transfers between devices: 6.43 us -> 3.62 us  [along_tok(): return lax.ppermute(values, 'tok', [(i, (i + by) % 16) for i in range(16)])]
    ppermute x5, starting transfers between devices: 4.11 us -> 6.41 us  [across_core(): return lax.ppermute(values, 'tok', [(i, i ^ 1) for i in range(16)])]
    ppermute x6 -> x4, waiting for transfers between devices: 9.65 us -> 9.91 us  [along_tok(): return lax.ppermute(values, 'tok', [(i, (i + by) % 16) for i in range(16)])]
  transfers between devices with their start and end apart: 25 -> 23, of which waited for: 10 -> 9; matrix products, arithmetic and copies ran while one was open for 1% -> 1% of each run, Pallas kernels for 32% -> 32%
where the time goes in v7:
time: 138 us; the launch traced here: 137 us
  Pallas kernels  70.8 us (51%)
  starting transfers between devices  28 us (20%)
  waiting for transfers between devices  25 us (18%)
  local copies, waits for them, and re-layouts  11.4 us (8%)
    pallas_call x2, Pallas kernels, attend(): pl.pallas_call(functools.partial(attend_kernel, count, len(before)), grid...  20.1 us
    pallas_call x2, Pallas kernels, keys(): pl.pallas_call(keys_kernel, grid=(1,), out_shape=jax.ShapeDtypeStruct((GR...  13.7 us
    unnamed x77, local copies, waits for them, and re-layouts  11.2 us
    ppermute x4, waiting for transfers between devices, along_tok(): return lax.ppermute(values, 'tok', [(i, (i + by) % 16) for i in range(16)])  9.91 us
    pallas_call x1, Pallas kernels, encode(): pl.pallas_call(encode_kernel, out_shape=(jax.ShapeDtypeStruct((SEEDS, ATO...  9.24 us
    ppermute x2, waiting for transfers between devices, along_z(): return lax.ppermute(values, 'seed', [(i, i ^ 1) for i in range(8)])  7.74 us
    ppermute x5, starting transfers between devices, along_y(): lax.ppermute(values, 'seed', [(i, (i + 2 * by) % 8) for i in range(8)])  7.38 us
    pallas_call x1, Pallas kernels, decode(): pl.pallas_call(decode_kernel, out_shape=jax.ShapeDtypeStruct((SEEDS * ATO...  7.13 us
  transfers between devices with their start and end apart: 23, of which 9 were waited for; matrix products, arithmetic and copies ran while one was open for 1% of the time, Pallas kernels for 32%

profile of v7, /device:TPU:7, one launch (start us, length us, event | category | flops | bytes accessed | tf_op | source)
XLA Modules:
  0.0 137.0 jit_solution(4970596832661420248)
XLA Ops:
  1.2 3.0 %pack.1 = (bf16[304,128]{1,0:T(8,128)(2,1)}, bf16[112,128]{1,0:T(8,128)(2,1)}, bf16[128,2048]{1,0:T(8,128)(2,1)}, bf16[256,2048]{1,0:T(8,128)(2,1)}) custom-call(s32[2]{0:T(128)} %pad_add_fusion.place, bf16[2048,128]{1,0:T(8,128)(2,1)} %bitcast.43, bf16[4096,128]{1,0:T(8,128)(2,1)} %bitcast.41, s32[8,128]{1,0:T(8,128)} %bitcast.38, ...), custom_call_target="tpu_custom_call" | custom-call | flops 1000000 | bytes 10000 | tf_op jit(solution)/shard_map/pack/pallas_call | solution.py:141
  6.5 5.6 %collective-permute-done.1.high = bf16[112,128]{1,0:T(8,128)(2,1)S(1)} collective-permute-done((bf16[112,128]{1,0:T(8,128)(2,1)}, bf16[112,128]{1,0:T(8,128)(2,1)S(1)}, u32[]{:S(2)}, u32[]{:S(2)}) %collective-permute-start.1) | collective-permute-done | bytes 28704 | tf_op jit(solution)/shard_map/ppermute | solution.py:622
  12.9 1.8 %join.1.fence.refs_3_ = bf16[256,2048]{1,0:T(8,128)(2,1)} custom-call(bf16[256,2048]{1,0:T(8,128)(2,1)} %get-tuple-element.39.joined, bf16[128,2048]{1,0:T(8,128)(2,1)} %copy-done.35, bf16[304,128]{1,0:T(8,128)(2,1)} %copy-done.21, bf16[112,128]{1,0:T(8,128)(2,1)} %copy-done.24), custom_call_target="tpu_custom_call", output_to_operand_aliasing={{}: (0, {})} | custom-call | flops 1000000 | bytes 10000 | tf_op jit(solution)/shard_map/join/pallas_call | solution.py:172
  14.8 3.4 %collective-permute-start.10 = (bf16[256,2048]{1,0:T(8,128)(2,1)}, bf16[256,2048]{1,0:T(8,128)(2,1)}, u32[]{:S(2)}, u32[]{:S(2)}) collective-permute-start(bf16[256,2048]{1,0:T(8,128)(2,1)} %join.1.fence.refs_3_), channel_id=1, source_target_pairs={{0,16},{16,0},{32,48},{48,32},{64,80},{80,64},{96,112},{112,96},{1... | collective-permute-start | bytes 3145736 | tf_op jit(solution)/shard_map/ppermute | solution.py:642
  20.9 9.2 %encode.1 = (bf16[2,1024,128]{2,1,0:T(8,128)(2,1)}, bf16[2,48,128]{2,1,0:T(8,128)(2,1)}, bf16[2,48,128]{2,1,0:T(8,128)(2,1)}, f32[2,128,768]{2,1,0:T(8,128)}, bf...) custom-call(s32[2]{0:T(128)} %pad_add_fusion.place, bf16[2048,128]{1,0:T(8,128)(2,1)} %bitcast.44, ...), custom_call_target="tpu_custom_call" | custom-call | flops 1000000 | bytes 10000 | tf_op jit(solution)/shard_map/encode/pallas_call | solution.py:244
  31.6 7.7 %collective-permute-done.10.refs_5_ = bf16[256,2048]{1,0:T(8,128)(2,1)} collective-permute-done((bf16[256,2048]{1,0:T(8,128)(2,1)}, bf16[256,2048]{1,0:T(8,128)(2,1)}, u32[]{:S(2)}, u32[]{:S(2)}) %collective-permute-start.10) | collective-permute-done | bytes 1048608 | tf_op jit(solution)/shard_map/ppermute | solution.py:642
  39.4 3.4 %collective-permute-done.3.refs_0_ = bf16[256,2048]{1,0:T(8,128)(2,1)S(1)} collective-permute-done((bf16[256,2048]{1,0:T(8,128)(2,1)}, bf16[256,2048]{1,0:T(8,128)(2,1)S(1)}, u32[]{:S(2)}, u32[]{:S(2)}) %collective-permute-start.3) | collective-permute-done | bytes 1048608 | tf_op jit(solution)/shard_map/ppermute | solution.py:638
  45.9 2.0 %collective-permute-start.5 = (bf16[256,2048]{1,0:T(8,128)(2,1)}, bf16[256,2048]{1,0:T(8,128)(2,1)}, u32[]{:S(2)}, u32[]{:S(2)}) collective-permute-start(bf16[256,2048]{1,0:T(8,128)(2,1)} %get-tuple-element.43.rest_0_), channel_id=1, source_target_pairs={{0,64},{16,80},{32,96},{48,112},{64,0},{80,16},{96,32},{112,48},{1... | collective-permute-start | bytes 3145736 | tf_op jit(solution)/shard_map/ppermute | solution.py:638
  47.8 6.6 %spaced.1.refs_4_ = bf16[2,4,768,256]{3,2,1,0:T(8,128)(2,1)} custom-call(s32[2]{0:T(128)} %pad_add_fusion.place, bf16[768,3072]{1,0:T(8,128)(2,1)} %second.1, bf16[768,3072]{1,0:T(8,128)(2,1)} %second.1, bf16[256,2048]{1,0:T(8,128)(2,1)} %get-tuple-element.46.fence.rest_1_), custom_call_target="tpu_custom_call" | custom-call | flops 70000001024 | bytes 10000 | tf_op jit(solution)/shard_map/spaced/pallas_call | solution.py:350
  54.4 1.7 %collective-permute-start.13 = (bf16[2,128,768]{2,1,0:T(8,128)(2,1)S(1)}, bf16[2,128,768]{2,1,0:T(8,128)(2,1)S(1)}, u32[]{:S(2)}, u32[]{:S(2)}) collective-permute-start(bf16[2,128,768]{2,1,0:T(8,128)(2,1)S(1)} %copy-done.6), channel_id=1, source_target_pairs={{0,1},{1,0},{2,3},{3,2},{4,5},{5,4},{6,7},{7,6},{8,9},{9,8},{10,11... | collective-permute-start | bytes 1179656 | tf_op jit(solution)/shard_map/ppermute | solution.py:626
  57.7 1.5 %collective-permute-start.11 = (bf16[2,128,768]{2,1,0:T(8,128)(2,1)}, bf16[2,128,768]{2,1,0:T(8,128)(2,1)S(1)}, u32[]{:S(2)}, u32[]{:S(2)}) collective-permute-start(bf16[2,128,768]{2,1,0:T(8,128)(2,1)} %get-tuple-element.48.fence.refs_3_), channel_id=1, source_target_pairs={{0,2},{1,3},{2,4},{3,5},{4,6},{5,7},{6,0},{7,1},{8,10},{9,11},{10,... | collective-permute-start | bytes 1179656 | tf_op jit(solution)/shard_map/ppermute | solution.py:630
  64.5 3.8 %queries.1 = (bf16[8,2,256,128]{3,2,1,0:T(8,128)(2,1)S(1)}, f32[8,2,256,128]{3,2,1,0:T(8,128)}) custom-call(s32[2]{0:T(128)S(1)} %copy-done.32, bf16[2,128,768]{2,1,0:T(8,128)(2,1)S(1)} %copy-done.6, bf16[2,128,768]{2,1,0:T(8,128)(2,1)S(1)} %collective-permute-done.13.other, bf16[2,4,768,256]{3,2,1,0:T(8,128)(2,1)} %get-tuple-element.49.weight, ...), custom_call_target="tpu_custom_call" | custom-call | flops 1000000 | bytes 10000 | tf_op jit(solution)/shard_map/queries/pallas_call | solution.py:387
  69.4 1.8 %collective-permute-done.12.refs_3_ = bf16[2,128,768]{2,1,0:T(8,128)(2,1)S(1)} collective-permute-done((bf16[2,128,768]{2,1,0:T(8,128)(2,1)}, bf16[2,128,768]{2,1,0:T(8,128)(2,1)S(1)}, u32[]{:S(2)}, u32[]{:S(2)}) %collective-permute-start.12) | collective-permute-done | bytes 393248 | tf_op jit(solution)/shard_map/ppermute | solution.py:630
  76.1 2.0 %collective-permute-start.18 = (bf16[256,2048]{1,0:T(8,128)(2,1)}, bf16[256,2048]{1,0:T(8,128)(2,1)}, u32[]{:S(2)}, u32[]{:S(2)}) collective-permute-start(bf16[256,2048]{1,0:T(8,128)(2,1)} %get-tuple-element.58.rest_4_), channel_id=1, source_target_pairs={{0,96},{16,112},{32,0},{48,16},{64,32},{80,48},{96,64},{112,80},{1... | collective-permute-start | bytes 3145736 | tf_op jit(solution)/shard_map/ppermute | solution.py:638
  79.7 6.7 %keys.2.rest_0_ = bf16[8,2,2048,128]{3,2,1,0:T(8,128)(2,1)} custom-call(s32[10]{0:T(128)S(1)} %concatenate.9.place, bf16[4,2,128,768]{3,2,1,0:T(8,128)(2,1)S(1)} %stack.119.own, bf16[4,2,128,768]{3,2,1,0:T(8,128)(2,1)} %collective-permute-done.16.received, bf16[2,4,768,256]{3,2,1,0:T(8,128)(2,1)} %get-tuple-element.49.weight), custom_call_target="tpu_custom_call" | custom-call | flops 1000000 | bytes 10000 | tf_op jit(solution)/shard_map/keys/pallas_call | solution.py:453
  86.5 6.9 %keys.3.key_value = bf16[8,2,2048,128]{3,2,1,0:T(8,128)(2,1)} custom-call(s32[10]{0:T(128)S(1)} %concatenate.8.place, bf16[4,2,128,768]{3,2,1,0:T(8,128)(2,1)S(1)} %stack.118.own, bf16[4,2,128,768]{3,2,1,0:T(8,128)(2,1)} %collective-permute-done.15.received, bf16[2,4,768,256]{3,2,1,0:T(8,128)(2,1)} %get-tuple-element.49.weight, ...), custom_call_target="tpu_custom_call", output_to_operand_aliasing={{}: (4, {})} | custom-call | flops 1000000 | bytes 10000 | tf_op jit(solution)/shard_map/keys/pallas_call | solution.py:453
  93.5 10.6 %attend.2 = (bf16[8,2,128,128]{3,2,1,0:T(8,128)(2,1)S(1)}, bf16[8,2,128,128]{3,2,1,0:T(8,128)(2,1)S(1)}) custom-call(s32[5]{0:T(128)S(1)} %stack.117.group_ids, bf16[8,2,256,128]{3,2,1,0:T(8,128)(2,1)S(1)} %copy-done.2, f32[8,2,256,128]{3,2,1,0:T(8,128)} %get-tuple-element.52.gate, bf16[8,2,2048,128]{3,2,1,0:T(8,128)(2,1)} %keys.3.key_value, ...), custom_call_target="tpu_custom_call" | custom-call | flops 1000000 | bytes 10000 | tf_op jit(solution)/shard_map/attend/pallas_call | solution.py:540
  104.2 9.5 %attend.3 = (bf16[8,2,128,128]{3,2,1,0:T(8,128)(2,1)S(1)}, bf16[8,2,128,128]{3,2,1,0:T(8,128)(2,1)S(1)}) custom-call(s32[3]{0:T(128)S(1)} %pad_add_fusion.1.group_ids, bf16[8,2,256,128]{3,2,1,0:T(8,128)(2,1)S(1)} %copy-done.2, f32[8,2,256,128]{3,2,1,0:T(8,128)} %get-tuple-element.52.gate, ...), custom_call_target="tpu_custom_call", output_to_operand_aliasing={{0}: (7, {}), {1}: (8, {})} | custom-call | flops 1000000 | bytes 10000 | tf_op jit(solution)/shard_map/attend/pallas_call | solution.py:540
  113.7 1.6 %collective-permute-start.20 = (bf16[8,2,128,128]{3,2,1,0:T(8,128)(2,1)S(1)}, bf16[8,2,128,128]{3,2,1,0:T(8,128)(2,1)S(1)}, u32[]{:S(2)}, u32[]{:S(2)}) collective-permute-start(bf16[8,2,128,128]{3,2,1,0:T(8,128)(2,1)S(1)} %get-tuple-element.64), channel_id=1, source_target_pairs={{0,1},{1,0},{2,3},{3,2},{4,5},{5,4},{6,7},{7,6},{8,9},{9,8},{10,11... | collective-permute-start | bytes 1572872 | tf_op jit(solution)/shard_map/ppermute | solution.py:626
  115.3 1.5 %collective-permute-done.20.received = bf16[8,2,128,128]{3,2,1,0:T(8,128)(2,1)S(1)} collective-permute-done((bf16[8,2,128,128]{3,2,1,0:T(8,128)(2,1)S(1)}, bf16[8,2,128,128]{3,2,1,0:T(8,128)(2,1)S(1)}, u32[]{:S(2)}, u32[]{:S(2)}) %collective-permute-start.20) | collective-permute-done | bytes 524320 | tf_op jit(solution)/shard_map/ppermute | solution.py:626
  117.0 5.2 %finish.1 = (bf16[2,128,768]{2,1,0:T(8,128)(2,1)S(1)}, bf16[2,128,128]{2,1,0:T(8,128)(2,1)S(1)}, bf16[2,64,128]{2,1,0:T(8,128)(2,1)S(1)}, bf16[2,64,128]{2,1,0:T(8,128)(2,1)S(1)}) custom-call(f32[2,128,768]{2,1,0:T(8,128)S(1)} %copy-done.20, bf16[8,2,128,128]{3,2,1,0:T(8,128)(2,1)S(1)} %get-tuple-element.63.own, ...), custom_call_target="tpu_custom_call" | custom-call | flops 1000000 | bytes 10000 | tf_op jit(solution)/shard_map/finish/pallas_call | solution.py:597
  122.2 2.1 %collective-permute-start.21 = (bf16[2,64,128]{2,1,0:T(8,128)(2,1)S(1)}, bf16[2,64,128]{2,1,0:T(8,128)(2,1)S(1)}, u32[]{:S(2)}, u32[]{:S(2)}) collective-permute-start(bf16[2,64,128]{2,1,0:T(8,128)(2,1)S(1)} %get-tuple-element.70), channel_id=1, source_target_pairs={{0,1},{1,2},{2,3},{3,4},{4,5},{5,6},{6,7},{7,8},{8,9},{9,10},{10,1... | collective-permute-start | bytes 98312 | tf_op jit(solution)/shard_map/ppermute | solution.py:622
  125.5 4.3 %collective-permute-done.22.edge_high = bf16[2,64,128]{2,1,0:T(8,128)(2,1)S(1)} collective-permute-done((bf16[2,64,128]{2,1,0:T(8,128)(2,1)S(1)}, bf16[2,64,128]{2,1,0:T(8,128)(2,1)S(1)}, u32[]{:S(2)}, u32[]{:S(2)}) %collective-permute-start.22) | collective-permute-done | bytes 32800 | tf_op jit(solution)/shard_map/ppermute | solution.py:622
  129.8 7.1 %decode.1 = bf16[2048,128]{1,0:T(8,128)(2,1)} custom-call(s32[2]{0:T(128)S(1)} %copy-done.32, bf16[2,1024,128]{2,1,0:T(8,128)(2,1)S(1)} %copy-done.23, bf16[2,128,128]{2,1,0:T(8,128)(2,1)S(1)} %get-tuple-element.69.spread, bf16[2,64,128]{2,1,0:T(8,128)(2,1)S(1)} %collective-permute-done.21.edge_low, ...), custom_call_target="tpu_custom_call" | custom-call | flops 1000000 | bytes 10000 | tf_op jit(solution)/shard_map/decode/pallas_call | solution.py:310
  (121 shorter events, 26.7 us)
Async XLA Ops:
  4.2 7.9 %collective-permute-start.2 = (bf16[128,2048]{1,0:T(8,128)(2,1)}, bf16[128,2048]{1,0:T(8,128)(2,1)S(1)}, u32[]{:S(2)}, u32[]{:S(2)}) collective-permute-start(bf16[128,2048]{1,0:T(8,128)(2,1)} %get-tuple-element.40), channel_id=1, source_target_pairs={{0,1},{1,0},{2,3},{3,2},{4,5},{5,4},{6,7},{7,6},{8,9},{9,8},{10,11... | collective-permute-start | bytes 1572872 | tf_op jit(solution)/shard_map/ppermute | solution.py:626
  5.0 7.1 %collective-permute-start = (bf16[304,128]{1,0:T(8,128)(2,1)}, bf16[304,128]{1,0:T(8,128)(2,1)S(1)}, u32[]{:S(2)}, u32[]{:S(2)}) collective-permute-start(bf16[304,128]{1,0:T(8,128)(2,1)} %get-tuple-element.37), channel_id=1, source_target_pairs={{0,1},{1,2},{2,3},{3,4},{4,5},{5,6},{6,7},{7,8},{8,9},{9,10},{10,1... | collective-permute-start | bytes 233480 | tf_op jit(solution)/shard_map/ppermute | solution.py:622
  6.5 5.6 %collective-permute-start.1 = (bf16[112,128]{1,0:T(8,128)(2,1)}, bf16[112,128]{1,0:T(8,128)(2,1)S(1)}, u32[]{:S(2)}, u32[]{:S(2)}) collective-permute-start(bf16[112,128]{1,0:T(8,128)(2,1)} %get-tuple-element.38), channel_id=1, source_target_pairs={{0,15},{1,0},{2,1},{3,2},{4,3},{5,4},{6,5},{7,6},{8,7},{9,8},{10,9... | collective-permute-start | bytes 86024 | tf_op jit(solution)/shard_map/ppermute | solution.py:622
  14.8 24.6 %collective-permute-start.10 = (bf16[256,2048]{1,0:T(8,128)(2,1)}, bf16[256,2048]{1,0:T(8,128)(2,1)}, u32[]{:S(2)}, u32[]{:S(2)}) collective-permute-start(bf16[256,2048]{1,0:T(8,128)(2,1)} %join.1.fence.refs_3_), channel_id=1, source_target_pairs={{0,16},{16,0},{32,48},{48,32},{64,80},{80,64},{96,112},{112,96},{1... | collective-permute-start | bytes 3145736 | tf_op jit(solution)/shard_map/ppermute | solution.py:642
  18.2 24.6 %collective-permute-start.3 = (bf16[256,2048]{1,0:T(8,128)(2,1)}, bf16[256,2048]{1,0:T(8,128)(2,1)S(1)}, u32[]{:S(2)}, u32[]{:S(2)}) collective-permute-start(bf16[256,2048]{1,0:T(8,128)(2,1)} %join.1.fence.refs_3_), channel_id=1, source_target_pairs={{0,32},{16,48},{32,64},{48,80},{64,96},{80,112},{96,0},{112,16},{1... | collective-permute-start | bytes 3145736 | tf_op jit(solution)/shard_map/ppermute | solution.py:638
  19.5 23.4 %collective-permute-start.4 = (bf16[256,2048]{1,0:T(8,128)(2,1)}, bf16[256,2048]{1,0:T(8,128)(2,1)S(1)}, u32[]{:S(2)}, u32[]{:S(2)}) collective-permute-start(bf16[256,2048]{1,0:T(8,128)(2,1)} %join.1.fence.refs_3_), channel_id=1, source_target_pairs={{0,96},{16,112},{32,0},{48,16},{64,32},{80,48},{96,64},{112,80},{1... | collective-permute-start | bytes 3145736 | tf_op jit(solution)/shard_map/ppermute | solution.py:638
  30.2 24.3 %collective-permute-start.7 = (bf16[2,128,768]{2,1,0:T(8,128)(2,1)}, bf16[2,128,768]{2,1,0:T(8,128)(2,1)S(1)}, u32[]{:S(2)}, u32[]{:S(2)}) collective-permute-start(bf16[2,128,768]{2,1,0:T(8,128)(2,1)} %get-tuple-element.45), channel_id=1, source_target_pairs={{0,2},{1,3},{2,4},{3,5},{4,6},{5,7},{6,0},{7,1},{8,10},{9,11},{10,... | collective-permute-start | bytes 1179656 | tf_op jit(solution)/shard_map/ppermute | solution.py:630
  30.2 26.0 %collective-permute-start.8 = (bf16[2,128,768]{2,1,0:T(8,128)(2,1)}, bf16[2,128,768]{2,1,0:T(8,128)(2,1)S(1)}, u32[]{:S(2)}, u32[]{:S(2)}) collective-permute-start(bf16[2,128,768]{2,1,0:T(8,128)(2,1)} %get-tuple-element.45), channel_id=1, source_target_pairs={{0,6},{1,7},{2,0},{3,1},{4,2},{5,3},{6,4},{7,5},{8,14},{9,15},{10,... | collective-permute-start | bytes 1179656 | tf_op jit(solution)/shard_map/ppermute | solution.py:630
  44.1 12.0 %collective-permute-start.6 = (bf16[2,128,768]{2,1,0:T(8,128)(2,1)}, bf16[2,128,768]{2,1,0:T(8,128)(2,1)S(1)}, u32[]{:S(2)}, u32[]{:S(2)}) collective-permute-start(bf16[2,128,768]{2,1,0:T(8,128)(2,1)} %get-tuple-element.44.normed.refs_0_), channel_id=1, source_target_pairs={{0,8},{1,9},{2,10},{3,11},{4,12},{5,13},{6,14},{7,15},{8,0},{9,1},... | collective-permute-start | bytes 1179656 | tf_op jit(solution)/shard_map/ppermute | solution.py:634
  44.6 12.0 %collective-permute-start.9 = (bf16[2,128,768]{2,1,0:T(8,128)(2,1)}, bf16[2,128,768]{2,1,0:T(8,128)(2,1)S(1)}, u32[]{:S(2)}, u32[]{:S(2)}) collective-permute-start(bf16[2,128,768]{2,1,0:T(8,128)(2,1)} %get-tuple-element.44.normed.refs_0_), channel_id=1, source_target_pairs={{0,4},{1,5},{2,6},{3,7},{4,0},{5,1},{6,2},{7,3},{8,12},{9,13},{10,... | collective-permute-start | bytes 1179656 | tf_op jit(solution)/shard_map/ppermute | solution.py:630
  45.9 25.4 %collective-permute-start.5 = (bf16[256,2048]{1,0:T(8,128)(2,1)}, bf16[256,2048]{1,0:T(8,128)(2,1)}, u32[]{:S(2)}, u32[]{:S(2)}) collective-permute-start(bf16[256,2048]{1,0:T(8,128)(2,1)} %get-tuple-element.43.rest_0_), channel_id=1, source_target_pairs={{0,64},{16,80},{32,96},{48,112},{64,0},{80,16},{96,32},{112,48},{1... | collective-permute-start | bytes 3145736 | tf_op jit(solution)/shard_map/ppermute | solution.py:638
  54.4 9.2 %collective-permute-start.13 = (bf16[2,128,768]{2,1,0:T(8,128)(2,1)S(1)}, bf16[2,128,768]{2,1,0:T(8,128)(2,1)S(1)}, u32[]{:S(2)}, u32[]{:S(2)}) collective-permute-start(bf16[2,128,768]{2,1,0:T(8,128)(2,1)S(1)} %copy-done.6), channel_id=1, source_target_pairs={{0,1},{1,0},{2,3},{3,2},{4,5},{5,4},{6,7},{7,6},{8,9},{9,8},{10,11... | collective-permute-start | bytes 1179656 | tf_op jit(solution)/shard_map/ppermute | solution.py:626
  57.7 11.7 %collective-permute-start.11 = (bf16[2,128,768]{2,1,0:T(8,128)(2,1)}, bf16[2,128,768]{2,1,0:T(8,128)(2,1)S(1)}, u32[]{:S(2)}, u32[]{:S(2)}) collective-permute-start(bf16[2,128,768]{2,1,0:T(8,128)(2,1)} %get-tuple-element.48.fence.refs_3_), channel_id=1, source_target_pairs={{0,2},{1,3},{2,4},{3,5},{4,6},{5,7},{6,0},{7,1},{8,10},{9,11},{10,... | collective-permute-start | bytes 1179656 | tf_op jit(solution)/shard_map/ppermute | solution.py:630
  59.3 11.9 %collective-permute-start.12 = (bf16[2,128,768]{2,1,0:T(8,128)(2,1)}, bf16[2,128,768]{2,1,0:T(8,128)(2,1)S(1)}, u32[]{:S(2)}, u32[]{:S(2)}) collective-permute-start(bf16[2,128,768]{2,1,0:T(8,128)(2,1)} %get-tuple-element.48.fence.refs_3_), channel_id=1, source_target_pairs={{0,6},{1,7},{2,0},{3,1},{4,2},{5,3},{6,4},{7,5},{8,14},{9,15},{10,... | collective-permute-start | bytes 1179656 | tf_op jit(solution)/shard_map/ppermute | solution.py:630
  59.3 12.7 %collective-permute-start.14 = (bf16[2,128,768]{2,1,0:T(8,128)(2,1)}, bf16[2,128,768]{2,1,0:T(8,128)(2,1)S(1)}, u32[]{:S(2)}, u32[]{:S(2)}) collective-permute-start(bf16[2,128,768]{2,1,0:T(8,128)(2,1)} %get-tuple-element.53.refs_0_), channel_id=1, source_target_pairs={{0,8},{1,9},{2,10},{3,11},{4,12},{5,13},{6,14},{7,15},{8,0},{9,1},... | collective-permute-start | bytes 1179656 | tf_op jit(solution)/shard_map/ppermute | solution.py:634
  63.6 16.1 %collective-permute-start.16 = (bf16[4,2,128,768]{3,2,1,0:T(8,128)(2,1)S(1)}, bf16[4,2,128,768]{3,2,1,0:T(8,128)(2,1)}, u32[]{:S(2)}, u32[]{:S(2)}) collective-permute-start(bf16[4,2,128,768]{3,2,1,0:T(8,128)(2,1)S(1)} %stack.119.own), channel_id=1, source_target_pairs={{0,1},{1,0},{2,3},{3,2},{4,5},{5,4},{6,7},{7,6},{8,9},{9,8},{10,11... | collective-permute-start | bytes 4718600 | tf_op jit(solution)/shard_map/ppermute | solution.py:626
  74.0 12.5 %collective-permute-start.15 = (bf16[4,2,128,768]{3,2,1,0:T(8,128)(2,1)S(1)}, bf16[4,2,128,768]{3,2,1,0:T(8,128)(2,1)}, u32[]{:S(2)}, u32[]{:S(2)}) collective-permute-start(bf16[4,2,128,768]{3,2,1,0:T(8,128)(2,1)S(1)} %stack.118.own), channel_id=1, source_target_pairs={{0,1},{1,0},{2,3},{3,2},{4,5},{5,4},{6,7},{7,6},{8,9},{9,8},{10,11... | collective-permute-start | bytes 4718600 | tf_op jit(solution)/shard_map/ppermute | solution.py:626
  75.5 28.7 %collective-permute-start.17 = (bf16[256,2048]{1,0:T(8,128)(2,1)}, bf16[256,2048]{1,0:T(8,128)(2,1)}, u32[]{:S(2)}, u32[]{:S(2)}) collective-permute-start(bf16[256,2048]{1,0:T(8,128)(2,1)} %get-tuple-element.58.rest_4_), channel_id=1, source_target_pairs={{0,32},{16,48},{32,64},{48,80},{64,96},{80,112},{96,0},{112,16},{1... | collective-permute-start | bytes 3145736 | tf_op jit(solution)/shard_map/ppermute | solution.py:638
  76.1 28.0 %collective-permute-start.18 = (bf16[256,2048]{1,0:T(8,128)(2,1)}, bf16[256,2048]{1,0:T(8,128)(2,1)}, u32[]{:S(2)}, u32[]{:S(2)}) collective-permute-start(bf16[256,2048]{1,0:T(8,128)(2,1)} %get-tuple-element.58.rest_4_), channel_id=1, source_target_pairs={{0,96},{16,112},{32,0},{48,16},{64,32},{80,48},{96,64},{112,80},{1... | collective-permute-start | bytes 3145736 | tf_op jit(solution)/shard_map/ppermute | solution.py:638
  78.1 26.0 %collective-permute-start.19 = (bf16[256,2048]{1,0:T(8,128)(2,1)}, bf16[256,2048]{1,0:T(8,128)(2,1)}, u32[]{:S(2)}, u32[]{:S(2)}) collective-permute-start(bf16[256,2048]{1,0:T(8,128)(2,1)} %get-tuple-element.59.rest_3_), channel_id=1, source_target_pairs={{0,16},{16,0},{32,48},{48,32},{64,80},{80,64},{96,112},{112,96},{1... | collective-permute-start | bytes 3145736 | tf_op jit(solution)/shard_map/ppermute | solution.py:642
  113.7 3.2 %collective-permute-start.20 = (bf16[8,2,128,128]{3,2,1,0:T(8,128)(2,1)S(1)}, bf16[8,2,128,128]{3,2,1,0:T(8,128)(2,1)S(1)}, u32[]{:S(2)}, u32[]{:S(2)}) collective-permute-start(bf16[8,2,128,128]{3,2,1,0:T(8,128)(2,1)S(1)} %get-tuple-element.64), channel_id=1, source_target_pairs={{0,1},{1,0},{2,3},{3,2},{4,5},{5,4},{6,7},{7,6},{8,9},{9,8},{10,11... | collective-permute-start | bytes 1572872 | tf_op jit(solution)/shard_map/ppermute | solution.py:626
  116.9 12.9 %copy-start.19 = (bf16[1024,4,128]{2,1,0:T(4,128)(2,1)S(1)}, bf16[1024,4,128]{2,1,0:T(4,128)(2,1)}, u32[]{:S(2)}) copy-start(bf16[1024,4,128]{2,1,0:T(4,128)(2,1)} %param.21) | copy-start | bytes 3145732
  122.2 3.3 %collective-permute-start.21 = (bf16[2,64,128]{2,1,0:T(8,128)(2,1)S(1)}, bf16[2,64,128]{2,1,0:T(8,128)(2,1)S(1)}, u32[]{:S(2)}, u32[]{:S(2)}) collective-permute-start(bf16[2,64,128]{2,1,0:T(8,128)(2,1)S(1)} %get-tuple-element.70), channel_id=1, source_target_pairs={{0,1},{1,2},{2,3},{3,4},{4,5},{5,6},{6,7},{7,8},{8,9},{9,10},{10,1... | collective-permute-start | bytes 98312 | tf_op jit(solution)/shard_map/ppermute | solution.py:622
  124.3 5.4 %collective-permute-start.22 = (bf16[2,64,128]{2,1,0:T(8,128)(2,1)S(1)}, bf16[2,64,128]{2,1,0:T(8,128)(2,1)S(1)}, u32[]{:S(2)}, u32[]{:S(2)}) collective-permute-start(bf16[2,64,128]{2,1,0:T(8,128)(2,1)S(1)} %get-tuple-element.71), channel_id=1, source_target_pairs={{0,15},{1,0},{2,1},{3,2},{4,3},{5,4},{6,5},{7,6},{8,7},{9,8},{10,9... | collective-permute-start | bytes 98312 | tf_op jit(solution)/shard_map/ppermute | solution.py:622
  (37 other events, 227.1 us)

commit v8 on v7

--- a/solution.py
+++ b/solution.py
@@ -122,8 +122,6 @@
     head = (index[0:1] - base).astype(F32)
     rows[low_rows:UP_ROWS] = jnp.broadcast_to(tail, (16, CA)).astype(BF16)
     rows[UP_ROWS + high_rows :] = jnp.broadcast_to(head, (16, CA)).astype(BF16)
-    for copy in loads:
-        copy.wait()
     stores = (
         (rows.at[pl.ds(0, UP_ROWS)], up),
         (rows.at[pl.ds(UP_ROWS, DOWN_ROWS)], down),
@@ -131,8 +129,13 @@
         (heads.at[core], joined.at[pl.ds(0, TOKS)]),
     )
     stores = [pltpu.make_async_copy(a, b, sems.at[4 + i]) for i, (a, b) in enumerate(stores)]
-    for copy in stores:
-        copy.start()
+    for copy in loads[1:]:
+        copy.wait()
+    stores[0].start()
+    stores[1].start()
+    loads[0].wait()
+    stores[2].start()
+    stores[3].start()
     for copy in stores:
         copy.wait()
 
@@ -376,7 +379,7 @@
             part = product[:, side * 128 : side * 128 + 128]
             group = 2 * pair + side
             queried = jnp.where(in_query, part * (HEAD**-0.5), 0.0).astype(BF16)
-            opened = jnp.where(in_gate, jax.nn.sigmoid(part), 0.0)
+            opened = jnp.where(in_gate, jax.nn.sigmoid(part), 0.0).astype(BF16)
             for seed in range(SEEDS):
                 at = slice(seed * 2 * TOKS, (seed + 1) * 2 * TOKS)
                 query[group, seed] = queried[at]
@@ -389,7 +392,7 @@
         grid=(1,),
         out_shape=(
             jax.ShapeDtypeStruct((GROUPS, SEEDS, 2 * TOKS, 128), BF16),
-            jax.ShapeDtypeStruct((GROUPS, SEEDS, 2 * TOKS, 128), F32),
+            jax.ShapeDtypeStruct((GROUPS, SEEDS, 2 * TOKS, 128), BF16),
         ),
         in_specs=[pl.BlockSpec(memory_space=pltpu.SMEM)]
         + vmem(2)
@@ -509,7 +512,7 @@
                 jnp.exp(scores[seed, :, cols] - tops[seed]).astype(BF16), key_value[0, seed, cols, :]
             )
             total = part if total is None else total + part
-        gated = (total / total[:, PAIR : PAIR + 1] * gate[0, seed]).astype(BF16)
+        gated = (total / total[:, PAIR : PAIR + 1] * gate[0, seed].astype(F32)).astype(BF16)
         own[0, seed] = gated[:TOKS]
         sent[0, seed] = gated[TOKS:]
 

time: 138 us -> 138 us (level)
  starting transfers between devices: 28 us -> 26.6 us
    pallas_call x2, Pallas kernels: 20.1 us -> 21.5 us  [attend(): pl.pallas_call(functools.partial(attend_kernel, count, len(before)), grid...]
    unnamed x77 -> x79, local copies, waits for them, and re-layouts: 11.2 us -> 12.1 us
where the time goes in v8:
time: 138 us; the launch traced here: 137 us
  Pallas kernels  71 us (51%)
  starting transfers between devices  26.6 us (19%)
  waiting for transfers between devices  25.3 us (18%)
  local copies, waits for them, and re-layouts  12.4 us (9%)
    pallas_call x2, Pallas kernels, attend(): pl.pallas_call(functools.partial(attend_kernel, count, len(before)), grid...  21.5 us
    pallas_call x2, Pallas kernels, keys(): pl.pallas_call(keys_kernel, grid=(1,), out_shape=jax.ShapeDtypeStruct((GR...  13.7 us
    unnamed x79, local copies, waits for them, and re-layouts  12.1 us
    ppermute x4, waiting for transfers between devices, along_tok(): return lax.ppermute(values, 'tok', [(i, (i + by) % 16) for i in range(16)])  9.91 us
    pallas_call x1, Pallas kernels, encode(): pl.pallas_call(encode_kernel, out_shape=(jax.ShapeDtypeStruct((SEEDS, ATO...  9.29 us
    ppermute x2, waiting for transfers between devices, along_z(): return lax.ppermute(values, 'seed', [(i, i ^ 1) for i in range(8)])  7.69 us
    ppermute x5, starting transfers between devices, along_y(): lax.ppermute(values, 'seed', [(i, (i + 2 * by) % 8) for i in range(8)])  7.39 us
    pallas_call x1, Pallas kernels, decode(): pl.pallas_call(decode_kernel, out_shape=jax.ShapeDtypeStruct((SEEDS * ATO...  7.08 us
  transfers between devices with their start and end apart: 23, of which 9 were waited for; matrix products, arithmetic and copies ran while one was open for 1% of the time, Pallas kernels for 32%

profile of v8, /device:TPU:7, one launch (start us, length us, event | category | flops | bytes accessed | tf_op | source)
XLA Modules:
  0.0 137.1 jit_solution(18038104705397885262)
XLA Ops:
  1.3 3.0 %pack.1 = (bf16[304,128]{1,0:T(8,128)(2,1)}, bf16[112,128]{1,0:T(8,128)(2,1)}, bf16[128,2048]{1,0:T(8,128)(2,1)}, bf16[256,2048]{1,0:T(8,128)(2,1)}) custom-call(s32[2]{0:T(128)} %pad_add_fusion.place, bf16[2048,128]{1,0:T(8,128)(2,1)} %bitcast.43, bf16[4096,128]{1,0:T(8,128)(2,1)} %bitcast.41, s32[8,128]{1,0:T(8,128)} %bitcast.38, ...), custom_call_target="tpu_custom_call" | custom-call | flops 1000000 | bytes 10000 | tf_op jit(solution)/shard_map/pack/pallas_call | solution.py:144
  5.1 1.5 %collective-permute-start = (bf16[304,128]{1,0:T(8,128)(2,1)}, bf16[304,128]{1,0:T(8,128)(2,1)S(1)}, u32[]{:S(2)}, u32[]{:S(2)}) collective-permute-start(bf16[304,128]{1,0:T(8,128)(2,1)} %get-tuple-element.37), channel_id=1, source_target_pairs={{0,1},{1,2},{2,3},{3,4},{4,5},{5,6},{6,7},{7,8},{8,9},{9,10},{10,1... | collective-permute-start | bytes 233480 | tf_op jit(solution)/shard_map/ppermute | solution.py:625
  6.6 5.6 %collective-permute-done.1.high = bf16[112,128]{1,0:T(8,128)(2,1)S(1)} collective-permute-done((bf16[112,128]{1,0:T(8,128)(2,1)}, bf16[112,128]{1,0:T(8,128)(2,1)S(1)}, u32[]{:S(2)}, u32[]{:S(2)}) %collective-permute-start.1) | collective-permute-done | bytes 28704 | tf_op jit(solution)/shard_map/ppermute | solution.py:625
  13.0 1.9 %join.1.fence.refs_3_ = bf16[256,2048]{1,0:T(8,128)(2,1)} custom-call(bf16[256,2048]{1,0:T(8,128)(2,1)} %get-tuple-element.39.joined, bf16[128,2048]{1,0:T(8,128)(2,1)} %copy-done.36, bf16[304,128]{1,0:T(8,128)(2,1)} %copy-done.22, bf16[112,128]{1,0:T(8,128)(2,1)} %copy-done.25), custom_call_target="tpu_custom_call", output_to_operand_aliasing={{}: (0, {})} | custom-call | flops 1000000 | bytes 10000 | tf_op jit(solution)/shard_map/join/pallas_call | solution.py:175
  14.9 3.4 %collective-permute-start.10 = (bf16[256,2048]{1,0:T(8,128)(2,1)}, bf16[256,2048]{1,0:T(8,128)(2,1)}, u32[]{:S(2)}, u32[]{:S(2)}) collective-permute-start(bf16[256,2048]{1,0:T(8,128)(2,1)} %join.1.fence.refs_3_), channel_id=1, source_target_pairs={{0,16},{16,0},{32,48},{48,32},{64,80},{80,64},{96,112},{112,96},{1... | collective-permute-start | bytes 3145736 | tf_op jit(solution)/shard_map/ppermute | solution.py:645
  21.1 9.3 %encode.1 = (bf16[2,1024,128]{2,1,0:T(8,128)(2,1)}, bf16[2,48,128]{2,1,0:T(8,128)(2,1)}, bf16[2,48,128]{2,1,0:T(8,128)(2,1)}, f32[2,128,768]{2,1,0:T(8,128)}, bf...) custom-call(s32[2]{0:T(128)} %pad_add_fusion.place, bf16[2048,128]{1,0:T(8,128)(2,1)} %bitcast.44, ...), custom_call_target="tpu_custom_call" | custom-call | flops 1000000 | bytes 10000 | tf_op jit(solution)/shard_map/encode/pallas_call | solution.py:247
  30.4 1.5 %collective-permute-start.8 = (bf16[2,128,768]{2,1,0:T(8,128)(2,1)}, bf16[2,128,768]{2,1,0:T(8,128)(2,1)S(1)}, u32[]{:S(2)}, u32[]{:S(2)}) collective-permute-start(bf16[2,128,768]{2,1,0:T(8,128)(2,1)} %get-tuple-element.45), channel_id=1, source_target_pairs={{0,6},{1,7},{2,0},{3,1},{4,2},{5,3},{6,4},{7,5},{8,14},{9,15},{10,... | collective-permute-start | bytes 1179656 | tf_op jit(solution)/shard_map/ppermute | solution.py:633
  31.8 7.7 %collective-permute-done.10.refs_5_ = bf16[256,2048]{1,0:T(8,128)(2,1)} collective-permute-done((bf16[256,2048]{1,0:T(8,128)(2,1)}, bf16[256,2048]{1,0:T(8,128)(2,1)}, u32[]{:S(2)}, u32[]{:S(2)}) %collective-permute-start.10) | collective-permute-done | bytes 1048608 | tf_op jit(solution)/shard_map/ppermute | solution.py:645
  39.5 3.4 %collective-permute-done.3.refs_0_ = bf16[256,2048]{1,0:T(8,128)(2,1)S(1)} collective-permute-done((bf16[256,2048]{1,0:T(8,128)(2,1)}, bf16[256,2048]{1,0:T(8,128)(2,1)S(1)}, u32[]{:S(2)}, u32[]{:S(2)}) %collective-permute-start.3) | collective-permute-done | bytes 1048608 | tf_op jit(solution)/shard_map/ppermute | solution.py:641
  46.0 2.0 %collective-permute-start.5 = (bf16[256,2048]{1,0:T(8,128)(2,1)}, bf16[256,2048]{1,0:T(8,128)(2,1)}, u32[]{:S(2)}, u32[]{:S(2)}) collective-permute-start(bf16[256,2048]{1,0:T(8,128)(2,1)} %get-tuple-element.43.rest_0_), channel_id=1, source_target_pairs={{0,64},{16,80},{32,96},{48,112},{64,0},{80,16},{96,32},{112,48},{1... | collective-permute-start | bytes 3145736 | tf_op jit(solution)/shard_map/ppermute | solution.py:641
  48.0 6.6 %spaced.1.refs_4_ = bf16[2,4,768,256]{3,2,1,0:T(8,128)(2,1)} custom-call(s32[2]{0:T(128)} %pad_add_fusion.place, bf16[768,3072]{1,0:T(8,128)(2,1)} %second.1, bf16[768,3072]{1,0:T(8,128)(2,1)} %second.1, bf16[256,2048]{1,0:T(8,128)(2,1)} %get-tuple-element.46.fence.rest_1_), custom_call_target="tpu_custom_call" | custom-call | flops 70000001024 | bytes 10000 | tf_op jit(solution)/shard_map/spaced/pallas_call | solution.py:353
  54.6 1.7 %collective-permute-start.13 = (bf16[2,128,768]{2,1,0:T(8,128)(2,1)S(1)}, bf16[2,128,768]{2,1,0:T(8,128)(2,1)S(1)}, u32[]{:S(2)}, u32[]{:S(2)}) collective-permute-start(bf16[2,128,768]{2,1,0:T(8,128)(2,1)S(1)} %copy-done.7), channel_id=1, source_target_pairs={{0,1},{1,0},{2,3},{3,2},{4,5},{5,4},{6,7},{7,6},{8,9},{9,8},{10,11... | collective-permute-start | bytes 1179656 | tf_op jit(solution)/shard_map/ppermute | solution.py:629
  57.9 1.5 %collective-permute-start.11 = (bf16[2,128,768]{2,1,0:T(8,128)(2,1)}, bf16[2,128,768]{2,1,0:T(8,128)(2,1)S(1)}, u32[]{:S(2)}, u32[]{:S(2)}) collective-permute-start(bf16[2,128,768]{2,1,0:T(8,128)(2,1)} %get-tuple-element.48.fence.refs_3_), channel_id=1, source_target_pairs={{0,2},{1,3},{2,4},{3,5},{4,6},{5,7},{6,0},{7,1},{8,10},{9,11},{10,... | collective-permute-start | bytes 1179656 | tf_op jit(solution)/shard_map/ppermute | solution.py:633
  64.7 2.5 %queries.1 = (bf16[8,2,256,128]{3,2,1,0:T(8,128)(2,1)S(1)}, bf16[8,2,256,128]{3,2,1,0:T(8,128)(2,1)S(1)}) custom-call(s32[2]{0:T(128)S(1)} %copy-done.33, bf16[2,128,768]{2,1,0:T(8,128)(2,1)S(1)} %copy-done.7, bf16[2,128,768]{2,1,0:T(8,128)(2,1)S(1)} %collective-permute-done.13.other, bf16[2,4,768,256]{3,2,1,0:T(8,128)(2,1)} %get-tuple-element.49.weight, ...), custom_call_target="tpu_custom_call" | custom-call | flops 1000000 | bytes 10000 | tf_op jit(solution)/shard_map/queries/pallas_call | solution.py:390
  69.2 2.1 %collective-permute-done.12.refs_3_ = bf16[2,128,768]{2,1,0:T(8,128)(2,1)S(1)} collective-permute-done((bf16[2,128,768]{2,1,0:T(8,128)(2,1)}, bf16[2,128,768]{2,1,0:T(8,128)(2,1)S(1)}, u32[]{:S(2)}, u32[]{:S(2)}) %collective-permute-start.12) | collective-permute-done | bytes 393248 | tf_op jit(solution)/shard_map/ppermute | solution.py:633
  76.3 2.0 %collective-permute-start.18 = (bf16[256,2048]{1,0:T(8,128)(2,1)}, bf16[256,2048]{1,0:T(8,128)(2,1)}, u32[]{:S(2)}, u32[]{:S(2)}) collective-permute-start(bf16[256,2048]{1,0:T(8,128)(2,1)} %get-tuple-element.58.rest_4_), channel_id=1, source_target_pairs={{0,96},{16,112},{32,0},{48,16},{64,32},{80,48},{96,64},{112,80},{1... | collective-permute-start | bytes 3145736 | tf_op jit(solution)/shard_map/ppermute | solution.py:641
  79.9 6.8 %keys.2.rest_0_ = bf16[8,2,2048,128]{3,2,1,0:T(8,128)(2,1)} custom-call(s32[10]{0:T(128)S(1)} %concatenate.9.place, bf16[4,2,128,768]{3,2,1,0:T(8,128)(2,1)S(1)} %stack.119.own, bf16[4,2,128,768]{3,2,1,0:T(8,128)(2,1)} %collective-permute-done.16.received, bf16[2,4,768,256]{3,2,1,0:T(8,128)(2,1)} %get-tuple-element.49.weight), custom_call_target="tpu_custom_call" | custom-call | flops 1000000 | bytes 10000 | tf_op jit(solution)/shard_map/keys/pallas_call | solution.py:456
  86.7 7.0 %keys.3.key_value = bf16[8,2,2048,128]{3,2,1,0:T(8,128)(2,1)} custom-call(s32[10]{0:T(128)S(1)} %concatenate.8.place, bf16[4,2,128,768]{3,2,1,0:T(8,128)(2,1)S(1)} %stack.118.own, bf16[4,2,128,768]{3,2,1,0:T(8,128)(2,1)} %collective-permute-done.15.received, bf16[2,4,768,256]{3,2,1,0:T(8,128)(2,1)} %get-tuple-element.49.weight, ...), custom_call_target="tpu_custom_call", output_to_operand_aliasing={{}: (4, {})} | custom-call | flops 1000000 | bytes 10000 | tf_op jit(solution)/shard_map/keys/pallas_call | solution.py:456
  93.7 12.0 %attend.2 = (bf16[8,2,128,128]{3,2,1,0:T(8,128)(2,1)S(1)}, bf16[8,2,128,128]{3,2,1,0:T(8,128)(2,1)S(1)}) custom-call(s32[5]{0:T(128)S(1)} %stack.117.group_ids, bf16[8,2,256,128]{3,2,1,0:T(8,128)(2,1)S(1)} %copy-done.1, bf16[8,2,256,128]{3,2,1,0:T(8,128)(2,1)S(1)} %copy-done.3, bf16[8,2,2048,128]{3,2,1,0:T(8,128)(2,1)} %keys.3.key_value, ...), custom_call_target="tpu_custom_call" | custom-call | flops 1000000 | bytes 10000 | tf_op jit(solution)/shard_map/attend/pallas_call | solution.py:543
  105.8 9.5 %attend.3 = (bf16[8,2,128,128]{3,2,1,0:T(8,128)(2,1)S(1)}, bf16[8,2,128,128]{3,2,1,0:T(8,128)(2,1)S(1)}) custom-call(s32[3]{0:T(128)S(1)} %pad_add_fusion.1.group_ids, bf16[8,2,256,128]{3,2,1,0:T(8,128)(2,1)S(1)} %copy-done.1, bf16[8,2,256,128]{3,2,1,0:T(8,128)(2,1)S(1)} %copy-done.3, ...), custom_call_target="tpu_custom_call", output_to_operand_aliasing={{0}: (7, {}), {1}: (8, {})} | custom-call | flops 1000000 | bytes 10000 | tf_op jit(solution)/shard_map/attend/pallas_call | solution.py:543
  116.7 1.5 %collective-permute-done.20.received = bf16[8,2,128,128]{3,2,1,0:T(8,128)(2,1)S(1)} collective-permute-done((bf16[8,2,128,128]{3,2,1,0:T(8,128)(2,1)S(1)}, bf16[8,2,128,128]{3,2,1,0:T(8,128)(2,1)S(1)}, u32[]{:S(2)}, u32[]{:S(2)}) %collective-permute-start.20) | collective-permute-done | bytes 524320 | tf_op jit(solution)/shard_map/ppermute | solution.py:629
  118.4 5.2 %finish.1 = (bf16[2,128,768]{2,1,0:T(8,128)(2,1)S(1)}, bf16[2,128,128]{2,1,0:T(8,128)(2,1)S(1)}, bf16[2,64,128]{2,1,0:T(8,128)(2,1)S(1)}, bf16[2,64,128]{2,1,0:T(8,128)(2,1)S(1)}) custom-call(f32[2,128,768]{2,1,0:T(8,128)S(1)} %copy-done.21, bf16[8,2,128,128]{3,2,1,0:T(8,128)(2,1)S(1)} %get-tuple-element.63.own, ...), custom_call_target="tpu_custom_call" | custom-call | flops 1000000 | bytes 10000 | tf_op jit(solution)/shard_map/finish/pallas_call | solution.py:600
  125.7 4.3 %collective-permute-done.22.edge_high = bf16[2,64,128]{2,1,0:T(8,128)(2,1)S(1)} collective-permute-done((bf16[2,64,128]{2,1,0:T(8,128)(2,1)S(1)}, bf16[2,64,128]{2,1,0:T(8,128)(2,1)S(1)}, u32[]{:S(2)}, u32[]{:S(2)}) %collective-permute-start.22) | collective-permute-done | bytes 32800 | tf_op jit(solution)/shard_map/ppermute | solution.py:625
  130.0 7.1 %decode.1 = bf16[2048,128]{1,0:T(8,128)(2,1)} custom-call(s32[2]{0:T(128)S(1)} %copy-done.33, bf16[2,1024,128]{2,1,0:T(8,128)(2,1)S(1)} %copy-done.24, bf16[2,128,128]{2,1,0:T(8,128)(2,1)S(1)} %get-tuple-element.69.spread, bf16[2,64,128]{2,1,0:T(8,128)(2,1)S(1)} %collective-permute-done.21.edge_low, ...), custom_call_target="tpu_custom_call" | custom-call | flops 1000000 | bytes 10000 | tf_op jit(solution)/shard_map/decode/pallas_call | solution.py:313
  (123 shorter events, 27.0 us)
Async XLA Ops:
  4.3 7.9 %collective-permute-start.2 = (bf16[128,2048]{1,0:T(8,128)(2,1)}, bf16[128,2048]{1,0:T(8,128)(2,1)S(1)}, u32[]{:S(2)}, u32[]{:S(2)}) collective-permute-start(bf16[128,2048]{1,0:T(8,128)(2,1)} %get-tuple-element.40), channel_id=1, source_target_pairs={{0,1},{1,0},{2,3},{3,2},{4,5},{5,4},{6,7},{7,6},{8,9},{9,8},{10,11... | collective-permute-start | bytes 1572872 | tf_op jit(solution)/shard_map/ppermute | solution.py:629
  5.1 7.1 %collective-permute-start = (bf16[304,128]{1,0:T(8,128)(2,1)}, bf16[304,128]{1,0:T(8,128)(2,1)S(1)}, u32[]{:S(2)}, u32[]{:S(2)}) collective-permute-start(bf16[304,128]{1,0:T(8,128)(2,1)} %get-tuple-element.37), channel_id=1, source_target_pairs={{0,1},{1,2},{2,3},{3,4},{4,5},{5,6},{6,7},{7,8},{8,9},{9,10},{10,1... | collective-permute-start | bytes 233480 | tf_op jit(solution)/shard_map/ppermute | solution.py:625
  6.6 5.6 %collective-permute-start.1 = (bf16[112,128]{1,0:T(8,128)(2,1)}, bf16[112,128]{1,0:T(8,128)(2,1)S(1)}, u32[]{:S(2)}, u32[]{:S(2)}) collective-permute-start(bf16[112,128]{1,0:T(8,128)(2,1)} %get-tuple-element.38), channel_id=1, source_target_pairs={{0,15},{1,0},{2,1},{3,2},{4,3},{5,4},{6,5},{7,6},{8,7},{9,8},{10,9... | collective-permute-start | bytes 86024 | tf_op jit(solution)/shard_map/ppermute | solution.py:625
  14.9 24.6 %collective-permute-start.10 = (bf16[256,2048]{1,0:T(8,128)(2,1)}, bf16[256,2048]{1,0:T(8,128)(2,1)}, u32[]{:S(2)}, u32[]{:S(2)}) collective-permute-start(bf16[256,2048]{1,0:T(8,128)(2,1)} %join.1.fence.refs_3_), channel_id=1, source_target_pairs={{0,16},{16,0},{32,48},{48,32},{64,80},{80,64},{96,112},{112,96},{1... | collective-permute-start | bytes 3145736 | tf_op jit(solution)/shard_map/ppermute | solution.py:645
  18.3 24.6 %collective-permute-start.3 = (bf16[256,2048]{1,0:T(8,128)(2,1)}, bf16[256,2048]{1,0:T(8,128)(2,1)S(1)}, u32[]{:S(2)}, u32[]{:S(2)}) collective-permute-start(bf16[256,2048]{1,0:T(8,128)(2,1)} %join.1.fence.refs_3_), channel_id=1, source_target_pairs={{0,32},{16,48},{32,64},{48,80},{64,96},{80,112},{96,0},{112,16},{1... | collective-permute-start | bytes 3145736 | tf_op jit(solution)/shard_map/ppermute | solution.py:641
  19.6 23.4 %collective-permute-start.4 = (bf16[256,2048]{1,0:T(8,128)(2,1)}, bf16[256,2048]{1,0:T(8,128)(2,1)S(1)}, u32[]{:S(2)}, u32[]{:S(2)}) collective-permute-start(bf16[256,2048]{1,0:T(8,128)(2,1)} %join.1.fence.refs_3_), channel_id=1, source_target_pairs={{0,96},{16,112},{32,0},{48,16},{64,32},{80,48},{96,64},{112,80},{1... | collective-permute-start | bytes 3145736 | tf_op jit(solution)/shard_map/ppermute | solution.py:641
  30.4 24.2 %collective-permute-start.7 = (bf16[2,128,768]{2,1,0:T(8,128)(2,1)}, bf16[2,128,768]{2,1,0:T(8,128)(2,1)S(1)}, u32[]{:S(2)}, u32[]{:S(2)}) collective-permute-start(bf16[2,128,768]{2,1,0:T(8,128)(2,1)} %get-tuple-element.45), channel_id=1, source_target_pairs={{0,2},{1,3},{2,4},{3,5},{4,6},{5,7},{6,0},{7,1},{8,10},{9,11},{10,... | collective-permute-start | bytes 1179656 | tf_op jit(solution)/shard_map/ppermute | solution.py:633
  30.4 25.9 %collective-permute-start.8 = (bf16[2,128,768]{2,1,0:T(8,128)(2,1)}, bf16[2,128,768]{2,1,0:T(8,128)(2,1)S(1)}, u32[]{:S(2)}, u32[]{:S(2)}) collective-permute-start(bf16[2,128,768]{2,1,0:T(8,128)(2,1)} %get-tuple-element.45), channel_id=1, source_target_pairs={{0,6},{1,7},{2,0},{3,1},{4,2},{5,3},{6,4},{7,5},{8,14},{9,15},{10,... | collective-permute-start | bytes 1179656 | tf_op jit(solution)/shard_map/ppermute | solution.py:633
  44.3 12.0 %collective-permute-start.6 = (bf16[2,128,768]{2,1,0:T(8,128)(2,1)}, bf16[2,128,768]{2,1,0:T(8,128)(2,1)S(1)}, u32[]{:S(2)}, u32[]{:S(2)}) collective-permute-start(bf16[2,128,768]{2,1,0:T(8,128)(2,1)} %get-tuple-element.44.normed.refs_0_), channel_id=1, source_target_pairs={{0,8},{1,9},{2,10},{3,11},{4,12},{5,13},{6,14},{7,15},{8,0},{9,1},... | collective-permute-start | bytes 1179656 | tf_op jit(solution)/shard_map/ppermute | solution.py:637
  44.8 12.0 %collective-permute-start.9 = (bf16[2,128,768]{2,1,0:T(8,128)(2,1)}, bf16[2,128,768]{2,1,0:T(8,128)(2,1)S(1)}, u32[]{:S(2)}, u32[]{:S(2)}) collective-permute-start(bf16[2,128,768]{2,1,0:T(8,128)(2,1)} %get-tuple-element.44.normed.refs_0_), channel_id=1, source_target_pairs={{0,4},{1,5},{2,6},{3,7},{4,0},{5,1},{6,2},{7,3},{8,12},{9,13},{10,... | collective-permute-start | bytes 1179656 | tf_op jit(solution)/shard_map/ppermute | solution.py:633
  46.0 25.4 %collective-permute-start.5 = (bf16[256,2048]{1,0:T(8,128)(2,1)}, bf16[256,2048]{1,0:T(8,128)(2,1)}, u32[]{:S(2)}, u32[]{:S(2)}) collective-permute-start(bf16[256,2048]{1,0:T(8,128)(2,1)} %get-tuple-element.43.rest_0_), channel_id=1, source_target_pairs={{0,64},{16,80},{32,96},{48,112},{64,0},{80,16},{96,32},{112,48},{1... | collective-permute-start | bytes 3145736 | tf_op jit(solution)/shard_map/ppermute | solution.py:641
  54.6 9.2 %collective-permute-start.13 = (bf16[2,128,768]{2,1,0:T(8,128)(2,1)S(1)}, bf16[2,128,768]{2,1,0:T(8,128)(2,1)S(1)}, u32[]{:S(2)}, u32[]{:S(2)}) collective-permute-start(bf16[2,128,768]{2,1,0:T(8,128)(2,1)S(1)} %copy-done.7), channel_id=1, source_target_pairs={{0,1},{1,0},{2,3},{3,2},{4,5},{5,4},{6,7},{7,6},{8,9},{9,8},{10,11... | collective-permute-start | bytes 1179656 | tf_op jit(solution)/shard_map/ppermute | solution.py:629
  57.9 11.3 %collective-permute-start.11 = (bf16[2,128,768]{2,1,0:T(8,128)(2,1)}, bf16[2,128,768]{2,1,0:T(8,128)(2,1)S(1)}, u32[]{:S(2)}, u32[]{:S(2)}) collective-permute-start(bf16[2,128,768]{2,1,0:T(8,128)(2,1)} %get-tuple-element.48.fence.refs_3_), channel_id=1, source_target_pairs={{0,2},{1,3},{2,4},{3,5},{4,6},{5,7},{6,0},{7,1},{8,10},{9,11},{10,... | collective-permute-start | bytes 1179656 | tf_op jit(solution)/shard_map/ppermute | solution.py:633
  59.4 11.9 %collective-permute-start.12 = (bf16[2,128,768]{2,1,0:T(8,128)(2,1)}, bf16[2,128,768]{2,1,0:T(8,128)(2,1)S(1)}, u32[]{:S(2)}, u32[]{:S(2)}) collective-permute-start(bf16[2,128,768]{2,1,0:T(8,128)(2,1)} %get-tuple-element.48.fence.refs_3_), channel_id=1, source_target_pairs={{0,6},{1,7},{2,0},{3,1},{4,2},{5,3},{6,4},{7,5},{8,14},{9,15},{10,... | collective-permute-start | bytes 1179656 | tf_op jit(solution)/shard_map/ppermute | solution.py:633
  59.4 12.7 %collective-permute-start.14 = (bf16[2,128,768]{2,1,0:T(8,128)(2,1)}, bf16[2,128,768]{2,1,0:T(8,128)(2,1)S(1)}, u32[]{:S(2)}, u32[]{:S(2)}) collective-permute-start(bf16[2,128,768]{2,1,0:T(8,128)(2,1)} %get-tuple-element.53.refs_0_), channel_id=1, source_target_pairs={{0,8},{1,9},{2,10},{3,11},{4,12},{5,13},{6,14},{7,15},{8,0},{9,1},... | collective-permute-start | bytes 1179656 | tf_op jit(solution)/shard_map/ppermute | solution.py:637
  63.8 16.1 %collective-permute-start.16 = (bf16[4,2,128,768]{3,2,1,0:T(8,128)(2,1)S(1)}, bf16[4,2,128,768]{3,2,1,0:T(8,128)(2,1)}, u32[]{:S(2)}, u32[]{:S(2)}) collective-permute-start(bf16[4,2,128,768]{3,2,1,0:T(8,128)(2,1)S(1)} %stack.119.own), channel_id=1, source_target_pairs={{0,1},{1,0},{2,3},{3,2},{4,5},{5,4},{6,7},{7,6},{8,9},{9,8},{10,11... | collective-permute-start | bytes 4718600 | tf_op jit(solution)/shard_map/ppermute | solution.py:629
  74.2 12.5 %collective-permute-start.15 = (bf16[4,2,128,768]{3,2,1,0:T(8,128)(2,1)S(1)}, bf16[4,2,128,768]{3,2,1,0:T(8,128)(2,1)}, u32[]{:S(2)}, u32[]{:S(2)}) collective-permute-start(bf16[4,2,128,768]{3,2,1,0:T(8,128)(2,1)S(1)} %stack.118.own), channel_id=1, source_target_pairs={{0,1},{1,0},{2,3},{3,2},{4,5},{5,4},{6,7},{7,6},{8,9},{9,8},{10,11... | collective-permute-start | bytes 4718600 | tf_op jit(solution)/shard_map/ppermute | solution.py:629
  75.6 30.1 %collective-permute-start.17 = (bf16[256,2048]{1,0:T(8,128)(2,1)}, bf16[256,2048]{1,0:T(8,128)(2,1)}, u32[]{:S(2)}, u32[]{:S(2)}) collective-permute-start(bf16[256,2048]{1,0:T(8,128)(2,1)} %get-tuple-element.58.rest_4_), channel_id=1, source_target_pairs={{0,32},{16,48},{32,64},{48,80},{64,96},{80,112},{96,0},{112,16},{1... | collective-permute-start | bytes 3145736 | tf_op jit(solution)/shard_map/ppermute | solution.py:641
  76.3 29.4 %collective-permute-start.18 = (bf16[256,2048]{1,0:T(8,128)(2,1)}, bf16[256,2048]{1,0:T(8,128)(2,1)}, u32[]{:S(2)}, u32[]{:S(2)}) collective-permute-start(bf16[256,2048]{1,0:T(8,128)(2,1)} %get-tuple-element.58.rest_4_), channel_id=1, source_target_pairs={{0,96},{16,112},{32,0},{48,16},{64,32},{80,48},{96,64},{112,80},{1... | collective-permute-start | bytes 3145736 | tf_op jit(solution)/shard_map/ppermute | solution.py:641
  78.3 27.4 %collective-permute-start.19 = (bf16[256,2048]{1,0:T(8,128)(2,1)}, bf16[256,2048]{1,0:T(8,128)(2,1)}, u32[]{:S(2)}, u32[]{:S(2)}) collective-permute-start(bf16[256,2048]{1,0:T(8,128)(2,1)} %get-tuple-element.59.rest_3_), channel_id=1, source_target_pairs={{0,16},{16,0},{32,48},{48,32},{64,80},{80,64},{96,112},{112,96},{1... | collective-permute-start | bytes 3145736 | tf_op jit(solution)/shard_map/ppermute | solution.py:645
  105.7 12.6 %slice-start = ((s8[4718592]{0:T(1024)(128)(4,1)}), s8[4194304]{0:T(1024)(128)(4,1)S(1)}, s32[]{:S(2)}) async-start(s8[4718592]{0:T(1024)(128)(4,1)} %bitcast.33), calls=%async_computation | async-start | bytes 8388608
  115.3 3.0 %collective-permute-start.20 = (bf16[8,2,128,128]{3,2,1,0:T(8,128)(2,1)S(1)}, bf16[8,2,128,128]{3,2,1,0:T(8,128)(2,1)S(1)}, u32[]{:S(2)}, u32[]{:S(2)}) collective-permute-start(bf16[8,2,128,128]{3,2,1,0:T(8,128)(2,1)S(1)} %get-tuple-element.64), channel_id=1, source_target_pairs={{0,1},{1,0},{2,3},{3,2},{4,5},{5,4},{6,7},{7,6},{8,9},{9,8},{10,11... | collective-permute-start | bytes 1572872 | tf_op jit(solution)/shard_map/ppermute | solution.py:629
  123.6 2.1 %collective-permute-start.21 = (bf16[2,64,128]{2,1,0:T(8,128)(2,1)S(1)}, bf16[2,64,128]{2,1,0:T(8,128)(2,1)S(1)}, u32[]{:S(2)}, u32[]{:S(2)}) collective-permute-start(bf16[2,64,128]{2,1,0:T(8,128)(2,1)S(1)} %get-tuple-element.70), channel_id=1, source_target_pairs={{0,1},{1,2},{2,3},{3,4},{4,5},{5,6},{6,7},{7,8},{8,9},{9,10},{10,1... | collective-permute-start | bytes 98312 | tf_op jit(solution)/shard_map/ppermute | solution.py:625
  124.5 5.4 %collective-permute-start.22 = (bf16[2,64,128]{2,1,0:T(8,128)(2,1)S(1)}, bf16[2,64,128]{2,1,0:T(8,128)(2,1)S(1)}, u32[]{:S(2)}, u32[]{:S(2)}) collective-permute-start(bf16[2,64,128]{2,1,0:T(8,128)(2,1)S(1)} %get-tuple-element.71), channel_id=1, source_target_pairs={{0,15},{1,0},{2,1},{3,2},{4,3},{5,4},{6,5},{7,6},{8,7},{9,8},{10,9... | collective-permute-start | bytes 98312 | tf_op jit(solution)/shard_map/ppermute | solution.py:625
  (38 other events, 227.2 us)
